TPU v7x, 256 devices: a whole 4x4x8 slice. The times are simulated.
256 devices in a mesh: gx: 16 (over y, x), gy: 16 (over z, core).
Axes of the slice: x: 4, y: 4, z: 8, core: 2. Of those that a mesh axis runs over, the one named last changes fastest.
Arguments:
- labels: int32 [32, 256, 2048], P(None, 'gx', 'gy'), may hold values from 0 to 1
- guess: float32 [3, 32, 256, 2048], P(None, None, 'gx', 'gy'), may hold values from -6 to 6
Outputs:
- solution: float32 [3, 32, 256, 2048], P(None, None, 'gx', 'gy')
All inputs are finite; a program needn't handle non-finite values.
Results may differ from a plain program's by a relative error of at most 0.0003.
Values sent between devices are 32-bit elements; how exact they have to be, the bound alone decides.
No kernel may reach another device: no remote copies, remote signals or barrier semaphores. Data moves between devices by JAX's collectives and lax.ppermute only.
A program may use at most 128 MiB of HBM per device.

v0:
```python
import jax
import jax.numpy as jnp
from jax import lax
from jax.sharding import PartitionSpec as P

LEVELS = 4
SWEEPS = 2
COARSE_SWEEPS = 6


SOLID = 0.1
OMEGA = 0.8


def padded_2(x, sides, width):
    for axis, dim in sides:
        count, length = (lax.axis_size(axis), x.shape[dim])
        up = [(i, (i + 1) % count) for i in range(count - 1)]
        down = [(j, i) for i, j in up]
        last = lax.slice_in_dim(x, length - width, length, axis=dim)
        leading = lax.slice_in_dim(x, 0, width, axis=dim)
        before = lax.ppermute(last, axis, up)
        after = lax.ppermute(leading, axis, down)
        x = jnp.concatenate([before, x, after], axis=dim)
    return x


def harmonic(first, second):
    return 2.0 * first * second / (first + second)


def face_weights(coef, padded, scale):
    return (
        scale * harmonic(coef, padded[1:-1, :-2, 1:-1]),
        scale * harmonic(coef, padded[1:-1, 2:, 1:-1]),
        scale * harmonic(coef, padded[1:-1, 1:-1, :-2]),
        scale * harmonic(coef, padded[1:-1, 1:-1, 2:]),
        scale * harmonic(coef, padded[:-2, 1:-1, 1:-1]),
        scale * harmonic(coef, padded[2:, 1:-1, 1:-1]),
    )


def operate(weights, padded, field):
    total = weights[0] * (field - padded[..., 1:-1, :-2, 1:-1])
    total = total + weights[1] * (field - padded[..., 1:-1, 2:, 1:-1])
    total = total + weights[2] * (field - padded[..., 1:-1, 1:-1, :-2])
    total = total + weights[3] * (field - padded[..., 1:-1, 1:-1, 2:])
    total = total + weights[4] * (field - padded[..., :-2, 1:-1, 1:-1])
    total = total + weights[5] * (field - padded[..., 2:, 1:-1, 1:-1])
    return total


def restrict(field):
    shape = field.shape
    blocks = field.reshape(shape[:-3] + (shape[-3] // 2, 2, shape[-2] // 2, 2, shape[-1] // 2, 2))
    return jnp.mean(blocks, axis=(-5, -3, -1))


def prolong(field):
    return jnp.repeat(jnp.repeat(jnp.repeat(field, 2, axis=-3), 2, axis=-2), 2, axis=-1)


def shared_field_pad(field):
    padded = padded_2(field, (("gx", 2), ("gy", 3)), 1)
    return jnp.pad(padded, ((0, 0), (1, 1), (0, 0), (0, 0)))


def shared_coef_pad(coef):
    padded = padded_2(coef - 1.0, (("gx", 1), ("gy", 2)), 1) + 1.0
    return jnp.pad(padded, ((1, 1), (0, 0), (0, 0)), constant_values=1.0)


def whole_field_pad(field):
    return jnp.pad(field, ((0, 0), (1, 1), (1, 1), (1, 1)))


def whole_coef_pad(coef):
    return jnp.pad(coef, 1, constant_values=1.0)


def smooth_level(coef, rhs, scale, count, coef_pad, field_pad, aggregate):
    weights = face_weights(coef, coef_pad(coef), scale)
    diag = sum(weights)
    correction = OMEGA * rhs / diag
    for step in range(count - 1):
        correction = (
            correction + OMEGA * (rhs - operate(weights, field_pad(correction), correction)) / diag
        )
    left = rhs - operate(weights, field_pad(correction), correction)
    if aggregate:
        shift = jnp.sum(left, axis=(1, 2, 3), keepdims=True) / jnp.sum(diag)
        return (correction + shift, left)
    return (correction, left)


def gather_grid(rhs, coef):
    rows = (
        lax.all_gather(rhs, "gy", axis=3, tiled=True),
        lax.all_gather(coef, "gy", axis=2, tiled=True),
    )
    whole = (
        lax.all_gather(rows[0], "gx", axis=2, tiled=True),
        lax.all_gather(rows[1], "gx", axis=1, tiled=True),
    )
    return (whole[0], whole[1])


def local(labels, guess):
    coef = jnp.where(labels == 1, 1.0, SOLID).astype(jnp.float32)
    weights = face_weights(coef, shared_coef_pad(coef), 1.0)
    source = jnp.stack([weights[1] - weights[0], weights[3] - weights[2], weights[5] - weights[4]])
    diag = sum(weights)
    field = guess
    for step in range(SWEEPS):
        field = field + OMEGA * (source - operate(weights, shared_field_pad(field), field)) / diag
    resid = source - operate(weights, shared_field_pad(field), field)
    top = LEVELS
    corrections = []
    for level in range(1, top):
        coef = restrict(coef)
        rhs = restrict(resid)
        correction, resid = smooth_level(
            coef, rhs, 0.25**level, SWEEPS, shared_coef_pad, shared_field_pad, False
        )
        corrections.append(correction)
    coef = restrict(coef)
    rhs = restrict(resid)
    block_x, block_y = (coef.shape[1], coef.shape[2])
    whole_rhs, whole_coef = gather_grid(rhs, coef)
    level = 4
    count = COARSE_SWEEPS
    correction, whole_resid = smooth_level(
        whole_coef, whole_rhs, 0.25**level, count, whole_coef_pad, whole_field_pad, level == LEVELS
    )
    upper = [correction]
    total = upper[-1]
    start_x = lax.axis_index("gx") * block_x
    start_y = lax.axis_index("gy") * block_y
    zero = jnp.zeros((), jnp.int32)
    total = lax.dynamic_slice(
        total, (zero, zero, start_x, start_y), (3, total.shape[1], block_x, block_y)
    )
    for finer in reversed(corrections):
        total = finer + prolong(total)
    return field + prolong(total)


def solution(mesh):
    return jax.shard_map(
        local,
        mesh=mesh,
        in_specs=(P(None, "gx", "gy"), P(None, None, "gx", "gy")),
        out_specs=P(None, None, "gx", "gy"),
        check_vma=False,
    )
```

profile of v0, /device:TPU:1, one launch (start us, length us, event | category | flops | bytes accessed | tf_op | source)
XLA Modules:
  0.0 442.7 jit_solution(17430389288480116197)
XLA Ops:
  3.1 5.2 %collective-permute-start.4 = (f32[3,32,1,128]{3,2,1,0:T(1,128)}, f32[3,32,1,128]{3,2,1,0:T(1,128)}, u32[]{:S(2)}, u32[]{:S(2)}) collective-permute-start(f32[3,32,1,128]{3,2,1,0:T(1,128)} %get-tuple-element.61), channel_id=1, source_target_pairs={{0,16},{16,32},{32,48},{48,64},{64,80},{80,96},{96,112},{112,128},... | collective-permute-start | bytes 147464 | tf_op jit(solution)/shard_map/ppermute | solution.py:22
  9.3 18.1 %reshape.122 = f32[16,2,8,2,64,2]{5,4,3,2,1,0:T(8,128)} reshape(f32[32,16,128]{2,1,0:T(8,128)S(1)} %get-tuple-element.34) | data formatting | bytes 524288 | tf_op jit(solution)/shard_map/reshape | solution.py:55
  27.4 7.0 %reduce_sum.105 = f32[16,8,64]{2,1,0:T(8,128)S(1)} reduce(f32[16,2,8,2,64,2]{5,4,3,2,1,0:T(8,128)} %reshape.122, f32[]{:T(128)} %constant.27.clone.1), dimensions={1,3,5}, to_apply=%region_1.2 | reduce | flops 57344 | bytes 294916 | tf_op jit(solution)/shard_map/reduce_sum | solution.py:56
  35.7 4.0 collective-permute-start.16
  41.4 5.7 %collective-permute-start.19 = (f32[16,10,1]{2,1,0:T(8,128)S(1)}, f32[16,10,1]{2,1,0:T(8,128)S(1)}, u32[]{:S(2)}, u32[]{:S(2)}) collective-permute-start(f32[16,10,1]{2,1,0:T(8,128)S(1)} %get-tuple-element.80), channel_id=1, source_target_pairs={{1,0},{2,1},{3,2},{4,3},{5,4},{6,5},{7,6},{8,7},{9,8},{10,9},{11,1... | collective-permute-start | bytes 1928 | tf_op jit(solution)/shard_map/ppermute | solution.py:23
  49.5 4.3 collective-permute-start
  65.5 4.0 collective-permute-start.28
  93.4 5.9 %collective-permute-start.8 = (f32[3,32,1,128]{3,2,1,0:T(1,128)S(1)}, f32[3,32,1,128]{3,2,1,0:T(1,128)S(1)}, u32[]{:S(2)}, u32[]{:S(2)}) collective-permute-start(f32[3,32,1,128]{3,2,1,0:T(1,128)S(1)} %get-tuple-element.59), channel_id=1, source_target_pairs={{0,16},{16,32},{32,48},{48,64},{64,80},{80,96},{96,112},{112,128},... | collective-permute-start | bytes 147464 | tf_op jit(solution)/shard_map/ppermute | solution.py:22
  105.8 4.6 %collective-permute-start.10 = (f32[3,32,18,1]{1,3,2,0:T(1,128)S(1)}, f32[3,32,18,1]{1,3,2,0:T(1,128)S(1)}, u32[]{:S(2)}, u32[]{:S(2)}) collective-permute-start(f32[3,32,18,1]{1,3,2,0:T(1,128)S(1)} %copy.418), channel_id=1, source_target_pairs={{0,1},{1,2},{2,3},{3,4},{4,5},{5,6},{6,7},{7,8},{8,9},{9,10},{10,1... | collective-permute-start | bytes 20744 | tf_op jit(solution)/shard_map/ppermute | solution.py:22
  113.0 3.6 collective-permute-start.30
  124.9 6.4 %collective-permute-start.12 = (f32[3,32,1,128]{3,2,1,0:T(1,128)S(1)}, f32[3,32,1,128]{3,2,1,0:T(1,128)S(1)}, u32[]{:S(2)}, u32[]{:S(2)}) collective-permute-start(f32[3,32,1,128]{3,2,1,0:T(1,128)S(1)} %get-tuple-element.57), channel_id=1, source_target_pairs={{0,16},{16,32},{32,48},{48,64},{64,80},{80,96},{96,112},{112,128},... | collective-permute-start | bytes 147464 | tf_op jit(solution)/shard_map/ppermute | solution.py:22
  146.9 52.3 %reshape.121 = f32[3,16,2,8,2,64,2]{6,5,4,3,2,1,0:T(8,128)} reshape(f32[3,32,16,128]{3,2,1,0:T(8,128)} %fusion.3) | data formatting | bytes 1572864 | tf_op jit(solution)/shard_map/reshape | solution.py:55
  199.2 17.8 %reduce_sum.104 = f32[3,16,8,64]{3,2,1,0:T(8,128)S(1)} reduce(f32[3,16,2,8,2,64,2]{6,5,4,3,2,1,0:T(8,128)} %reshape.121, f32[]{:T(128)} %constant.27.clone.1), dimensions={2,4,6}, to_apply=%region_0.1 | reduce | flops 172032 | bytes 884740 | tf_op jit(solution)/shard_map/reduce_sum | solution.py:56
  218.6 6.1 %collective-permute-start.20 = (f32[3,16,1,64]{3,2,1,0:T(1,128)S(1)}, f32[3,16,1,64]{3,2,1,0:T(1,128)S(1)}, u32[]{:S(2)}, u32[]{:S(2)}) collective-permute-start(f32[3,16,1,64]{3,2,1,0:T(1,128)S(1)} %get-tuple-element.77), channel_id=1, source_target_pairs={{0,16},{16,32},{32,48},{48,64},{64,80},{80,96},{96,112},{112,128},... | collective-permute-start | bytes 36872 | tf_op jit(solution)/shard_map/ppermute | solution.py:22
  228.1 4.4 collective-permute-start.22
  233.8 6.4 %collective-permute-start.40 = (f32[4,1,16]{2,0,1:T(4,128)S(1)}, f32[4,1,16]{2,0,1:T(4,128)S(1)}, u32[]{:S(2)}, u32[]{:S(2)}) collective-permute-start(f32[4,1,16]{2,0,1:T(4,128)S(1)} %get-tuple-element.112), channel_id=1, source_target_pairs={{0,16},{16,32},{32,48},{48,64},{64,80},{80,96},{96,112},{112,128},... | collective-permute-start | bytes 776 | tf_op jit(solution)/shard_map/ppermute | solution.py:22
  242.5 6.7 %collective-permute-start.24 = (f32[3,16,1,64]{3,2,1,0:T(1,128)S(1)}, f32[3,16,1,64]{3,2,1,0:T(1,128)S(1)}, u32[]{:S(2)}, u32[]{:S(2)}) collective-permute-start(f32[3,16,1,64]{3,2,1,0:T(1,128)S(1)} %get-tuple-element.75), channel_id=1, source_target_pairs={{0,16},{16,32},{32,48},{48,64},{64,80},{80,96},{96,112},{112,128},... | collective-permute-start | bytes 36872 | tf_op jit(solution)/shard_map/ppermute | solution.py:22
  252.2 3.6 collective-permute-start.26
  257.9 3.6 collective-permute-start.42
  262.4 7.8 %reshape.123 = f32[3,8,2,4,2,32,2]{6,5,4,3,2,1,0:T(8,128)} reshape(f32[3,16,8,64]{3,2,1,0:T(8,128)S(1)} %fusion.81) | data formatting | bytes 196608 | tf_op jit(solution)/shard_map/reshape | solution.py:55
  275.0 6.6 %collective-permute-start.32 = (f32[3,8,1,32]{3,2,1,0:T(1,128)S(1)}, f32[3,8,1,32]{3,2,1,0:T(1,128)S(1)}, u32[]{:S(2)}, u32[]{:S(2)}) collective-permute-start(f32[3,8,1,32]{3,2,1,0:T(1,128)S(1)} %get-tuple-element.94), channel_id=1, source_target_pairs={{0,16},{16,32},{32,48},{48,64},{64,80},{80,96},{96,112},{112,128},... | collective-permute-start | bytes 9224 | tf_op jit(solution)/shard_map/ppermute | solution.py:22
  284.5 5.9 %collective-permute-start.34 = (f32[3,8,6,1]{3,1,2,0:T(8,128)S(1)}, f32[3,8,6,1]{3,1,2,0:T(8,128)S(1)}, u32[]{:S(2)}, u32[]{:S(2)}) collective-permute-start(f32[3,8,6,1]{3,1,2,0:T(8,128)S(1)} %get-tuple-element.87), channel_id=1, source_target_pairs={{0,1},{1,2},{2,3},{3,4},{4,5},{5,6},{6,7},{7,8},{8,9},{9,10},{10,1... | collective-permute-start | bytes 1736 | tf_op jit(solution)/shard_map/ppermute | solution.py:22
  293.6 6.4 %collective-permute-start.36 = (f32[3,8,1,32]{3,2,1,0:T(1,128)S(1)}, f32[3,8,1,32]{3,2,1,0:T(1,128)S(1)}, u32[]{:S(2)}, u32[]{:S(2)}) collective-permute-start(f32[3,8,1,32]{3,2,1,0:T(1,128)S(1)} %get-tuple-element.92), channel_id=1, source_target_pairs={{0,16},{16,32},{32,48},{48,64},{64,80},{80,96},{96,112},{112,128},... | collective-permute-start | bytes 9224 | tf_op jit(solution)/shard_map/ppermute | solution.py:22
  302.8 5.1 %collective-permute-start.38 = (f32[3,8,6,1]{3,1,2,0:T(8,128)S(1)}, f32[3,8,6,1]{3,1,2,0:T(8,128)S(1)}, u32[]{:S(2)}, u32[]{:S(2)}) collective-permute-start(f32[3,8,6,1]{3,1,2,0:T(8,128)S(1)} %get-tuple-element.83), channel_id=1, source_target_pairs={{0,1},{1,2},{2,3},{3,4},{4,5},{5,6},{6,7},{7,8},{8,9},{9,10},{10,1... | collective-permute-start | bytes 1736 | tf_op jit(solution)/shard_map/ppermute | solution.py:22
  308.0 25.0 %all-gather.4 = f32[16,8,2]{1,2,0:T(2,128)S(1)} all-gather(f32[1,8,2]{1,2,0:T(2,128)S(1)} %multiply_bitcast_fusion), channel_id=4, replica_groups=mesh['gx'=16,'gy'=16] {'gy'}, dimensions={0}, use_global_device_ids=true | all-gather | bytes 1088 | tf_op jit(solution)/shard_map/all_gather | solution.py:99
  335.4 6.1 %collective-permute-start.44 = (f32[3,4,1,16]{3,1,2,0:T(4,128)S(1)}, f32[3,4,1,16]{3,1,2,0:T(4,128)S(1)}, u32[]{:S(2)}, u32[]{:S(2)}) collective-permute-start(f32[3,4,1,16]{3,1,2,0:T(4,128)S(1)} %get-tuple-element.107), channel_id=1, source_target_pairs={{0,16},{16,32},{32,48},{48,64},{64,80},{80,96},{96,112},{112,128},... | collective-permute-start | bytes 2312 | tf_op jit(solution)/shard_map/ppermute | solution.py:22
  341.5 26.8 %all-gather.3 = f32[2,2048]{1,0:T(2,128)S(1)} all-gather(f32[2,128]{1,0:T(2,128)S(1)} %bitcast.91), channel_id=5, replica_groups=mesh['gx'=16,'gy'=16] {'gx'}, dimensions={1}, use_global_device_ids=true | all-gather | bytes 17408 | tf_op jit(solution)/shard_map/all_gather | solution.py:103
  368.4 8.1 %collective-permute-start.47 = (f32[3,4,4,1]{3,1,2,0:T(4,128)S(1)}, f32[3,4,4,1]{3,1,2,0:T(4,128)S(1)}, u32[]{:S(2)}, u32[]{:S(2)}) collective-permute-start(f32[3,4,4,1]{3,1,2,0:T(4,128)S(1)} %get-tuple-element.101), channel_id=1, source_target_pairs={{1,0},{2,1},{3,2},{4,3},{5,4},{6,5},{7,6},{8,7},{9,8},{10,9},{11,1... | collective-permute-start | bytes 584 | tf_op jit(solution)/shard_map/ppermute | solution.py:23
  382.5 4.0 collective-permute-start.48
  389.3 5.3 %collective-permute-start.50 = (f32[3,4,4,1]{3,1,2,0:T(4,128)S(1)}, f32[3,4,4,1]{3,1,2,0:T(4,128)S(1)}, u32[]{:S(2)}, u32[]{:S(2)}) collective-permute-start(f32[3,4,4,1]{3,1,2,0:T(4,128)S(1)} %get-tuple-element.98), channel_id=1, source_target_pairs={{0,1},{1,2},{2,3},{3,4},{4,5},{5,6},{6,7},{7,8},{8,9},{9,10},{10,1... | collective-permute-start | bytes 584 | tf_op jit(solution)/shard_map/ppermute | solution.py:22
  396.1 18.2 %all-gather = f32[3,2,128]{0,1,2:T(2,128)S(1)} all-gather(f32[3,2,8]{0,1,2:T(2,128)S(1)} %copy.456), channel_id=2, replica_groups=mesh['gx'=16,'gy'=16] {'gy'}, dimensions={2}, use_global_device_ids=true | all-gather | bytes 3264 | tf_op jit(solution)/shard_map/all_gather | solution.py:98
  414.3 19.3 %all-gather.1 = f32[3,2,2048]{2,1,0:T(2,128)S(1)} all-gather(f32[3,2,128]{2,1,0:T(2,128)S(1)} %copy.457), channel_id=3, replica_groups=mesh['gx'=16,'gy'=16] {'gx'}, dimensions={2}, use_global_device_ids=true | all-gather | bytes 52224 | tf_op jit(solution)/shard_map/all_gather | solution.py:102
  (347 shorter events, 125.9 us)
Async XLA Ops:
  1.8 69.8 %collective-permute-start.5 = (f32[3,32,1,128]{3,2,1,0:T(1,128)}, f32[3,32,1,128]{3,2,1,0:T(1,128)}, u32[]{:S(2)}, u32[]{:S(2)}) collective-permute-start(f32[3,32,1,128]{3,2,1,0:T(1,128)} %get-tuple-element.62), channel_id=1, source_target_pairs={{16,0},{32,16},{48,32},{64,48},{80,64},{96,80},{112,96},{128,112},... | collective-permute-start | bytes 147464 | tf_op jit(solution)/shard_map/ppermute | solution.py:23
  3.1 68.5 %collective-permute-start.4 = (f32[3,32,1,128]{3,2,1,0:T(1,128)}, f32[3,32,1,128]{3,2,1,0:T(1,128)}, u32[]{:S(2)}, u32[]{:S(2)}) collective-permute-start(f32[3,32,1,128]{3,2,1,0:T(1,128)} %get-tuple-element.61), channel_id=1, source_target_pairs={{0,16},{16,32},{32,48},{48,64},{64,80},{80,96},{96,112},{112,128},... | collective-permute-start | bytes 147464 | tf_op jit(solution)/shard_map/ppermute | solution.py:22
  39.8 17.5 %collective-permute-start.1 = (f32[32,1,128]{2,1,0:T(1,128)S(1)}, f32[32,1,128]{2,1,0:T(1,128)S(1)}, u32[]{:S(2)}, u32[]{:S(2)}) collective-permute-start(f32[32,1,128]{2,1,0:T(1,128)S(1)} %get-tuple-element.66), channel_id=1, source_target_pairs={{16,0},{32,16},{48,32},{64,48},{80,64},{96,80},{112,96},{128,112},... | collective-permute-start | bytes 49160 | tf_op jit(solution)/shard_map/ppermute | solution.py:23
  41.4 8.1 %collective-permute-start.19 = (f32[16,10,1]{2,1,0:T(8,128)S(1)}, f32[16,10,1]{2,1,0:T(8,128)S(1)}, u32[]{:S(2)}, u32[]{:S(2)}) collective-permute-start(f32[16,10,1]{2,1,0:T(8,128)S(1)} %get-tuple-element.80), channel_id=1, source_target_pairs={{1,0},{2,1},{3,2},{4,3},{5,4},{6,5},{7,6},{8,7},{9,8},{10,9},{11,1... | collective-permute-start | bytes 1928 | tf_op jit(solution)/shard_map/ppermute | solution.py:23
  49.5 7.8 %collective-permute-start = (f32[32,1,128]{2,1,0:T(1,128)S(1)}, f32[32,1,128]{2,1,0:T(1,128)S(1)}, u32[]{:S(2)}, u32[]{:S(2)}) collective-permute-start(f32[32,1,128]{2,1,0:T(1,128)S(1)} %get-tuple-element.65), channel_id=1, source_target_pairs={{0,16},{16,32},{32,48},{48,64},{64,80},{80,96},{96,112},{112,128},... | collective-permute-start | bytes 49160 | tf_op jit(solution)/shard_map/ppermute | solution.py:22
  57.5 8.0 %collective-permute-start.3 = (f32[32,18,1]{2,0,1:T(8,128)S(1)}, f32[32,18,1]{2,0,1:T(8,128)S(1)}, u32[]{:S(2)}, u32[]{:S(2)}) collective-permute-start(f32[32,18,1]{2,0,1:T(8,128)S(1)} %get-tuple-element.64), channel_id=1, source_target_pairs={{1,0},{2,1},{3,2},{4,3},{5,4},{6,5},{7,6},{8,7},{9,8},{10,9},{11,1... | collective-permute-start | bytes 6920 | tf_op jit(solution)/shard_map/ppermute | solution.py:23
  59.7 9.8 %collective-permute-start.2 = (f32[32,18,1]{2,0,1:T(8,128)S(1)}, f32[32,18,1]{2,0,1:T(8,128)S(1)}, u32[]{:S(2)}, u32[]{:S(2)}) collective-permute-start(f32[32,18,1]{2,0,1:T(8,128)S(1)} %get-tuple-element.63), channel_id=1, source_target_pairs={{0,1},{1,2},{2,3},{3,4},{4,5},{5,6},{6,7},{7,8},{8,9},{9,10},{10,1... | collective-permute-start | bytes 6920 | tf_op jit(solution)/shard_map/ppermute | solution.py:22
  63.7 35.6 %collective-permute-start.29 = (f32[8,1,32]{2,1,0:T(1,128)}, f32[8,1,32]{2,1,0:T(1,128)}, u32[]{:S(2)}, u32[]{:S(2)}) collective-permute-start(f32[8,1,32]{2,1,0:T(1,128)} %get-tuple-element.104), channel_id=1, source_target_pairs={{16,0},{32,16},{48,32},{64,48},{80,64},{96,80},{112,96},{128,112},... | collective-permute-start | bytes 3080 | tf_op jit(solution)/shard_map/ppermute | solution.py:23
  65.5 33.8 %collective-permute-start.28 = (f32[8,1,32]{2,1,0:T(1,128)}, f32[8,1,32]{2,1,0:T(1,128)}, u32[]{:S(2)}, u32[]{:S(2)}) collective-permute-start(f32[8,1,32]{2,1,0:T(1,128)} %get-tuple-element.103), channel_id=1, source_target_pairs={{0,16},{16,32},{32,48},{48,64},{64,80},{80,96},{96,112},{112,128},... | collective-permute-start | bytes 3080 | tf_op jit(solution)/shard_map/ppermute | solution.py:22
  76.2 8.1 %collective-permute-start.7 = (f32[3,32,18,1]{1,3,2,0:T(1,128)S(1)}, f32[3,32,18,1]{1,3,2,0:T(1,128)S(1)}, u32[]{:S(2)}, u32[]{:S(2)}) collective-permute-start(f32[3,32,18,1]{1,3,2,0:T(1,128)S(1)} %copy.414), channel_id=1, source_target_pairs={{1,0},{2,1},{3,2},{4,3},{5,4},{6,5},{7,6},{8,7},{9,8},{10,9},{11,1... | collective-permute-start | bytes 20744 | tf_op jit(solution)/shard_map/ppermute | solution.py:23
  92.1 8.0 %collective-permute-start.9 = (f32[3,32,1,128]{3,2,1,0:T(1,128)S(1)}, f32[3,32,1,128]{3,2,1,0:T(1,128)S(1)}, u32[]{:S(2)}, u32[]{:S(2)}) collective-permute-start(f32[3,32,1,128]{3,2,1,0:T(1,128)S(1)} %get-tuple-element.60), channel_id=1, source_target_pairs={{16,0},{32,16},{48,32},{64,48},{80,64},{96,80},{112,96},{128,112},... | collective-permute-start | bytes 147464 | tf_op jit(solution)/shard_map/ppermute | solution.py:23
  103.5 13.1 %collective-permute-start.11 = (f32[3,32,18,1]{1,3,2,0:T(1,128)S(1)}, f32[3,32,18,1]{1,3,2,0:T(1,128)S(1)}, u32[]{:S(2)}, u32[]{:S(2)}) collective-permute-start(f32[3,32,18,1]{1,3,2,0:T(1,128)S(1)} %copy.420), channel_id=1, source_target_pairs={{1,0},{2,1},{3,2},{4,3},{5,4},{6,5},{7,6},{8,7},{9,8},{10,9},{11,1... | collective-permute-start | bytes 20744 | tf_op jit(solution)/shard_map/ppermute | solution.py:23
  105.8 11.3 %collective-permute-start.10 = (f32[3,32,18,1]{1,3,2,0:T(1,128)S(1)}, f32[3,32,18,1]{1,3,2,0:T(1,128)S(1)}, u32[]{:S(2)}, u32[]{:S(2)}) collective-permute-start(f32[3,32,18,1]{1,3,2,0:T(1,128)S(1)} %copy.418), channel_id=1, source_target_pairs={{0,1},{1,2},{2,3},{3,4},{4,5},{5,6},{6,7},{7,8},{8,9},{9,10},{10,1... | collective-permute-start | bytes 20744 | tf_op jit(solution)/shard_map/ppermute | solution.py:22
  111.1 20.2 %collective-permute-start.31 = (f32[8,6,1]{2,1,0:T(8,128)}, f32[8,6,1]{2,1,0:T(8,128)S(1)}, u32[]{:S(2)}, u32[]{:S(2)}) collective-permute-start(f32[8,6,1]{2,1,0:T(8,128)} %get-tuple-element.97), channel_id=1, source_target_pairs={{1,0},{2,1},{3,2},{4,3},{5,4},{6,5},{7,6},{8,7},{9,8},{10,9},{11,1... | collective-permute-start | bytes 584 | tf_op jit(solution)/shard_map/ppermute | solution.py:23
  113.0 18.3 %collective-permute-start.30 = (f32[8,6,1]{2,1,0:T(8,128)S(1)}, f32[8,6,1]{2,1,0:T(8,128)}, u32[]{:S(2)}, u32[]{:S(2)}) collective-permute-start(f32[8,6,1]{2,1,0:T(8,128)S(1)} %get-tuple-element.96), channel_id=1, source_target_pairs={{0,1},{1,2},{2,3},{3,4},{4,5},{5,6},{6,7},{7,8},{8,9},{9,10},{10,1... | collective-permute-start | bytes 584 | tf_op jit(solution)/shard_map/ppermute | solution.py:22
  123.6 8.6 %collective-permute-start.13 = (f32[3,32,1,128]{3,2,1,0:T(1,128)S(1)}, f32[3,32,1,128]{3,2,1,0:T(1,128)S(1)}, u32[]{:S(2)}, u32[]{:S(2)}) collective-permute-start(f32[3,32,1,128]{3,2,1,0:T(1,128)S(1)} %get-tuple-element.58), channel_id=1, source_target_pairs={{16,0},{32,16},{48,32},{64,48},{80,64},{96,80},{112,96},{128,112},... | collective-permute-start | bytes 147464 | tf_op jit(solution)/shard_map/ppermute | solution.py:23
  225.9 14.3 %collective-permute-start.23 = (f32[3,16,10,1]{3,1,2,0:T(8,128)S(1)}, f32[3,16,10,1]{3,1,2,0:T(8,128)S(1)}, u32[]{:S(2)}, u32[]{:S(2)}) collective-permute-start(f32[3,16,10,1]{3,1,2,0:T(8,128)S(1)} %get-tuple-element.74), channel_id=1, source_target_pairs={{1,0},{2,1},{3,2},{4,3},{5,4},{6,5},{7,6},{8,7},{9,8},{10,9},{11,1... | collective-permute-start | bytes 5768 | tf_op jit(solution)/shard_map/ppermute | solution.py:23
  228.1 12.1 %collective-permute-start.22 = (f32[3,16,10,1]{3,1,2,0:T(8,128)S(1)}, f32[3,16,10,1]{3,1,2,0:T(8,128)S(1)}, u32[]{:S(2)}, u32[]{:S(2)}) collective-permute-start(f32[3,16,10,1]{3,1,2,0:T(8,128)S(1)} %get-tuple-element.73), channel_id=1, source_target_pairs={{0,1},{1,2},{2,3},{3,4},{4,5},{5,6},{6,7},{7,8},{8,9},{9,10},{10,1... | collective-permute-start | bytes 5768 | tf_op jit(solution)/shard_map/ppermute | solution.py:22
  232.5 16.7 %collective-permute-start.41 = (f32[4,1,16]{2,0,1:T(4,128)S(1)}, f32[4,1,16]{2,0,1:T(4,128)S(1)}, u32[]{:S(2)}, u32[]{:S(2)}) collective-permute-start(f32[4,1,16]{2,0,1:T(4,128)S(1)} %get-tuple-element.113), channel_id=1, source_target_pairs={{16,0},{32,16},{48,32},{64,48},{80,64},{96,80},{112,96},{128,112},... | collective-permute-start | bytes 776 | tf_op jit(solution)/shard_map/ppermute | solution.py:23
  233.8 15.4 %collective-permute-start.40 = (f32[4,1,16]{2,0,1:T(4,128)S(1)}, f32[4,1,16]{2,0,1:T(4,128)S(1)}, u32[]{:S(2)}, u32[]{:S(2)}) collective-permute-start(f32[4,1,16]{2,0,1:T(4,128)S(1)} %get-tuple-element.112), channel_id=1, source_target_pairs={{0,16},{16,32},{32,48},{48,64},{64,80},{80,96},{96,112},{112,128},... | collective-permute-start | bytes 776 | tf_op jit(solution)/shard_map/ppermute | solution.py:22
  241.2 8.1 %collective-permute-start.25 = (f32[3,16,1,64]{3,2,1,0:T(1,128)S(1)}, f32[3,16,1,64]{3,2,1,0:T(1,128)S(1)}, u32[]{:S(2)}, u32[]{:S(2)}) collective-permute-start(f32[3,16,1,64]{3,2,1,0:T(1,128)S(1)} %get-tuple-element.76), channel_id=1, source_target_pairs={{16,0},{32,16},{48,32},{64,48},{80,64},{96,80},{112,96},{128,112},... | collective-permute-start | bytes 36872 | tf_op jit(solution)/shard_map/ppermute | solution.py:23
  250.3 11.2 %collective-permute-start.27 = (f32[3,16,10,1]{3,1,2,0:T(8,128)S(1)}, f32[3,16,10,1]{3,1,2,0:T(8,128)S(1)}, u32[]{:S(2)}, u32[]{:S(2)}) collective-permute-start(f32[3,16,10,1]{3,1,2,0:T(8,128)S(1)} %get-tuple-element.70), channel_id=1, source_target_pairs={{1,0},{2,1},{3,2},{4,3},{5,4},{6,5},{7,6},{8,7},{9,8},{10,9},{11,1... | collective-permute-start | bytes 5768 | tf_op jit(solution)/shard_map/ppermute | solution.py:23
  252.2 9.3 %collective-permute-start.26 = (f32[3,16,10,1]{3,1,2,0:T(8,128)S(1)}, f32[3,16,10,1]{3,1,2,0:T(8,128)S(1)}, u32[]{:S(2)}, u32[]{:S(2)}) collective-permute-start(f32[3,16,10,1]{3,1,2,0:T(8,128)S(1)} %get-tuple-element.69), channel_id=1, source_target_pairs={{0,1},{1,2},{2,3},{3,4},{4,5},{5,6},{6,7},{7,8},{8,9},{9,10},{10,1... | collective-permute-start | bytes 5768 | tf_op jit(solution)/shard_map/ppermute | solution.py:22
  256.0 25.7 %collective-permute-start.43 = (f32[4,4,1]{2,0,1:T(4,128)S(1)}, f32[4,4,1]{2,0,1:T(4,128)S(1)}, u32[]{:S(2)}, u32[]{:S(2)}) collective-permute-start(f32[4,4,1]{2,0,1:T(4,128)S(1)} %get-tuple-element.110), channel_id=1, source_target_pairs={{1,0},{2,1},{3,2},{4,3},{5,4},{6,5},{7,6},{8,7},{9,8},{10,9},{11,1... | collective-permute-start | bytes 200 | tf_op jit(solution)/shard_map/ppermute | solution.py:23
  257.9 23.8 %collective-permute-start.42 = (f32[4,4,1]{2,0,1:T(4,128)S(1)}, f32[4,4,1]{2,0,1:T(4,128)S(1)}, u32[]{:S(2)}, u32[]{:S(2)}) collective-permute-start(f32[4,4,1]{2,0,1:T(4,128)S(1)} %get-tuple-element.109), channel_id=1, source_target_pairs={{0,1},{1,2},{2,3},{3,4},{4,5},{5,6},{6,7},{7,8},{8,9},{9,10},{10,1... | collective-permute-start | bytes 200 | tf_op jit(solution)/shard_map/ppermute | solution.py:22
  273.7 8.0 %collective-permute-start.33 = (f32[3,8,1,32]{3,2,1,0:T(1,128)S(1)}, f32[3,8,1,32]{3,2,1,0:T(1,128)S(1)}, u32[]{:S(2)}, u32[]{:S(2)}) collective-permute-start(f32[3,8,1,32]{3,2,1,0:T(1,128)S(1)} %get-tuple-element.95), channel_id=1, source_target_pairs={{16,0},{32,16},{48,32},{64,48},{80,64},{96,80},{112,96},{128,112},... | collective-permute-start | bytes 9224 | tf_op jit(solution)/shard_map/ppermute | solution.py:23
  282.6 8.1 %collective-permute-start.35 = (f32[3,8,6,1]{3,1,2,0:T(8,128)S(1)}, f32[3,8,6,1]{3,1,2,0:T(8,128)S(1)}, u32[]{:S(2)}, u32[]{:S(2)}) collective-permute-start(f32[3,8,6,1]{3,1,2,0:T(8,128)S(1)} %get-tuple-element.88), channel_id=1, source_target_pairs={{1,0},{2,1},{3,2},{4,3},{5,4},{6,5},{7,6},{8,7},{9,8},{10,9},{11,1... | collective-permute-start | bytes 1736 | tf_op jit(solution)/shard_map/ppermute | solution.py:23
  300.9 32.2 %collective-permute-start.39 = (f32[3,8,6,1]{3,1,2,0:T(8,128)S(1)}, f32[3,8,6,1]{3,1,2,0:T(8,128)S(1)}, u32[]{:S(2)}, u32[]{:S(2)}) collective-permute-start(f32[3,8,6,1]{3,1,2,0:T(8,128)S(1)} %get-tuple-element.84), channel_id=1, source_target_pairs={{1,0},{2,1},{3,2},{4,3},{5,4},{6,5},{7,6},{8,7},{9,8},{10,9},{11,1... | collective-permute-start | bytes 1736 | tf_op jit(solution)/shard_map/ppermute | solution.py:23
  302.8 30.2 %collective-permute-start.38 = (f32[3,8,6,1]{3,1,2,0:T(8,128)S(1)}, f32[3,8,6,1]{3,1,2,0:T(8,128)S(1)}, u32[]{:S(2)}, u32[]{:S(2)}) collective-permute-start(f32[3,8,6,1]{3,1,2,0:T(8,128)S(1)} %get-tuple-element.83), channel_id=1, source_target_pairs={{0,1},{1,2},{2,3},{3,4},{4,5},{5,6},{6,7},{7,8},{8,9},{9,10},{10,1... | collective-permute-start | bytes 1736 | tf_op jit(solution)/shard_map/ppermute | solution.py:22
  334.1 34.2 %collective-permute-start.45 = (f32[3,4,1,16]{3,1,2,0:T(4,128)S(1)}, f32[3,4,1,16]{3,1,2,0:T(4,128)S(1)}, u32[]{:S(2)}, u32[]{:S(2)}) collective-permute-start(f32[3,4,1,16]{3,1,2,0:T(4,128)S(1)} %get-tuple-element.108), channel_id=1, source_target_pairs={{16,0},{32,16},{48,32},{64,48},{80,64},{96,80},{112,96},{128,112},... | collective-permute-start | bytes 2312 | tf_op jit(solution)/shard_map/ppermute | solution.py:23
  335.4 32.9 %collective-permute-start.44 = (f32[3,4,1,16]{3,1,2,0:T(4,128)S(1)}, f32[3,4,1,16]{3,1,2,0:T(4,128)S(1)}, u32[]{:S(2)}, u32[]{:S(2)}) collective-permute-start(f32[3,4,1,16]{3,1,2,0:T(4,128)S(1)} %get-tuple-element.107), channel_id=1, source_target_pairs={{0,16},{16,32},{32,48},{48,64},{64,80},{80,96},{96,112},{112,128},... | collective-permute-start | bytes 2312 | tf_op jit(solution)/shard_map/ppermute | solution.py:22
  368.4 11.7 %collective-permute-start.47 = (f32[3,4,4,1]{3,1,2,0:T(4,128)S(1)}, f32[3,4,4,1]{3,1,2,0:T(4,128)S(1)}, u32[]{:S(2)}, u32[]{:S(2)}) collective-permute-start(f32[3,4,4,1]{3,1,2,0:T(4,128)S(1)} %get-tuple-element.101), channel_id=1, source_target_pairs={{1,0},{2,1},{3,2},{4,3},{5,4},{6,5},{7,6},{8,7},{9,8},{10,9},{11,1... | collective-permute-start | bytes 584 | tf_op jit(solution)/shard_map/ppermute | solution.py:23
  (75 other events, 638.0 us)
where the time goes:
time: 449 us; the launch traced here: 443 us
  starting transfers between devices  177 us (39%)
  local copies, waits for them, and re-layouts  109 us (24%)
  blocking collectives  89.3 us (20%)
  other arithmetic  57.6 us (13%)
  waiting for transfers between devices  8.13 us (2%)
    ppermute x26, starting transfers between devices, padded_2(): before = lax.ppermute(last, axis, up)  124 us
    reshape x4, local copies, waits for them, and re-layouts, restrict(): field.reshape(shape[:-3] + (shape[-3] // 2, 2, shape[-2] // 2, 2, shape[-...  78.7 us
    ppermute x26, starting transfers between devices, padded_2(): after = lax.ppermute(leading, axis, down)  52.6 us
    reduce_sum x9, other arithmetic, restrict(): return jnp.mean(blocks, axis=(-5, -3, -1))  29 us
    all_gather x1, blocking collectives, gather_grid(): lax.all_gather(rows[1], 'gx', axis=1, tiled=True)  26.8 us
    all_gather x1, blocking collectives, gather_grid(): lax.all_gather(coef, 'gy', axis=2, tiled=True)  25 us
    all_gather x1, blocking collectives, gather_grid(): lax.all_gather(rows[0], 'gx', axis=2, tiled=True)  19.3 us
    all_gather x1, blocking collectives, gather_grid(): lax.all_gather(rhs, 'gy', axis=3, tiled=True)  18.2 us
  transfers between devices with their start and end apart: 52, of which 12 were waited for; matrix products, arithmetic and copies ran while one was open for 16% of the time, Pallas kernels for 0%

commit v1 on v0

v1 whole, which is shorter than its diff:
```python
import jax
import jax.numpy as jnp
from jax import lax
from jax.experimental import pallas as pl
from jax.experimental.pallas import tpu as pltpu
from jax.sharding import PartitionSpec as P


F32 = jnp.float32
NX, NY = 16, 16
BETWEEN = 2.0 * 0.1 / 1.1
ANY = pl.BlockSpec(memory_space=pltpu.HBM)


def dot(a, b):
    return jnp.dot(a, b, precision=lax.Precision.HIGHEST, preferred_element_type=F32)


def iota(shape, dim):
    return lax.broadcasted_iota(jnp.int32, shape, dim)


def roll(x, shift, axis=1):
    shift = shift % x.shape[axis]
    return x if shift == 0 else pltpu.roll(x, shift, axis)


def turn(x, shift):
    return pltpu.roll(x, lax.rem(shift + 256, 128), 1)


def recip(x):
    guess = pl.reciprocal(x, approx=True)
    return guess * (2.0 - x * guess)


def call(kernel, outs, scratch, flops=1_000_000, **kw):
    return pl.pallas_call(
        kernel,
        out_shape=[jax.ShapeDtypeStruct(s, F32) for s in outs],
        scratch_shapes=[pltpu.VMEM(s, F32) if isinstance(s, tuple) else s for s in scratch],
        compiler_params=pltpu.CompilerParams(vmem_limit_bytes=48 * 1024 * 1024),
        cost_estimate=pl.CostEstimate(flops=flops, bytes_accessed=4_000_000, transcendentals=0),
        **kw,
    )


def loop(count, body, unroll=1):
    def step(i, carry):
        body(i)
        return carry

    lax.fori_loop(0, count, step, 0, unroll=unroll)


def weigh(weights, values):
    parts = [w * v for w, v in zip(weights, values)]
    while len(parts) > 1:
        parts = [sum(parts[i : i + 2][1:], parts[i]) for i in range(0, len(parts), 2)]
    return parts[0]


def rows_kernel(guess, labels, up, down, own, phase, sems):
    copies = [pltpu.make_async_copy(labels, phase, sems.at[3])]
    for f in range(3):
        copies.append(pltpu.make_async_copy(guess.at[f], own.at[f], sems.at[f]))
    for copy in copies:
        copy.start()
    copies[0].wait()
    own[3] = jnp.where(phase[...] == 1, 0.0, 1.0).astype(F32)
    flat = own.reshape(4 * 32 * 16, 128)
    for ch in (3, 0, 1, 2):
        if ch < 3:
            copies[ch + 1].wait()
        for row in range(3):
            up[3 * ch + row] = flat[pl.ds(512 * ch + 13 + row, 32, stride=16), :]
            down[3 * ch + row] = flat[pl.ds(512 * ch + row, 32, stride=16), :]


def pack_kernel(own, before, after, near, far, held):
    first_core = lax.rem(lax.axis_index("gy"), 2) == 0
    flat = held.reshape(4 * 34 * 32, 128)
    for ch in range(4):
        first = (ch * 34 + 1) * 32
        for row in range(3):
            flat[pl.ds(first + row, 32, stride=32), :] = before[3 * ch + row]
            flat[pl.ds(first + 19 + row, 32, stride=32), :] = after[3 * ch + row]
        held[ch, 0] = jnp.zeros((32, 128), F32)
        held[ch, 33] = jnp.zeros((32, 128), F32)

    def plane(z):
        for ch in range(4):
            held[ch, z + 1, 3:19, :] = own[ch, z]

    loop(32, plane, 4)
    group = iota((24, 128), 1) // 16

    def some(low):
        for ch in range(4):
            to_right = jnp.zeros((24, 128), F32)
            to_left = jnp.zeros((24, 128), F32)
            for h in range(8):
                moved = roll(held[ch, 4 * h + low + 1, 0:24, :], 16 * h + 16)
                to_right = jnp.where(group == h, moved, to_right)
                to_left = jnp.where(group == (h + 1) % 8, moved, to_left)
            near[ch, low] = jnp.where(first_core, to_right, to_left)
            far[ch, low] = jnp.where(first_core, to_left, to_right)

    loop(4, some)


def six_of(ref, lead, z, first, count):
    own = ref[(*lead, z, pl.ds(first, count), slice(None))]
    return own, (
        ref[(*lead, z, pl.ds(first - 1, count), slice(None))],
        ref[(*lead, z, pl.ds(first + 1, count), slice(None))],
        roll(own, 1),
        roll(own, -1),
        ref[(*lead, z - 1, pl.ds(first, count), slice(None))],
        ref[(*lead, z + 1, pl.ds(first, count), slice(None))],
    )


def face(total):
    return jnp.where(total < 0.5, 1.0, jnp.where(total < 1.5, BETWEEN, 0.1))


def rows_inside(gx, shape):
    row = iota(shape, 0) + 1
    low, high = jnp.where(gx > 0, 1, 0), jnp.where(gx < NX - 1, 1, 0)
    return jnp.where(row < 3, low, jnp.where(row >= 19, high, 1))


def fine_sweeps(planes, start, share, one, two, weights, diags, halves, omega, wrap, keep, unroll):
    def first_sweep(z):
        own, six = six_of(share, (), z + 1, 1, 24)
        faces = [face(own + other) for other in six]
        diag = (faces[0] + faces[1]) + (faces[2] + faces[3]) + (faces[4] + faces[5])
        gain = omega * recip(diag)
        diags[z, 1:25, :] = 1.25 * diag
        w = [gain * value for value in faces]
        for i in range(6):
            weights[i, z, 1:25, :] = w[i]
        for f in range(3):
            own, six = six_of(start, (f,), z + 1, 1, 24)
            one[f, z + 1, 1:25, :] = (0.2 * own + (w[2 * f + 1] - w[2 * f])) + weigh(w, six)

    loop(planes, first_sweep, unroll)
    wrap(one)

    def second_sweep(z):
        w = [weights[i, z, 2:26, :] for i in range(6)]
        for f in range(3):
            own, six = six_of(one, (f,), z + 1, 2, 24)
            two[f, z + 1, 2:26, :] = (0.2 * own + (w[2 * f + 1] - w[2 * f])) + weigh(w, six)

    loop(planes, second_sweep, unroll)
    wrap(two)

    def residual(pair):
        sums = {}
        for k in range(2):
            z = 2 * pair + k
            w = [weights[i, z, 3:19, :] for i in range(6)]
            diag = diags[z, 3:19, :]
            for f in range(3):
                own, six = six_of(two, (f,), z + 1, 3, 16)
                keep[f, z] = own
                value = (((w[2 * f + 1] - w[2 * f]) - 0.8 * own) + weigh(w, six)) * diag
                sums[f] = value if k == 0 else sums[f] + value
            value = share[z + 1, 3:19, :]
            sums[3] = value if k == 0 else sums[3] + value
        for ch, value in sums.items():
            halves[ch, pair] = value

    loop(planes // 2, residual, unroll // 2)


def own_kernel(held, field, coarse, edges, one, two, weights, diags, halves, pooled):
    gx = lax.axis_index("gx")
    for ref in (one, two):
        for f in range(3):
            ref[f, 0] = jnp.zeros((32, 128), F32)
            ref[f, 33] = jnp.zeros((32, 128), F32)
    omega = 0.8 * rows_inside(gx, (24, 128)).astype(F32)
    fine_sweeps(
        32, held, held.at[3], one, two, weights, diags, halves, omega, lambda ref: None, field, 4
    )
    pool = jnp.where(iota((128, 128), 0) // 2 == iota((128, 128), 1), 0.125, 0.0)
    pooled[...] = dot(halves[...].reshape(1024, 128), pool)
    for ch in range(4):
        even = pooled[pl.ds(256 * ch, 128, stride=2), :]
        odd = pooled[pl.ds(256 * ch + 1, 128, stride=2), :]
        coarse[ch] = (even + odd).reshape(16, 8, 128)
    lane = iota((24, 128), 1)

    def edge(z):
        for ch in range(4):
            value = jnp.zeros((24, 128), F32)
            for half in range(2):
                source = held[ch, z + 16 * half + 1, 0:24, :]
                base = 64 * half
                value = jnp.where((lane >= base) & (lane < base + 7), roll(source, base + 7), value)
                value = jnp.where((lane >= base + 57) & (lane < base + 64), roll(source, base + 57), value)
            edges[ch, z] = value

    loop(16, edge)


def rim_kernel(
    edges, owned, near, far, field, coarse, packed,
    start, share, one, two, weights, diags, halves, pooled,
):
    gx, gy = lax.axis_index("gx"), lax.axis_index("gy")
    lane = iota((24, 128), 1)
    part = lane % 64
    is_after = (part >= 7) & (part < 22)
    is_before = (part >= 42) & (part < 57)
    first_core = lax.rem(gy, 2) == 0

    def unpack(low):
        for ch in range(4):
            target = start.at[ch] if ch < 3 else share
            from_right = jnp.where(first_core, near[ch, low], far[ch, low])
            from_left = jnp.where(first_core, far[ch, low], near[ch, low])
            for h in range(4):
                z = 4 * h + low
                after_y = roll(from_right, 7 - 16 * (h + 1))
                before_y = roll(from_left, 41 - 16 * h)
                target[z + 1, 0:24, :] = jnp.where(
                    is_after, after_y, jnp.where(is_before, before_y, edges[ch, z])
                )

    loop(4, unpack)

    def wrap_one(ref):
        ref[0, 0:24, :] = jnp.where(lane >= 64, roll(ref[16, 0:24, :], 64), 0.0)
        ref[17, 0:24, :] = jnp.where(lane < 64, roll(ref[1, 0:24, :], 64), 0.0)

    def wrap(ref):
        for f in range(3):
            wrap_one(ref.at[f])

    wrap_one(share)
    wrap(start)
    inside_y = jnp.where(
        part < 32,
        jnp.where((part < 7) | (gy < NY - 1), 1, 0),
        jnp.where((part >= 57) | (gy > 0), 1, 0),
    )
    omega = 0.8 * (rows_inside(gx, (24, 128)) * inside_y).astype(F32)
    fine_sweeps(16, start, share, one, two, weights, diags, halves, omega, wrap, field, 4)

    source, target = iota((128, 128), 0), iota((128, 128), 1)
    spot = source % 64
    column = jnp.where(spot < 32, 121 + spot, 128 + spot - 57)
    to = jnp.where(spot < 32, column // 2, (column // 2 + 64) % 128)
    from_rim = (iota((128, 128), 1) < 2) | (iota((128, 128), 1) >= 62)
    mixed = halves[...].reshape(512, 128)
    for half in range(2):
        pool = jnp.where((to == target) & (source // 64 == half), 0.125, 0.0)
        pooled[...] = dot(mixed, pool)
        for ch in range(4):
            even = pooled[pl.ds(128 * ch, 64, stride=2), :]
            odd = pooled[pl.ds(128 * ch + 1, 64, stride=2), :]
            at = pl.ds(8 * half, 8)
            rest = owned[ch, at].reshape(64, 128)
            coarse[ch, at] = jnp.where(from_rim[:64], even + odd, rest).reshape(8, 8, 128)

    lane = iota((8, 128), 1)
    for ch in range(4):
        for group in range(2):
            tiles = [None] * 5
            for k in range(8):
                moved = roll(coarse[ch, 8 * group + k], 8 + 80 * k)
                tile, off = divmod(80 * k, 128)
                tiles[tile] = moved if off == 0 else jnp.where(lane >= off, moved, tiles[tile])
                if off + 80 > 128:
                    tiles[tile + 1] = moved
            for tile in range(5):
                packed[ch, group, tile] = tiles[tile]


def patch_kernel(owned, rim, field):
    lane = iota((16, 128), 1)

    def plane(z):
        for f in range(3):
            value = rim[f, z]
            for half in range(2):
                base = 64 * half
                low = roll(value, -57 - base)
                high = roll(value, 121 - base)
                at = z + 16 * half
                field[f, at] = jnp.where(lane < 3, low, jnp.where(lane >= 125, high, owned[f, at]))

    loop(16, plane, 2)


def resist(share):
    return recip(1.0 - 0.9 * share)


def level_weights(own, six, omega):
    faces = [2.0 * recip(own + other) for other in six]
    diag = (faces[0] + faces[1]) + (faces[2] + faces[3]) + (faces[4] + faces[5])
    gain = omega * recip(diag)
    return gain, [gain * w for w in faces], diag


def middle_kernel(
    mine, before, after, sent, e_one, e_two,
    share, rest, rhs, first, second, weights, diags, halves, pooled,
    rest2, first2, second2, rhs2, share2, weights2, diags2,
):
    gx, gy = lax.axis_index("gx"), lax.axis_index("gy")
    low_x, high_x = jnp.where(gx > 0, 1, 0), jnp.where(gx < NX - 1, 1, 0)
    low_y, high_y = jnp.where(gy > 0, 1, 0), jnp.where(gy < NY - 1, 1, 0)

    for f in range(3):
        for ref in (first, second):
            ref[f, 0] = jnp.zeros((32, 128), F32)
            ref[f, 17] = jnp.zeros((32, 128), F32)
    for z in (0, 17):
        rest[z] = jnp.ones((32, 128), F32)
    lane = iota((8, 128), 1)

    def fill(group):
        for k in range(8):
            z = 8 * group + k
            tile, off = divmod(80 * k, 128)
            for ch in range(4):
                parts = []
                for ref in (before, after):
                    value = ref[ch, group, tile]
                    if off + 80 > 128:
                        value = jnp.where(lane >= off, value, ref[ch, group, tile + 1])
                    parts.append(roll(value, -8 - 80 * k))
                parts.insert(1, mine[ch, z])
                for i, value in enumerate(parts):
                    if ch < 3:
                        rhs[ch, z, 8 * i : 8 * i + 8, :] = value
                    else:
                        share[z, 8 * i : 8 * i + 8, :] = value
                        rest[z + 1, 8 * i : 8 * i + 8, :] = resist(value)
            rest[z + 1, 24:32, :] = jnp.ones((8, 128), F32)

    loop(2, fill)

    row, lane = iota((24, 128), 0) + 1, iota((24, 128), 1)
    in_x = jnp.where(row < 8, low_x, jnp.where(row >= 16, high_x, 1))
    in_y = jnp.where(lane < 64, 1, jnp.where(lane < 96, high_y, low_y))
    omega = 0.8 * (in_x * in_y).astype(F32)

    def start(z):
        own, six = six_of(rest, (), z + 1, 1, 24)
        gain, w, diag = level_weights(own, six, omega)
        for i in range(6):
            weights[i, z, 1:25, :] = w[i]
        diags[z, 1:25, :] = (1.25 * 0.25) * diag
        for f in range(3):
            first[f, z + 1, 1:25, :] = (4.0 * gain) * rhs[f, z, 1:25, :]

    loop(16, start, 2)

    def sweep(z):
        w = [weights[i, z, 3:27, :] for i in range(6)]
        for f in range(3):
            own, six = six_of(first, (f,), z + 1, 3, 24)
            second[f, z + 1, 3:27, :] = 1.2 * own + weigh(w, six)

    loop(16, sweep, 4)

    def left(pair):
        sums = {}
        for k in range(2):
            z = 2 * pair + k
            w = [weights[i, z, 4:20, :] for i in range(6)]
            diag = diags[z, 4:20, :]
            for f in range(3):
                own, six = six_of(second, (f,), z + 1, 4, 16)
                change = (first[f, z + 1, 4:20, :] - 0.8 * own) + weigh(w, six)
                value = change * diag
                sums[f] = value if k == 0 else sums[f] + value
                e_one[f, z] = second[f, z + 1, 8:16, :]
        for f in range(3):
            halves[f, pair, 0:16, :] = sums[f]
            halves[f, pair, 16:24, :] = jnp.zeros((8, 128), F32)
        halves[3, pair] = share[2 * pair] + share[2 * pair + 1]

    loop(8, left, 2)

    source, target = iota((128, 128), 0), iota((128, 128), 1)
    pool = jnp.where(source // 2 + jnp.where(source >= 96, 64, 0) == target, 0.125, 0.0)
    pooled[...] = dot(halves[...].reshape(4 * 8 * 24, 128), pool)
    for z in (0, 9):
        rest2[z] = jnp.ones((24, 128), F32)
        for f in range(3):
            first2[f, z] = jnp.zeros((24, 128), F32)
            second2[f, z] = jnp.zeros((24, 128), F32)
    for z in range(8):
        for f in range(3):
            base = (f * 8 + z) * 24
            rhs2[f, z] = pooled[pl.ds(base, 8, stride=2), :] + pooled[pl.ds(base + 1, 8, stride=2), :]
        base = (3 * 8 + z) * 24
        value = pooled[pl.ds(base + 2, 8, stride=2), :] + pooled[pl.ds(base + 3, 8, stride=2), :]
        rest2[z + 1, 0:8, :] = resist(value)
        value = pooled[pl.ds(base + 8, 8, stride=2), :] + pooled[pl.ds(base + 9, 8, stride=2), :]
        rest2[z + 1, 3:11, :] = resist(value)
        share2[z] = value

    row, lane = iota((8, 128), 0) + 1, iota((8, 128), 1)
    in_x = jnp.where(row < 3, low_x, jnp.where(row >= 7, high_x, 1))
    in_y = jnp.where(lane < 32, 1, jnp.where(lane < 96, high_y, low_y))
    omega2 = 0.8 * (in_x * in_y).astype(F32)

    def start2(z):
        own, six = six_of(rest2, (), z + 1, 1, 8)
        gain, w, diag = level_weights(own, six, omega2)
        for i in range(6):
            weights2[i, z, 1:9, :] = w[i]
        diags2[z, 1:9, :] = (1.25 * 0.0625) * diag
        for f in range(3):
            first2[f, z + 1, 1:9, :] = (16.0 * gain) * rhs2[f, z]

    loop(8, start2, 8)

    def sweep2(z):
        w = [weights2[i, z, 2:10, :] for i in range(6)]
        for f in range(3):
            own, six = six_of(first2, (f,), z + 1, 2, 8)
            second2[f, z + 1, 2:10, :] = 1.2 * own + weigh(w, six)

    loop(8, sweep2, 8)

    own_row = iota((8, 128), 0) < 4
    parts = []
    for pair in range(4):
        sums = {}
        for k in range(2):
            z = 2 * pair + k
            w = [weights2[i, z, 3:11, :] for i in range(6)]
            diag = diags2[z, 3:11, :]
            for f in range(3):
                own, six = six_of(second2, (f,), z + 1, 3, 8)
                e_two[f, z] = own
                change = (first2[f, z + 1, 3:11, :] - 0.8 * own) + weigh(w, six)
                value = jnp.where(own_row, change * diag, 0.0)
                sums[f] = value if k == 0 else sums[f] + value
            value = jnp.where(own_row, share2[z], 0.0)
            sums[3] = value if k == 0 else sums[3] + value
        parts.append(sums)

    pool = jnp.where((source < 32) & (source // 2 == target % 16), 0.125, 0.0)
    rows = jnp.concatenate([parts[pair][ch] for ch in range(4) for pair in range(4)], axis=0)
    spread = dot(rows, pool)
    at, to = iota((32, 128), 0), iota((32, 128), 1)
    keep = (at // 8 == to // 32) & ((at % 8) // 2 == (to // 16) % 2)
    result = jnp.concatenate(
        [
            jnp.sum(jnp.where(keep, spread[32 * ch : 32 * ch + 32], 0.0), axis=0, keepdims=True)
            for ch in range(4)
        ],
        axis=0,
    )
    for copy in range(NY):
        sent[copy] = result


def turn_kernel(column, sent):
    sub, group = iota((8, 128), 0), iota((8, 128), 1) // 16
    tiles = [column[8 * j : 8 * j + 8, :] for j in range(8)]
    moved = [[roll(tile, 16 * d) for d in range(8)] for tile in tiles]
    for q in range(8):
        for half in range(2):
            value = jnp.zeros((8, 128), F32)
            for j in range(4):
                for odd in range(2):
                    to = 2 * j + odd
                    mask = (sub // 4 == odd) & (group == to)
                    value = jnp.where(mask, moved[4 * half + j][(to - q) % 8], value)
            value = value + roll(value, 4, 0)
            row = (q * 2 + half) * 4
            for copy in range(NX):
                sent[copy, row : row + 4, :] = value[0:4]


def top_kernel(
    gathered, field, e_one, e_two, out,
    first, second, four, weights, diags, lefts, wide, final, sems,
):
    gx, gy = lax.axis_index("gx"), lax.axis_index("gy")
    lane, sub = iota((16, 128), 1), iota((16, 128), 0)
    cells = [(z, x, half) for z in range(4) for x in range(2) for half in range(2)]

    def plane(ch, z, x, half):
        return gathered[pl.ds(((z * 2 + x) * 2 + half) * 4 + ch, 16, stride=64), :]

    def neighbours(at, z, x, half, outside):
        own, other = at(z, x, half), at(z, 1 - x, half)
        beside = at(z, x, 1 - half)
        shifted = roll(other, 1 if x == 0 else -1, 0)
        low, high = (shifted, other) if x == 0 else (other, shifted)
        left, right = roll(own, 1), roll(own, -1)
        if half == 0:
            right = jnp.where(lane == 127, roll(beside, -1), right)
        else:
            left = jnp.where(lane == 0, roll(beside, 1), left)
        down = at(z - 1, x, half) if z > 0 else outside
        up = at(z + 1, x, half) if z < 3 else outside
        return own, [low, high, left, right, down, up]

    def edge_masks(x, half):
        return [
            sub > 0 if x == 0 else None,
            sub < 15 if x == 1 else None,
            lane > 0 if half == 0 else None,
            lane < 127 if half == 1 else None,
            None,
            None,
        ]

    def key(z, x, half):
        return (z * 2 + x) * 2 + half

    shares = {c: plane(3, *c) for c in cells}
    rests = {c: resist(shares[c]) for c in cells}
    ones, zeros = jnp.ones((16, 128), F32), jnp.zeros((16, 128), F32)
    for z, x, half in cells:
        own, six = neighbours(lambda *c: rests[c], z, x, half, ones)
        masks = edge_masks(x, half)
        six = [s if m is None else jnp.where(m, s, 1.0) for s, m in zip(six, masks)]
        gain, w, diag = level_weights(own, six, 0.8)
        at = key(z, x, half)
        for i in range(6):
            weights[i, at] = w[i] if masks[i] is None else jnp.where(masks[i], w[i], 0.0)
        diags[at] = (1.25 * 0.25**3) * diag
        for f in range(3):
            first[f, at] = (64.0 * gain) * plane(f, z, x, half)

    for z, x, half in cells:
        at = key(z, x, half)
        w = [weights[i, at] for i in range(6)]
        for f in range(3):
            own, six = neighbours(lambda *c: first[f, key(*c)], z, x, half, zeros)
            second[half, f, z * 2 + x] = 1.2 * own + weigh(w, six)

    for z4 in range(2):
        for half in range(2):
            sums = [None] * 4
            for z in (2 * z4, 2 * z4 + 1):
                for x in range(2):
                    at = key(z, x, half)
                    w = [weights[i, at] for i in range(6)]
                    diag = diags[at]
                    for f in range(3):
                        own, six = neighbours(
                            lambda c, d, e: second[e, f, c * 2 + d], z, x, half, zeros
                        )
                        value = ((first[f, at] - 0.8 * own) + weigh(w, six)) * diag
                        sums[f] = value if sums[f] is None else sums[f] + value
                    share = shares[z, x, half]
                    sums[3] = share if sums[3] is None else sums[3] + share
            for ch in range(4):
                lefts[ch, z4, :, 128 * half : 128 * half + 128] = sums[ch]

    pool = jnp.where(iota((256, 128), 0) // 2 == iota((256, 128), 1), 0.125, 0.0)
    level = dot(lefts[...].reshape(128, 256), pool)

    def coarsest(ch, z):
        return level[(ch * 2 + z) * 16 : (ch * 2 + z) * 16 + 16, :]

    masks = [sub > 0, sub < 15, lane > 0, lane < 127]
    resists = [resist(coarsest(3, z)) for z in range(2)]
    gains, ws, ds = [], [], []
    for z in range(2):
        own, other = resists[z], resists[1 - z]
        six = [roll(own, 1, 0), roll(own, -1, 0), roll(own, 1), roll(own, -1)]
        six = [jnp.where(m, s, 1.0) for m, s in zip(masks, six)] + [other, ones]
        gain, w, diag = level_weights(own, six, 0.8)
        gains.append(gain)
        ds.append(diag)
        ws.append([jnp.where(m, v, 0.0) for m, v in zip(masks, w)] + [w[4]])
    whole = jnp.sum(ds[0] + ds[1], keepdims=True)

    def around(values, z):
        own, other = values[z], values[1 - z]
        return weigh(ws[z], (roll(own, 1, 0), roll(own, -1, 0), roll(own, 1), roll(own, -1), other))

    begin = [[256.0 * gains[z] * coarsest(f, z) for z in range(2)] for f in range(3)]
    values = begin
    for step in range(5):
        values = [
            [(0.2 * values[f][z] + begin[f][z]) + around(values[f], z) for z in range(2)] for f in range(3)
        ]
    for f in range(3):
        change = [(begin[f][z] - 0.8 * values[f][z]) + around(values[f], z) for z in range(2)]
        total = jnp.sum(1.25 * (change[0] * ds[0] + change[1] * ds[1]), keepdims=True)
        for z in range(2):
            four[2 * f + z] = values[f][z] + total / whole

    copy = jnp.where(iota((128, 128), 0) == iota((128, 128), 1) // 2, 1.0, 0.0)
    rows = four.reshape(96, 128)[pl.ds(gx, 6, stride=16), :]
    rows = jnp.concatenate([jnp.broadcast_to(rows[i : i + 1], (4, 128)) for i in range(6)], axis=0)
    three = dot(turn(rows, -8 * gy), copy)
    flat = second.reshape(768, 128)
    halves = [flat[pl.ds(gx + 384 * half, 24, stride=16), :] for half in range(2)]
    three = three + turn(jnp.where(gy < 8, halves[0], halves[1]), -16 * lax.rem(gy, 8))

    three = dot(three, copy)
    low = iota((8, 128), 0) < 2
    tiles = []
    for f in range(3):
        for z in range(4):
            at = f * 8 + z * 2
            tile = jnp.where(
                low,
                jnp.broadcast_to(three[at : at + 1], (8, 128)),
                jnp.broadcast_to(three[at + 1 : at + 2], (8, 128)),
            )
            tiles += [e_two[f, 2 * z] + tile, e_two[f, 2 * z + 1] + tile]

    two = dot(jnp.concatenate(tiles, axis=0), copy)
    for block in range(24):
        value = two[8 * block : 8 * block + 4, :]
        wide[pl.ds(8 * block, 4, stride=2), :] = value
        wide[pl.ds(8 * block + 1, 4, stride=2), :] = value
    one = e_one[...].reshape(24, 2, 8, 128) + wide[...].reshape(24, 1, 8, 128)

    one = dot(one.reshape(384, 128), copy)
    flat_in = field.reshape(3 * 32 * 16, 128)
    flat_out = final.reshape(3 * 32 * 16, 128)
    copies = []
    for f in range(3):
        for block in range(16 * f, 16 * f + 16):
            value = one[8 * block : 8 * block + 8, :]
            for k in range(2):
                for half in range(2):
                    at = pl.ds(32 * block + 16 * k + half, 8, stride=2)
                    flat_out[at, :] = flat_in[at, :] + value
        copies.append(pltpu.make_async_copy(final.at[f], out.at[f], sems.at[f]))
        copies[-1].start()
    for copy in copies:
        copy.wait()


def local(labels, guess):
    up = [(i, i + 1) for i in range(NX - 1)]
    down = [(i + 1, i) for i in range(NX - 1)]
    to_up, to_down, own = call(
        rows_kernel,
        [(12, 32, 128)] * 2 + [(4, 32, 16, 128)],
        [pltpu.VMEM((32, 16, 128), jnp.int32), pltpu.SemaphoreType.DMA((4,))],
        in_specs=[ANY, ANY],
    )(pltpu.with_memory_space_constraint(guess, pltpu.HBM), pltpu.with_memory_space_constraint(labels, pltpu.HBM))
    before = lax.ppermute(to_up, "gx", up)
    after = lax.ppermute(to_down, "gx", down)
    swap_near = [(i, i ^ 1) for i in range(NY)]
    swap_far = [(i, j) for k in range(1, NY - 1, 2) for i, j in ((k, k + 1), (k + 1, k))]
    to_near, to_far, held = call(pack_kernel, [(4, 4, 24, 128)] * 2 + [(4, 34, 32, 128)], [])(
        own, before, after
    )
    from_far = lax.ppermute(to_far, "gy", swap_far)
    from_near = lax.ppermute(to_near, "gy", swap_near)
    owned, part, edges = call(
        own_kernel,
        [(3, 32, 16, 128), (4, 16, 8, 128), (4, 16, 24, 128)],
        [(3, 34, 32, 128)] * 2
        + [(6, 32, 32, 128), (32, 32, 128)]
        + [(4, 16, 16, 128), (1024, 128)],
        flops=20_000_000,
    )(held)
    rim, coarse, packed = call(
        rim_kernel,
        [(3, 16, 16, 128), (4, 16, 8, 128), (4, 2, 5, 8, 128)],
        [(3, 18, 32, 128), (18, 32, 128)]
        + [(3, 18, 32, 128)] * 2
        + [(6, 16, 32, 128), (16, 32, 128)]
        + [(4, 8, 16, 128), (512, 128)],
        flops=10_000_000,
    )(edges, part, from_near, from_far)
    before = lax.ppermute(packed, "gx", up)
    after = lax.ppermute(packed, "gx", down)
    (field,) = call(patch_kernel, [(3, 32, 16, 128)], [])(owned, rim)
    sent, e_one, e_two = call(
        middle_kernel,
        [(NY, 4, 128), (3, 16, 8, 128), (3, 8, 8, 128)],
        [(16, 24, 128), (18, 32, 128), (3, 16, 32, 128), (3, 18, 32, 128), (3, 18, 32, 128)]
        + [(6, 16, 32, 128), (16, 32, 128), (4, 8, 24, 128), (768, 128)]
        + [(10, 24, 128), (3, 10, 24, 128), (3, 10, 24, 128), (3, 8, 8, 128), (8, 8, 128)]
        + [(6, 8, 16, 128), (8, 16, 128)],
    )(coarse, before, after)
    column = lax.all_to_all(sent, "gy", split_axis=0, concat_axis=0, tiled=True).reshape(64, 128)
    (copies,) = call(turn_kernel, [(NX, 64, 128)], [])(column)
    gathered = lax.all_to_all(copies, "gx", split_axis=0, concat_axis=0, tiled=True).reshape(1024, 128)
    (out,) = call(
        top_kernel,
        [(3, 32, 16, 128)],
        [(3, 16, 16, 128), (2, 3, 8, 16, 128), (6, 16, 128), (6, 16, 16, 128), (16, 16, 128)]
        + [(4, 2, 16, 256), (192, 128), (3, 32, 16, 128), pltpu.SemaphoreType.DMA((3,))],
        out_specs=[ANY],
    )(gathered, field, e_one, e_two)
    return out


def solution(mesh):
    return jax.shard_map(
        local,
        mesh=mesh,
        in_specs=(P(None, "gx", "gy"), P(None, None, "gx", "gy")),
        out_specs=P(None, None, "gx", "gy"),
        check_vma=False,
    )
```

time: 449 us -> 84.7 us (0.19); the launches traced: 443 us -> 84.3 us
  starting transfers between devices: 177 us -> 27.5 us
  local copies, waits for them, and re-layouts: 109 us -> 0 us
  blocking collectives: 89.3 us -> 16.9 us
  other arithmetic: 57.6 us -> 0 us
  Pallas kernels: 0 us -> 21.7 us
  waiting for transfers between devices: 8.13 us -> 18 us
    ppermute x52 -> x6, starting transfers between devices: 177 us -> 15.9 us  [the longest x1 4 us: local(): before = lax.ppermute(packed, 'gx', up)]
    all_gather x4 -> x0, blocking collectives: 89.3 us -> none  [the longest x1 26.8 us: gather_grid(): lax.all_gather(rows[1], 'gx', axis=1, tiled=True)]
    reshape x10 -> x0, local copies, waits for them, and re-layouts: 82 us -> none  [the longest x4 78.7 us: restrict(): field.reshape(shape[:-3] + (shape[-3] // 2, 2, shape[-2] // 2, 2, shape[-...]
    reduce_sum x11 -> x0, other arithmetic: 29.9 us -> none  [the longest x9 29 us: restrict(): return jnp.mean(blocks, axis=(-5, -3, -1))]
    pallas_call x0 -> x8, Pallas kernels: none -> 21.7 us  [the longest x1 6.4 us: local(): call(own_kernel, [(3, 32, 16, 128), (4, 16, 8, 128), (4, 16, 24, 128)], [...]
    all_to_all x0 -> x1, blocking collectives: none -> 16.9 us  [local(): lax.all_to_all(sent, 'gy', split_axis=0, concat_axis=0, tiled=True)]
    slice x32 -> x0, local copies, waits for them, and re-layouts: 14.5 us -> none  [the longest x29 10.2 us: padded_2(): last = lax.slice_in_dim(x, length - width, length, axis=dim)]
    all_to_all x0 -> x1, starting transfers between devices: none -> 11.6 us  [local(): lax.all_to_all(copies, 'gx', split_axis=0, concat_axis=0, tiled=True)]
  transfers between devices with their start and end apart: 52 -> 7, of which waited for: 12 -> 5; matrix products, arithmetic and copies ran while one was open for 16% -> 0% of each run, Pallas kernels for 0% -> 9%
where the time goes in v1:
time: 84.7 us; the launch traced here: 84.3 us
  starting transfers between devices  27.5 us (32%)
  Pallas kernels  21.7 us (26%)
  waiting for transfers between devices  18 us (21%)
  blocking collectives  16.9 us (20%)
    all_to_all x1, blocking collectives, local(): lax.all_to_all(sent, 'gy', split_axis=0, concat_axis=0, tiled=True)  16.9 us
    all_to_all x1, starting transfers between devices, local(): lax.all_to_all(copies, 'gx', split_axis=0, concat_axis=0, tiled=True)  11.6 us
    all_to_all x1, waiting for transfers between devices, local(): lax.all_to_all(copies, 'gx', split_axis=0, concat_axis=0, tiled=True)  9.74 us
    pallas_call x1, Pallas kernels, local(): call(own_kernel, [(3, 32, 16, 128), (4, 16, 8, 128), (4, 16, 24, 128)], [...  6.4 us
    pallas_call x1, Pallas kernels, local(): call(top_kernel, [(3, 32, 16, 128)], [(3, 16, 16, 128), (2, 3, 8, 16, 128...  4 us
    ppermute x1, starting transfers between devices, local(): before = lax.ppermute(packed, 'gx', up)  4 us
    ppermute x1, starting transfers between devices, local(): before = lax.ppermute(to_up, 'gx', up)  3.96 us
    ppermute x1, waiting for transfers between devices, local(): after = lax.ppermute(to_down, 'gx', down)  3.8 us
  transfers between devices with their start and end apart: 7, of which 5 were waited for; matrix products, arithmetic and copies ran while one was open for 0% of the time, Pallas kernels for 9%

profile of v1, /device:TPU:1, one launch (start us, length us, event | category | flops | bytes accessed | tf_op | source)
XLA Modules:
  0.0 84.3 jit_solution(11091979607805743765)
XLA Ops:
  0.0 1.3 %shard_map.28 = (f32[12,32,128]{2,1,0:T(8,128)S(1)}, f32[12,32,128]{2,1,0:T(8,128)S(1)}, f32[4,32,16,128]{3,2,1,0:T(8,128)S(1)}) custom-call(f32[3,32,16,128]{3,2,1,0:T(8,128)} %guess.1, s32[32,16,128]{2,1,0:T(8,128)} %labels.1), custom_call_target="tpu_custom_call" | custom-call | flops 1000000 | bytes 4000000 | tf_op jit(solution)/shard_map/pallas_call | solution.py:650
  1.3 4.0 %collective-permute-start = (f32[12,32,128]{2,1,0:T(8,128)S(1)}, f32[12,32,128]{2,1,0:T(8,128)S(1)}, u32[]{:S(2)}, u32[]{:S(2)}) collective-permute-start(f32[12,32,128]{2,1,0:T(8,128)S(1)} %get-tuple-element.21), channel_id=1, source_target_pairs={{0,16},{16,32},{32,48},{48,64},{64,80},{80,96},{96,112},{112,128},... | collective-permute-start | bytes 589832 | tf_op jit(solution)/shard_map/ppermute | solution.py:656
  5.2 1.3 %collective-permute-start.1 = (f32[12,32,128]{2,1,0:T(8,128)S(1)}, f32[12,32,128]{2,1,0:T(8,128)S(1)}, u32[]{:S(2)}, u32[]{:S(2)}) collective-permute-start(f32[12,32,128]{2,1,0:T(8,128)S(1)} %get-tuple-element.22), channel_id=1, source_target_pairs={{16,0},{32,16},{48,32},{64,48},{80,64},{96,80},{112,96},{128,112},... | collective-permute-start | bytes 589832 | tf_op jit(solution)/shard_map/ppermute | solution.py:657
  6.5 2.2 %collective-permute-done.before = f32[12,32,128]{2,1,0:T(8,128)S(1)} collective-permute-done((f32[12,32,128]{2,1,0:T(8,128)S(1)}, f32[12,32,128]{2,1,0:T(8,128)S(1)}, u32[]{:S(2)}, u32[]{:S(2)}) %collective-permute-start) | collective-permute-done | bytes 196640 | tf_op jit(solution)/shard_map/ppermute | solution.py:656
  8.8 3.8 %collective-permute-done.1.after = f32[12,32,128]{2,1,0:T(8,128)S(1)} collective-permute-done((f32[12,32,128]{2,1,0:T(8,128)S(1)}, f32[12,32,128]{2,1,0:T(8,128)S(1)}, u32[]{:S(2)}, u32[]{:S(2)}) %collective-permute-start.1) | collective-permute-done | bytes 196640 | tf_op jit(solution)/shard_map/ppermute | solution.py:657
  12.6 1.1 %shard_map.29 = (f32[4,4,24,128]{3,2,1,0:T(8,128)S(1)}, f32[4,4,24,128]{3,2,1,0:T(8,128)S(1)}, f32[4,34,32,128]{3,2,1,0:T(8,128)S(1)}) custom-call(f32[4,32,16,128]{3,2,1,0:T(8,128)S(1)} %get-tuple-element.20.own, f32[12,32,128]{2,1,0:T(8,128)S(1)} %collective-permute-done.before, f32[12,32,128]{2,1,0:T(8,128)S(1)} %collective-permute-done.1.after), custom_call_target="tpu_custom_call" | custom-call | flops 1000000 | bytes 4000000 | tf_op jit(solution)/shard_map/pallas_call | solution.py:660
  13.7 2.0 %collective-permute-start.2 = (f32[4,4,24,128]{3,2,1,0:T(8,128)S(1)}, f32[4,4,24,128]{3,2,1,0:T(8,128)S(1)}, u32[]{:S(2)}, u32[]{:S(2)}) collective-permute-start(f32[4,4,24,128]{3,2,1,0:T(8,128)S(1)} %get-tuple-element.26), channel_id=1, source_target_pairs={{0,1},{1,0},{2,3},{3,2},{4,5},{5,4},{6,7},{7,6},{8,9},{9,8},{10,11... | collective-permute-start | bytes 589832 | tf_op jit(solution)/shard_map/ppermute | solution.py:664
  15.6 3.4 %collective-permute-start.3 = (f32[4,4,24,128]{3,2,1,0:T(8,128)S(1)}, f32[4,4,24,128]{3,2,1,0:T(8,128)S(1)}, u32[]{:S(2)}, u32[]{:S(2)}) collective-permute-start(f32[4,4,24,128]{3,2,1,0:T(8,128)S(1)} %get-tuple-element.27), channel_id=1, source_target_pairs={{1,2},{2,1},{3,4},{4,3},{5,6},{6,5},{7,8},{8,7},{9,10},{10,9},{11,... | collective-permute-start | bytes 589832 | tf_op jit(solution)/shard_map/ppermute | solution.py:663
  19.1 6.4 %shard_map.30 = (f32[3,32,16,128]{3,2,1,0:T(8,128)S(1)}, f32[4,16,8,128]{3,2,1,0:T(8,128)S(1)}, f32[4,16,24,128]{3,2,1,0:T(8,128)S(1)}) custom-call(f32[4,34,32,128]{3,2,1,0:T(8,128)S(1)} %get-tuple-element.23.held), custom_call_target="tpu_custom_call" | custom-call | flops 20000000 | bytes 4000000 | tf_op jit(solution)/shard_map/pallas_call | solution.py:665
  25.5 0.0 collective-permute-done.2.near
  25.5 0.0 collective-permute-done.3.far
  25.5 3.6 %shard_map.31 = (f32[3,16,16,128]{3,2,1,0:T(8,128)S(1)}, f32[4,16,8,128]{3,2,1,0:T(8,128)S(1)}, f32[4,2,5,8,128]{4,3,2,1,0:T(8,128)S(1)}) custom-call(f32[4,16,24,128]{3,2,1,0:T(8,128)S(1)} %get-tuple-element.24.edges, f32[4,16,8,128]{3,2,1,0:T(8,128)S(1)} %get-tuple-element.25.owned, f32[4,4,24,128]{3,2,1,0:T(8,128)S(1)} %collective-permute-done.2.near, ...), custom_call_target="tpu_custom_call" | custom-call | flops 10000000 | bytes 4000000 | tf_op jit(solution)/shard_map/pallas_call | solution.py:673
  29.1 1.3 %collective-permute-start.5 = (f32[4,2,5,8,128]{4,3,2,1,0:T(8,128)S(1)}, f32[4,2,5,8,128]{4,3,2,1,0:T(8,128)S(1)}, u32[]{:S(2)}, u32[]{:S(2)}) collective-permute-start(f32[4,2,5,8,128]{4,3,2,1,0:T(8,128)S(1)} %get-tuple-element.29), channel_id=1, source_target_pairs={{16,0},{32,16},{48,32},{64,48},{80,64},{96,80},{112,96},{128,112},... | collective-permute-start | bytes 491528 | tf_op jit(solution)/shard_map/ppermute | solution.py:683
  30.4 4.0 %collective-permute-start.4 = (f32[4,2,5,8,128]{4,3,2,1,0:T(8,128)S(1)}, f32[4,2,5,8,128]{4,3,2,1,0:T(8,128)S(1)}, u32[]{:S(2)}, u32[]{:S(2)}) collective-permute-start(f32[4,2,5,8,128]{4,3,2,1,0:T(8,128)S(1)} %get-tuple-element.29), channel_id=1, source_target_pairs={{0,16},{16,32},{32,48},{48,64},{64,80},{80,96},{96,112},{112,128},... | collective-permute-start | bytes 491528 | tf_op jit(solution)/shard_map/ppermute | solution.py:682
  34.4 0.8 collective-permute-done.5.after
  35.2 1.5 %collective-permute-done.4.before = f32[4,2,5,8,128]{4,3,2,1,0:T(8,128)S(1)} collective-permute-done((f32[4,2,5,8,128]{4,3,2,1,0:T(8,128)S(1)}, f32[4,2,5,8,128]{4,3,2,1,0:T(8,128)S(1)}, u32[]{:S(2)}, u32[]{:S(2)}) %collective-permute-start.4) | collective-permute-done | bytes 163872 | tf_op jit(solution)/shard_map/ppermute | solution.py:682
  36.7 3.4 %shard_map.32 = (f32[16,4,128]{2,1,0:T(4,128)S(1)}, f32[3,16,8,128]{3,2,1,0:T(8,128)S(1)}, f32[3,8,8,128]{3,2,1,0:T(8,128)S(1)}) custom-call(f32[4,16,8,128]{3,2,1,0:T(8,128)S(1)} %get-tuple-element.28.mine, f32[4,2,5,8,128]{4,3,2,1,0:T(8,128)S(1)} %collective-permute-done.4.before, f32[4,2,5,8,128]{4,3,2,1,0:T(8,128)S(1)} %collective-permute-done.5.after), custom_call_target="tpu_custom_call" | custom-call | flops 1000000 | bytes 4000000 | tf_op jit(solution)/shard_map/pallas_call | solution.py:685
  40.1 16.9 %all_to_all.10 = f32[16,4,128]{2,1,0:T(4,128)S(1)} all-to-all(f32[16,4,128]{2,1,0:T(4,128)S(1)} %get-tuple-element.30), channel_id=1, replica_groups=mesh['gx'=16,'gy'=16] {'gy'}, dimensions={0} | all-to-all | bytes 65536 | tf_op jit(solution)/shard_map/all_to_all | solution.py:693
  57.0 1.0 %shard_map.33 = f32[16,64,128]{2,1,0:T(8,128)} custom-call(f32[64,128]{1,0:T(8,128)S(1)} %bitcast.3), custom_call_target="tpu_custom_call" | custom-call | flops 1000000 | bytes 4000000 | tf_op jit(solution)/shard_map/pallas_call | solution.py:694
  58.0 11.6 %all-to-all-start.1 = ((f32[16,64,128]{2,1,0:T(8,128)}), f32[16,64,128]{2,1,0:T(8,128)S(1)}, u32[]{:S(2)}, u32[]{:S(2)}) async-start(f32[16,64,128]{2,1,0:T(8,128)} %shard_map.33), calls=%async_computation.1 | async-start | bytes 1048576 | tf_op jit(solution)/shard_map/all_to_all | solution.py:695
  69.6 0.9 %shard_map.34.field = f32[3,32,16,128]{3,2,1,0:T(8,128)S(1)} custom-call(f32[3,32,16,128]{3,2,1,0:T(8,128)S(1)} %get-tuple-element.31.owned, f32[3,16,16,128]{3,2,1,0:T(8,128)S(1)} %get-tuple-element.32.rim), custom_call_target="tpu_custom_call" | custom-call | flops 1000000 | bytes 4000000 | tf_op jit(solution)/shard_map/pallas_call | solution.py:684
  70.6 9.7 %all-to-all-done.1 = f32[16,64,128]{2,1,0:T(8,128)S(1)} async-done(((f32[16,64,128]{2,1,0:T(8,128)}), f32[16,64,128]{2,1,0:T(8,128)S(1)}, u32[]{:S(2)}, u32[]{:S(2)}) %all-to-all-start.1) | async-done | bytes 524320 | tf_op jit(solution)/shard_map/all_to_all | solution.py:695
  80.3 4.0 %shard_map.35 = f32[3,32,16,128]{3,2,1,0:T(8,128)} custom-call(f32[1024,128]{1,0:T(8,128)S(1)} %bitcast.2, f32[3,32,16,128]{3,2,1,0:T(8,128)S(1)} %shard_map.34.field, f32[3,16,8,128]{3,2,1,0:T(8,128)S(1)} %get-tuple-element.33.e_one, f32[3,8,8,128]{3,2,1,0:T(8,128)S(1)} %get-tuple-element.34.e_two), custom_call_target="tpu_custom_call" | custom-call | flops 1000000 | bytes 4000000 | tf_op jit(solution)/shard_map/pallas_call | solution.py:696
Async XLA Ops:
  1.3 7.5 %collective-permute-start = (f32[12,32,128]{2,1,0:T(8,128)S(1)}, f32[12,32,128]{2,1,0:T(8,128)S(1)}, u32[]{:S(2)}, u32[]{:S(2)}) collective-permute-start(f32[12,32,128]{2,1,0:T(8,128)S(1)} %get-tuple-element.21), channel_id=1, source_target_pairs={{0,16},{16,32},{32,48},{48,64},{64,80},{80,96},{96,112},{112,128},... | collective-permute-start | bytes 589832 | tf_op jit(solution)/shard_map/ppermute | solution.py:656
  5.2 7.3 %collective-permute-start.1 = (f32[12,32,128]{2,1,0:T(8,128)S(1)}, f32[12,32,128]{2,1,0:T(8,128)S(1)}, u32[]{:S(2)}, u32[]{:S(2)}) collective-permute-start(f32[12,32,128]{2,1,0:T(8,128)S(1)} %get-tuple-element.22), channel_id=1, source_target_pairs={{16,0},{32,16},{48,32},{64,48},{80,64},{96,80},{112,96},{128,112},... | collective-permute-start | bytes 589832 | tf_op jit(solution)/shard_map/ppermute | solution.py:657
  13.7 11.8 %collective-permute-start.2 = (f32[4,4,24,128]{3,2,1,0:T(8,128)S(1)}, f32[4,4,24,128]{3,2,1,0:T(8,128)S(1)}, u32[]{:S(2)}, u32[]{:S(2)}) collective-permute-start(f32[4,4,24,128]{3,2,1,0:T(8,128)S(1)} %get-tuple-element.26), channel_id=1, source_target_pairs={{0,1},{1,0},{2,3},{3,2},{4,5},{5,4},{6,7},{7,6},{8,9},{9,8},{10,11... | collective-permute-start | bytes 589832 | tf_op jit(solution)/shard_map/ppermute | solution.py:664
  15.6 9.9 %collective-permute-start.3 = (f32[4,4,24,128]{3,2,1,0:T(8,128)S(1)}, f32[4,4,24,128]{3,2,1,0:T(8,128)S(1)}, u32[]{:S(2)}, u32[]{:S(2)}) collective-permute-start(f32[4,4,24,128]{3,2,1,0:T(8,128)S(1)} %get-tuple-element.27), channel_id=1, source_target_pairs={{1,2},{2,1},{3,4},{4,3},{5,6},{6,5},{7,8},{8,7},{9,10},{10,9},{11,... | collective-permute-start | bytes 589832 | tf_op jit(solution)/shard_map/ppermute | solution.py:663
  29.1 6.1 %collective-permute-start.5 = (f32[4,2,5,8,128]{4,3,2,1,0:T(8,128)S(1)}, f32[4,2,5,8,128]{4,3,2,1,0:T(8,128)S(1)}, u32[]{:S(2)}, u32[]{:S(2)}) collective-permute-start(f32[4,2,5,8,128]{4,3,2,1,0:T(8,128)S(1)} %get-tuple-element.29), channel_id=1, source_target_pairs={{16,0},{32,16},{48,32},{64,48},{80,64},{96,80},{112,96},{128,112},... | collective-permute-start | bytes 491528 | tf_op jit(solution)/shard_map/ppermute | solution.py:683
  30.4 6.2 %collective-permute-start.4 = (f32[4,2,5,8,128]{4,3,2,1,0:T(8,128)S(1)}, f32[4,2,5,8,128]{4,3,2,1,0:T(8,128)S(1)}, u32[]{:S(2)}, u32[]{:S(2)}) collective-permute-start(f32[4,2,5,8,128]{4,3,2,1,0:T(8,128)S(1)} %get-tuple-element.29), channel_id=1, source_target_pairs={{0,16},{16,32},{32,48},{48,64},{64,80},{80,96},{96,112},{112,128},... | collective-permute-start | bytes 491528 | tf_op jit(solution)/shard_map/ppermute | solution.py:682
  58.0 22.3 %all-to-all-start.1 = ((f32[16,64,128]{2,1,0:T(8,128)}), f32[16,64,128]{2,1,0:T(8,128)S(1)}, u32[]{:S(2)}, u32[]{:S(2)}) async-start(f32[16,64,128]{2,1,0:T(8,128)} %shard_map.33), calls=%async_computation.1 | async-start | bytes 1048576 | tf_op jit(solution)/shard_map/all_to_all | solution.py:695

commit v2 on v1

--- a/solution.py
+++ b/solution.py
@@ -39,7 +39,7 @@
         kernel,
         out_shape=[jax.ShapeDtypeStruct(s, F32) for s in outs],
         scratch_shapes=[pltpu.VMEM(s, F32) if isinstance(s, tuple) else s for s in scratch],
-        compiler_params=pltpu.CompilerParams(vmem_limit_bytes=48 * 1024 * 1024),
+        compiler_params=pltpu.CompilerParams(vmem_limit_bytes=32 * 1024 * 1024),
         cost_estimate=pl.CostEstimate(flops=flops, bytes_accessed=4_000_000, transcendentals=0),
         **kw,
     )
@@ -60,7 +60,9 @@
     return parts[0]
 
 
-def rows_kernel(guess, labels, up, down, own, phase, sems):
+def rows_kernel(guess, labels, near, far, own, phase, sems):
+    even = lax.rem(lax.axis_index("gx"), 2) == 0
+    near_row, far_row = jnp.where(even, 13, 0), jnp.where(even, 0, 13)
     copies = [pltpu.make_async_copy(labels, phase, sems.at[3])]
     for f in range(3):
         copies.append(pltpu.make_async_copy(guess.at[f], own.at[f], sems.at[f]))
@@ -73,40 +75,52 @@
         if ch < 3:
             copies[ch + 1].wait()
         for row in range(3):
-            up[3 * ch + row] = flat[pl.ds(512 * ch + 13 + row, 32, stride=16), :]
-            down[3 * ch + row] = flat[pl.ds(512 * ch + row, 32, stride=16), :]
-
-
-def pack_kernel(own, before, after, near, far, held):
+            near[3 * ch + row] = flat[pl.ds(512 * ch + near_row + row, 32, stride=16), :]
+            far[3 * ch + row] = flat[pl.ds(512 * ch + far_row + row, 32, stride=16), :]
+
+
+def pack_kernel(to_right, to_left, x_near, x_far, near, far, rim):
     first_core = lax.rem(lax.axis_index("gy"), 2) == 0
-    flat = held.reshape(4 * 34 * 32, 128)
+    even = lax.rem(lax.axis_index("gx"), 2) == 0
+    near_row, far_row = jnp.where(even, 0, 5), jnp.where(even, 5, 0)
+    flat = rim.reshape(4 * 32 * 8, 128)
     for ch in range(4):
-        first = (ch * 34 + 1) * 32
         for row in range(3):
-            flat[pl.ds(first + row, 32, stride=32), :] = before[3 * ch + row]
-            flat[pl.ds(first + 19 + row, 32, stride=32), :] = after[3 * ch + row]
-        held[ch, 0] = jnp.zeros((32, 128), F32)
-        held[ch, 33] = jnp.zeros((32, 128), F32)
-
-    def plane(z):
-        for ch in range(4):
-            held[ch, z + 1, 3:19, :] = own[ch, z]
-
-    loop(32, plane, 4)
-    group = iota((24, 128), 1) // 16
+            flat[pl.ds(256 * ch + near_row + row, 32, stride=8), :] = x_near[3 * ch + row]
+            flat[pl.ds(256 * ch + far_row + row, 32, stride=8), :] = x_far[3 * ch + row]
 
     def some(low):
         for ch in range(4):
-            to_right = jnp.zeros((24, 128), F32)
-            to_left = jnp.zeros((24, 128), F32)
-            for h in range(8):
-                moved = roll(held[ch, 4 * h + low + 1, 0:24, :], 16 * h + 16)
-                to_right = jnp.where(group == h, moved, to_right)
-                to_left = jnp.where(group == (h + 1) % 8, moved, to_left)
-            near[ch, low] = jnp.where(first_core, to_right, to_left)
-            far[ch, low] = jnp.where(first_core, to_left, to_right)
+            right, left = pack_planes(lambda z: rim[ch, z], low, (8, 128))
+            for at, right, left in (
+                (slice(0, 16), to_right[ch, low], to_left[ch, low]),
+                (slice(16, 24), right, left),
+            ):
+                near[ch, low, at, :] = jnp.where(first_core, right, left)
+                far[ch, low, at, :] = jnp.where(first_core, left, right)
 
     loop(4, some)
+
+
+def pack_planes(plane, low, shape):
+    group = iota(shape, 1) // 16
+    right = left = jnp.zeros(shape, F32)
+    for h in range(8):
+        moved = roll(plane(4 * h + low), 16 * h + 16)
+        right = jnp.where(group == h, moved, right)
+        left = jnp.where(group == (h + 1) % 8, moved, left)
+    return right, left
+
+
+def edge_columns(plane, z, shape):
+    lane = iota(shape, 1)
+    value = jnp.zeros(shape, F32)
+    for half in range(2):
+        source = plane(z + 16 * half)
+        base = 64 * half
+        value = jnp.where((lane >= base) & (lane < base + 7), roll(source, base + 7), value)
+        value = jnp.where((lane >= base + 57) & (lane < base + 64), roll(source, base + 57), value)
+    return value
 
 
 def six_of(ref, lead, z, first, count):
@@ -125,90 +139,199 @@
     return jnp.where(total < 0.5, 1.0, jnp.where(total < 1.5, BETWEEN, 0.1))
 
 
-def rows_inside(gx, shape):
-    row = iota(shape, 0) + 1
-    low, high = jnp.where(gx > 0, 1, 0), jnp.where(gx < NX - 1, 1, 0)
-    return jnp.where(row < 3, low, jnp.where(row >= 19, high, 1))
-
-
-def fine_sweeps(planes, start, share, one, two, weights, diags, halves, omega, wrap, keep, unroll):
+def fine_weights(own, six, omega):
+    faces = [face(own + other) for other in six]
+    diag = (faces[0] + faces[1]) + (faces[2] + faces[3]) + (faces[4] + faces[5])
+    gain = omega * recip(diag)
+    return [gain * value for value in faces], 1.25 * diag
+
+
+def fine_sweep(w, f, own, six):
+    return (0.2 * own + (w[2 * f + 1] - w[2 * f])) + weigh(w, six)
+
+
+def fine_left(w, f, own, six, diag):
+    return (((w[2 * f + 1] - w[2 * f]) - 0.8 * own) + weigh(w, six)) * diag
+
+
+def fine_sweeps(planes, windows, start, share, one, two, weights, diags, halves, omega, wrap, keep):
+    first, count = windows[0]
+
     def first_sweep(z):
-        own, six = six_of(share, (), z + 1, 1, 24)
-        faces = [face(own + other) for other in six]
-        diag = (faces[0] + faces[1]) + (faces[2] + faces[3]) + (faces[4] + faces[5])
-        gain = omega * recip(diag)
-        diags[z, 1:25, :] = 1.25 * diag
-        w = [gain * value for value in faces]
+        own, six = six_of(share, (), z + 1, first, count)
+        w, diag = fine_weights(own, six, omega)
+        diags[z, pl.ds(first, count), :] = diag
         for i in range(6):
-            weights[i, z, 1:25, :] = w[i]
-        for f in range(3):
-            own, six = six_of(start, (f,), z + 1, 1, 24)
-            one[f, z + 1, 1:25, :] = (0.2 * own + (w[2 * f + 1] - w[2 * f])) + weigh(w, six)
-
-    loop(planes, first_sweep, unroll)
+            weights[i, z, pl.ds(first, count), :] = w[i]
+        for f in range(3):
+            own, six = six_of(start, (f,), z + 1, first, count)
+            one[f, z + 1, pl.ds(first, count), :] = fine_sweep(w, f, own, six)
+
+    loop(planes, first_sweep, 4)
     wrap(one)
+    second, count2 = windows[1]
 
     def second_sweep(z):
-        w = [weights[i, z, 2:26, :] for i in range(6)]
-        for f in range(3):
-            own, six = six_of(one, (f,), z + 1, 2, 24)
-            two[f, z + 1, 2:26, :] = (0.2 * own + (w[2 * f + 1] - w[2 * f])) + weigh(w, six)
-
-    loop(planes, second_sweep, unroll)
+        w = [weights[i, z, pl.ds(second, count2), :] for i in range(6)]
+        for f in range(3):
+            own, six = six_of(one, (f,), z + 1, second, count2)
+            two[f, z + 1, pl.ds(second, count2), :] = fine_sweep(w, f, own, six)
+
+    loop(planes, second_sweep, 4)
     wrap(two)
 
     def residual(pair):
         sums = {}
         for k in range(2):
             z = 2 * pair + k
-            w = [weights[i, z, 3:19, :] for i in range(6)]
-            diag = diags[z, 3:19, :]
+            w = [weights[i, z, 8:24, :] for i in range(6)]
+            diag = diags[z, 8:24, :]
             for f in range(3):
-                own, six = six_of(two, (f,), z + 1, 3, 16)
-                keep[f, z] = own
-                value = (((w[2 * f + 1] - w[2 * f]) - 0.8 * own) + weigh(w, six)) * diag
+                own, six = six_of(two, (f,), z + 1, 8, 16)
+                if keep is not None:
+                    keep[f, z] = own
+                value = fine_left(w, f, own, six, diag)
                 sums[f] = value if k == 0 else sums[f] + value
-            value = share[z + 1, 3:19, :]
+            value = share[z + 1, 8:24, :]
             sums[3] = value if k == 0 else sums[3] + value
         for ch, value in sums.items():
             halves[ch, pair] = value
 
-    loop(planes // 2, residual, unroll // 2)
-
-
-def own_kernel(held, field, coarse, edges, one, two, weights, diags, halves, pooled):
+    loop(planes // 2, residual, 2)
+
+
+def own_kernel(own, one, two, halves, to_right, to_left, edges, held, weights, diags):
+    zero = jnp.zeros((32, 128), F32)
+    for z in (0, 33):
+        for ch in range(4):
+            held[ch, z] = zero
+        for ref in (one, two):
+            for f in range(3):
+                ref[f, z] = zero
+
+    def plane(z):
+        for ch in range(4):
+            held[ch, z + 1, 8:24, :] = own[ch, z]
+
+    loop(32, plane, 4)
+    fine_sweeps(
+        32, [(8, 16)] * 2, held, held.at[3], one, two, weights, diags, halves, 0.8, lambda ref: None, None
+    )
+
+    def some(low):
+        for ch in range(4):
+            to_right[ch, low], to_left[ch, low] = pack_planes(lambda z: own[ch, z], low, (16, 128))
+
+    loop(4, some)
+
+    def edge(z):
+        for ch in range(4):
+            edges[ch, z] = edge_columns(lambda at: own[ch, at], z, (16, 128))
+
+    loop(16, edge, 2)
+
+
+def rows_edge_kernel(own, rim, own_one, own_two, own_halves, two, coarse, edges, start, one, weights, diags, halves, pooled):
     gx = lax.axis_index("gx")
-    for ref in (one, two):
-        for f in range(3):
-            ref[f, 0] = jnp.zeros((32, 128), F32)
-            ref[f, 33] = jnp.zeros((32, 128), F32)
-    omega = 0.8 * rows_inside(gx, (24, 128)).astype(F32)
-    fine_sweeps(
-        32, held, held.at[3], one, two, weights, diags, halves, omega, lambda ref: None, field, 4
-    )
+    zero = jnp.zeros((24, 128), F32)
+    for z in (0, 33):
+        for ch in range(4):
+            start[ch, z] = zero
+        for ref in (one, two):
+            for f in range(3):
+                ref[f, z] = zero
+
+    def fill(z):
+        for ch in range(4):
+            start[ch, z + 1, 0:8, :] = own[ch, z, 8:16, :]
+            start[ch, z + 1, 8:16, :] = rim[ch, z]
+            start[ch, z + 1, 16:24, :] = own[ch, z, 0:8, :]
+        for f in range(3):
+            for ref, source in ((one, own_one), (two, own_two)):
+                ref[f, z + 1, 0:8, :] = source[f, z + 1, 16:24, :]
+                ref[f, z + 1, 16:24, :] = source[f, z + 1, 8:16, :]
+
+    loop(32, fill, 4)
+    upper = iota((8, 128), 0) < 4
+
+    def both(ref, lead, step, shift=0):
+        high = ref[(*lead, pl.ds(8 - step + shift, 8), slice(None))]
+        low = ref[(*lead, pl.ds(8 + step + shift, 8), slice(None))]
+        return jnp.where(upper, high, low)
+
+    def six_both(ref, f, z, step):
+        value = both(ref, (f, z), step)
+        return value, (
+            both(ref, (f, z), step, -1),
+            both(ref, (f, z), step, 1),
+            roll(value, 1),
+            roll(value, -1),
+            both(ref, (f, z - 1), step),
+            both(ref, (f, z + 1), step),
+        )
+
+    def put(ref, f, z, step, value):
+        ref[f, z, pl.ds(8 - step, 4), :] = value[0:4]
+        ref[f, z, pl.ds(12 + step, 4), :] = value[4:8]
+
+    row = iota((16, 128), 0) + 5
+    low, high = jnp.where(gx > 0, 1, 0), jnp.where(gx < NX - 1, 1, 0)
+    inside = jnp.where((row >= 8) & (row < 12), high, jnp.where((row >= 12) & (row < 16), low, 1))
+    omega = 0.8 * inside.astype(F32)
+
+    def weigh_all(z):
+        value, six = six_of(start, (3,), z + 1, 5, 16)
+        w, diag = fine_weights(value, six, omega)
+        diags[z, 5:21, :] = diag
+        for i in range(6):
+            weights[i, z, 5:21, :] = w[i]
+
+    loop(32, weigh_all, 4)
+
+    for step, source, target in ((1, start, one), (2, one, two)):
+
+        def sweep(z):
+            w = [both(weights, (i, z), step) for i in range(6)]
+            for f in range(3):
+                value, six = six_both(source, f, z + 1, step)
+                put(target, f, z + 1, step, fine_sweep(w, f, value, six))
+
+        loop(32, sweep, 4)
+
+    sub = iota((8, 128), 0)
+
+    def residual(pair):
+        sums = {}
+        for k in range(2):
+            z = 2 * pair + k
+            w = [both(weights, (i, z), 3) for i in range(6)]
+            diag = both(diags, (z,), 3)
+            for f in range(3):
+                value, six = six_both(two, f, z + 1, 3)
+                value = fine_left(w, f, value, six, diag)
+                sums[f] = value if k == 0 else sums[f] + value
+        for f in range(3):
+            halves[f, pair, 0:8, :] = jnp.where(sub < 3, roll(sums[f], 3, 0), own_halves[f, pair, 0:8, :])
+            halves[f, pair, 8:16, :] = jnp.where(sub >= 5, roll(sums[f], 5, 0), own_halves[f, pair, 8:16, :])
+        halves[3, pair] = own_halves[3, pair]
+
+    loop(16, residual, 2)
     pool = jnp.where(iota((128, 128), 0) // 2 == iota((128, 128), 1), 0.125, 0.0)
     pooled[...] = dot(halves[...].reshape(1024, 128), pool)
     for ch in range(4):
         even = pooled[pl.ds(256 * ch, 128, stride=2), :]
         odd = pooled[pl.ds(256 * ch + 1, 128, stride=2), :]
         coarse[ch] = (even + odd).reshape(16, 8, 128)
-    lane = iota((24, 128), 1)
 
     def edge(z):
         for ch in range(4):
-            value = jnp.zeros((24, 128), F32)
-            for half in range(2):
-                source = held[ch, z + 16 * half + 1, 0:24, :]
-                base = 64 * half
-                value = jnp.where((lane >= base) & (lane < base + 7), roll(source, base + 7), value)
-                value = jnp.where((lane >= base + 57) & (lane < base + 64), roll(source, base + 57), value)
-            edges[ch, z] = value
-
-    loop(16, edge)
+            edges[ch, z] = edge_columns(lambda at: rim[ch, at], z, (8, 128))
+
+    loop(16, edge, 2)
 
 
 def rim_kernel(
-    edges, owned, near, far, field, coarse, packed,
+    edges, edges_rim, owned, near, far, field, coarse, packed,
     start, share, one, two, weights, diags, halves, pooled,
 ):
     gx, gy = lax.axis_index("gx"), lax.axis_index("gy")
@@ -227,15 +350,19 @@
                 z = 4 * h + low
                 after_y = roll(from_right, 7 - 16 * (h + 1))
                 before_y = roll(from_left, 41 - 16 * h)
-                target[z + 1, 0:24, :] = jnp.where(
-                    is_after, after_y, jnp.where(is_before, before_y, edges[ch, z])
-                )
+                own = jnp.concatenate([edges[ch, z], edges_rim[ch, z]], axis=0)
+                value = jnp.where(is_after, after_y, jnp.where(is_before, before_y, own))
+                target[z + 1, 8:24, :] = value[0:16]
+                target[z + 1, 0:8, :] = value[16:24]
+                target[z + 1, 24:32, :] = value[16:24]
 
     loop(4, unpack)
 
+    half_of = iota((32, 128), 1)
+
     def wrap_one(ref):
-        ref[0, 0:24, :] = jnp.where(lane >= 64, roll(ref[16, 0:24, :], 64), 0.0)
-        ref[17, 0:24, :] = jnp.where(lane < 64, roll(ref[1, 0:24, :], 64), 0.0)
+        ref[0] = jnp.where(half_of >= 64, roll(ref[16], 64), 0.0)
+        ref[17] = jnp.where(half_of < 64, roll(ref[1], 64), 0.0)
 
     def wrap(ref):
         for f in range(3):
@@ -243,19 +370,24 @@
 
     wrap_one(share)
     wrap(start)
+    row = iota((24, 128), 0) + 6
+    low, high = jnp.where(gx > 0, 1, 0), jnp.where(gx < NX - 1, 1, 0)
+    inside_x = jnp.where(row < 8, low, jnp.where(row >= 24, high, 1))
     inside_y = jnp.where(
         part < 32,
         jnp.where((part < 7) | (gy < NY - 1), 1, 0),
         jnp.where((part >= 57) | (gy > 0), 1, 0),
     )
-    omega = 0.8 * (rows_inside(gx, (24, 128)) * inside_y).astype(F32)
-    fine_sweeps(16, start, share, one, two, weights, diags, halves, omega, wrap, field, 4)
+    omega = 0.8 * (inside_x * inside_y).astype(F32)
+    fine_sweeps(
+        16, [(6, 24), (7, 24)], start, share, one, two, weights, diags, halves, omega, wrap, field
+    )
 
     source, target = iota((128, 128), 0), iota((128, 128), 1)
     spot = source % 64
     column = jnp.where(spot < 32, 121 + spot, 128 + spot - 57)
     to = jnp.where(spot < 32, column // 2, (column // 2 + 64) % 128)
-    from_rim = (iota((128, 128), 1) < 2) | (iota((128, 128), 1) >= 62)
+    from_rim = (iota((64, 128), 1) < 2) | (iota((64, 128), 1) >= 62)
     mixed = halves[...].reshape(512, 128)
     for half in range(2):
         pool = jnp.where((to == target) & (source // 64 == half), 0.125, 0.0)
@@ -265,7 +397,7 @@
             odd = pooled[pl.ds(128 * ch + 1, 64, stride=2), :]
             at = pl.ds(8 * half, 8)
             rest = owned[ch, at].reshape(64, 128)
-            coarse[ch, at] = jnp.where(from_rim[:64], even + odd, rest).reshape(8, 8, 128)
+            coarse[ch, at] = jnp.where(from_rim, even + odd, rest).reshape(8, 8, 128)
 
     lane = iota((8, 128), 1)
     for ch in range(4):
@@ -281,7 +413,7 @@
                 packed[ch, group, tile] = tiles[tile]
 
 
-def patch_kernel(owned, rim, field):
+def patch_kernel(two, rim, field):
     lane = iota((16, 128), 1)
 
     def plane(z):
@@ -292,7 +424,8 @@
                 low = roll(value, -57 - base)
                 high = roll(value, 121 - base)
                 at = z + 16 * half
-                field[f, at] = jnp.where(lane < 3, low, jnp.where(lane >= 125, high, owned[f, at]))
+                own = jnp.concatenate([two[f, at + 1, 16:24, :], two[f, at + 1, 0:8, :]], axis=0)
+                field[f, at] = jnp.where(lane < 3, low, jnp.where(lane >= 125, high, own))
 
     loop(16, plane, 2)
 
@@ -309,7 +442,7 @@
 
 
 def middle_kernel(
-    mine, before, after, sent, e_one, e_two,
+    mine, near, far, sent, e_one, e_two,
     share, rest, rhs, first, second, weights, diags, halves, pooled,
     rest2, first2, second2, rhs2, share2, weights2, diags2,
 ):
@@ -324,6 +457,9 @@
     for z in (0, 17):
         rest[z] = jnp.ones((32, 128), F32)
     lane = iota((8, 128), 1)
+    even = lax.rem(gx, 2) == 0
+    near_row, far_row = jnp.where(even, 16, 0), jnp.where(even, 0, 16)
+    starts = (pl.multiple_of(near_row, 8), pl.multiple_of(far_row, 8), 8)
 
     def fill(group):
         for k in range(8):
@@ -331,18 +467,18 @@
             tile, off = divmod(80 * k, 128)
             for ch in range(4):
                 parts = []
-                for ref in (before, after):
+                for ref in (near, far):
                     value = ref[ch, group, tile]
                     if off + 80 > 128:
                         value = jnp.where(lane >= off, value, ref[ch, group, tile + 1])
                     parts.append(roll(value, -8 - 80 * k))
-                parts.insert(1, mine[ch, z])
-                for i, value in enumerate(parts):
+                parts.append(mine[ch, z])
+                for at, value in zip(starts, parts):
                     if ch < 3:
-                        rhs[ch, z, 8 * i : 8 * i + 8, :] = value
+                        rhs[ch, z, pl.ds(at, 8), :] = value
                     else:
-                        share[z, 8 * i : 8 * i + 8, :] = value
-                        rest[z + 1, 8 * i : 8 * i + 8, :] = resist(value)
+                        share[z, pl.ds(at, 8), :] = value
+                        rest[z + 1, pl.ds(at, 8), :] = resist(value)
             rest[z + 1, 24:32, :] = jnp.ones((8, 128), F32)
 
     loop(2, fill)
@@ -472,6 +608,7 @@
     tiles = [column[8 * j : 8 * j + 8, :] for j in range(8)]
     moved = [[roll(tile, 16 * d) for d in range(8)] for tile in tiles]
     for q in range(8):
+        halves = []
         for half in range(2):
             value = jnp.zeros((8, 128), F32)
             for j in range(4):
@@ -479,10 +616,10 @@
                     to = 2 * j + odd
                     mask = (sub // 4 == odd) & (group == to)
                     value = jnp.where(mask, moved[4 * half + j][(to - q) % 8], value)
-            value = value + roll(value, 4, 0)
-            row = (q * 2 + half) * 4
-            for copy in range(NX):
-                sent[copy, row : row + 4, :] = value[0:4]
+            halves.append(value + roll(value, 4, 0))
+        tile = jnp.where(sub < 4, halves[0], halves[1])
+        for copy in range(NX):
+            sent[copy, 8 * q : 8 * q + 8, :] = tile
 
 
 def top_kernel(
@@ -638,38 +775,44 @@
                 for half in range(2):
                     at = pl.ds(32 * block + 16 * k + half, 8, stride=2)
                     flat_out[at, :] = flat_in[at, :] + value
-        copies.append(pltpu.make_async_copy(final.at[f], out.at[f], sems.at[f]))
-        copies[-1].start()
+            if block % 8 == 7:
+                part = (f, pl.ds(2 * (block % 16) - 14, 16))
+                copy = pltpu.make_async_copy(final.at[part], out.at[part], sems.at[len(copies)])
+                copy.start()
+                copies.append(copy)
     for copy in copies:
         copy.wait()
 
 
 def local(labels, guess):
-    up = [(i, i + 1) for i in range(NX - 1)]
-    down = [(i + 1, i) for i in range(NX - 1)]
-    to_up, to_down, own = call(
+    swap_near = [(i, i ^ 1) for i in range(NY)]
+    swap_far = [(i, j) for k in range(1, NY - 1, 2) for i, j in ((k, k + 1), (k + 1, k))]
+    to_near, to_far, own = call(
         rows_kernel,
         [(12, 32, 128)] * 2 + [(4, 32, 16, 128)],
         [pltpu.VMEM((32, 16, 128), jnp.int32), pltpu.SemaphoreType.DMA((4,))],
         in_specs=[ANY, ANY],
     )(pltpu.with_memory_space_constraint(guess, pltpu.HBM), pltpu.with_memory_space_constraint(labels, pltpu.HBM))
-    before = lax.ppermute(to_up, "gx", up)
-    after = lax.ppermute(to_down, "gx", down)
-    swap_near = [(i, i ^ 1) for i in range(NY)]
-    swap_far = [(i, j) for k in range(1, NY - 1, 2) for i, j in ((k, k + 1), (k + 1, k))]
-    to_near, to_far, held = call(pack_kernel, [(4, 4, 24, 128)] * 2 + [(4, 34, 32, 128)], [])(
-        own, before, after
+    from_near = lax.ppermute(to_near, "gx", swap_near)
+    from_far = lax.ppermute(to_far, "gx", swap_far)
+    own_one, own_two, halves, to_right, to_left, edges = call(
+        own_kernel,
+        [(3, 34, 32, 128)] * 2 + [(4, 16, 16, 128)] + [(4, 4, 16, 128)] * 2 + [(4, 16, 16, 128)],
+        [(4, 34, 32, 128), (6, 32, 32, 128), (32, 32, 128)],
+        flops=20_000_000,
+    )(own)
+    to_near, to_far, rim_rows = call(pack_kernel, [(4, 4, 24, 128)] * 2 + [(4, 32, 8, 128)], [])(
+        to_right, to_left, from_near, from_far
     )
     from_far = lax.ppermute(to_far, "gy", swap_far)
     from_near = lax.ppermute(to_near, "gy", swap_near)
-    owned, part, edges = call(
-        own_kernel,
-        [(3, 32, 16, 128), (4, 16, 8, 128), (4, 16, 24, 128)],
-        [(3, 34, 32, 128)] * 2
-        + [(6, 32, 32, 128), (32, 32, 128)]
+    two, part, edges_rim = call(
+        rows_edge_kernel,
+        [(3, 34, 24, 128), (4, 16, 8, 128), (4, 16, 8, 128)],
+        [(4, 34, 24, 128), (3, 34, 24, 128), (6, 32, 24, 128), (32, 24, 128)]
         + [(4, 16, 16, 128), (1024, 128)],
-        flops=20_000_000,
-    )(held)
+        flops=10_000_000,
+    )(own, rim_rows, own_one, own_two, halves)
     rim, coarse, packed = call(
         rim_kernel,
         [(3, 16, 16, 128), (4, 16, 8, 128), (4, 2, 5, 8, 128)],
@@ -678,10 +821,10 @@
         + [(6, 16, 32, 128), (16, 32, 128)]
         + [(4, 8, 16, 128), (512, 128)],
         flops=10_000_000,
-    )(edges, part, from_near, from_far)
-    before = lax.ppermute(packed, "gx", up)
-    after = lax.ppermute(packed, "gx", down)
-    (field,) = call(patch_kernel, [(3, 32, 16, 128)], [])(owned, rim)
+    )(edges, edges_rim, part, from_near, from_far)
+    from_near = lax.ppermute(packed, "gx", swap_near)
+    from_far = lax.ppermute(packed, "gx", swap_far)
+    (field,) = call(patch_kernel, [(3, 32, 16, 128)], [])(two, rim)
     sent, e_one, e_two = call(
         middle_kernel,
         [(NY, 4, 128), (3, 16, 8, 128), (3, 8, 8, 128)],
@@ -689,7 +832,7 @@
         + [(6, 16, 32, 128), (16, 32, 128), (4, 8, 24, 128), (768, 128)]
         + [(10, 24, 128), (3, 10, 24, 128), (3, 10, 24, 128), (3, 8, 8, 128), (8, 8, 128)]
         + [(6, 8, 16, 128), (8, 16, 128)],
-    )(coarse, before, after)
+    )(coarse, from_near, from_far)
     column = lax.all_to_all(sent, "gy", split_axis=0, concat_axis=0, tiled=True).reshape(64, 128)
     (copies,) = call(turn_kernel, [(NX, 64, 128)], [])(column)
     gathered = lax.all_to_all(copies, "gx", split_axis=0, concat_axis=0, tiled=True).reshape(1024, 128)
@@ -697,7 +840,7 @@
         top_kernel,
         [(3, 32, 16, 128)],
         [(3, 16, 16, 128), (2, 3, 8, 16, 128), (6, 16, 128), (6, 16, 16, 128), (16, 16, 128)]
-        + [(4, 2, 16, 256), (192, 128), (3, 32, 16, 128), pltpu.SemaphoreType.DMA((3,))],
+        + [(4, 2, 16, 256), (192, 128), (3, 32, 16, 128), pltpu.SemaphoreType.DMA((6,))],
         out_specs=[ANY],
     )(gathered, field, e_one, e_two)
     return out

time: 84.7 us -> 78.3 us (0.924)
  waiting for transfers between devices: 18 us -> 12.5 us
  starting transfers between devices: 27.5 us -> 23.2 us
  Pallas kernels: 21.7 us -> 24.9 us
    ppermute x4, waiting for transfers between devices: 8.28 us -> 2.71 us  [the longest x1 2.71 us: local(): from_near = lax.ppermute(packed, 'gx', swap_near)]
    pallas_call x3 -> x4, Pallas kernels: 8.44 us -> 11.7 us  [the longest x1 5.27 us: local(): call(rows_edge_kernel, [(3, 34, 24, 128), (4, 16, 8, 128), (4, 16, 8, 128...]
    all_to_all x1, starting transfers between devices: 11.6 us -> 9.27 us  [local(): lax.all_to_all(copies, 'gx', split_axis=0, concat_axis=0, tiled=True)]
    ppermute x4, starting transfers between devices: 10.5 us -> 9.46 us  [the longest x1 6 us: local(): from_near = lax.ppermute(packed, 'gx', swap_near)]
  transfers between devices with their start and end apart: 7 -> 7, of which waited for: 5 -> 2; matrix products, arithmetic and copies ran while one was open for 0% -> 0% of each run, Pallas kernels for 9% -> 14%
where the time goes in v2:
time: 78.3 us; the launch traced here: 77.9 us
  Pallas kernels  24.9 us (32%)
  starting transfers between devices  23.2 us (30%)
  blocking collectives  17.2 us (22%)
  waiting for transfers between devices  12.5 us (16%)
    all_to_all x1, blocking collectives, local(): lax.all_to_all(sent, 'gy', split_axis=0, concat_axis=0, tiled=True)  17.2 us
    all_to_all x1, waiting for transfers between devices, local(): lax.all_to_all(copies, 'gx', split_axis=0, concat_axis=0, tiled=True)  9.74 us
    all_to_all x1, starting transfers between devices, local(): lax.all_to_all(copies, 'gx', split_axis=0, concat_axis=0, tiled=True)  9.27 us
    ppermute x1, starting transfers between devices, local(): from_near = lax.ppermute(packed, 'gx', swap_near)  6 us
    pallas_call x1, Pallas kernels, local(): call(rows_edge_kernel, [(3, 34, 24, 128), (4, 16, 8, 128), (4, 16, 8, 128...  5.27 us
    pallas_call x1, Pallas kernels, local(): call(own_kernel, [(3, 34, 32, 128)] * 2 + [(4, 16, 16, 128)] + [(4, 4, 16...  4.99 us
    pallas_call x1, Pallas kernels, local(): call(top_kernel, [(3, 32, 16, 128)], [(3, 16, 16, 128), (2, 3, 8, 16, 128...  4.01 us
    pallas_call x1, Pallas kernels, local(): call(rim_kernel, [(3, 16, 16, 128), (4, 16, 8, 128), (4, 2, 5, 8, 128)],...  3.62 us
  transfers between devices with their start and end apart: 7, of which 2 were waited for; matrix products, arithmetic and copies ran while one was open for 0% of the time, Pallas kernels for 14%

profile of v2, /device:TPU:1, one launch (start us, length us, event | category | flops | bytes accessed | tf_op | source)
XLA Modules:
  0.0 77.9 jit_solution(4775166957953711352)
XLA Ops:
  0.0 1.3 %shard_map.28 = (f32[12,32,128]{2,1,0:T(8,128)S(1)}, f32[12,32,128]{2,1,0:T(8,128)S(1)}, f32[4,32,16,128]{3,2,1,0:T(8,128)S(1)}) custom-call(f32[3,32,16,128]{3,2,1,0:T(8,128)} %guess.1, s32[32,16,128]{2,1,0:T(8,128)} %labels.1), custom_call_target="tpu_custom_call" | custom-call | flops 1000000 | bytes 4000000 | tf_op jit(solution)/shard_map/pallas_call | solution.py:790
  1.3 2.1 %collective-permute-start = (f32[12,32,128]{2,1,0:T(8,128)S(1)}, f32[12,32,128]{2,1,0:T(8,128)S(1)}, u32[]{:S(2)}, u32[]{:S(2)}) collective-permute-start(f32[12,32,128]{2,1,0:T(8,128)S(1)} %get-tuple-element.30), channel_id=1, source_target_pairs={{0,16},{16,0},{32,48},{48,32},{64,80},{80,64},{96,112},{112,96},{1... | collective-permute-start | bytes 589832 | tf_op jit(solution)/shard_map/ppermute | solution.py:796
  3.4 0.7 collective-permute-start.1
  4.1 5.0 %shard_map.29 = (f32[3,34,32,128]{3,2,1,0:T(8,128)S(1)}, f32[3,34,32,128]{3,2,1,0:T(8,128)S(1)}, f32[4,16,16,128]{3,2,1,0:T(8,128)S(1)}, f32[4,4,16,128]{3,2,1,0...) custom-call(f32[4,32,16,128]{3,2,1,0:T(8,128)S(1)} %get-tuple-element.26.own), custom_call_target="tpu_custom_call" | custom-call | flops 20000000 | bytes 4000000 | tf_op jit(solution)/shard_map/pallas_call | solution.py:798
  9.1 0.0 collective-permute-done.x_near
  9.1 0.0 collective-permute-done.1.x_far
  9.1 0.5 shard_map.30
  9.6 1.3 %collective-permute-start.2 = (f32[4,4,24,128]{3,2,1,0:T(8,128)S(1)}, f32[4,4,24,128]{3,2,1,0:T(8,128)S(1)}, u32[]{:S(2)}, u32[]{:S(2)}) collective-permute-start(f32[4,4,24,128]{3,2,1,0:T(8,128)S(1)} %get-tuple-element.38), channel_id=1, source_target_pairs={{0,1},{1,0},{2,3},{3,2},{4,5},{5,4},{6,7},{7,6},{8,9},{9,8},{10,11... | collective-permute-start | bytes 589832 | tf_op jit(solution)/shard_map/ppermute | solution.py:808
  10.9 3.2 %collective-permute-start.3 = (f32[4,4,24,128]{3,2,1,0:T(8,128)S(1)}, f32[4,4,24,128]{3,2,1,0:T(8,128)S(1)}, u32[]{:S(2)}, u32[]{:S(2)}) collective-permute-start(f32[4,4,24,128]{3,2,1,0:T(8,128)S(1)} %get-tuple-element.39), channel_id=1, source_target_pairs={{1,2},{2,1},{3,4},{4,3},{5,6},{6,5},{7,8},{8,7},{9,10},{10,9},{11,... | collective-permute-start | bytes 589832 | tf_op jit(solution)/shard_map/ppermute | solution.py:807
  14.1 5.3 %shard_map.31 = (f32[3,34,24,128]{3,2,1,0:T(8,128)S(1)}, f32[4,16,8,128]{3,2,1,0:T(8,128)S(1)}, f32[4,16,8,128]{3,2,1,0:T(8,128)S(1)}) custom-call(f32[4,32,16,128]{3,2,1,0:T(8,128)S(1)} %get-tuple-element.26.own, f32[4,32,8,128]{3,2,1,0:T(8,128)S(1)} %get-tuple-element.32.rim, f32[3,34,32,128]{3,2,1,0:T(8,128)S(1)} %get-tuple-element.33.own_one, ...), custom_call_target="tpu_custom_call" | custom-call | flops 10000000 | bytes 4000000 | tf_op jit(solution)/shard_map/pallas_call | solution.py:809
  19.3 0.0 collective-permute-done.2.near
  19.4 0.0 collective-permute-done.3.far
  19.4 3.6 %shard_map.32 = (f32[3,16,16,128]{3,2,1,0:T(8,128)S(1)}, f32[4,16,8,128]{3,2,1,0:T(8,128)S(1)}, f32[4,2,5,8,128]{4,3,2,1,0:T(8,128)S(1)}) custom-call(f32[4,16,16,128]{3,2,1,0:T(8,128)S(1)} %get-tuple-element.27.edges, f32[4,16,8,128]{3,2,1,0:T(8,128)S(1)} %get-tuple-element.36.edges_rim, f32[4,16,8,128]{3,2,1,0:T(8,128)S(1)} %get-tuple-element.37.owned, ...), custom_call_target="tpu_custom_call" | custom-call | flops 10000000 | bytes 4000000 | tf_op jit(solution)/shard_map/pallas_call | solution.py:816
  23.0 0.7 collective-permute-start.5
  23.7 6.0 %collective-permute-start.4 = (f32[4,2,5,8,128]{4,3,2,1,0:T(8,128)S(1)}, f32[4,2,5,8,128]{4,3,2,1,0:T(8,128)S(1)}, u32[]{:S(2)}, u32[]{:S(2)}) collective-permute-start(f32[4,2,5,8,128]{4,3,2,1,0:T(8,128)S(1)} %get-tuple-element.41), channel_id=1, source_target_pairs={{0,16},{16,0},{32,48},{48,32},{64,80},{80,64},{96,112},{112,96},{1... | collective-permute-start | bytes 491528 | tf_op jit(solution)/shard_map/ppermute | solution.py:825
  29.7 0.0 collective-permute-done.5.far
  29.7 2.7 %collective-permute-done.4.near = f32[4,2,5,8,128]{4,3,2,1,0:T(8,128)S(1)} collective-permute-done((f32[4,2,5,8,128]{4,3,2,1,0:T(8,128)S(1)}, f32[4,2,5,8,128]{4,3,2,1,0:T(8,128)S(1)}, u32[]{:S(2)}, u32[]{:S(2)}) %collective-permute-start.4) | collective-permute-done | bytes 163872 | tf_op jit(solution)/shard_map/ppermute | solution.py:825
  32.4 3.4 %shard_map.33 = (f32[16,4,128]{2,1,0:T(4,128)S(1)}, f32[3,16,8,128]{3,2,1,0:T(8,128)S(1)}, f32[3,8,8,128]{3,2,1,0:T(8,128)S(1)}) custom-call(f32[4,16,8,128]{3,2,1,0:T(8,128)S(1)} %get-tuple-element.40.mine, f32[4,2,5,8,128]{4,3,2,1,0:T(8,128)S(1)} %collective-permute-done.4.near, f32[4,2,5,8,128]{4,3,2,1,0:T(8,128)S(1)} %collective-permute-done.5.far), custom_call_target="tpu_custom_call" | custom-call | flops 1000000 | bytes 4000000 | tf_op jit(solution)/shard_map/pallas_call | solution.py:828
  35.8 17.2 %all_to_all.10 = f32[16,4,128]{2,1,0:T(4,128)S(1)} all-to-all(f32[16,4,128]{2,1,0:T(4,128)S(1)} %get-tuple-element.42), channel_id=1, replica_groups=mesh['gx'=16,'gy'=16] {'gy'}, dimensions={0} | all-to-all | bytes 65536 | tf_op jit(solution)/shard_map/all_to_all | solution.py:836
  53.0 1.0 %shard_map.34 = f32[16,64,128]{2,1,0:T(8,128)} custom-call(f32[64,128]{1,0:T(8,128)S(1)} %bitcast.3), custom_call_target="tpu_custom_call" | custom-call | flops 1000000 | bytes 4000000 | tf_op jit(solution)/shard_map/pallas_call | solution.py:837
  54.0 9.3 %all-to-all-start.1 = ((f32[16,64,128]{2,1,0:T(8,128)}), f32[16,64,128]{2,1,0:T(8,128)S(1)}, u32[]{:S(2)}, u32[]{:S(2)}) async-start(f32[16,64,128]{2,1,0:T(8,128)} %shard_map.34), calls=%async_computation.1 | async-start | bytes 1048576 | tf_op jit(solution)/shard_map/all_to_all | solution.py:838
  63.2 0.9 %shard_map.35.field = f32[3,32,16,128]{3,2,1,0:T(8,128)S(1)} custom-call(f32[3,34,24,128]{3,2,1,0:T(8,128)S(1)} %get-tuple-element.43.two, f32[3,16,16,128]{3,2,1,0:T(8,128)S(1)} %get-tuple-element.44.rim), custom_call_target="tpu_custom_call" | custom-call | flops 1000000 | bytes 4000000 | tf_op jit(solution)/shard_map/pallas_call | solution.py:827
  64.2 9.7 %all-to-all-done.1 = f32[16,64,128]{2,1,0:T(8,128)S(1)} async-done(((f32[16,64,128]{2,1,0:T(8,128)}), f32[16,64,128]{2,1,0:T(8,128)S(1)}, u32[]{:S(2)}, u32[]{:S(2)}) %all-to-all-start.1) | async-done | bytes 524320 | tf_op jit(solution)/shard_map/all_to_all | solution.py:838
  73.9 4.0 %shard_map.36 = f32[3,32,16,128]{3,2,1,0:T(8,128)} custom-call(f32[1024,128]{1,0:T(8,128)S(1)} %bitcast.2, f32[3,32,16,128]{3,2,1,0:T(8,128)S(1)} %shard_map.35.field, f32[3,16,8,128]{3,2,1,0:T(8,128)S(1)} %get-tuple-element.45.e_one, f32[3,8,8,128]{3,2,1,0:T(8,128)S(1)} %get-tuple-element.46.e_two), custom_call_target="tpu_custom_call" | custom-call | flops 1000000 | bytes 4000000 | tf_op jit(solution)/shard_map/pallas_call | solution.py:839
Async XLA Ops:
  1.3 7.8 %collective-permute-start = (f32[12,32,128]{2,1,0:T(8,128)S(1)}, f32[12,32,128]{2,1,0:T(8,128)S(1)}, u32[]{:S(2)}, u32[]{:S(2)}) collective-permute-start(f32[12,32,128]{2,1,0:T(8,128)S(1)} %get-tuple-element.30), channel_id=1, source_target_pairs={{0,16},{16,0},{32,48},{48,32},{64,80},{80,64},{96,112},{112,96},{1... | collective-permute-start | bytes 589832 | tf_op jit(solution)/shard_map/ppermute | solution.py:796
  3.4 5.7 %collective-permute-start.1 = (f32[12,32,128]{2,1,0:T(8,128)S(1)}, f32[12,32,128]{2,1,0:T(8,128)S(1)}, u32[]{:S(2)}, u32[]{:S(2)}) collective-permute-start(f32[12,32,128]{2,1,0:T(8,128)S(1)} %get-tuple-element.31), channel_id=1, source_target_pairs={{16,32},{32,16},{48,64},{64,48},{80,96},{96,80},{112,128},{128,112... | collective-permute-start | bytes 589832 | tf_op jit(solution)/shard_map/ppermute | solution.py:797
  9.6 9.8 %collective-permute-start.2 = (f32[4,4,24,128]{3,2,1,0:T(8,128)S(1)}, f32[4,4,24,128]{3,2,1,0:T(8,128)S(1)}, u32[]{:S(2)}, u32[]{:S(2)}) collective-permute-start(f32[4,4,24,128]{3,2,1,0:T(8,128)S(1)} %get-tuple-element.38), channel_id=1, source_target_pairs={{0,1},{1,0},{2,3},{3,2},{4,5},{5,4},{6,7},{7,6},{8,9},{9,8},{10,11... | collective-permute-start | bytes 589832 | tf_op jit(solution)/shard_map/ppermute | solution.py:808
  10.9 8.5 %collective-permute-start.3 = (f32[4,4,24,128]{3,2,1,0:T(8,128)S(1)}, f32[4,4,24,128]{3,2,1,0:T(8,128)S(1)}, u32[]{:S(2)}, u32[]{:S(2)}) collective-permute-start(f32[4,4,24,128]{3,2,1,0:T(8,128)S(1)} %get-tuple-element.39), channel_id=1, source_target_pairs={{1,2},{2,1},{3,4},{4,3},{5,6},{6,5},{7,8},{8,7},{9,10},{10,9},{11,... | collective-permute-start | bytes 589832 | tf_op jit(solution)/shard_map/ppermute | solution.py:807
  23.0 6.7 %collective-permute-start.5 = (f32[4,2,5,8,128]{4,3,2,1,0:T(8,128)S(1)}, f32[4,2,5,8,128]{4,3,2,1,0:T(8,128)S(1)}, u32[]{:S(2)}, u32[]{:S(2)}) collective-permute-start(f32[4,2,5,8,128]{4,3,2,1,0:T(8,128)S(1)} %get-tuple-element.41), channel_id=1, source_target_pairs={{16,32},{32,16},{48,64},{64,48},{80,96},{96,80},{112,128},{128,112... | collective-permute-start | bytes 491528 | tf_op jit(solution)/shard_map/ppermute | solution.py:826
  23.7 8.7 %collective-permute-start.4 = (f32[4,2,5,8,128]{4,3,2,1,0:T(8,128)S(1)}, f32[4,2,5,8,128]{4,3,2,1,0:T(8,128)S(1)}, u32[]{:S(2)}, u32[]{:S(2)}) collective-permute-start(f32[4,2,5,8,128]{4,3,2,1,0:T(8,128)S(1)} %get-tuple-element.41), channel_id=1, source_target_pairs={{0,16},{16,0},{32,48},{48,32},{64,80},{80,64},{96,112},{112,96},{1... | collective-permute-start | bytes 491528 | tf_op jit(solution)/shard_map/ppermute | solution.py:825
  54.0 20.0 %all-to-all-start.1 = ((f32[16,64,128]{2,1,0:T(8,128)}), f32[16,64,128]{2,1,0:T(8,128)S(1)}, u32[]{:S(2)}, u32[]{:S(2)}) async-start(f32[16,64,128]{2,1,0:T(8,128)} %shard_map.34), calls=%async_computation.1 | async-start | bytes 1048576 | tf_op jit(solution)/shard_map/all_to_all | solution.py:838

commit v3 on v2

--- a/solution.py
+++ b/solution.py
@@ -7,7 +7,7 @@
 
 
 F32 = jnp.float32
-NX, NY = 16, 16
+NX, NY, CHIPS = 16, 16, 128
 BETWEEN = 2.0 * 0.1 / 1.1
 ANY = pl.BlockSpec(memory_space=pltpu.HBM)
 
@@ -413,21 +413,35 @@
                 packed[ch, group, tile] = tiles[tile]
 
 
-def patch_kernel(two, rim, field):
+def base_kernel(two, rim, e_one, e_two, base, wide, spread):
+    copy = jnp.where(iota((128, 128), 0) == iota((128, 128), 1) // 2, 1.0, 0.0)
+    value = dot(e_two[...].reshape(192, 128), copy)
+    for block in range(24):
+        rows = value[8 * block : 8 * block + 4, :]
+        wide[pl.ds(8 * block, 4, stride=2), :] = rows
+        wide[pl.ds(8 * block + 1, 4, stride=2), :] = rows
+    value = e_one[...].reshape(24, 2, 8, 128) + wide[...].reshape(24, 1, 8, 128)
+    value = dot(value.reshape(384, 128), copy)
+    flat = spread.reshape(768, 128)
+    for block in range(48):
+        rows = value[8 * block : 8 * block + 8, :]
+        flat[pl.ds(16 * block, 8, stride=2), :] = rows
+        flat[pl.ds(16 * block + 1, 8, stride=2), :] = rows
     lane = iota((16, 128), 1)
 
-    def plane(z):
-        for f in range(3):
-            value = rim[f, z]
-            for half in range(2):
-                base = 64 * half
-                low = roll(value, -57 - base)
-                high = roll(value, 121 - base)
-                at = z + 16 * half
-                own = jnp.concatenate([two[f, at + 1, 16:24, :], two[f, at + 1, 0:8, :]], axis=0)
-                field[f, at] = jnp.where(lane < 3, low, jnp.where(lane >= 125, high, own))
-
-    loop(16, plane, 2)
+    def pair(k):
+        for f in range(3):
+            for z in (2 * k, 2 * k + 1):
+                value = rim[f, z]
+                for half in range(2):
+                    low = roll(value, -57 - 64 * half)
+                    high = roll(value, 121 - 64 * half)
+                    at = z + 16 * half
+                    own = jnp.concatenate([two[f, at + 1, 16:24, :], two[f, at + 1, 0:8, :]], axis=0)
+                    own = jnp.where(lane < 3, low, jnp.where(lane >= 125, high, own))
+                    base[f, at] = own + spread[f, k + 8 * half]
+
+    loop(8, pair, 1)
 
 
 def resist(share):
@@ -599,39 +613,45 @@
         ],
         axis=0,
     )
-    for copy in range(NY):
+    for copy in range(CHIPS):
         sent[copy] = result
 
 
-def turn_kernel(column, sent):
+def swap_blocks(x):
     sub, group = iota((8, 128), 0), iota((8, 128), 1) // 16
-    tiles = [column[8 * j : 8 * j + 8, :] for j in range(8)]
-    moved = [[roll(tile, 16 * d) for d in range(8)] for tile in tiles]
-    for q in range(8):
-        halves = []
-        for half in range(2):
-            value = jnp.zeros((8, 128), F32)
-            for j in range(4):
-                for odd in range(2):
-                    to = 2 * j + odd
-                    mask = (sub // 4 == odd) & (group == to)
-                    value = jnp.where(mask, moved[4 * half + j][(to - q) % 8], value)
-            halves.append(value + roll(value, 4, 0))
-        tile = jnp.where(sub < 4, halves[0], halves[1])
-        for copy in range(NX):
-            sent[copy, 8 * q : 8 * q + 8, :] = tile
+    for bit in (4, 2, 1):
+        up = roll(roll(x, -bit, 0), 16 * bit)
+        down = up if bit == 4 else roll(roll(x, bit, 0), -16 * bit)
+        sub_set, group_set = (sub & bit) != 0, (group & bit) != 0
+        x = jnp.where(sub_set == group_set, x, jnp.where(sub_set, down, up))
+    return x
 
 
 def top_kernel(
-    gathered, field, e_one, e_two, out,
-    first, second, four, weights, diags, lefts, wide, final, sems,
+    mine, other, base, out,
+    natural, first, second, four, weights, diags, lefts, final, sems,
 ):
     gx, gy = lax.axis_index("gx"), lax.axis_index("gy")
+    first_core = lax.rem(gy, 2) == 0
     lane, sub = iota((16, 128), 1), iota((16, 128), 0)
     cells = [(z, x, half) for z in range(4) for x in range(2) for half in range(2)]
 
+    def lay(g):
+        for ch in range(4):
+            rows = pl.ds(32 * g + ch, 8, stride=4)
+            pair = mine[rows, :], other[rows, :]
+            natural[ch, 0, pl.ds(pl.multiple_of(8 * g, 8), 8), :] = swap_blocks(
+                jnp.where(first_core, pair[0], pair[1])
+            )
+            natural[ch, 1, pl.ds(pl.multiple_of(8 * g, 8), 8), :] = swap_blocks(
+                jnp.where(first_core, pair[1], pair[0])
+            )
+
+    loop(16, lay, 4)
+    flat = natural.reshape(1024, 128)
+
     def plane(ch, z, x, half):
-        return gathered[pl.ds(((z * 2 + x) * 2 + half) * 4 + ch, 16, stride=64), :]
+        return flat[pl.ds((ch * 2 + half) * 128 + z * 2 + x, 16, stride=8), :]
 
     def neighbours(at, z, x, half, outside):
         own, other = at(z, x, half), at(z, 1 - x, half)
@@ -639,10 +659,8 @@
         shifted = roll(other, 1 if x == 0 else -1, 0)
         low, high = (shifted, other) if x == 0 else (other, shifted)
         left, right = roll(own, 1), roll(own, -1)
-        if half == 0:
-            right = jnp.where(lane == 127, roll(beside, -1), right)
-        else:
-            left = jnp.where(lane == 0, roll(beside, 1), left)
+        left = jnp.where(lane % 16 == 0, roll(beside, 1 if half == 0 else -15), left)
+        right = jnp.where(lane % 16 == 15, roll(beside, 15 if half == 0 else -1), right)
         down = at(z - 1, x, half) if z > 0 else outside
         up = at(z + 1, x, half) if z < 3 else outside
         return own, [low, high, left, right, down, up]
@@ -701,7 +719,9 @@
             for ch in range(4):
                 lefts[ch, z4, :, 128 * half : 128 * half + 128] = sums[ch]
 
-    pool = jnp.where(iota((256, 128), 0) // 2 == iota((256, 128), 1), 0.125, 0.0)
+    source = iota((256, 128), 0)
+    column = ((source % 128) // 16) * 16 + (source // 128) * 8 + (source % 16) // 2
+    pool = jnp.where(column == iota((256, 128), 1), 0.125, 0.0)
     level = dot(lefts[...].reshape(128, 256), pool)
 
     def coarsest(ch, z):
@@ -742,41 +762,20 @@
     three = dot(turn(rows, -8 * gy), copy)
     flat = second.reshape(768, 128)
     halves = [flat[pl.ds(gx + 384 * half, 24, stride=16), :] for half in range(2)]
-    three = three + turn(jnp.where(gy < 8, halves[0], halves[1]), -16 * lax.rem(gy, 8))
-
+    three = three + turn(jnp.where(first_core, halves[0], halves[1]), -16 * lax.div(gy, 2))
+
+    copy = jnp.where(iota((128, 128), 0) == iota((128, 128), 1) // 8, 1.0, 0.0)
     three = dot(three, copy)
-    low = iota((8, 128), 0) < 2
-    tiles = []
+    copies = []
     for f in range(3):
         for z in range(4):
-            at = f * 8 + z * 2
-            tile = jnp.where(
-                low,
-                jnp.broadcast_to(three[at : at + 1], (8, 128)),
-                jnp.broadcast_to(three[at + 1 : at + 2], (8, 128)),
-            )
-            tiles += [e_two[f, 2 * z] + tile, e_two[f, 2 * z + 1] + tile]
-
-    two = dot(jnp.concatenate(tiles, axis=0), copy)
-    for block in range(24):
-        value = two[8 * block : 8 * block + 4, :]
-        wide[pl.ds(8 * block, 4, stride=2), :] = value
-        wide[pl.ds(8 * block + 1, 4, stride=2), :] = value
-    one = e_one[...].reshape(24, 2, 8, 128) + wide[...].reshape(24, 1, 8, 128)
-
-    one = dot(one.reshape(384, 128), copy)
-    flat_in = field.reshape(3 * 32 * 16, 128)
-    flat_out = final.reshape(3 * 32 * 16, 128)
-    copies = []
-    for f in range(3):
-        for block in range(16 * f, 16 * f + 16):
-            value = one[8 * block : 8 * block + 8, :]
-            for k in range(2):
-                for half in range(2):
-                    at = pl.ds(32 * block + 16 * k + half, 8, stride=2)
-                    flat_out[at, :] = flat_in[at, :] + value
-            if block % 8 == 7:
-                part = (f, pl.ds(2 * (block % 16) - 14, 16))
+            for x in range(2):
+                at = f * 8 + z * 2 + x
+                value = jnp.broadcast_to(three[at : at + 1], (8, 128))
+                for k in range(8 * z, 8 * z + 8):
+                    final[f, k, 8 * x : 8 * x + 8, :] = base[f, k, 8 * x : 8 * x + 8, :] + value
+            if z % 2 == 1:
+                part = (f, pl.ds(8 * z - 8, 16))
                 copy = pltpu.make_async_copy(final.at[part], out.at[part], sems.at[len(copies)])
                 copy.start()
                 copies.append(copy)
@@ -824,25 +823,27 @@
     )(edges, edges_rim, part, from_near, from_far)
     from_near = lax.ppermute(packed, "gx", swap_near)
     from_far = lax.ppermute(packed, "gx", swap_far)
-    (field,) = call(patch_kernel, [(3, 32, 16, 128)], [])(two, rim)
     sent, e_one, e_two = call(
         middle_kernel,
-        [(NY, 4, 128), (3, 16, 8, 128), (3, 8, 8, 128)],
+        [(CHIPS, 4, 128), (3, 16, 8, 128), (3, 8, 8, 128)],
         [(16, 24, 128), (18, 32, 128), (3, 16, 32, 128), (3, 18, 32, 128), (3, 18, 32, 128)]
         + [(6, 16, 32, 128), (16, 32, 128), (4, 8, 24, 128), (768, 128)]
         + [(10, 24, 128), (3, 10, 24, 128), (3, 10, 24, 128), (3, 8, 8, 128), (8, 8, 128)]
         + [(6, 8, 16, 128), (8, 16, 128)],
     )(coarse, from_near, from_far)
-    column = lax.all_to_all(sent, "gy", split_axis=0, concat_axis=0, tiled=True).reshape(64, 128)
-    (copies,) = call(turn_kernel, [(NX, 64, 128)], [])(column)
-    gathered = lax.all_to_all(copies, "gx", split_axis=0, concat_axis=0, tiled=True).reshape(1024, 128)
+    groups = [[i for i in range(NX * NY) if i % 2 == core] for core in range(2)]
+    mine = lax.all_to_all(
+        sent, ("gx", "gy"), split_axis=0, concat_axis=0, axis_index_groups=groups, tiled=True
+    )
+    (base,) = call(base_kernel, [(3, 32, 16, 128)], [(192, 128), (3, 16, 16, 128)])(two, rim, e_one, e_two)
+    other = lax.ppermute(mine, "gy", swap_near)
     (out,) = call(
         top_kernel,
         [(3, 32, 16, 128)],
-        [(3, 16, 16, 128), (2, 3, 8, 16, 128), (6, 16, 128), (6, 16, 16, 128), (16, 16, 128)]
-        + [(4, 2, 16, 256), (192, 128), (3, 32, 16, 128), pltpu.SemaphoreType.DMA((6,))],
+        [(4, 2, 128, 128), (3, 16, 16, 128), (2, 3, 8, 16, 128), (6, 16, 128), (6, 16, 16, 128)]
+        + [(16, 16, 128), (4, 2, 16, 256), (3, 32, 16, 128), pltpu.SemaphoreType.DMA((6,))],
         out_specs=[ANY],
-    )(gathered, field, e_one, e_two)
+    )(mine.reshape(512, 128), other.reshape(512, 128), base)
     return out
 
 

time: 78.3 us -> 76.5 us (0.977)
  blocking collectives: 17.2 us -> 31.3 us
  waiting for transfers between devices: 12.5 us -> 2.72 us
  starting transfers between devices: 23.2 us -> 16.9 us
    all_to_all x1, blocking collectives: 17.2 us -> 31.3 us  [local(): lax.all_to_all(sent, ('gx', 'gy'), split_axis=0, concat_axis=0, axis_inde...]
    all_to_all x1 -> x0, waiting for transfers between devices: 9.74 us -> none  [local(): lax.all_to_all(copies, 'gx', split_axis=0, concat_axis=0, tiled=True)]
    all_to_all x1 -> x0, starting transfers between devices: 9.27 us -> none  [local(): lax.all_to_all(copies, 'gx', split_axis=0, concat_axis=0, tiled=True)]
    ppermute x0 -> x1, starting transfers between devices: none -> 2.95 us  [local(): other = lax.ppermute(mine, 'gy', swap_near)]
    pallas_call x4 -> x3, Pallas kernels: 9.32 us -> 9.63 us  [the longest x1 4.6 us: local(): call(top_kernel, [(3, 32, 16, 128)], [(4, 2, 128, 128), (3, 16, 16, 128),...]
  transfers between devices with their start and end apart: 7 -> 7, of which waited for: 2 -> 1; matrix products, arithmetic and copies ran while one was open for 0% -> 0% of each run, Pallas kernels for 14% -> 16%
where the time goes in v3:
time: 76.5 us; the launch traced here: 76.3 us
  blocking collectives  31.3 us (41%)
  Pallas kernels  25.2 us (33%)
  starting transfers between devices  16.9 us (22%)
  waiting for transfers between devices  2.72 us (4%)
    all_to_all x1, blocking collectives, local(): lax.all_to_all(sent, ('gx', 'gy'), split_axis=0, concat_axis=0, axis_inde...  31.3 us
    ppermute x1, starting transfers between devices, local(): from_near = lax.ppermute(packed, 'gx', swap_near)  6 us
    pallas_call x1, Pallas kernels, local(): call(rows_edge_kernel, [(3, 34, 24, 128), (4, 16, 8, 128), (4, 16, 8, 128...  5.27 us
    pallas_call x1, Pallas kernels, local(): call(own_kernel, [(3, 34, 32, 128)] * 2 + [(4, 16, 16, 128)] + [(4, 4, 16...  4.99 us
    pallas_call x1, Pallas kernels, local(): call(top_kernel, [(3, 32, 16, 128)], [(4, 2, 128, 128), (3, 16, 16, 128),...  4.6 us
    pallas_call x1, Pallas kernels, local(): call(rim_kernel, [(3, 16, 16, 128), (4, 16, 8, 128), (4, 2, 5, 8, 128)],...  3.63 us
    pallas_call x1, Pallas kernels, local(): call(middle_kernel, [(CHIPS, 4, 128), (3, 16, 8, 128), (3, 8, 8, 128)], [...  3.43 us
    ppermute x1, starting transfers between devices, local(): from_far = lax.ppermute(to_far, 'gy', swap_far)  3.17 us
  transfers between devices with their start and end apart: 7, of which 1 were waited for; matrix products, arithmetic and copies ran while one was open for 0% of the time, Pallas kernels for 16%

profile of v3, /device:TPU:1, one launch (start us, length us, event | category | flops | bytes accessed | tf_op | source)
XLA Modules:
  0.0 76.3 jit_solution(15630725397081352097)
XLA Ops:
  0.0 1.3 %shard_map.28 = (f32[12,32,128]{2,1,0:T(8,128)S(1)}, f32[12,32,128]{2,1,0:T(8,128)S(1)}, f32[4,32,16,128]{3,2,1,0:T(8,128)S(1)}) custom-call(f32[3,32,16,128]{3,2,1,0:T(8,128)} %guess.1, s32[32,16,128]{2,1,0:T(8,128)} %labels.1), custom_call_target="tpu_custom_call" | custom-call | flops 1000000 | bytes 4000000 | tf_op jit(solution)/shard_map/pallas_call | solution.py:789
  1.3 2.1 %collective-permute-start = (f32[12,32,128]{2,1,0:T(8,128)S(1)}, f32[12,32,128]{2,1,0:T(8,128)S(1)}, u32[]{:S(2)}, u32[]{:S(2)}) collective-permute-start(f32[12,32,128]{2,1,0:T(8,128)S(1)} %get-tuple-element.30), channel_id=1, source_target_pairs={{0,16},{16,0},{32,48},{48,32},{64,80},{80,64},{96,112},{112,96},{1... | collective-permute-start | bytes 589832 | tf_op jit(solution)/shard_map/ppermute | solution.py:795
  3.4 0.7 collective-permute-start.1
  4.1 5.0 %shard_map.29 = (f32[3,34,32,128]{3,2,1,0:T(8,128)S(1)}, f32[3,34,32,128]{3,2,1,0:T(8,128)S(1)}, f32[4,16,16,128]{3,2,1,0:T(8,128)S(1)}, f32[4,4,16,128]{3,2,1,0...) custom-call(f32[4,32,16,128]{3,2,1,0:T(8,128)S(1)} %get-tuple-element.26.own), custom_call_target="tpu_custom_call" | custom-call | flops 20000000 | bytes 4000000 | tf_op jit(solution)/shard_map/pallas_call | solution.py:797
  9.1 0.0 collective-permute-done.x_near
  9.1 0.0 collective-permute-done.1.x_far
  9.1 0.5 shard_map.30
  9.6 1.3 %collective-permute-start.2 = (f32[4,4,24,128]{3,2,1,0:T(8,128)S(1)}, f32[4,4,24,128]{3,2,1,0:T(8,128)S(1)}, u32[]{:S(2)}, u32[]{:S(2)}) collective-permute-start(f32[4,4,24,128]{3,2,1,0:T(8,128)S(1)} %get-tuple-element.38), channel_id=1, source_target_pairs={{0,1},{1,0},{2,3},{3,2},{4,5},{5,4},{6,7},{7,6},{8,9},{9,8},{10,11... | collective-permute-start | bytes 589832 | tf_op jit(solution)/shard_map/ppermute | solution.py:807
  10.9 3.2 %collective-permute-start.3 = (f32[4,4,24,128]{3,2,1,0:T(8,128)S(1)}, f32[4,4,24,128]{3,2,1,0:T(8,128)S(1)}, u32[]{:S(2)}, u32[]{:S(2)}) collective-permute-start(f32[4,4,24,128]{3,2,1,0:T(8,128)S(1)} %get-tuple-element.39), channel_id=1, source_target_pairs={{1,2},{2,1},{3,4},{4,3},{5,6},{6,5},{7,8},{8,7},{9,10},{10,9},{11,... | collective-permute-start | bytes 589832 | tf_op jit(solution)/shard_map/ppermute | solution.py:806
  14.1 5.3 %shard_map.31 = (f32[3,34,24,128]{3,2,1,0:T(8,128)S(1)}, f32[4,16,8,128]{3,2,1,0:T(8,128)S(1)}, f32[4,16,8,128]{3,2,1,0:T(8,128)S(1)}) custom-call(f32[4,32,16,128]{3,2,1,0:T(8,128)S(1)} %get-tuple-element.26.own, f32[4,32,8,128]{3,2,1,0:T(8,128)S(1)} %get-tuple-element.32.rim, f32[3,34,32,128]{3,2,1,0:T(8,128)S(1)} %get-tuple-element.33.own_one, ...), custom_call_target="tpu_custom_call" | custom-call | flops 10000000 | bytes 4000000 | tf_op jit(solution)/shard_map/pallas_call | solution.py:808
  19.3 0.0 collective-permute-done.2.near
  19.4 0.0 collective-permute-done.3.far
  19.4 3.6 %shard_map.32 = (f32[3,16,16,128]{3,2,1,0:T(8,128)S(1)}, f32[4,16,8,128]{3,2,1,0:T(8,128)S(1)}, f32[4,2,5,8,128]{4,3,2,1,0:T(8,128)S(1)}) custom-call(f32[4,16,16,128]{3,2,1,0:T(8,128)S(1)} %get-tuple-element.27.edges, f32[4,16,8,128]{3,2,1,0:T(8,128)S(1)} %get-tuple-element.36.edges_rim, f32[4,16,8,128]{3,2,1,0:T(8,128)S(1)} %get-tuple-element.37.owned, ...), custom_call_target="tpu_custom_call" | custom-call | flops 10000000 | bytes 4000000 | tf_op jit(solution)/shard_map/pallas_call | solution.py:815
  23.0 0.7 collective-permute-start.5
  23.7 6.0 %collective-permute-start.4 = (f32[4,2,5,8,128]{4,3,2,1,0:T(8,128)S(1)}, f32[4,2,5,8,128]{4,3,2,1,0:T(8,128)S(1)}, u32[]{:S(2)}, u32[]{:S(2)}) collective-permute-start(f32[4,2,5,8,128]{4,3,2,1,0:T(8,128)S(1)} %get-tuple-element.41), channel_id=1, source_target_pairs={{0,16},{16,0},{32,48},{48,32},{64,80},{80,64},{96,112},{112,96},{1... | collective-permute-start | bytes 491528 | tf_op jit(solution)/shard_map/ppermute | solution.py:824
  29.7 0.0 collective-permute-done.5.far
  29.7 2.7 %collective-permute-done.4.near = f32[4,2,5,8,128]{4,3,2,1,0:T(8,128)S(1)} collective-permute-done((f32[4,2,5,8,128]{4,3,2,1,0:T(8,128)S(1)}, f32[4,2,5,8,128]{4,3,2,1,0:T(8,128)S(1)}, u32[]{:S(2)}, u32[]{:S(2)}) %collective-permute-start.4) | collective-permute-done | bytes 163872 | tf_op jit(solution)/shard_map/ppermute | solution.py:824
  32.4 3.4 %shard_map.33 = (f32[128,4,128]{2,1,0:T(4,128)S(1)}, f32[3,16,8,128]{3,2,1,0:T(8,128)S(1)}, f32[3,8,8,128]{3,2,1,0:T(8,128)S(1)}) custom-call(f32[4,16,8,128]{3,2,1,0:T(8,128)S(1)} %get-tuple-element.40.mine, f32[4,2,5,8,128]{4,3,2,1,0:T(8,128)S(1)} %collective-permute-done.4.near, f32[4,2,5,8,128]{4,3,2,1,0:T(8,128)S(1)} %collective-permute-done.5.far), custom_call_target="tpu_custom_call" | custom-call | flops 1000000 | bytes 4000000 | tf_op jit(solution)/shard_map/pallas_call | solution.py:826
  35.8 31.3 %all_to_all.5 = f32[128,4,128]{2,1,0:T(4,128)S(1)} all-to-all(f32[128,4,128]{2,1,0:T(4,128)S(1)} %get-tuple-element.42), channel_id=1, replica_groups={{0,2,4,6,8,10,12,14,16,18,20,22,24,26,28,30,32,34,36,38,40,42,44,46,48,..., dimensions={0} | all-to-all | bytes 524288 | tf_op jit(solution)/shard_map/all_to_all | solution.py:835
  67.1 3.0 %collective-permute-start.6 = (f32[128,4,128]{2,1,0:T(4,128)S(1)}, f32[128,4,128]{2,1,0:T(4,128)S(1)}, u32[]{:S(2)}, u32[]{:S(2)}) collective-permute-start(f32[128,4,128]{2,1,0:T(4,128)S(1)} %all_to_all.5), channel_id=1, source_target_pairs={{0,1},{1,0},{2,3},{3,2},{4,5},{5,4},{6,7},{7,6},{8,9},{9,8},{10,11... | collective-permute-start | bytes 786440 | tf_op jit(solution)/shard_map/ppermute | solution.py:839
  70.0 1.6 %shard_map.34.base = f32[3,32,16,128]{3,2,1,0:T(8,128)S(1)} custom-call(f32[3,34,24,128]{3,2,1,0:T(8,128)S(1)} %get-tuple-element.43.two, f32[3,16,16,128]{3,2,1,0:T(8,128)S(1)} %get-tuple-element.44.rim, f32[3,16,8,128]{3,2,1,0:T(8,128)S(1)} %get-tuple-element.45.e_one, f32[3,8,8,128]{3,2,1,0:T(8,128)S(1)} %get-tuple-element.46.e_two), custom_call_target="tpu_custom_call" | custom-call | flops 1000000 | bytes 4000000 | tf_op jit(solution)/shard_map/pallas_call | solution.py:838
  71.7 0.0 collective-permute-done.6
  71.7 4.6 %shard_map.35 = f32[3,32,16,128]{3,2,1,0:T(8,128)} custom-call(f32[512,128]{1,0:T(8,128)S(1)} %bitcast.2, f32[512,128]{1,0:T(8,128)S(1)} %bitcast.3, f32[3,32,16,128]{3,2,1,0:T(8,128)S(1)} %shard_map.34.base), custom_call_target="tpu_custom_call" | custom-call | flops 1000000 | bytes 4000000 | tf_op jit(solution)/shard_map/pallas_call | solution.py:840
Async XLA Ops:
  1.3 7.8 %collective-permute-start = (f32[12,32,128]{2,1,0:T(8,128)S(1)}, f32[12,32,128]{2,1,0:T(8,128)S(1)}, u32[]{:S(2)}, u32[]{:S(2)}) collective-permute-start(f32[12,32,128]{2,1,0:T(8,128)S(1)} %get-tuple-element.30), channel_id=1, source_target_pairs={{0,16},{16,0},{32,48},{48,32},{64,80},{80,64},{96,112},{112,96},{1... | collective-permute-start | bytes 589832 | tf_op jit(solution)/shard_map/ppermute | solution.py:795
  3.4 5.7 %collective-permute-start.1 = (f32[12,32,128]{2,1,0:T(8,128)S(1)}, f32[12,32,128]{2,1,0:T(8,128)S(1)}, u32[]{:S(2)}, u32[]{:S(2)}) collective-permute-start(f32[12,32,128]{2,1,0:T(8,128)S(1)} %get-tuple-element.31), channel_id=1, source_target_pairs={{16,32},{32,16},{48,64},{64,48},{80,96},{96,80},{112,128},{128,112... | collective-permute-start | bytes 589832 | tf_op jit(solution)/shard_map/ppermute | solution.py:796
  9.6 9.8 %collective-permute-start.2 = (f32[4,4,24,128]{3,2,1,0:T(8,128)S(1)}, f32[4,4,24,128]{3,2,1,0:T(8,128)S(1)}, u32[]{:S(2)}, u32[]{:S(2)}) collective-permute-start(f32[4,4,24,128]{3,2,1,0:T(8,128)S(1)} %get-tuple-element.38), channel_id=1, source_target_pairs={{0,1},{1,0},{2,3},{3,2},{4,5},{5,4},{6,7},{7,6},{8,9},{9,8},{10,11... | collective-permute-start | bytes 589832 | tf_op jit(solution)/shard_map/ppermute | solution.py:807
  10.9 8.5 %collective-permute-start.3 = (f32[4,4,24,128]{3,2,1,0:T(8,128)S(1)}, f32[4,4,24,128]{3,2,1,0:T(8,128)S(1)}, u32[]{:S(2)}, u32[]{:S(2)}) collective-permute-start(f32[4,4,24,128]{3,2,1,0:T(8,128)S(1)} %get-tuple-element.39), channel_id=1, source_target_pairs={{1,2},{2,1},{3,4},{4,3},{5,6},{6,5},{7,8},{8,7},{9,10},{10,9},{11,... | collective-permute-start | bytes 589832 | tf_op jit(solution)/shard_map/ppermute | solution.py:806
  23.0 6.7 %collective-permute-start.5 = (f32[4,2,5,8,128]{4,3,2,1,0:T(8,128)S(1)}, f32[4,2,5,8,128]{4,3,2,1,0:T(8,128)S(1)}, u32[]{:S(2)}, u32[]{:S(2)}) collective-permute-start(f32[4,2,5,8,128]{4,3,2,1,0:T(8,128)S(1)} %get-tuple-element.41), channel_id=1, source_target_pairs={{16,32},{32,16},{48,64},{64,48},{80,96},{96,80},{112,128},{128,112... | collective-permute-start | bytes 491528 | tf_op jit(solution)/shard_map/ppermute | solution.py:825
  23.7 8.7 %collective-permute-start.4 = (f32[4,2,5,8,128]{4,3,2,1,0:T(8,128)S(1)}, f32[4,2,5,8,128]{4,3,2,1,0:T(8,128)S(1)}, u32[]{:S(2)}, u32[]{:S(2)}) collective-permute-start(f32[4,2,5,8,128]{4,3,2,1,0:T(8,128)S(1)} %get-tuple-element.41), channel_id=1, source_target_pairs={{0,16},{16,0},{32,48},{48,32},{64,80},{80,64},{96,112},{112,96},{1... | collective-permute-start | bytes 491528 | tf_op jit(solution)/shard_map/ppermute | solution.py:824
  67.1 4.6 %collective-permute-start.6 = (f32[128,4,128]{2,1,0:T(4,128)S(1)}, f32[128,4,128]{2,1,0:T(4,128)S(1)}, u32[]{:S(2)}, u32[]{:S(2)}) collective-permute-start(f32[128,4,128]{2,1,0:T(4,128)S(1)} %all_to_all.5), channel_id=1, source_target_pairs={{0,1},{1,0},{2,3},{3,2},{4,5},{5,4},{6,7},{7,6},{8,9},{9,8},{10,11... | collective-permute-start | bytes 786440 | tf_op jit(solution)/shard_map/ppermute | solution.py:839

commit v4 on v3

--- a/solution.py
+++ b/solution.py
@@ -135,6 +135,24 @@
     )
 
 
+def block_of(ref, lead, z, planes, first, count):
+    rows = pl.ds(first, count)
+    own = [ref[(*lead, z + k, rows, slice(None))] for k in range(-1, planes + 1)]
+    result = []
+    for k in range(planes):
+        value = own[k + 1]
+        six = (
+            ref[(*lead, z + k, pl.ds(first - 1, count), slice(None))],
+            ref[(*lead, z + k, pl.ds(first + 1, count), slice(None))],
+            roll(value, 1),
+            roll(value, -1),
+            own[k],
+            own[k + 2],
+        )
+        result.append((value, six))
+    return result
+
+
 def face(total):
     return jnp.where(total < 0.5, 1.0, jnp.where(total < 1.5, BETWEEN, 0.1))
 
@@ -157,47 +175,50 @@
 def fine_sweeps(planes, windows, start, share, one, two, weights, diags, halves, omega, wrap, keep):
     first, count = windows[0]
 
-    def first_sweep(z):
-        own, six = six_of(share, (), z + 1, first, count)
-        w, diag = fine_weights(own, six, omega)
-        diags[z, pl.ds(first, count), :] = diag
-        for i in range(6):
-            weights[i, z, pl.ds(first, count), :] = w[i]
-        for f in range(3):
-            own, six = six_of(start, (f,), z + 1, first, count)
-            one[f, z + 1, pl.ds(first, count), :] = fine_sweep(w, f, own, six)
-
-    loop(planes, first_sweep, 4)
+    def first_sweep(step):
+        z = 4 * step
+        w = []
+        for k, (own, six) in enumerate(block_of(share, (), z + 1, 4, first, count)):
+            now, diag = fine_weights(own, six, omega)
+            diags[z + k, pl.ds(first, count), :] = diag
+            for i in range(6):
+                weights[i, z + k, pl.ds(first, count), :] = now[i]
+            w.append(now)
+        for f in range(3):
+            for k, (own, six) in enumerate(block_of(start, (f,), z + 1, 4, first, count)):
+                one[f, z + k + 1, pl.ds(first, count), :] = fine_sweep(w[k], f, own, six)
+
+    loop(planes // 4, first_sweep)
     wrap(one)
     second, count2 = windows[1]
 
-    def second_sweep(z):
-        w = [weights[i, z, pl.ds(second, count2), :] for i in range(6)]
-        for f in range(3):
-            own, six = six_of(one, (f,), z + 1, second, count2)
-            two[f, z + 1, pl.ds(second, count2), :] = fine_sweep(w, f, own, six)
-
-    loop(planes, second_sweep, 4)
+    def second_sweep(step):
+        z = 4 * step
+        w = [[weights[i, z + k, pl.ds(second, count2), :] for i in range(6)] for k in range(4)]
+        for f in range(3):
+            for k, (own, six) in enumerate(block_of(one, (f,), z + 1, 4, second, count2)):
+                two[f, z + k + 1, pl.ds(second, count2), :] = fine_sweep(w[k], f, own, six)
+
+    loop(planes // 4, second_sweep)
     wrap(two)
 
-    def residual(pair):
-        sums = {}
-        for k in range(2):
-            z = 2 * pair + k
-            w = [weights[i, z, 8:24, :] for i in range(6)]
-            diag = diags[z, 8:24, :]
-            for f in range(3):
-                own, six = six_of(two, (f,), z + 1, 8, 16)
+    def residual(step):
+        z = 4 * step
+        w = [[weights[i, z + k, 8:24, :] for i in range(6)] for k in range(4)]
+        diag = [diags[z + k, 8:24, :] for k in range(4)]
+        for f in range(3):
+            values = []
+            for k, (own, six) in enumerate(block_of(two, (f,), z + 1, 4, 8, 16)):
                 if keep is not None:
-                    keep[f, z] = own
-                value = fine_left(w, f, own, six, diag)
-                sums[f] = value if k == 0 else sums[f] + value
-            value = share[z + 1, 8:24, :]
-            sums[3] = value if k == 0 else sums[3] + value
-        for ch, value in sums.items():
-            halves[ch, pair] = value
-
-    loop(planes // 2, residual, 2)
+                    keep[f, z + k] = own
+                values.append(fine_left(w[k], f, own, six, diag[k]))
+            for pair in range(2):
+                halves[f, 2 * step + pair] = values[2 * pair] + values[2 * pair + 1]
+        for pair in range(2):
+            at = z + 2 * pair + 1
+            halves[3, 2 * step + pair] = share[at, 8:24, :] + share[at + 1, 8:24, :]
+
+    loop(planes // 4, residual)
 
 
 def own_kernel(own, one, two, halves, to_right, to_left, edges, held, weights, diags):
@@ -231,7 +252,7 @@
     loop(16, edge, 2)
 
 
-def rows_edge_kernel(own, rim, own_one, own_two, own_halves, two, coarse, edges, start, one, weights, diags, halves, pooled):
+def rows_edge_kernel(own, rim, own_one, own_two, own_halves, two, packed, edges, start, one, weights, diags, halves, pooled):
     gx = lax.axis_index("gx")
     zero = jnp.zeros((24, 128), F32)
     for z in (0, 33):
@@ -259,16 +280,14 @@
         low = ref[(*lead, pl.ds(8 + step + shift, 8), slice(None))]
         return jnp.where(upper, high, low)
 
-    def six_both(ref, f, z, step):
-        value = both(ref, (f, z), step)
-        return value, (
-            both(ref, (f, z), step, -1),
-            both(ref, (f, z), step, 1),
-            roll(value, 1),
-            roll(value, -1),
-            both(ref, (f, z - 1), step),
-            both(ref, (f, z + 1), step),
-        )
+    def block_both(ref, f, z, step):
+        own = [both(ref, (f, z + k), step) for k in range(-1, 5)]
+        result = []
+        for k in range(4):
+            value = own[k + 1]
+            low, high = both(ref, (f, z + k), step, -1), both(ref, (f, z + k), step, 1)
+            result.append((value, (low, high, roll(value, 1), roll(value, -1), own[k], own[k + 2])))
+        return result
 
     def put(ref, f, z, step, value):
         ref[f, z, pl.ds(8 - step, 4), :] = value[0:4]
@@ -279,49 +298,54 @@
     inside = jnp.where((row >= 8) & (row < 12), high, jnp.where((row >= 12) & (row < 16), low, 1))
     omega = 0.8 * inside.astype(F32)
 
-    def weigh_all(z):
-        value, six = six_of(start, (3,), z + 1, 5, 16)
-        w, diag = fine_weights(value, six, omega)
-        diags[z, 5:21, :] = diag
-        for i in range(6):
-            weights[i, z, 5:21, :] = w[i]
-
-    loop(32, weigh_all, 4)
+    def weigh_all(step):
+        z = 4 * step
+        for k, (value, six) in enumerate(block_of(start, (3,), z + 1, 4, 5, 16)):
+            w, diag = fine_weights(value, six, omega)
+            diags[z + k, 5:21, :] = diag
+            for i in range(6):
+                weights[i, z + k, 5:21, :] = w[i]
+
+    loop(8, weigh_all)
 
     for step, source, target in ((1, start, one), (2, one, two)):
 
-        def sweep(z):
-            w = [both(weights, (i, z), step) for i in range(6)]
+        def sweep(block):
+            z = 4 * block
+            w = [[both(weights, (i, z + k), step) for i in range(6)] for k in range(4)]
             for f in range(3):
-                value, six = six_both(source, f, z + 1, step)
-                put(target, f, z + 1, step, fine_sweep(w, f, value, six))
-
-        loop(32, sweep, 4)
+                for k, (value, six) in enumerate(block_both(source, f, z + 1, step)):
+                    put(target, f, z + k + 1, step, fine_sweep(w[k], f, value, six))
+
+        loop(8, sweep)
 
     sub = iota((8, 128), 0)
 
-    def residual(pair):
-        sums = {}
+    def residual(block):
+        z = 4 * block
+        w = [[both(weights, (i, z + k), 3) for i in range(6)] for k in range(4)]
+        diag = [both(diags, (z + k,), 3) for k in range(4)]
+        for f in range(3):
+            values = []
+            for k, (value, six) in enumerate(block_both(two, f, z + 1, 3)):
+                values.append(fine_left(w[k], f, value, six, diag[k]))
+            for k in range(2):
+                pair = 2 * block + k
+                value = values[2 * k] + values[2 * k + 1]
+                halves[f, pair, 0:8, :] = jnp.where(sub < 3, roll(value, 3, 0), own_halves[f, pair, 0:8, :])
+                halves[f, pair, 8:16, :] = jnp.where(sub >= 5, roll(value, 5, 0), own_halves[f, pair, 8:16, :])
         for k in range(2):
-            z = 2 * pair + k
-            w = [both(weights, (i, z), 3) for i in range(6)]
-            diag = both(diags, (z,), 3)
-            for f in range(3):
-                value, six = six_both(two, f, z + 1, 3)
-                value = fine_left(w, f, value, six, diag)
-                sums[f] = value if k == 0 else sums[f] + value
-        for f in range(3):
-            halves[f, pair, 0:8, :] = jnp.where(sub < 3, roll(sums[f], 3, 0), own_halves[f, pair, 0:8, :])
-            halves[f, pair, 8:16, :] = jnp.where(sub >= 5, roll(sums[f], 5, 0), own_halves[f, pair, 8:16, :])
-        halves[3, pair] = own_halves[3, pair]
-
-    loop(16, residual, 2)
-    pool = jnp.where(iota((128, 128), 0) // 2 == iota((128, 128), 1), 0.125, 0.0)
-    pooled[...] = dot(halves[...].reshape(1024, 128), pool)
-    for ch in range(4):
-        even = pooled[pl.ds(256 * ch, 128, stride=2), :]
-        odd = pooled[pl.ds(256 * ch + 1, 128, stride=2), :]
-        coarse[ch] = (even + odd).reshape(16, 8, 128)
+            halves[3, 2 * block + k] = own_halves[3, 2 * block + k]
+
+    loop(8, residual)
+    source, target = iota((128, 128), 0), iota((128, 128), 1)
+    value = None
+    for half in range(2):
+        pool = jnp.where(source // 2 + 64 * half == target, 0.125, 0.0)
+        part = dot(halves[:, 8 * half : 8 * half + 8].reshape(512, 128), pool)
+        value = part if value is None else value + part
+    pooled[...] = value
+    packed[...] = (pooled[pl.ds(0, 256, stride=2), :] + pooled[pl.ds(1, 256, stride=2), :]).reshape(4, 8, 8, 128)
 
     def edge(z):
         for ch in range(4):
@@ -331,7 +355,7 @@
 
 
 def rim_kernel(
-    edges, edges_rim, owned, near, far, field, coarse, packed,
+    edges, edges_rim, near, far, field, packed,
     start, share, one, two, weights, diags, halves, pooled,
 ):
     gx, gy = lax.axis_index("gx"), lax.axis_index("gy")
@@ -385,32 +409,17 @@
 
     source, target = iota((128, 128), 0), iota((128, 128), 1)
     spot = source % 64
-    column = jnp.where(spot < 32, 121 + spot, 128 + spot - 57)
-    to = jnp.where(spot < 32, column // 2, (column // 2 + 64) % 128)
-    from_rim = (iota((64, 128), 1) < 2) | (iota((64, 128), 1) >= 62)
-    mixed = halves[...].reshape(512, 128)
-    for half in range(2):
-        pool = jnp.where((to == target) & (source // 64 == half), 0.125, 0.0)
-        pooled[...] = dot(mixed, pool)
-        for ch in range(4):
-            even = pooled[pl.ds(128 * ch, 64, stride=2), :]
-            odd = pooled[pl.ds(128 * ch + 1, 64, stride=2), :]
-            at = pl.ds(8 * half, 8)
-            rest = owned[ch, at].reshape(64, 128)
-            coarse[ch, at] = jnp.where(from_rim, even + odd, rest).reshape(8, 8, 128)
-
-    lane = iota((8, 128), 1)
-    for ch in range(4):
-        for group in range(2):
-            tiles = [None] * 5
-            for k in range(8):
-                moved = roll(coarse[ch, 8 * group + k], 8 + 80 * k)
-                tile, off = divmod(80 * k, 128)
-                tiles[tile] = moved if off == 0 else jnp.where(lane >= off, moved, tiles[tile])
-                if off + 80 > 128:
-                    tiles[tile + 1] = moved
-            for tile in range(5):
-                packed[ch, group, tile] = tiles[tile]
+    column = jnp.where(spot < 32, 121 + spot, 71 + spot) // 2
+    to = jnp.where(spot < 32, column - 62, column - 48)
+    keep = ((spot < 32) & (to >= 0) & (to < 9)) | ((spot >= 32) & (to >= 9) & (to < 18))
+    mixed = halves[...].reshape(4, 4, 2, 16, 128)
+    value = None
+    for odd in range(2):
+        pool = jnp.where(keep & (to + 64 * odd + 32 * (source // 64) == target), 0.125, 0.0)
+        part = dot(mixed[:, :, odd].reshape(256, 128), pool)
+        value = part if value is None else value + part
+    pooled[...] = value
+    packed[...] = (pooled[pl.ds(0, 128, stride=2), :] + pooled[pl.ds(1, 128, stride=2), :]).reshape(4, 4, 8, 128)
 
 
 def base_kernel(two, rim, e_one, e_two, base, wide, spread):
@@ -456,9 +465,9 @@
 
 
 def middle_kernel(
-    mine, near, far, sent, e_one, e_two,
+    main, main_near, main_far, rim, rim_near, rim_far, sent, e_one, e_two,
     share, rest, rhs, first, second, weights, diags, halves, pooled,
-    rest2, first2, second2, rhs2, share2, weights2, diags2,
+    rest2, first2, second2, rhs2, share2, weights2,
 ):
     gx, gy = lax.axis_index("gx"), lax.axis_index("gy")
     low_x, high_x = jnp.where(gx > 0, 1, 0), jnp.where(gx < NX - 1, 1, 0)
@@ -475,70 +484,71 @@
     near_row, far_row = jnp.where(even, 16, 0), jnp.where(even, 0, 16)
     starts = (pl.multiple_of(near_row, 8), pl.multiple_of(far_row, 8), 8)
 
-    def fill(group):
-        for k in range(8):
-            z = 8 * group + k
-            tile, off = divmod(80 * k, 128)
-            for ch in range(4):
-                parts = []
-                for ref in (near, far):
-                    value = ref[ch, group, tile]
-                    if off + 80 > 128:
-                        value = jnp.where(lane >= off, value, ref[ch, group, tile + 1])
-                    parts.append(roll(value, -8 - 80 * k))
-                parts.append(mine[ch, z])
-                for at, value in zip(starts, parts):
-                    if ch < 3:
-                        rhs[ch, z, pl.ds(at, 8), :] = value
-                    else:
-                        share[z, pl.ds(at, 8), :] = value
-                        rest[z + 1, pl.ds(at, 8), :] = resist(value)
-            rest[z + 1, 24:32, :] = jnp.ones((8, 128), F32)
-
-    loop(2, fill)
+    sources = zip(starts, ((main_near, rim_near), (main_far, rim_far), (main, rim)))
+    sources = list(sources)
+
+    def fill(q):
+        for odd in range(2):
+            for half in range(2):
+                z = 2 * q + odd + 8 * half
+                base = 64 * odd + 32 * half
+                for at, (inner, outer) in sources:
+                    for ch in range(4):
+                        edge = outer[ch, q]
+                        value = jnp.where(lane < 62, roll(inner[ch, 2 * q + odd], 64 * half), roll(edge, 62 - base))
+                        value = jnp.where((lane >= 96) | (lane < 2), roll(edge, 112 - base), value)
+                        if ch < 3:
+                            rhs[ch, z, pl.ds(at, 8), :] = value
+                        else:
+                            share[z, pl.ds(at, 8), :] = value
+                            rest[z + 1, pl.ds(at, 8), :] = resist(value)
+                rest[z + 1, 24:32, :] = jnp.ones((8, 128), F32)
+
+    loop(4, fill)
 
     row, lane = iota((24, 128), 0) + 1, iota((24, 128), 1)
     in_x = jnp.where(row < 8, low_x, jnp.where(row >= 16, high_x, 1))
     in_y = jnp.where(lane < 64, 1, jnp.where(lane < 96, high_y, low_y))
     omega = 0.8 * (in_x * in_y).astype(F32)
 
-    def start(z):
-        own, six = six_of(rest, (), z + 1, 1, 24)
-        gain, w, diag = level_weights(own, six, omega)
-        for i in range(6):
-            weights[i, z, 1:25, :] = w[i]
-        diags[z, 1:25, :] = (1.25 * 0.25) * diag
-        for f in range(3):
-            first[f, z + 1, 1:25, :] = (4.0 * gain) * rhs[f, z, 1:25, :]
-
-    loop(16, start, 2)
-
-    def sweep(z):
-        w = [weights[i, z, 3:27, :] for i in range(6)]
-        for f in range(3):
-            own, six = six_of(first, (f,), z + 1, 3, 24)
-            second[f, z + 1, 3:27, :] = 1.2 * own + weigh(w, six)
-
-    loop(16, sweep, 4)
-
-    def left(pair):
-        sums = {}
+    def start(step):
+        z = 4 * step
+        for k, (own, six) in enumerate(block_of(rest, (), z + 1, 4, 1, 24)):
+            gain, w, diag = level_weights(own, six, omega)
+            for i in range(6):
+                weights[i, z + k, 1:25, :] = w[i]
+            diags[z + k, 1:25, :] = (1.25 * 0.25) * diag
+            for f in range(3):
+                first[f, z + k + 1, 1:25, :] = (4.0 * gain) * rhs[f, z + k, 1:25, :]
+
+    loop(4, start)
+
+    def sweep(step):
+        z = 4 * step
+        w = [[weights[i, z + k, 3:27, :] for i in range(6)] for k in range(4)]
+        for f in range(3):
+            for k, (own, six) in enumerate(block_of(first, (f,), z + 1, 4, 3, 24)):
+                second[f, z + k + 1, 3:27, :] = 1.2 * own + weigh(w[k], six)
+
+    loop(4, sweep)
+
+    def left(step):
+        z = 4 * step
+        w = [[weights[i, z + k, 4:20, :] for i in range(6)] for k in range(4)]
+        diag = [diags[z + k, 4:20, :] for k in range(4)]
+        for f in range(3):
+            values = []
+            for k, (own, six) in enumerate(block_of(second, (f,), z + 1, 4, 4, 16)):
+                change = (first[f, z + k + 1, 4:20, :] - 0.8 * own) + weigh(w[k], six)
+                values.append(change * diag[k])
+                e_one[f, z + k] = second[f, z + k + 1, 8:16, :]
+            for k in range(2):
+                halves[f, 2 * step + k, 0:16, :] = values[2 * k] + values[2 * k + 1]
+                halves[f, 2 * step + k, 16:24, :] = jnp.zeros((8, 128), F32)
         for k in range(2):
-            z = 2 * pair + k
-            w = [weights[i, z, 4:20, :] for i in range(6)]
-            diag = diags[z, 4:20, :]
-            for f in range(3):
-                own, six = six_of(second, (f,), z + 1, 4, 16)
-                change = (first[f, z + 1, 4:20, :] - 0.8 * own) + weigh(w, six)
-                value = change * diag
-                sums[f] = value if k == 0 else sums[f] + value
-                e_one[f, z] = second[f, z + 1, 8:16, :]
-        for f in range(3):
-            halves[f, pair, 0:16, :] = sums[f]
-            halves[f, pair, 16:24, :] = jnp.zeros((8, 128), F32)
-        halves[3, pair] = share[2 * pair] + share[2 * pair + 1]
-
-    loop(8, left, 2)
+            halves[3, 2 * step + k] = share[z + 2 * k] + share[z + 2 * k + 1]
+
+    loop(4, left)
 
     source, target = iota((128, 128), 0), iota((128, 128), 1)
     pool = jnp.where(source // 2 + jnp.where(source >= 96, 64, 0) == target, 0.125, 0.0)
@@ -564,42 +574,31 @@
     in_y = jnp.where(lane < 32, 1, jnp.where(lane < 96, high_y, low_y))
     omega2 = 0.8 * (in_x * in_y).astype(F32)
 
-    def start2(z):
-        own, six = six_of(rest2, (), z + 1, 1, 8)
+    for z, (own, six) in enumerate(block_of(rest2, (), 1, 8, 1, 8)):
         gain, w, diag = level_weights(own, six, omega2)
         for i in range(6):
             weights2[i, z, 1:9, :] = w[i]
-        diags2[z, 1:9, :] = (1.25 * 0.0625) * diag
+        weights2[6, z, 1:9, :] = (1.25 * 0.0625) * diag
         for f in range(3):
             first2[f, z + 1, 1:9, :] = (16.0 * gain) * rhs2[f, z]
-
-    loop(8, start2, 8)
-
-    def sweep2(z):
-        w = [weights2[i, z, 2:10, :] for i in range(6)]
-        for f in range(3):
-            own, six = six_of(first2, (f,), z + 1, 2, 8)
-            second2[f, z + 1, 2:10, :] = 1.2 * own + weigh(w, six)
-
-    loop(8, sweep2, 8)
-
+    w = [[weights2[i, z, 2:10, :] for i in range(6)] for z in range(8)]
+    for f in range(3):
+        for z, (own, six) in enumerate(block_of(first2, (f,), 1, 8, 2, 8)):
+            second2[f, z + 1, 2:10, :] = 1.2 * own + weigh(w[z], six)
+    w = [[weights2[i, z, 3:11, :] for i in range(7)] for z in range(8)]
     own_row = iota((8, 128), 0) < 4
-    parts = []
-    for pair in range(4):
-        sums = {}
-        for k in range(2):
-            z = 2 * pair + k
-            w = [weights2[i, z, 3:11, :] for i in range(6)]
-            diag = diags2[z, 3:11, :]
-            for f in range(3):
-                own, six = six_of(second2, (f,), z + 1, 3, 8)
-                e_two[f, z] = own
-                change = (first2[f, z + 1, 3:11, :] - 0.8 * own) + weigh(w, six)
-                value = jnp.where(own_row, change * diag, 0.0)
-                sums[f] = value if k == 0 else sums[f] + value
-            value = jnp.where(own_row, share2[z], 0.0)
-            sums[3] = value if k == 0 else sums[3] + value
-        parts.append(sums)
+    parts = [{} for pair in range(4)]
+    for f in range(3):
+        for z, (own, six) in enumerate(block_of(second2, (f,), 1, 8, 3, 8)):
+            e_two[f, z] = own
+            change = (first2[f, z + 1, 3:11, :] - 0.8 * own) + weigh(w[z], six)
+            value = jnp.where(own_row, change * w[z][6], 0.0)
+            sums = parts[z // 2]
+            sums[f] = value if z % 2 == 0 else sums[f] + value
+    for z in range(8):
+        value = jnp.where(own_row, share2[z], 0.0)
+        sums = parts[z // 2]
+        sums[3] = value if z % 2 == 0 else sums[3] + value
 
     pool = jnp.where((source < 32) & (source // 2 == target % 16), 0.125, 0.0)
     rows = jnp.concatenate([parts[pair][ch] for ch in range(4) for pair in range(4)], axis=0)
@@ -805,32 +804,34 @@
     )
     from_far = lax.ppermute(to_far, "gy", swap_far)
     from_near = lax.ppermute(to_near, "gy", swap_near)
-    two, part, edges_rim = call(
+    two, main, edges_rim = call(
         rows_edge_kernel,
-        [(3, 34, 24, 128), (4, 16, 8, 128), (4, 16, 8, 128)],
+        [(3, 34, 24, 128), (4, 8, 8, 128), (4, 16, 8, 128)],
         [(4, 34, 24, 128), (3, 34, 24, 128), (6, 32, 24, 128), (32, 24, 128)]
-        + [(4, 16, 16, 128), (1024, 128)],
+        + [(4, 16, 16, 128), (512, 128)],
         flops=10_000_000,
     )(own, rim_rows, own_one, own_two, halves)
-    rim, coarse, packed = call(
+    main_near = lax.ppermute(main, "gx", swap_near)
+    main_far = lax.ppermute(main, "gx", swap_far)
+    rim, rim_one = call(
         rim_kernel,
-        [(3, 16, 16, 128), (4, 16, 8, 128), (4, 2, 5, 8, 128)],
+        [(3, 16, 16, 128), (4, 4, 8, 128)],
         [(3, 18, 32, 128), (18, 32, 128)]
         + [(3, 18, 32, 128)] * 2
         + [(6, 16, 32, 128), (16, 32, 128)]
-        + [(4, 8, 16, 128), (512, 128)],
+        + [(4, 8, 16, 128), (256, 128)],
         flops=10_000_000,
-    )(edges, edges_rim, part, from_near, from_far)
-    from_near = lax.ppermute(packed, "gx", swap_near)
-    from_far = lax.ppermute(packed, "gx", swap_far)
+    )(edges, edges_rim, from_near, from_far)
+    rim_near = lax.ppermute(rim_one, "gx", swap_near)
+    rim_far = lax.ppermute(rim_one, "gx", swap_far)
     sent, e_one, e_two = call(
         middle_kernel,
         [(CHIPS, 4, 128), (3, 16, 8, 128), (3, 8, 8, 128)],
         [(16, 24, 128), (18, 32, 128), (3, 16, 32, 128), (3, 18, 32, 128), (3, 18, 32, 128)]
         + [(6, 16, 32, 128), (16, 32, 128), (4, 8, 24, 128), (768, 128)]
         + [(10, 24, 128), (3, 10, 24, 128), (3, 10, 24, 128), (3, 8, 8, 128), (8, 8, 128)]
-        + [(6, 8, 16, 128), (8, 16, 128)],
-    )(coarse, from_near, from_far)
+        + [(7, 8, 16, 128)],
+    )(main, main_near, main_far, rim_one, rim_near, rim_far)
     groups = [[i for i in range(NX * NY) if i % 2 == core] for core in range(2)]
     mine = lax.all_to_all(
         sent, ("gx", "gy"), split_axis=0, concat_axis=0, axis_index_groups=groups, tiled=True

time: 76.5 us -> 78.2 us (1.022)
  starting transfers between devices: 16.9 us -> 23.3 us
  blocking collectives: 31.3 us -> 27.9 us
  waiting for transfers between devices: 2.72 us -> 1.66 us
    ppermute x2 -> x4, starting transfers between devices: 6.67 us -> 13.2 us  [the longest x1 6.04 us: local(): main_near = lax.ppermute(main, 'gx', swap_near)]
    all_to_all x1, blocking collectives: 31.3 us -> 27.9 us  [local(): lax.all_to_all(sent, ('gx', 'gy'), split_axis=0, concat_axis=0, axis_inde...]
    ppermute x2 -> x4, waiting for transfers between devices: 2.71 us -> 1.65 us  [the longest x1 1.64 us: local(): rim_near = lax.ppermute(rim_one, 'gx', swap_near)]
  transfers between devices with their start and end apart: 7 -> 9, of which waited for: 1 -> 1; matrix products, arithmetic and copies ran while one was open for 0% -> 0% of each run, Pallas kernels for 16% -> 19%
where the time goes in v4:
time: 78.2 us; the launch traced here: 78 us
  blocking collectives  27.9 us (36%)
  Pallas kernels  25 us (32%)
  starting transfers between devices  23.3 us (30%)
  waiting for transfers between devices  1.66 us (2%)
    all_to_all x1, blocking collectives, local(): lax.all_to_all(sent, ('gx', 'gy'), split_axis=0, concat_axis=0, axis_inde...  27.9 us
    ppermute x1, starting transfers between devices, local(): main_near = lax.ppermute(main, 'gx', swap_near)  6.04 us
    ppermute x1, starting transfers between devices, local(): rim_near = lax.ppermute(rim_one, 'gx', swap_near)  5.86 us
    pallas_call x1, Pallas kernels, local(): call(rows_edge_kernel, [(3, 34, 24, 128), (4, 8, 8, 128), (4, 16, 8, 128)...  5.2 us
    pallas_call x1, Pallas kernels, local(): call(own_kernel, [(3, 34, 32, 128)] * 2 + [(4, 16, 16, 128)] + [(4, 4, 16...  4.96 us
    pallas_call x1, Pallas kernels, local(): call(top_kernel, [(3, 32, 16, 128)], [(4, 2, 128, 128), (3, 16, 16, 128),...  4.6 us
    pallas_call x1, Pallas kernels, local(): call(middle_kernel, [(CHIPS, 4, 128), (3, 16, 8, 128), (3, 8, 8, 128)], [...  3.62 us
    pallas_call x1, Pallas kernels, local(): call(rim_kernel, [(3, 16, 16, 128), (4, 4, 8, 128)], [(3, 18, 32, 128), (...  3.3 us
  transfers between devices with their start and end apart: 9, of which 1 were waited for; matrix products, arithmetic and copies ran while one was open for 0% of the time, Pallas kernels for 19%

profile of v4, /device:TPU:1, one launch (start us, length us, event | category | flops | bytes accessed | tf_op | source)
XLA Modules:
  0.0 78.0 jit_solution(13690102775819636940)
XLA Ops:
  0.0 1.3 %shard_map.28 = (f32[12,32,128]{2,1,0:T(8,128)S(1)}, f32[12,32,128]{2,1,0:T(8,128)S(1)}, f32[4,32,16,128]{3,2,1,0:T(8,128)S(1)}) custom-call(f32[3,32,16,128]{3,2,1,0:T(8,128)} %guess.1, s32[32,16,128]{2,1,0:T(8,128)} %labels.1), custom_call_target="tpu_custom_call" | custom-call | flops 1000000 | bytes 4000000 | tf_op jit(solution)/shard_map/pallas_call | solution.py:788
  1.3 2.1 %collective-permute-start = (f32[12,32,128]{2,1,0:T(8,128)S(1)}, f32[12,32,128]{2,1,0:T(8,128)S(1)}, u32[]{:S(2)}, u32[]{:S(2)}) collective-permute-start(f32[12,32,128]{2,1,0:T(8,128)S(1)} %get-tuple-element.28), channel_id=1, source_target_pairs={{0,16},{16,0},{32,48},{48,32},{64,80},{80,64},{96,112},{112,96},{1... | collective-permute-start | bytes 589832 | tf_op jit(solution)/shard_map/ppermute | solution.py:794
  3.4 0.7 collective-permute-start.1
  4.1 5.0 %shard_map.29 = (f32[3,34,32,128]{3,2,1,0:T(8,128)S(1)}, f32[3,34,32,128]{3,2,1,0:T(8,128)S(1)}, f32[4,16,16,128]{3,2,1,0:T(8,128)S(1)}, f32[4,4,16,128]{3,2,1,0...) custom-call(f32[4,32,16,128]{3,2,1,0:T(8,128)S(1)} %get-tuple-element.25.own), custom_call_target="tpu_custom_call" | custom-call | flops 20000000 | bytes 4000000 | tf_op jit(solution)/shard_map/pallas_call | solution.py:796
  9.0 0.0 collective-permute-done.x_near
  9.0 0.0 collective-permute-done.1.x_far
  9.0 0.5 shard_map.30
  9.5 1.3 %collective-permute-start.4 = (f32[4,4,24,128]{3,2,1,0:T(8,128)S(1)}, f32[4,4,24,128]{3,2,1,0:T(8,128)S(1)}, u32[]{:S(2)}, u32[]{:S(2)}) collective-permute-start(f32[4,4,24,128]{3,2,1,0:T(8,128)S(1)} %get-tuple-element.37), channel_id=1, source_target_pairs={{0,1},{1,0},{2,3},{3,2},{4,5},{5,4},{6,7},{7,6},{8,9},{9,8},{10,11... | collective-permute-start | bytes 589832 | tf_op jit(solution)/shard_map/ppermute | solution.py:806
  10.8 3.2 %collective-permute-start.5 = (f32[4,4,24,128]{3,2,1,0:T(8,128)S(1)}, f32[4,4,24,128]{3,2,1,0:T(8,128)S(1)}, u32[]{:S(2)}, u32[]{:S(2)}) collective-permute-start(f32[4,4,24,128]{3,2,1,0:T(8,128)S(1)} %get-tuple-element.38), channel_id=1, source_target_pairs={{1,2},{2,1},{3,4},{4,3},{5,6},{6,5},{7,8},{8,7},{9,10},{10,9},{11,... | collective-permute-start | bytes 589832 | tf_op jit(solution)/shard_map/ppermute | solution.py:805
  14.0 5.2 %shard_map.31 = (f32[3,34,24,128]{3,2,1,0:T(8,128)S(1)}, f32[4,8,8,128]{3,2,1,0:T(8,128)S(1)}, f32[4,16,8,128]{3,2,1,0:T(8,128)S(1)}) custom-call(f32[4,32,16,128]{3,2,1,0:T(8,128)S(1)} %get-tuple-element.25.own, f32[4,32,8,128]{3,2,1,0:T(8,128)S(1)} %get-tuple-element.30.rim, f32[3,34,32,128]{3,2,1,0:T(8,128)S(1)} %get-tuple-element.31.own_one, ...), custom_call_target="tpu_custom_call" | custom-call | flops 10000000 | bytes 4000000 | tf_op jit(solution)/shard_map/pallas_call | solution.py:807
  19.2 0.7 collective-permute-start.3
  19.9 6.0 %collective-permute-start.2 = (f32[4,8,8,128]{3,2,1,0:T(8,128)S(1)}, f32[4,8,8,128]{3,2,1,0:T(8,128)S(1)}, u32[]{:S(2)}, u32[]{:S(2)}) collective-permute-start(f32[4,8,8,128]{3,2,1,0:T(8,128)S(1)} %get-tuple-element.34.main), channel_id=1, source_target_pairs={{0,16},{16,0},{32,48},{48,32},{64,80},{80,64},{96,112},{112,96},{1... | collective-permute-start | bytes 393224 | tf_op jit(solution)/shard_map/ppermute | solution.py:814
  26.0 0.0 collective-permute-done.4.near
  26.0 0.0 collective-permute-done.5.far
  26.0 3.3 %shard_map.32 = (f32[3,16,16,128]{3,2,1,0:T(8,128)S(1)}, f32[4,4,8,128]{3,2,1,0:T(8,128)S(1)}) custom-call(f32[4,16,16,128]{3,2,1,0:T(8,128)S(1)} %get-tuple-element.35.edges, f32[4,16,8,128]{3,2,1,0:T(8,128)S(1)} %get-tuple-element.36.edges_rim, f32[4,4,24,128]{3,2,1,0:T(8,128)S(1)} %collective-permute-done.4.near, ...), custom_call_target="tpu_custom_call" | custom-call | flops 10000000 | bytes 4000000 | tf_op jit(solution)/shard_map/pallas_call | solution.py:816
  29.3 0.7 collective-permute-start.7
  29.9 5.9 %collective-permute-start.6 = (f32[4,4,8,128]{3,2,1,0:T(8,128)S(1)}, f32[4,4,8,128]{3,2,1,0:T(8,128)S(1)}, u32[]{:S(2)}, u32[]{:S(2)}) collective-permute-start(f32[4,4,8,128]{3,2,1,0:T(8,128)S(1)} %get-tuple-element.39.rim), channel_id=1, source_target_pairs={{0,16},{16,0},{32,48},{48,32},{64,80},{80,64},{96,112},{112,96},{1... | collective-permute-start | bytes 196616 | tf_op jit(solution)/shard_map/ppermute | solution.py:825
  35.8 0.0 collective-permute-done.3.main_far
  35.8 0.0 collective-permute-done.2.main_near
  35.8 0.0 collective-permute-done.7.rim_far
  35.8 1.6 %collective-permute-done.6.rim_near = f32[4,4,8,128]{3,2,1,0:T(8,128)S(1)} collective-permute-done((f32[4,4,8,128]{3,2,1,0:T(8,128)S(1)}, f32[4,4,8,128]{3,2,1,0:T(8,128)S(1)}, u32[]{:S(2)}, u32[]{:S(2)}) %collective-permute-start.6) | collective-permute-done | bytes 65568 | tf_op jit(solution)/shard_map/ppermute | solution.py:825
  37.5 3.6 %shard_map.33 = (f32[128,4,128]{2,1,0:T(4,128)S(1)}, f32[3,16,8,128]{3,2,1,0:T(8,128)S(1)}, f32[3,8,8,128]{3,2,1,0:T(8,128)S(1)}) custom-call(f32[4,8,8,128]{3,2,1,0:T(8,128)S(1)} %get-tuple-element.34.main, f32[4,8,8,128]{3,2,1,0:T(8,128)S(1)} %collective-permute-done.2.main_near, f32[4,8,8,128]{3,2,1,0:T(8,128)S(1)} %collective-permute-done.3.main_far, ...), custom_call_target="tpu_custom_call" | custom-call | flops 1000000 | bytes 4000000 | tf_op jit(solution)/shard_map/pallas_call | solution.py:827
  41.1 27.9 %all_to_all.5 = f32[128,4,128]{2,1,0:T(4,128)S(1)} all-to-all(f32[128,4,128]{2,1,0:T(4,128)S(1)} %get-tuple-element.40), channel_id=1, replica_groups={{0,2,4,6,8,10,12,14,16,18,20,22,24,26,28,30,32,34,36,38,40,42,44,46,48,..., dimensions={0} | all-to-all | bytes 524288 | tf_op jit(solution)/shard_map/all_to_all | solution.py:836
  69.0 2.8 %collective-permute-start.8 = (f32[128,4,128]{2,1,0:T(4,128)S(1)}, f32[128,4,128]{2,1,0:T(4,128)S(1)}, u32[]{:S(2)}, u32[]{:S(2)}) collective-permute-start(f32[128,4,128]{2,1,0:T(4,128)S(1)} %all_to_all.5), channel_id=1, source_target_pairs={{0,1},{1,0},{2,3},{3,2},{4,5},{5,4},{6,7},{7,6},{8,9},{9,8},{10,11... | collective-permute-start | bytes 786440 | tf_op jit(solution)/shard_map/ppermute | solution.py:840
  71.8 1.6 %shard_map.34.base = f32[3,32,16,128]{3,2,1,0:T(8,128)S(1)} custom-call(f32[3,34,24,128]{3,2,1,0:T(8,128)S(1)} %get-tuple-element.41.two, f32[3,16,16,128]{3,2,1,0:T(8,128)S(1)} %get-tuple-element.42.rim, f32[3,16,8,128]{3,2,1,0:T(8,128)S(1)} %get-tuple-element.43.e_one, f32[3,8,8,128]{3,2,1,0:T(8,128)S(1)} %get-tuple-element.44.e_two), custom_call_target="tpu_custom_call" | custom-call | flops 1000000 | bytes 4000000 | tf_op jit(solution)/shard_map/pallas_call | solution.py:839
  73.4 0.0 collective-permute-done.8
  73.4 4.6 %shard_map.35 = f32[3,32,16,128]{3,2,1,0:T(8,128)} custom-call(f32[512,128]{1,0:T(8,128)S(1)} %bitcast.2, f32[512,128]{1,0:T(8,128)S(1)} %bitcast.3, f32[3,32,16,128]{3,2,1,0:T(8,128)S(1)} %shard_map.34.base), custom_call_target="tpu_custom_call" | custom-call | flops 1000000 | bytes 4000000 | tf_op jit(solution)/shard_map/pallas_call | solution.py:841
Async XLA Ops:
  1.3 7.8 %collective-permute-start = (f32[12,32,128]{2,1,0:T(8,128)S(1)}, f32[12,32,128]{2,1,0:T(8,128)S(1)}, u32[]{:S(2)}, u32[]{:S(2)}) collective-permute-start(f32[12,32,128]{2,1,0:T(8,128)S(1)} %get-tuple-element.28), channel_id=1, source_target_pairs={{0,16},{16,0},{32,48},{48,32},{64,80},{80,64},{96,112},{112,96},{1... | collective-permute-start | bytes 589832 | tf_op jit(solution)/shard_map/ppermute | solution.py:794
  3.4 5.6 %collective-permute-start.1 = (f32[12,32,128]{2,1,0:T(8,128)S(1)}, f32[12,32,128]{2,1,0:T(8,128)S(1)}, u32[]{:S(2)}, u32[]{:S(2)}) collective-permute-start(f32[12,32,128]{2,1,0:T(8,128)S(1)} %get-tuple-element.29), channel_id=1, source_target_pairs={{16,32},{32,16},{48,64},{64,48},{80,96},{96,80},{112,128},{128,112... | collective-permute-start | bytes 589832 | tf_op jit(solution)/shard_map/ppermute | solution.py:795
  9.5 16.4 %collective-permute-start.4 = (f32[4,4,24,128]{3,2,1,0:T(8,128)S(1)}, f32[4,4,24,128]{3,2,1,0:T(8,128)S(1)}, u32[]{:S(2)}, u32[]{:S(2)}) collective-permute-start(f32[4,4,24,128]{3,2,1,0:T(8,128)S(1)} %get-tuple-element.37), channel_id=1, source_target_pairs={{0,1},{1,0},{2,3},{3,2},{4,5},{5,4},{6,7},{7,6},{8,9},{9,8},{10,11... | collective-permute-start | bytes 589832 | tf_op jit(solution)/shard_map/ppermute | solution.py:806
  10.8 15.1 %collective-permute-start.5 = (f32[4,4,24,128]{3,2,1,0:T(8,128)S(1)}, f32[4,4,24,128]{3,2,1,0:T(8,128)S(1)}, u32[]{:S(2)}, u32[]{:S(2)}) collective-permute-start(f32[4,4,24,128]{3,2,1,0:T(8,128)S(1)} %get-tuple-element.38), channel_id=1, source_target_pairs={{1,2},{2,1},{3,4},{4,3},{5,6},{6,5},{7,8},{8,7},{9,10},{10,9},{11,... | collective-permute-start | bytes 589832 | tf_op jit(solution)/shard_map/ppermute | solution.py:805
  19.2 16.6 %collective-permute-start.3 = (f32[4,8,8,128]{3,2,1,0:T(8,128)S(1)}, f32[4,8,8,128]{3,2,1,0:T(8,128)S(1)}, u32[]{:S(2)}, u32[]{:S(2)}) collective-permute-start(f32[4,8,8,128]{3,2,1,0:T(8,128)S(1)} %get-tuple-element.34.main), channel_id=1, source_target_pairs={{16,32},{32,16},{48,64},{64,48},{80,96},{96,80},{112,128},{128,112... | collective-permute-start | bytes 393224 | tf_op jit(solution)/shard_map/ppermute | solution.py:815
  19.9 15.9 %collective-permute-start.2 = (f32[4,8,8,128]{3,2,1,0:T(8,128)S(1)}, f32[4,8,8,128]{3,2,1,0:T(8,128)S(1)}, u32[]{:S(2)}, u32[]{:S(2)}) collective-permute-start(f32[4,8,8,128]{3,2,1,0:T(8,128)S(1)} %get-tuple-element.34.main), channel_id=1, source_target_pairs={{0,16},{16,0},{32,48},{48,32},{64,80},{80,64},{96,112},{112,96},{1... | collective-permute-start | bytes 393224 | tf_op jit(solution)/shard_map/ppermute | solution.py:814
  29.3 6.5 %collective-permute-start.7 = (f32[4,4,8,128]{3,2,1,0:T(8,128)S(1)}, f32[4,4,8,128]{3,2,1,0:T(8,128)S(1)}, u32[]{:S(2)}, u32[]{:S(2)}) collective-permute-start(f32[4,4,8,128]{3,2,1,0:T(8,128)S(1)} %get-tuple-element.39.rim), channel_id=1, source_target_pairs={{16,32},{32,16},{48,64},{64,48},{80,96},{96,80},{112,128},{128,112... | collective-permute-start | bytes 196616 | tf_op jit(solution)/shard_map/ppermute | solution.py:826
  29.9 7.5 %collective-permute-start.6 = (f32[4,4,8,128]{3,2,1,0:T(8,128)S(1)}, f32[4,4,8,128]{3,2,1,0:T(8,128)S(1)}, u32[]{:S(2)}, u32[]{:S(2)}) collective-permute-start(f32[4,4,8,128]{3,2,1,0:T(8,128)S(1)} %get-tuple-element.39.rim), channel_id=1, source_target_pairs={{0,16},{16,0},{32,48},{48,32},{64,80},{80,64},{96,112},{112,96},{1... | collective-permute-start | bytes 196616 | tf_op jit(solution)/shard_map/ppermute | solution.py:825
  69.0 4.4 %collective-permute-start.8 = (f32[128,4,128]{2,1,0:T(4,128)S(1)}, f32[128,4,128]{2,1,0:T(4,128)S(1)}, u32[]{:S(2)}, u32[]{:S(2)}) collective-permute-start(f32[128,4,128]{2,1,0:T(4,128)S(1)} %all_to_all.5), channel_id=1, source_target_pairs={{0,1},{1,0},{2,3},{3,2},{4,5},{5,4},{6,7},{7,6},{8,9},{9,8},{10,11... | collective-permute-start | bytes 786440 | tf_op jit(solution)/shard_map/ppermute | solution.py:840

commit v5 on v4

--- a/solution.py
+++ b/solution.py
@@ -32,6 +32,10 @@
 def recip(x):
     guess = pl.reciprocal(x, approx=True)
     return guess * (2.0 - x * guess)
+
+
+def inner(index):
+    return (index > 0) & (index < 15)
 
 
 def call(kernel, outs, scratch, flops=1_000_000, **kw):
@@ -83,11 +87,12 @@
     first_core = lax.rem(lax.axis_index("gy"), 2) == 0
     even = lax.rem(lax.axis_index("gx"), 2) == 0
     near_row, far_row = jnp.where(even, 0, 5), jnp.where(even, 5, 0)
+    has_far = inner(lax.axis_index("gx"))
     flat = rim.reshape(4 * 32 * 8, 128)
     for ch in range(4):
         for row in range(3):
             flat[pl.ds(256 * ch + near_row + row, 32, stride=8), :] = x_near[3 * ch + row]
-            flat[pl.ds(256 * ch + far_row + row, 32, stride=8), :] = x_far[3 * ch + row]
+            flat[pl.ds(256 * ch + far_row + row, 32, stride=8), :] = jnp.where(has_far, x_far[3 * ch + row], 0.0)
 
     def some(low):
         for ch in range(4):
@@ -368,8 +373,9 @@
     def unpack(low):
         for ch in range(4):
             target = start.at[ch] if ch < 3 else share
-            from_right = jnp.where(first_core, near[ch, low], far[ch, low])
-            from_left = jnp.where(first_core, far[ch, low], near[ch, low])
+            from_near, from_far = near[ch, low], jnp.where(inner(gy), far[ch, low], 0.0)
+            from_right = jnp.where(first_core, from_near, from_far)
+            from_left = jnp.where(first_core, from_far, from_near)
             for h in range(4):
                 z = 4 * h + low
                 after_y = roll(from_right, 7 - 16 * (h + 1))
@@ -486,16 +492,19 @@
 
     sources = zip(starts, ((main_near, rim_near), (main_far, rim_far), (main, rim)))
     sources = list(sources)
+    has_far = inner(gx)
 
     def fill(q):
         for odd in range(2):
             for half in range(2):
                 z = 2 * q + odd + 8 * half
                 base = 64 * odd + 32 * half
-                for at, (inner, outer) in sources:
+                for at, (middle, outer) in sources:
                     for ch in range(4):
-                        edge = outer[ch, q]
-                        value = jnp.where(lane < 62, roll(inner[ch, 2 * q + odd], 64 * half), roll(edge, 62 - base))
+                        edge, body = outer[ch, q], middle[ch, 2 * q + odd]
+                        if outer is rim_far:
+                            edge, body = jnp.where(has_far, edge, 0.0), jnp.where(has_far, body, 0.0)
+                        value = jnp.where(lane < 62, roll(body, 64 * half), roll(edge, 62 - base))
                         value = jnp.where((lane >= 96) | (lane < 2), roll(edge, 112 - base), value)
                         if ch < 3:
                             rhs[ch, z, pl.ds(at, 8), :] = value
@@ -784,7 +793,7 @@
 
 def local(labels, guess):
     swap_near = [(i, i ^ 1) for i in range(NY)]
-    swap_far = [(i, j) for k in range(1, NY - 1, 2) for i, j in ((k, k + 1), (k + 1, k))]
+    swap_far = [(i, (i + 1 if i % 2 else i - 1) % NY) for i in range(NY)]
     to_near, to_far, own = call(
         rows_kernel,
         [(12, 32, 128)] * 2 + [(4, 32, 16, 128)],

time: 78.2 us -> 72.8 us (0.931)
  starting transfers between devices: 23.3 us -> 18.5 us
  blocking collectives: 27.9 us -> 24.1 us
  waiting for transfers between devices: 1.66 us -> 4.9 us
    ppermute x1, starting transfers between devices: 6.04 us -> 0.01 us  [local(): main_near = lax.ppermute(main, 'gx', swap_near)]
    ppermute x1, waiting for transfers between devices: 0.01 us -> 4.88 us  [local(): rim_far = lax.ppermute(rim_one, 'gx', swap_far)]
    ppermute x1, starting transfers between devices: 5.86 us -> 1.03 us  [local(): rim_near = lax.ppermute(rim_one, 'gx', swap_near)]
    all_to_all x1, blocking collectives: 27.9 us -> 24.1 us  [local(): lax.all_to_all(sent, ('gx', 'gy'), split_axis=0, concat_axis=0, axis_inde...]
    ppermute x1, starting transfers between devices: 0.67 us -> 4.35 us  [local(): main_far = lax.ppermute(main, 'gx', swap_far)]
    ppermute x1, starting transfers between devices: 0.66 us -> 4.27 us  [local(): from_far = lax.ppermute(to_far, 'gx', swap_far)]
    ppermute x1, waiting for transfers between devices: 1.64 us -> 0.01 us  [local(): rim_near = lax.ppermute(rim_one, 'gx', swap_near)]
    ppermute x1, starting transfers between devices: 3.17 us -> 1.62 us  [local(): from_far = lax.ppermute(to_far, 'gy', swap_far)]
  transfers between devices with their start and end apart: 9 -> 9, of which waited for: 1 -> 1; matrix products, arithmetic and copies ran while one was open for 0% -> 0% of each run, Pallas kernels for 19% -> 21%
where the time goes in v5:
time: 72.8 us; the launch traced here: 72.7 us
  Pallas kernels  25 us (34%)
  blocking collectives  24.1 us (33%)
  starting transfers between devices  18.5 us (25%)
  waiting for transfers between devices  4.9 us (7%)
    all_to_all x1, blocking collectives, local(): lax.all_to_all(sent, ('gx', 'gy'), split_axis=0, concat_axis=0, axis_inde...  24.1 us
    pallas_call x1, Pallas kernels, local(): call(rows_edge_kernel, [(3, 34, 24, 128), (4, 8, 8, 128), (4, 16, 8, 128)...  5.2 us
    pallas_call x1, Pallas kernels, local(): call(own_kernel, [(3, 34, 32, 128)] * 2 + [(4, 16, 16, 128)] + [(4, 4, 16...  4.95 us
    ppermute x1, waiting for transfers between devices, local(): rim_far = lax.ppermute(rim_one, 'gx', swap_far)  4.88 us
    pallas_call x1, Pallas kernels, local(): call(top_kernel, [(3, 32, 16, 128)], [(4, 2, 128, 128), (3, 16, 16, 128),...  4.6 us
    ppermute x1, starting transfers between devices, local(): main_far = lax.ppermute(main, 'gx', swap_far)  4.35 us
    ppermute x1, starting transfers between devices, local(): from_far = lax.ppermute(to_far, 'gx', swap_far)  4.27 us
    pallas_call x1, Pallas kernels, local(): call(middle_kernel, [(CHIPS, 4, 128), (3, 16, 8, 128), (3, 8, 8, 128)], [...  3.62 us
  transfers between devices with their start and end apart: 9, of which 1 were waited for; matrix products, arithmetic and copies ran while one was open for 0% of the time, Pallas kernels for 21%

profile of v5, /device:TPU:1, one launch (start us, length us, event | category | flops | bytes accessed | tf_op | source)
XLA Modules:
  0.0 72.7 jit_solution(5193894823884431594)
XLA Ops:
  0.0 1.3 %shard_map.28 = (f32[12,32,128]{2,1,0:T(8,128)S(1)}, f32[12,32,128]{2,1,0:T(8,128)S(1)}, f32[4,32,16,128]{3,2,1,0:T(8,128)S(1)}) custom-call(f32[3,32,16,128]{3,2,1,0:T(8,128)} %guess.1, s32[32,16,128]{2,1,0:T(8,128)} %labels.1), custom_call_target="tpu_custom_call" | custom-call | flops 1000000 | bytes 4000000 | tf_op jit(solution)/shard_map/pallas_call | solution.py:797
  1.3 2.1 %collective-permute-start = (f32[12,32,128]{2,1,0:T(8,128)S(1)}, f32[12,32,128]{2,1,0:T(8,128)S(1)}, u32[]{:S(2)}, u32[]{:S(2)}) collective-permute-start(f32[12,32,128]{2,1,0:T(8,128)S(1)} %get-tuple-element.28), channel_id=1, source_target_pairs={{0,16},{16,0},{32,48},{48,32},{64,80},{80,64},{96,112},{112,96},{1... | collective-permute-start | bytes 589832 | tf_op jit(solution)/shard_map/ppermute | solution.py:803
  3.4 4.3 %collective-permute-start.1 = (f32[12,32,128]{2,1,0:T(8,128)S(1)}, f32[12,32,128]{2,1,0:T(8,128)S(1)}, u32[]{:S(2)}, u32[]{:S(2)}) collective-permute-start(f32[12,32,128]{2,1,0:T(8,128)S(1)} %get-tuple-element.29), channel_id=1, source_target_pairs={{0,240},{16,32},{32,16},{48,64},{64,48},{80,96},{96,80},{112,128},... | collective-permute-start | bytes 589832 | tf_op jit(solution)/shard_map/ppermute | solution.py:804
  7.7 4.9 %shard_map.29 = (f32[3,34,32,128]{3,2,1,0:T(8,128)S(1)}, f32[3,34,32,128]{3,2,1,0:T(8,128)S(1)}, f32[4,16,16,128]{3,2,1,0:T(8,128)S(1)}, f32[4,4,16,128]{3,2,1,0...) custom-call(f32[4,32,16,128]{3,2,1,0:T(8,128)S(1)} %get-tuple-element.25.own), custom_call_target="tpu_custom_call" | custom-call | flops 20000000 | bytes 4000000 | tf_op jit(solution)/shard_map/pallas_call | solution.py:805
  12.6 0.0 collective-permute-done.x_near
  12.6 0.0 collective-permute-done.1.x_far
  12.6 0.5 shard_map.30
  13.1 1.5 %collective-permute-start.4 = (f32[4,4,24,128]{3,2,1,0:T(8,128)S(1)}, f32[4,4,24,128]{3,2,1,0:T(8,128)S(1)}, u32[]{:S(2)}, u32[]{:S(2)}) collective-permute-start(f32[4,4,24,128]{3,2,1,0:T(8,128)S(1)} %get-tuple-element.37), channel_id=1, source_target_pairs={{0,1},{1,0},{2,3},{3,2},{4,5},{5,4},{6,7},{7,6},{8,9},{9,8},{10,11... | collective-permute-start | bytes 589832 | tf_op jit(solution)/shard_map/ppermute | solution.py:815
  14.6 1.6 %collective-permute-start.5 = (f32[4,4,24,128]{3,2,1,0:T(8,128)S(1)}, f32[4,4,24,128]{3,2,1,0:T(8,128)S(1)}, u32[]{:S(2)}, u32[]{:S(2)}) collective-permute-start(f32[4,4,24,128]{3,2,1,0:T(8,128)S(1)} %get-tuple-element.38), channel_id=1, source_target_pairs={{0,15},{1,2},{2,1},{3,4},{4,3},{5,6},{6,5},{7,8},{8,7},{9,10},{10,... | collective-permute-start | bytes 589832 | tf_op jit(solution)/shard_map/ppermute | solution.py:814
  16.2 5.2 %shard_map.31 = (f32[3,34,24,128]{3,2,1,0:T(8,128)S(1)}, f32[4,8,8,128]{3,2,1,0:T(8,128)S(1)}, f32[4,16,8,128]{3,2,1,0:T(8,128)S(1)}) custom-call(f32[4,32,16,128]{3,2,1,0:T(8,128)S(1)} %get-tuple-element.25.own, f32[4,32,8,128]{3,2,1,0:T(8,128)S(1)} %get-tuple-element.30.rim, f32[3,34,32,128]{3,2,1,0:T(8,128)S(1)} %get-tuple-element.31.own_one, ...), custom_call_target="tpu_custom_call" | custom-call | flops 10000000 | bytes 4000000 | tf_op jit(solution)/shard_map/pallas_call | solution.py:816
  21.4 4.4 %collective-permute-start.3 = (f32[4,8,8,128]{3,2,1,0:T(8,128)S(1)}, f32[4,8,8,128]{3,2,1,0:T(8,128)S(1)}, u32[]{:S(2)}, u32[]{:S(2)}) collective-permute-start(f32[4,8,8,128]{3,2,1,0:T(8,128)S(1)} %get-tuple-element.34.main), channel_id=1, source_target_pairs={{0,240},{16,32},{32,16},{48,64},{64,48},{80,96},{96,80},{112,128},... | collective-permute-start | bytes 393224 | tf_op jit(solution)/shard_map/ppermute | solution.py:824
  25.8 0.0 collective-permute-start.2
  25.8 0.0 collective-permute-done.4.near
  25.8 0.0 collective-permute-done.5.far
  25.8 3.3 %shard_map.32 = (f32[3,16,16,128]{3,2,1,0:T(8,128)S(1)}, f32[4,4,8,128]{3,2,1,0:T(8,128)S(1)}) custom-call(f32[4,16,16,128]{3,2,1,0:T(8,128)S(1)} %get-tuple-element.35.edges, f32[4,16,8,128]{3,2,1,0:T(8,128)S(1)} %get-tuple-element.36.edges_rim, f32[4,4,24,128]{3,2,1,0:T(8,128)S(1)} %collective-permute-done.4.near, ...), custom_call_target="tpu_custom_call" | custom-call | flops 10000000 | bytes 4000000 | tf_op jit(solution)/shard_map/pallas_call | solution.py:825
  29.1 0.6 collective-permute-start.7
  29.7 1.0 %collective-permute-start.6 = (f32[4,4,8,128]{3,2,1,0:T(8,128)S(1)}, f32[4,4,8,128]{3,2,1,0:T(8,128)S(1)}, u32[]{:S(2)}, u32[]{:S(2)}) collective-permute-start(f32[4,4,8,128]{3,2,1,0:T(8,128)S(1)} %get-tuple-element.39.rim), channel_id=1, source_target_pairs={{0,16},{16,0},{32,48},{48,32},{64,80},{80,64},{96,112},{112,96},{1... | collective-permute-start | bytes 196616 | tf_op jit(solution)/shard_map/ppermute | solution.py:834
  30.7 0.0 collective-permute-done.3.main_far
  30.8 0.0 collective-permute-done.2.main_near
  30.8 4.9 %collective-permute-done.7.rim_far = f32[4,4,8,128]{3,2,1,0:T(8,128)S(1)} collective-permute-done((f32[4,4,8,128]{3,2,1,0:T(8,128)S(1)}, f32[4,4,8,128]{3,2,1,0:T(8,128)S(1)}, u32[]{:S(2)}, u32[]{:S(2)}) %collective-permute-start.7) | collective-permute-done | bytes 65568 | tf_op jit(solution)/shard_map/ppermute | solution.py:835
  35.6 0.0 collective-permute-done.6.rim_near
  35.6 3.6 %shard_map.33 = (f32[128,4,128]{2,1,0:T(4,128)S(1)}, f32[3,16,8,128]{3,2,1,0:T(8,128)S(1)}, f32[3,8,8,128]{3,2,1,0:T(8,128)S(1)}) custom-call(f32[4,8,8,128]{3,2,1,0:T(8,128)S(1)} %get-tuple-element.34.main, f32[4,8,8,128]{3,2,1,0:T(8,128)S(1)} %collective-permute-done.2.main_near, f32[4,8,8,128]{3,2,1,0:T(8,128)S(1)} %collective-permute-done.3.main_far, ...), custom_call_target="tpu_custom_call" | custom-call | flops 1000000 | bytes 4000000 | tf_op jit(solution)/shard_map/pallas_call | solution.py:836
  39.3 24.1 %all_to_all.5 = f32[128,4,128]{2,1,0:T(4,128)S(1)} all-to-all(f32[128,4,128]{2,1,0:T(4,128)S(1)} %get-tuple-element.40), channel_id=1, replica_groups={{0,2,4,6,8,10,12,14,16,18,20,22,24,26,28,30,32,34,36,38,40,42,44,46,48,..., dimensions={0} | all-to-all | bytes 524288 | tf_op jit(solution)/shard_map/all_to_all | solution.py:845
  63.4 3.0 %collective-permute-start.8 = (f32[128,4,128]{2,1,0:T(4,128)S(1)}, f32[128,4,128]{2,1,0:T(4,128)S(1)}, u32[]{:S(2)}, u32[]{:S(2)}) collective-permute-start(f32[128,4,128]{2,1,0:T(4,128)S(1)} %all_to_all.5), channel_id=1, source_target_pairs={{0,1},{1,0},{2,3},{3,2},{4,5},{5,4},{6,7},{7,6},{8,9},{9,8},{10,11... | collective-permute-start | bytes 786440 | tf_op jit(solution)/shard_map/ppermute | solution.py:849
  66.3 1.6 %shard_map.34.base = f32[3,32,16,128]{3,2,1,0:T(8,128)S(1)} custom-call(f32[3,34,24,128]{3,2,1,0:T(8,128)S(1)} %get-tuple-element.41.two, f32[3,16,16,128]{3,2,1,0:T(8,128)S(1)} %get-tuple-element.42.rim, f32[3,16,8,128]{3,2,1,0:T(8,128)S(1)} %get-tuple-element.43.e_one, f32[3,8,8,128]{3,2,1,0:T(8,128)S(1)} %get-tuple-element.44.e_two), custom_call_target="tpu_custom_call" | custom-call | flops 1000000 | bytes 4000000 | tf_op jit(solution)/shard_map/pallas_call | solution.py:848
  67.9 0.0 collective-permute-done.8
  67.9 4.6 %shard_map.35 = f32[3,32,16,128]{3,2,1,0:T(8,128)} custom-call(f32[512,128]{1,0:T(8,128)S(1)} %bitcast.2, f32[512,128]{1,0:T(8,128)S(1)} %bitcast.3, f32[3,32,16,128]{3,2,1,0:T(8,128)S(1)} %shard_map.34.base), custom_call_target="tpu_custom_call" | custom-call | flops 1000000 | bytes 4000000 | tf_op jit(solution)/shard_map/pallas_call | solution.py:850
Async XLA Ops:
  1.3 11.4 %collective-permute-start = (f32[12,32,128]{2,1,0:T(8,128)S(1)}, f32[12,32,128]{2,1,0:T(8,128)S(1)}, u32[]{:S(2)}, u32[]{:S(2)}) collective-permute-start(f32[12,32,128]{2,1,0:T(8,128)S(1)} %get-tuple-element.28), channel_id=1, source_target_pairs={{0,16},{16,0},{32,48},{48,32},{64,80},{80,64},{96,112},{112,96},{1... | collective-permute-start | bytes 589832 | tf_op jit(solution)/shard_map/ppermute | solution.py:803
  3.4 9.2 %collective-permute-start.1 = (f32[12,32,128]{2,1,0:T(8,128)S(1)}, f32[12,32,128]{2,1,0:T(8,128)S(1)}, u32[]{:S(2)}, u32[]{:S(2)}) collective-permute-start(f32[12,32,128]{2,1,0:T(8,128)S(1)} %get-tuple-element.29), channel_id=1, source_target_pairs={{0,240},{16,32},{32,16},{48,64},{64,48},{80,96},{96,80},{112,128},... | collective-permute-start | bytes 589832 | tf_op jit(solution)/shard_map/ppermute | solution.py:804
  13.1 12.7 %collective-permute-start.4 = (f32[4,4,24,128]{3,2,1,0:T(8,128)S(1)}, f32[4,4,24,128]{3,2,1,0:T(8,128)S(1)}, u32[]{:S(2)}, u32[]{:S(2)}) collective-permute-start(f32[4,4,24,128]{3,2,1,0:T(8,128)S(1)} %get-tuple-element.37), channel_id=1, source_target_pairs={{0,1},{1,0},{2,3},{3,2},{4,5},{5,4},{6,7},{7,6},{8,9},{9,8},{10,11... | collective-permute-start | bytes 589832 | tf_op jit(solution)/shard_map/ppermute | solution.py:815
  14.6 11.2 %collective-permute-start.5 = (f32[4,4,24,128]{3,2,1,0:T(8,128)S(1)}, f32[4,4,24,128]{3,2,1,0:T(8,128)S(1)}, u32[]{:S(2)}, u32[]{:S(2)}) collective-permute-start(f32[4,4,24,128]{3,2,1,0:T(8,128)S(1)} %get-tuple-element.38), channel_id=1, source_target_pairs={{0,15},{1,2},{2,1},{3,4},{4,3},{5,6},{6,5},{7,8},{8,7},{9,10},{10,... | collective-permute-start | bytes 589832 | tf_op jit(solution)/shard_map/ppermute | solution.py:814
  21.4 9.3 %collective-permute-start.3 = (f32[4,8,8,128]{3,2,1,0:T(8,128)S(1)}, f32[4,8,8,128]{3,2,1,0:T(8,128)S(1)}, u32[]{:S(2)}, u32[]{:S(2)}) collective-permute-start(f32[4,8,8,128]{3,2,1,0:T(8,128)S(1)} %get-tuple-element.34.main), channel_id=1, source_target_pairs={{0,240},{16,32},{32,16},{48,64},{64,48},{80,96},{96,80},{112,128},... | collective-permute-start | bytes 393224 | tf_op jit(solution)/shard_map/ppermute | solution.py:824
  25.8 5.0 %collective-permute-start.2 = (f32[4,8,8,128]{3,2,1,0:T(8,128)S(1)}, f32[4,8,8,128]{3,2,1,0:T(8,128)S(1)}, u32[]{:S(2)}, u32[]{:S(2)}) collective-permute-start(f32[4,8,8,128]{3,2,1,0:T(8,128)S(1)} %get-tuple-element.34.main), channel_id=1, source_target_pairs={{0,16},{16,0},{32,48},{48,32},{64,80},{80,64},{96,112},{112,96},{1... | collective-permute-start | bytes 393224 | tf_op jit(solution)/shard_map/ppermute | solution.py:823
  29.1 6.5 %collective-permute-start.7 = (f32[4,4,8,128]{3,2,1,0:T(8,128)S(1)}, f32[4,4,8,128]{3,2,1,0:T(8,128)S(1)}, u32[]{:S(2)}, u32[]{:S(2)}) collective-permute-start(f32[4,4,8,128]{3,2,1,0:T(8,128)S(1)} %get-tuple-element.39.rim), channel_id=1, source_target_pairs={{0,240},{16,32},{32,16},{48,64},{64,48},{80,96},{96,80},{112,128},... | collective-permute-start | bytes 196616 | tf_op jit(solution)/shard_map/ppermute | solution.py:835
  29.7 5.9 %collective-permute-start.6 = (f32[4,4,8,128]{3,2,1,0:T(8,128)S(1)}, f32[4,4,8,128]{3,2,1,0:T(8,128)S(1)}, u32[]{:S(2)}, u32[]{:S(2)}) collective-permute-start(f32[4,4,8,128]{3,2,1,0:T(8,128)S(1)} %get-tuple-element.39.rim), channel_id=1, source_target_pairs={{0,16},{16,0},{32,48},{48,32},{64,80},{80,64},{96,112},{112,96},{1... | collective-permute-start | bytes 196616 | tf_op jit(solution)/shard_map/ppermute | solution.py:834
  63.4 4.6 %collective-permute-start.8 = (f32[128,4,128]{2,1,0:T(4,128)S(1)}, f32[128,4,128]{2,1,0:T(4,128)S(1)}, u32[]{:S(2)}, u32[]{:S(2)}) collective-permute-start(f32[128,4,128]{2,1,0:T(4,128)S(1)} %all_to_all.5), channel_id=1, source_target_pairs={{0,1},{1,0},{2,3},{3,2},{4,5},{5,4},{6,7},{7,6},{8,9},{9,8},{10,11... | collective-permute-start | bytes 786440 | tf_op jit(solution)/shard_map/ppermute | solution.py:849

commit v6 on v5

--- a/solution.py
+++ b/solution.py
@@ -793,7 +793,15 @@
 
 def local(labels, guess):
     swap_near = [(i, i ^ 1) for i in range(NY)]
-    swap_far = [(i, (i + 1 if i % 2 else i - 1) % NY) for i in range(NY)]
+    far_x, far_y = [], []
+    for x in range(NX):
+        for y in range(NY):
+            across_x, across_y = x + 1 if x % 2 else x - 1, y + 1 if y % 2 else y - 1
+            to = (across_x, y) if 0 <= across_x < NX else (x, y ^ 1)
+            far_x.append((x * NY + y, to[0] * NY + to[1]))
+            to = (x, across_y) if 0 <= across_y < NY else (x ^ 1, y)
+            far_y.append((x * NY + y, to[0] * NY + to[1]))
+    both = ("gx", "gy")
     to_near, to_far, own = call(
         rows_kernel,
         [(12, 32, 128)] * 2 + [(4, 32, 16, 128)],
@@ -801,7 +809,7 @@
         in_specs=[ANY, ANY],
     )(pltpu.with_memory_space_constraint(guess, pltpu.HBM), pltpu.with_memory_space_constraint(labels, pltpu.HBM))
     from_near = lax.ppermute(to_near, "gx", swap_near)
-    from_far = lax.ppermute(to_far, "gx", swap_far)
+    from_far = lax.ppermute(to_far, both, far_x)
     own_one, own_two, halves, to_right, to_left, edges = call(
         own_kernel,
         [(3, 34, 32, 128)] * 2 + [(4, 16, 16, 128)] + [(4, 4, 16, 128)] * 2 + [(4, 16, 16, 128)],
@@ -811,7 +819,7 @@
     to_near, to_far, rim_rows = call(pack_kernel, [(4, 4, 24, 128)] * 2 + [(4, 32, 8, 128)], [])(
         to_right, to_left, from_near, from_far
     )
-    from_far = lax.ppermute(to_far, "gy", swap_far)
+    from_far = lax.ppermute(to_far, both, far_y)
     from_near = lax.ppermute(to_near, "gy", swap_near)
     two, main, edges_rim = call(
         rows_edge_kernel,
@@ -821,7 +829,7 @@
         flops=10_000_000,
     )(own, rim_rows, own_one, own_two, halves)
     main_near = lax.ppermute(main, "gx", swap_near)
-    main_far = lax.ppermute(main, "gx", swap_far)
+    main_far = lax.ppermute(main, both, far_x)
     rim, rim_one = call(
         rim_kernel,
         [(3, 16, 16, 128), (4, 4, 8, 128)],
@@ -832,7 +840,7 @@
         flops=10_000_000,
     )(edges, edges_rim, from_near, from_far)
     rim_near = lax.ppermute(rim_one, "gx", swap_near)
-    rim_far = lax.ppermute(rim_one, "gx", swap_far)
+    rim_far = lax.ppermute(rim_one, both, far_x)
     sent, e_one, e_two = call(
         middle_kernel,
         [(CHIPS, 4, 128), (3, 16, 8, 128), (3, 8, 8, 128)],

time: 72.8 us -> 70.9 us (0.974)
  blocking collectives: 24.1 us -> 28.1 us
  waiting for transfers between devices: 4.9 us -> 1.88 us
  starting transfers between devices: 18.5 us -> 15.6 us
    ppermute x4, starting transfers between devices: 10.8 us -> 5.57 us  [the longest x1 2.06 us: local(): rim_far = lax.ppermute(rim_one, both, far_x)]
    ppermute x4, waiting for transfers between devices: 4.88 us -> 0.01 us  [the longest x1 0.01 us: local(): from_far = lax.ppermute(to_far, both, far_x)]
    all_to_all x1, blocking collectives: 24.1 us -> 28.1 us  [local(): lax.all_to_all(sent, ('gx', 'gy'), split_axis=0, concat_axis=0, axis_inde...]
    ppermute x1, starting transfers between devices: 0.01 us -> 2.07 us  [local(): main_near = lax.ppermute(main, 'gx', swap_near)]
    ppermute x1, waiting for transfers between devices: 0.01 us -> 1.86 us  [local(): rim_near = lax.ppermute(rim_one, 'gx', swap_near)]
    ppermute x1, starting transfers between devices: 1.03 us -> 2.56 us  [local(): rim_near = lax.ppermute(rim_one, 'gx', swap_near)]
    ppermute x1, starting transfers between devices: 1.47 us -> 0.67 us  [local(): from_near = lax.ppermute(to_near, 'gy', swap_near)]
where the time goes in v6:
time: 70.9 us; the launch traced here: 70.8 us
  blocking collectives  28.1 us (40%)
  Pallas kernels  25 us (35%)
  starting transfers between devices  15.6 us (22%)
  waiting for transfers between devices  1.88 us (3%)
    all_to_all x1, blocking collectives, local(): lax.all_to_all(sent, ('gx', 'gy'), split_axis=0, concat_axis=0, axis_inde...  28.1 us
    pallas_call x1, Pallas kernels, local(): call(rows_edge_kernel, [(3, 34, 24, 128), (4, 8, 8, 128), (4, 16, 8, 128)...  5.2 us
    pallas_call x1, Pallas kernels, local(): call(own_kernel, [(3, 34, 32, 128)] * 2 + [(4, 16, 16, 128)] + [(4, 4, 16...  4.95 us
    pallas_call x1, Pallas kernels, local(): call(top_kernel, [(3, 32, 16, 128)], [(4, 2, 128, 128), (3, 16, 16, 128),...  4.6 us
    pallas_call x1, Pallas kernels, local(): call(middle_kernel, [(CHIPS, 4, 128), (3, 16, 8, 128), (3, 8, 8, 128)], [...  3.62 us
    pallas_call x1, Pallas kernels, local(): call(rim_kernel, [(3, 16, 16, 128), (4, 4, 8, 128)], [(3, 18, 32, 128), (...  3.3 us
    ppermute x1, starting transfers between devices, local(): rim_near = lax.ppermute(rim_one, 'gx', swap_near)  2.56 us
    ppermute x1, starting transfers between devices, local(): other = lax.ppermute(mine, 'gy', swap_near)  2.56 us
  transfers between devices with their start and end apart: 9, of which 1 were waited for; matrix products, arithmetic and copies ran while one was open for 0% of the time, Pallas kernels for 21%

profile of v6, /device:TPU:1, one launch (start us, length us, event | category | flops | bytes accessed | tf_op | source)
XLA Modules:
  0.0 70.8 jit_solution(1840183722054916289)
XLA Ops:
  0.0 1.3 %shard_map.28 = (f32[12,32,128]{2,1,0:T(8,128)S(1)}, f32[12,32,128]{2,1,0:T(8,128)S(1)}, f32[4,32,16,128]{3,2,1,0:T(8,128)S(1)}) custom-call(f32[3,32,16,128]{3,2,1,0:T(8,128)} %guess.1, s32[32,16,128]{2,1,0:T(8,128)} %labels.1), custom_call_target="tpu_custom_call" | custom-call | flops 1000000 | bytes 4000000 | tf_op jit(solution)/shard_map/pallas_call | solution.py:805
  1.3 2.1 %collective-permute-start = (f32[12,32,128]{2,1,0:T(8,128)S(1)}, f32[12,32,128]{2,1,0:T(8,128)S(1)}, u32[]{:S(2)}, u32[]{:S(2)}) collective-permute-start(f32[12,32,128]{2,1,0:T(8,128)S(1)} %get-tuple-element.28), channel_id=1, source_target_pairs={{0,16},{16,0},{32,48},{48,32},{64,80},{80,64},{96,112},{112,96},{1... | collective-permute-start | bytes 589832 | tf_op jit(solution)/shard_map/ppermute | solution.py:811
  3.4 1.3 %collective-permute-start.1 = (f32[12,32,128]{2,1,0:T(8,128)S(1)}, f32[12,32,128]{2,1,0:T(8,128)S(1)}, u32[]{:S(2)}, u32[]{:S(2)}) collective-permute-start(f32[12,32,128]{2,1,0:T(8,128)S(1)} %get-tuple-element.29), channel_id=1, source_target_pairs={{0,1},{1,0},{2,3},{3,2},{4,5},{5,4},{6,7},{7,6},{8,9},{9,8},{10,11... | collective-permute-start | bytes 589832 | tf_op jit(solution)/shard_map/ppermute | solution.py:812
  4.7 4.9 %shard_map.29 = (f32[3,34,32,128]{3,2,1,0:T(8,128)S(1)}, f32[3,34,32,128]{3,2,1,0:T(8,128)S(1)}, f32[4,16,16,128]{3,2,1,0:T(8,128)S(1)}, f32[4,4,16,128]{3,2,1,0...) custom-call(f32[4,32,16,128]{3,2,1,0:T(8,128)S(1)} %get-tuple-element.25.own), custom_call_target="tpu_custom_call" | custom-call | flops 20000000 | bytes 4000000 | tf_op jit(solution)/shard_map/pallas_call | solution.py:813
  9.7 0.0 collective-permute-done.x_near
  9.7 0.0 collective-permute-done.1.x_far
  9.7 0.5 shard_map.30
  10.2 0.7 collective-permute-start.4
  10.8 1.1 %collective-permute-start.5 = (f32[4,4,24,128]{3,2,1,0:T(8,128)S(1)}, f32[4,4,24,128]{3,2,1,0:T(8,128)S(1)}, u32[]{:S(2)}, u32[]{:S(2)}) collective-permute-start(f32[4,4,24,128]{3,2,1,0:T(8,128)S(1)} %get-tuple-element.38), channel_id=1, source_target_pairs={{0,16},{1,2},{2,1},{3,4},{4,3},{5,6},{6,5},{7,8},{8,7},{9,10},{10,... | collective-permute-start | bytes 589832 | tf_op jit(solution)/shard_map/ppermute | solution.py:822
  11.9 5.2 %shard_map.31 = (f32[3,34,24,128]{3,2,1,0:T(8,128)S(1)}, f32[4,8,8,128]{3,2,1,0:T(8,128)S(1)}, f32[4,16,8,128]{3,2,1,0:T(8,128)S(1)}) custom-call(f32[4,32,16,128]{3,2,1,0:T(8,128)S(1)} %get-tuple-element.25.own, f32[4,32,8,128]{3,2,1,0:T(8,128)S(1)} %get-tuple-element.30.rim, f32[3,34,32,128]{3,2,1,0:T(8,128)S(1)} %get-tuple-element.31.own_one, ...), custom_call_target="tpu_custom_call" | custom-call | flops 10000000 | bytes 4000000 | tf_op jit(solution)/shard_map/pallas_call | solution.py:824
  17.1 1.1 %collective-permute-start.3 = (f32[4,8,8,128]{3,2,1,0:T(8,128)S(1)}, f32[4,8,8,128]{3,2,1,0:T(8,128)S(1)}, u32[]{:S(2)}, u32[]{:S(2)}) collective-permute-start(f32[4,8,8,128]{3,2,1,0:T(8,128)S(1)} %get-tuple-element.34.main), channel_id=1, source_target_pairs={{0,1},{1,0},{2,3},{3,2},{4,5},{5,4},{6,7},{7,6},{8,9},{9,8},{10,11... | collective-permute-start | bytes 393224 | tf_op jit(solution)/shard_map/ppermute | solution.py:832
  18.3 2.1 %collective-permute-start.2 = (f32[4,8,8,128]{3,2,1,0:T(8,128)S(1)}, f32[4,8,8,128]{3,2,1,0:T(8,128)S(1)}, u32[]{:S(2)}, u32[]{:S(2)}) collective-permute-start(f32[4,8,8,128]{3,2,1,0:T(8,128)S(1)} %get-tuple-element.34.main), channel_id=1, source_target_pairs={{0,16},{16,0},{32,48},{48,32},{64,80},{80,64},{96,112},{112,96},{1... | collective-permute-start | bytes 393224 | tf_op jit(solution)/shard_map/ppermute | solution.py:831
  20.3 0.0 collective-permute-done.4.near
  20.3 0.0 collective-permute-done.5.far
  20.3 3.3 %shard_map.32 = (f32[3,16,16,128]{3,2,1,0:T(8,128)S(1)}, f32[4,4,8,128]{3,2,1,0:T(8,128)S(1)}) custom-call(f32[4,16,16,128]{3,2,1,0:T(8,128)S(1)} %get-tuple-element.35.edges, f32[4,16,8,128]{3,2,1,0:T(8,128)S(1)} %get-tuple-element.36.edges_rim, f32[4,4,24,128]{3,2,1,0:T(8,128)S(1)} %collective-permute-done.4.near, ...), custom_call_target="tpu_custom_call" | custom-call | flops 10000000 | bytes 4000000 | tf_op jit(solution)/shard_map/pallas_call | solution.py:833
  23.6 2.1 %collective-permute-start.7 = (f32[4,4,8,128]{3,2,1,0:T(8,128)S(1)}, f32[4,4,8,128]{3,2,1,0:T(8,128)S(1)}, u32[]{:S(2)}, u32[]{:S(2)}) collective-permute-start(f32[4,4,8,128]{3,2,1,0:T(8,128)S(1)} %get-tuple-element.39.rim), channel_id=1, source_target_pairs={{0,1},{1,0},{2,3},{3,2},{4,5},{5,4},{6,7},{7,6},{8,9},{9,8},{10,11... | collective-permute-start | bytes 196616 | tf_op jit(solution)/shard_map/ppermute | solution.py:843
  25.7 2.6 %collective-permute-start.6 = (f32[4,4,8,128]{3,2,1,0:T(8,128)S(1)}, f32[4,4,8,128]{3,2,1,0:T(8,128)S(1)}, u32[]{:S(2)}, u32[]{:S(2)}) collective-permute-start(f32[4,4,8,128]{3,2,1,0:T(8,128)S(1)} %get-tuple-element.39.rim), channel_id=1, source_target_pairs={{0,16},{16,0},{32,48},{48,32},{64,80},{80,64},{96,112},{112,96},{1... | collective-permute-start | bytes 196616 | tf_op jit(solution)/shard_map/ppermute | solution.py:842
  28.3 0.0 collective-permute-done.3.main_far
  28.3 0.0 collective-permute-done.2.main_near
  28.3 0.0 collective-permute-done.7.rim_far
  28.3 1.9 %collective-permute-done.6.rim_near = f32[4,4,8,128]{3,2,1,0:T(8,128)S(1)} collective-permute-done((f32[4,4,8,128]{3,2,1,0:T(8,128)S(1)}, f32[4,4,8,128]{3,2,1,0:T(8,128)S(1)}, u32[]{:S(2)}, u32[]{:S(2)}) %collective-permute-start.6) | collective-permute-done | bytes 65568 | tf_op jit(solution)/shard_map/ppermute | solution.py:842
  30.1 3.6 %shard_map.33 = (f32[128,4,128]{2,1,0:T(4,128)S(1)}, f32[3,16,8,128]{3,2,1,0:T(8,128)S(1)}, f32[3,8,8,128]{3,2,1,0:T(8,128)S(1)}) custom-call(f32[4,8,8,128]{3,2,1,0:T(8,128)S(1)} %get-tuple-element.34.main, f32[4,8,8,128]{3,2,1,0:T(8,128)S(1)} %collective-permute-done.2.main_near, f32[4,8,8,128]{3,2,1,0:T(8,128)S(1)} %collective-permute-done.3.main_far, ...), custom_call_target="tpu_custom_call" | custom-call | flops 1000000 | bytes 4000000 | tf_op jit(solution)/shard_map/pallas_call | solution.py:844
  33.8 28.1 %all_to_all.5 = f32[128,4,128]{2,1,0:T(4,128)S(1)} all-to-all(f32[128,4,128]{2,1,0:T(4,128)S(1)} %get-tuple-element.40), channel_id=1, replica_groups={{0,2,4,6,8,10,12,14,16,18,20,22,24,26,28,30,32,34,36,38,40,42,44,46,48,..., dimensions={0} | all-to-all | bytes 524288 | tf_op jit(solution)/shard_map/all_to_all | solution.py:853
  61.9 2.6 %collective-permute-start.8 = (f32[128,4,128]{2,1,0:T(4,128)S(1)}, f32[128,4,128]{2,1,0:T(4,128)S(1)}, u32[]{:S(2)}, u32[]{:S(2)}) collective-permute-start(f32[128,4,128]{2,1,0:T(4,128)S(1)} %all_to_all.5), channel_id=1, source_target_pairs={{0,1},{1,0},{2,3},{3,2},{4,5},{5,4},{6,7},{7,6},{8,9},{9,8},{10,11... | collective-permute-start | bytes 786440 | tf_op jit(solution)/shard_map/ppermute | solution.py:857
  64.4 1.6 %shard_map.34.base = f32[3,32,16,128]{3,2,1,0:T(8,128)S(1)} custom-call(f32[3,34,24,128]{3,2,1,0:T(8,128)S(1)} %get-tuple-element.41.two, f32[3,16,16,128]{3,2,1,0:T(8,128)S(1)} %get-tuple-element.42.rim, f32[3,16,8,128]{3,2,1,0:T(8,128)S(1)} %get-tuple-element.43.e_one, f32[3,8,8,128]{3,2,1,0:T(8,128)S(1)} %get-tuple-element.44.e_two), custom_call_target="tpu_custom_call" | custom-call | flops 1000000 | bytes 4000000 | tf_op jit(solution)/shard_map/pallas_call | solution.py:856
  66.0 0.0 collective-permute-done.8
  66.0 4.6 %shard_map.35 = f32[3,32,16,128]{3,2,1,0:T(8,128)} custom-call(f32[512,128]{1,0:T(8,128)S(1)} %bitcast.2, f32[512,128]{1,0:T(8,128)S(1)} %bitcast.3, f32[3,32,16,128]{3,2,1,0:T(8,128)S(1)} %shard_map.34.base), custom_call_target="tpu_custom_call" | custom-call | flops 1000000 | bytes 4000000 | tf_op jit(solution)/shard_map/pallas_call | solution.py:858
Async XLA Ops:
  1.3 8.4 %collective-permute-start = (f32[12,32,128]{2,1,0:T(8,128)S(1)}, f32[12,32,128]{2,1,0:T(8,128)S(1)}, u32[]{:S(2)}, u32[]{:S(2)}) collective-permute-start(f32[12,32,128]{2,1,0:T(8,128)S(1)} %get-tuple-element.28), channel_id=1, source_target_pairs={{0,16},{16,0},{32,48},{48,32},{64,80},{80,64},{96,112},{112,96},{1... | collective-permute-start | bytes 589832 | tf_op jit(solution)/shard_map/ppermute | solution.py:811
  3.4 6.3 %collective-permute-start.1 = (f32[12,32,128]{2,1,0:T(8,128)S(1)}, f32[12,32,128]{2,1,0:T(8,128)S(1)}, u32[]{:S(2)}, u32[]{:S(2)}) collective-permute-start(f32[12,32,128]{2,1,0:T(8,128)S(1)} %get-tuple-element.29), channel_id=1, source_target_pairs={{0,1},{1,0},{2,3},{3,2},{4,5},{5,4},{6,7},{7,6},{8,9},{9,8},{10,11... | collective-permute-start | bytes 589832 | tf_op jit(solution)/shard_map/ppermute | solution.py:812
  10.2 10.2 %collective-permute-start.4 = (f32[4,4,24,128]{3,2,1,0:T(8,128)S(1)}, f32[4,4,24,128]{3,2,1,0:T(8,128)S(1)}, u32[]{:S(2)}, u32[]{:S(2)}) collective-permute-start(f32[4,4,24,128]{3,2,1,0:T(8,128)S(1)} %get-tuple-element.37), channel_id=1, source_target_pairs={{0,1},{1,0},{2,3},{3,2},{4,5},{5,4},{6,7},{7,6},{8,9},{9,8},{10,11... | collective-permute-start | bytes 589832 | tf_op jit(solution)/shard_map/ppermute | solution.py:823
  10.8 9.5 %collective-permute-start.5 = (f32[4,4,24,128]{3,2,1,0:T(8,128)S(1)}, f32[4,4,24,128]{3,2,1,0:T(8,128)S(1)}, u32[]{:S(2)}, u32[]{:S(2)}) collective-permute-start(f32[4,4,24,128]{3,2,1,0:T(8,128)S(1)} %get-tuple-element.38), channel_id=1, source_target_pairs={{0,16},{1,2},{2,1},{3,4},{4,3},{5,6},{6,5},{7,8},{8,7},{9,10},{10,... | collective-permute-start | bytes 589832 | tf_op jit(solution)/shard_map/ppermute | solution.py:822
  17.1 11.1 %collective-permute-start.3 = (f32[4,8,8,128]{3,2,1,0:T(8,128)S(1)}, f32[4,8,8,128]{3,2,1,0:T(8,128)S(1)}, u32[]{:S(2)}, u32[]{:S(2)}) collective-permute-start(f32[4,8,8,128]{3,2,1,0:T(8,128)S(1)} %get-tuple-element.34.main), channel_id=1, source_target_pairs={{0,1},{1,0},{2,3},{3,2},{4,5},{5,4},{6,7},{7,6},{8,9},{9,8},{10,11... | collective-permute-start | bytes 393224 | tf_op jit(solution)/shard_map/ppermute | solution.py:832
  18.3 10.0 %collective-permute-start.2 = (f32[4,8,8,128]{3,2,1,0:T(8,128)S(1)}, f32[4,8,8,128]{3,2,1,0:T(8,128)S(1)}, u32[]{:S(2)}, u32[]{:S(2)}) collective-permute-start(f32[4,8,8,128]{3,2,1,0:T(8,128)S(1)} %get-tuple-element.34.main), channel_id=1, source_target_pairs={{0,16},{16,0},{32,48},{48,32},{64,80},{80,64},{96,112},{112,96},{1... | collective-permute-start | bytes 393224 | tf_op jit(solution)/shard_map/ppermute | solution.py:831
  23.6 4.6 %collective-permute-start.7 = (f32[4,4,8,128]{3,2,1,0:T(8,128)S(1)}, f32[4,4,8,128]{3,2,1,0:T(8,128)S(1)}, u32[]{:S(2)}, u32[]{:S(2)}) collective-permute-start(f32[4,4,8,128]{3,2,1,0:T(8,128)S(1)} %get-tuple-element.39.rim), channel_id=1, source_target_pairs={{0,1},{1,0},{2,3},{3,2},{4,5},{5,4},{6,7},{7,6},{8,9},{9,8},{10,11... | collective-permute-start | bytes 196616 | tf_op jit(solution)/shard_map/ppermute | solution.py:843
  25.7 4.4 %collective-permute-start.6 = (f32[4,4,8,128]{3,2,1,0:T(8,128)S(1)}, f32[4,4,8,128]{3,2,1,0:T(8,128)S(1)}, u32[]{:S(2)}, u32[]{:S(2)}) collective-permute-start(f32[4,4,8,128]{3,2,1,0:T(8,128)S(1)} %get-tuple-element.39.rim), channel_id=1, source_target_pairs={{0,16},{16,0},{32,48},{48,32},{64,80},{80,64},{96,112},{112,96},{1... | collective-permute-start | bytes 196616 | tf_op jit(solution)/shard_map/ppermute | solution.py:842
  61.9 4.2 %collective-permute-start.8 = (f32[128,4,128]{2,1,0:T(4,128)S(1)}, f32[128,4,128]{2,1,0:T(4,128)S(1)}, u32[]{:S(2)}, u32[]{:S(2)}) collective-permute-start(f32[128,4,128]{2,1,0:T(4,128)S(1)} %all_to_all.5), channel_id=1, source_target_pairs={{0,1},{1,0},{2,3},{3,2},{4,5},{5,4},{6,7},{7,6},{8,9},{9,8},{10,11... | collective-permute-start | bytes 786440 | tf_op jit(solution)/shard_map/ppermute | solution.py:857

commit v7 on v6

--- a/solution.py
+++ b/solution.py
@@ -36,6 +36,12 @@
 
 def inner(index):
     return (index > 0) & (index < 15)
+
+
+def span(start, count):
+    if start % 8 == 0:
+        return pl.ds(start, count)
+    return pl.ds(jnp.maximum(lax.axis_index("gx") - NX, 0) + start, count)
 
 
 def call(kernel, outs, scratch, flops=1_000_000, **kw):
@@ -141,14 +147,14 @@
 
 
 def block_of(ref, lead, z, planes, first, count):
-    rows = pl.ds(first, count)
+    rows = span(first, count)
     own = [ref[(*lead, z + k, rows, slice(None))] for k in range(-1, planes + 1)]
     result = []
     for k in range(planes):
         value = own[k + 1]
         six = (
-            ref[(*lead, z + k, pl.ds(first - 1, count), slice(None))],
-            ref[(*lead, z + k, pl.ds(first + 1, count), slice(None))],
+            ref[(*lead, z + k, span(first - 1, count), slice(None))],
+            ref[(*lead, z + k, span(first + 1, count), slice(None))],
             roll(value, 1),
             roll(value, -1),
             own[k],
@@ -185,13 +191,13 @@
         w = []
         for k, (own, six) in enumerate(block_of(share, (), z + 1, 4, first, count)):
             now, diag = fine_weights(own, six, omega)
-            diags[z + k, pl.ds(first, count), :] = diag
+            diags[z + k, span(first, count), :] = diag
             for i in range(6):
-                weights[i, z + k, pl.ds(first, count), :] = now[i]
+                weights[i, z + k, span(first, count), :] = now[i]
             w.append(now)
         for f in range(3):
             for k, (own, six) in enumerate(block_of(start, (f,), z + 1, 4, first, count)):
-                one[f, z + k + 1, pl.ds(first, count), :] = fine_sweep(w[k], f, own, six)
+                one[f, z + k + 1, span(first, count), :] = fine_sweep(w[k], f, own, six)
 
     loop(planes // 4, first_sweep)
     wrap(one)
@@ -199,10 +205,10 @@
 
     def second_sweep(step):
         z = 4 * step
-        w = [[weights[i, z + k, pl.ds(second, count2), :] for i in range(6)] for k in range(4)]
+        w = [[weights[i, z + k, span(second, count2), :] for i in range(6)] for k in range(4)]
         for f in range(3):
             for k, (own, six) in enumerate(block_of(one, (f,), z + 1, 4, second, count2)):
-                two[f, z + k + 1, pl.ds(second, count2), :] = fine_sweep(w[k], f, own, six)
+                two[f, z + k + 1, span(second, count2), :] = fine_sweep(w[k], f, own, six)
 
     loop(planes // 4, second_sweep)
     wrap(two)
@@ -281,8 +287,8 @@
     upper = iota((8, 128), 0) < 4
 
     def both(ref, lead, step, shift=0):
-        high = ref[(*lead, pl.ds(8 - step + shift, 8), slice(None))]
-        low = ref[(*lead, pl.ds(8 + step + shift, 8), slice(None))]
+        high = ref[(*lead, span(8 - step + shift, 8), slice(None))]
+        low = ref[(*lead, span(8 + step + shift, 8), slice(None))]
         return jnp.where(upper, high, low)
 
     def block_both(ref, f, z, step):
@@ -307,9 +313,9 @@
         z = 4 * step
         for k, (value, six) in enumerate(block_of(start, (3,), z + 1, 4, 5, 16)):
             w, diag = fine_weights(value, six, omega)
-            diags[z + k, 5:21, :] = diag
+            diags[z + k, span(5, 16), :] = diag
             for i in range(6):
-                weights[i, z + k, 5:21, :] = w[i]
+                weights[i, z + k, span(5, 16), :] = w[i]
 
     loop(8, weigh_all)
 
@@ -525,30 +531,30 @@
         for k, (own, six) in enumerate(block_of(rest, (), z + 1, 4, 1, 24)):
             gain, w, diag = level_weights(own, six, omega)
             for i in range(6):
-                weights[i, z + k, 1:25, :] = w[i]
-            diags[z + k, 1:25, :] = (1.25 * 0.25) * diag
+                weights[i, z + k, span(1, 24), :] = w[i]
+            diags[z + k, span(1, 24), :] = (1.25 * 0.25) * diag
             for f in range(3):
-                first[f, z + k + 1, 1:25, :] = (4.0 * gain) * rhs[f, z + k, 1:25, :]
+                first[f, z + k + 1, span(1, 24), :] = (4.0 * gain) * rhs[f, z + k, span(1, 24), :]
 
     loop(4, start)
 
     def sweep(step):
         z = 4 * step
-        w = [[weights[i, z + k, 3:27, :] for i in range(6)] for k in range(4)]
+        w = [[weights[i, z + k, span(3, 24), :] for i in range(6)] for k in range(4)]
         for f in range(3):
             for k, (own, six) in enumerate(block_of(first, (f,), z + 1, 4, 3, 24)):
-                second[f, z + k + 1, 3:27, :] = 1.2 * own + weigh(w[k], six)
+                second[f, z + k + 1, span(3, 24), :] = 1.2 * own + weigh(w[k], six)
 
     loop(4, sweep)
 
     def left(step):
         z = 4 * step
-        w = [[weights[i, z + k, 4:20, :] for i in range(6)] for k in range(4)]
-        diag = [diags[z + k, 4:20, :] for k in range(4)]
+        w = [[weights[i, z + k, span(4, 16), :] for i in range(6)] for k in range(4)]
+        diag = [diags[z + k, span(4, 16), :] for k in range(4)]
         for f in range(3):
             values = []
             for k, (own, six) in enumerate(block_of(second, (f,), z + 1, 4, 4, 16)):
-                change = (first[f, z + k + 1, 4:20, :] - 0.8 * own) + weigh(w[k], six)
+                change = (first[f, z + k + 1, span(4, 16), :] - 0.8 * own) + weigh(w[k], six)
                 values.append(change * diag[k])
                 e_one[f, z + k] = second[f, z + k + 1, 8:16, :]
             for k in range(2):
@@ -586,21 +592,21 @@
     for z, (own, six) in enumerate(block_of(rest2, (), 1, 8, 1, 8)):
         gain, w, diag = level_weights(own, six, omega2)
         for i in range(6):
-            weights2[i, z, 1:9, :] = w[i]
-        weights2[6, z, 1:9, :] = (1.25 * 0.0625) * diag
-        for f in range(3):
-            first2[f, z + 1, 1:9, :] = (16.0 * gain) * rhs2[f, z]
-    w = [[weights2[i, z, 2:10, :] for i in range(6)] for z in range(8)]
+            weights2[i, z, span(1, 8), :] = w[i]
+        weights2[6, z, span(1, 8), :] = (1.25 * 0.0625) * diag
+        for f in range(3):
+            first2[f, z + 1, span(1, 8), :] = (16.0 * gain) * rhs2[f, z]
+    w = [[weights2[i, z, span(2, 8), :] for i in range(6)] for z in range(8)]
     for f in range(3):
         for z, (own, six) in enumerate(block_of(first2, (f,), 1, 8, 2, 8)):
-            second2[f, z + 1, 2:10, :] = 1.2 * own + weigh(w[z], six)
-    w = [[weights2[i, z, 3:11, :] for i in range(7)] for z in range(8)]
+            second2[f, z + 1, span(2, 8), :] = 1.2 * own + weigh(w[z], six)
+    w = [[weights2[i, z, span(3, 8), :] for i in range(7)] for z in range(8)]
     own_row = iota((8, 128), 0) < 4
     parts = [{} for pair in range(4)]
     for f in range(3):
         for z, (own, six) in enumerate(block_of(second2, (f,), 1, 8, 3, 8)):
             e_two[f, z] = own
-            change = (first2[f, z + 1, 3:11, :] - 0.8 * own) + weigh(w[z], six)
+            change = (first2[f, z + 1, span(3, 8), :] - 0.8 * own) + weigh(w[z], six)
             value = jnp.where(own_row, change * w[z][6], 0.0)
             sums = parts[z // 2]
             sums[f] = value if z % 2 == 0 else sums[f] + value

time: 70.9 us -> 70.9 us (level)
  no operation moved by 1% of the time
where the time goes in v7:
time: 70.9 us; the launch traced here: 70.8 us
  blocking collectives  28.1 us (40%)
  Pallas kernels  25 us (35%)
  starting transfers between devices  15.6 us (22%)
  waiting for transfers between devices  1.88 us (3%)
    all_to_all x1, blocking collectives, local(): lax.all_to_all(sent, ('gx', 'gy'), split_axis=0, concat_axis=0, axis_inde...  28.1 us
    pallas_call x1, Pallas kernels, local(): call(rows_edge_kernel, [(3, 34, 24, 128), (4, 8, 8, 128), (4, 16, 8, 128)...  5.2 us
    pallas_call x1, Pallas kernels, local(): call(own_kernel, [(3, 34, 32, 128)] * 2 + [(4, 16, 16, 128)] + [(4, 4, 16...  4.95 us
    pallas_call x1, Pallas kernels, local(): call(top_kernel, [(3, 32, 16, 128)], [(4, 2, 128, 128), (3, 16, 16, 128),...  4.6 us
    pallas_call x1, Pallas kernels, local(): call(middle_kernel, [(CHIPS, 4, 128), (3, 16, 8, 128), (3, 8, 8, 128)], [...  3.63 us
    pallas_call x1, Pallas kernels, local(): call(rim_kernel, [(3, 16, 16, 128), (4, 4, 8, 128)], [(3, 18, 32, 128), (...  3.3 us
    ppermute x1, starting transfers between devices, local(): rim_near = lax.ppermute(rim_one, 'gx', swap_near)  2.56 us
    ppermute x1, starting transfers between devices, local(): other = lax.ppermute(mine, 'gy', swap_near)  2.56 us
  transfers between devices with their start and end apart: 9, of which 1 were waited for; matrix products, arithmetic and copies ran while one was open for 0% of the time, Pallas kernels for 21%

profile of v7, /device:TPU:1, one launch (start us, length us, event | category | flops | bytes accessed | tf_op | source)
XLA Modules:
  0.0 70.8 jit_solution(2442724615418524370)
XLA Ops:
  0.0 1.3 %shard_map.28 = (f32[12,32,128]{2,1,0:T(8,128)S(1)}, f32[12,32,128]{2,1,0:T(8,128)S(1)}, f32[4,32,16,128]{3,2,1,0:T(8,128)S(1)}) custom-call(f32[3,32,16,128]{3,2,1,0:T(8,128)} %guess.1, s32[32,16,128]{2,1,0:T(8,128)} %labels.1), custom_call_target="tpu_custom_call" | custom-call | flops 1000000 | bytes 4000000 | tf_op jit(solution)/shard_map/pallas_call | solution.py:811
  1.3 2.1 %collective-permute-start = (f32[12,32,128]{2,1,0:T(8,128)S(1)}, f32[12,32,128]{2,1,0:T(8,128)S(1)}, u32[]{:S(2)}, u32[]{:S(2)}) collective-permute-start(f32[12,32,128]{2,1,0:T(8,128)S(1)} %get-tuple-element.28), channel_id=1, source_target_pairs={{0,16},{16,0},{32,48},{48,32},{64,80},{80,64},{96,112},{112,96},{1... | collective-permute-start | bytes 589832 | tf_op jit(solution)/shard_map/ppermute | solution.py:817
  3.4 1.3 %collective-permute-start.1 = (f32[12,32,128]{2,1,0:T(8,128)S(1)}, f32[12,32,128]{2,1,0:T(8,128)S(1)}, u32[]{:S(2)}, u32[]{:S(2)}) collective-permute-start(f32[12,32,128]{2,1,0:T(8,128)S(1)} %get-tuple-element.29), channel_id=1, source_target_pairs={{0,1},{1,0},{2,3},{3,2},{4,5},{5,4},{6,7},{7,6},{8,9},{9,8},{10,11... | collective-permute-start | bytes 589832 | tf_op jit(solution)/shard_map/ppermute | solution.py:818
  4.7 5.0 %shard_map.29 = (f32[3,34,32,128]{3,2,1,0:T(8,128)S(1)}, f32[3,34,32,128]{3,2,1,0:T(8,128)S(1)}, f32[4,16,16,128]{3,2,1,0:T(8,128)S(1)}, f32[4,4,16,128]{3,2,1,0...) custom-call(f32[4,32,16,128]{3,2,1,0:T(8,128)S(1)} %get-tuple-element.25.own), custom_call_target="tpu_custom_call" | custom-call | flops 20000000 | bytes 4000000 | tf_op jit(solution)/shard_map/pallas_call | solution.py:819
  9.7 0.0 collective-permute-done.x_near
  9.7 0.0 collective-permute-done.1.x_far
  9.7 0.5 shard_map.30
  10.2 0.7 collective-permute-start.4
  10.8 1.1 %collective-permute-start.5 = (f32[4,4,24,128]{3,2,1,0:T(8,128)S(1)}, f32[4,4,24,128]{3,2,1,0:T(8,128)S(1)}, u32[]{:S(2)}, u32[]{:S(2)}) collective-permute-start(f32[4,4,24,128]{3,2,1,0:T(8,128)S(1)} %get-tuple-element.38), channel_id=1, source_target_pairs={{0,16},{1,2},{2,1},{3,4},{4,3},{5,6},{6,5},{7,8},{8,7},{9,10},{10,... | collective-permute-start | bytes 589832 | tf_op jit(solution)/shard_map/ppermute | solution.py:828
  11.9 5.2 %shard_map.31 = (f32[3,34,24,128]{3,2,1,0:T(8,128)S(1)}, f32[4,8,8,128]{3,2,1,0:T(8,128)S(1)}, f32[4,16,8,128]{3,2,1,0:T(8,128)S(1)}) custom-call(f32[4,32,16,128]{3,2,1,0:T(8,128)S(1)} %get-tuple-element.25.own, f32[4,32,8,128]{3,2,1,0:T(8,128)S(1)} %get-tuple-element.30.rim, f32[3,34,32,128]{3,2,1,0:T(8,128)S(1)} %get-tuple-element.31.own_one, ...), custom_call_target="tpu_custom_call" | custom-call | flops 10000000 | bytes 4000000 | tf_op jit(solution)/shard_map/pallas_call | solution.py:830
  17.1 1.1 %collective-permute-start.3 = (f32[4,8,8,128]{3,2,1,0:T(8,128)S(1)}, f32[4,8,8,128]{3,2,1,0:T(8,128)S(1)}, u32[]{:S(2)}, u32[]{:S(2)}) collective-permute-start(f32[4,8,8,128]{3,2,1,0:T(8,128)S(1)} %get-tuple-element.34.main), channel_id=1, source_target_pairs={{0,1},{1,0},{2,3},{3,2},{4,5},{5,4},{6,7},{7,6},{8,9},{9,8},{10,11... | collective-permute-start | bytes 393224 | tf_op jit(solution)/shard_map/ppermute | solution.py:838
  18.3 2.1 %collective-permute-start.2 = (f32[4,8,8,128]{3,2,1,0:T(8,128)S(1)}, f32[4,8,8,128]{3,2,1,0:T(8,128)S(1)}, u32[]{:S(2)}, u32[]{:S(2)}) collective-permute-start(f32[4,8,8,128]{3,2,1,0:T(8,128)S(1)} %get-tuple-element.34.main), channel_id=1, source_target_pairs={{0,16},{16,0},{32,48},{48,32},{64,80},{80,64},{96,112},{112,96},{1... | collective-permute-start | bytes 393224 | tf_op jit(solution)/shard_map/ppermute | solution.py:837
  20.3 0.0 collective-permute-done.4.near
  20.3 0.0 collective-permute-done.5.far
  20.3 3.3 %shard_map.32 = (f32[3,16,16,128]{3,2,1,0:T(8,128)S(1)}, f32[4,4,8,128]{3,2,1,0:T(8,128)S(1)}) custom-call(f32[4,16,16,128]{3,2,1,0:T(8,128)S(1)} %get-tuple-element.35.edges, f32[4,16,8,128]{3,2,1,0:T(8,128)S(1)} %get-tuple-element.36.edges_rim, f32[4,4,24,128]{3,2,1,0:T(8,128)S(1)} %collective-permute-done.4.near, ...), custom_call_target="tpu_custom_call" | custom-call | flops 10000000 | bytes 4000000 | tf_op jit(solution)/shard_map/pallas_call | solution.py:839
  23.6 2.1 %collective-permute-start.7 = (f32[4,4,8,128]{3,2,1,0:T(8,128)S(1)}, f32[4,4,8,128]{3,2,1,0:T(8,128)S(1)}, u32[]{:S(2)}, u32[]{:S(2)}) collective-permute-start(f32[4,4,8,128]{3,2,1,0:T(8,128)S(1)} %get-tuple-element.39.rim), channel_id=1, source_target_pairs={{0,1},{1,0},{2,3},{3,2},{4,5},{5,4},{6,7},{7,6},{8,9},{9,8},{10,11... | collective-permute-start | bytes 196616 | tf_op jit(solution)/shard_map/ppermute | solution.py:849
  25.7 2.6 %collective-permute-start.6 = (f32[4,4,8,128]{3,2,1,0:T(8,128)S(1)}, f32[4,4,8,128]{3,2,1,0:T(8,128)S(1)}, u32[]{:S(2)}, u32[]{:S(2)}) collective-permute-start(f32[4,4,8,128]{3,2,1,0:T(8,128)S(1)} %get-tuple-element.39.rim), channel_id=1, source_target_pairs={{0,16},{16,0},{32,48},{48,32},{64,80},{80,64},{96,112},{112,96},{1... | collective-permute-start | bytes 196616 | tf_op jit(solution)/shard_map/ppermute | solution.py:848
  28.3 0.0 collective-permute-done.3.main_far
  28.3 0.0 collective-permute-done.2.main_near
  28.3 0.0 collective-permute-done.7.rim_far
  28.3 1.9 %collective-permute-done.6.rim_near = f32[4,4,8,128]{3,2,1,0:T(8,128)S(1)} collective-permute-done((f32[4,4,8,128]{3,2,1,0:T(8,128)S(1)}, f32[4,4,8,128]{3,2,1,0:T(8,128)S(1)}, u32[]{:S(2)}, u32[]{:S(2)}) %collective-permute-start.6) | collective-permute-done | bytes 65568 | tf_op jit(solution)/shard_map/ppermute | solution.py:848
  30.1 3.6 %shard_map.33 = (f32[128,4,128]{2,1,0:T(4,128)S(1)}, f32[3,16,8,128]{3,2,1,0:T(8,128)S(1)}, f32[3,8,8,128]{3,2,1,0:T(8,128)S(1)}) custom-call(f32[4,8,8,128]{3,2,1,0:T(8,128)S(1)} %get-tuple-element.34.main, f32[4,8,8,128]{3,2,1,0:T(8,128)S(1)} %collective-permute-done.2.main_near, f32[4,8,8,128]{3,2,1,0:T(8,128)S(1)} %collective-permute-done.3.main_far, ...), custom_call_target="tpu_custom_call" | custom-call | flops 1000000 | bytes 4000000 | tf_op jit(solution)/shard_map/pallas_call | solution.py:850
  33.8 28.1 %all_to_all.5 = f32[128,4,128]{2,1,0:T(4,128)S(1)} all-to-all(f32[128,4,128]{2,1,0:T(4,128)S(1)} %get-tuple-element.40), channel_id=1, replica_groups={{0,2,4,6,8,10,12,14,16,18,20,22,24,26,28,30,32,34,36,38,40,42,44,46,48,..., dimensions={0} | all-to-all | bytes 524288 | tf_op jit(solution)/shard_map/all_to_all | solution.py:859
  61.9 2.6 %collective-permute-start.8 = (f32[128,4,128]{2,1,0:T(4,128)S(1)}, f32[128,4,128]{2,1,0:T(4,128)S(1)}, u32[]{:S(2)}, u32[]{:S(2)}) collective-permute-start(f32[128,4,128]{2,1,0:T(4,128)S(1)} %all_to_all.5), channel_id=1, source_target_pairs={{0,1},{1,0},{2,3},{3,2},{4,5},{5,4},{6,7},{7,6},{8,9},{9,8},{10,11... | collective-permute-start | bytes 786440 | tf_op jit(solution)/shard_map/ppermute | solution.py:863
  64.4 1.6 %shard_map.34.base = f32[3,32,16,128]{3,2,1,0:T(8,128)S(1)} custom-call(f32[3,34,24,128]{3,2,1,0:T(8,128)S(1)} %get-tuple-element.41.two, f32[3,16,16,128]{3,2,1,0:T(8,128)S(1)} %get-tuple-element.42.rim, f32[3,16,8,128]{3,2,1,0:T(8,128)S(1)} %get-tuple-element.43.e_one, f32[3,8,8,128]{3,2,1,0:T(8,128)S(1)} %get-tuple-element.44.e_two), custom_call_target="tpu_custom_call" | custom-call | flops 1000000 | bytes 4000000 | tf_op jit(solution)/shard_map/pallas_call | solution.py:862
  66.0 0.0 collective-permute-done.8
  66.0 4.6 %shard_map.35 = f32[3,32,16,128]{3,2,1,0:T(8,128)} custom-call(f32[512,128]{1,0:T(8,128)S(1)} %bitcast.2, f32[512,128]{1,0:T(8,128)S(1)} %bitcast.3, f32[3,32,16,128]{3,2,1,0:T(8,128)S(1)} %shard_map.34.base), custom_call_target="tpu_custom_call" | custom-call | flops 1000000 | bytes 4000000 | tf_op jit(solution)/shard_map/pallas_call | solution.py:864
Async XLA Ops:
  1.3 8.4 %collective-permute-start = (f32[12,32,128]{2,1,0:T(8,128)S(1)}, f32[12,32,128]{2,1,0:T(8,128)S(1)}, u32[]{:S(2)}, u32[]{:S(2)}) collective-permute-start(f32[12,32,128]{2,1,0:T(8,128)S(1)} %get-tuple-element.28), channel_id=1, source_target_pairs={{0,16},{16,0},{32,48},{48,32},{64,80},{80,64},{96,112},{112,96},{1... | collective-permute-start | bytes 589832 | tf_op jit(solution)/shard_map/ppermute | solution.py:817
  3.4 6.3 %collective-permute-start.1 = (f32[12,32,128]{2,1,0:T(8,128)S(1)}, f32[12,32,128]{2,1,0:T(8,128)S(1)}, u32[]{:S(2)}, u32[]{:S(2)}) collective-permute-start(f32[12,32,128]{2,1,0:T(8,128)S(1)} %get-tuple-element.29), channel_id=1, source_target_pairs={{0,1},{1,0},{2,3},{3,2},{4,5},{5,4},{6,7},{7,6},{8,9},{9,8},{10,11... | collective-permute-start | bytes 589832 | tf_op jit(solution)/shard_map/ppermute | solution.py:818
  10.2 10.2 %collective-permute-start.4 = (f32[4,4,24,128]{3,2,1,0:T(8,128)S(1)}, f32[4,4,24,128]{3,2,1,0:T(8,128)S(1)}, u32[]{:S(2)}, u32[]{:S(2)}) collective-permute-start(f32[4,4,24,128]{3,2,1,0:T(8,128)S(1)} %get-tuple-element.37), channel_id=1, source_target_pairs={{0,1},{1,0},{2,3},{3,2},{4,5},{5,4},{6,7},{7,6},{8,9},{9,8},{10,11... | collective-permute-start | bytes 589832 | tf_op jit(solution)/shard_map/ppermute | solution.py:829
  10.8 9.5 %collective-permute-start.5 = (f32[4,4,24,128]{3,2,1,0:T(8,128)S(1)}, f32[4,4,24,128]{3,2,1,0:T(8,128)S(1)}, u32[]{:S(2)}, u32[]{:S(2)}) collective-permute-start(f32[4,4,24,128]{3,2,1,0:T(8,128)S(1)} %get-tuple-element.38), channel_id=1, source_target_pairs={{0,16},{1,2},{2,1},{3,4},{4,3},{5,6},{6,5},{7,8},{8,7},{9,10},{10,... | collective-permute-start | bytes 589832 | tf_op jit(solution)/shard_map/ppermute | solution.py:828
  17.1 11.1 %collective-permute-start.3 = (f32[4,8,8,128]{3,2,1,0:T(8,128)S(1)}, f32[4,8,8,128]{3,2,1,0:T(8,128)S(1)}, u32[]{:S(2)}, u32[]{:S(2)}) collective-permute-start(f32[4,8,8,128]{3,2,1,0:T(8,128)S(1)} %get-tuple-element.34.main), channel_id=1, source_target_pairs={{0,1},{1,0},{2,3},{3,2},{4,5},{5,4},{6,7},{7,6},{8,9},{9,8},{10,11... | collective-permute-start | bytes 393224 | tf_op jit(solution)/shard_map/ppermute | solution.py:838
  18.3 10.0 %collective-permute-start.2 = (f32[4,8,8,128]{3,2,1,0:T(8,128)S(1)}, f32[4,8,8,128]{3,2,1,0:T(8,128)S(1)}, u32[]{:S(2)}, u32[]{:S(2)}) collective-permute-start(f32[4,8,8,128]{3,2,1,0:T(8,128)S(1)} %get-tuple-element.34.main), channel_id=1, source_target_pairs={{0,16},{16,0},{32,48},{48,32},{64,80},{80,64},{96,112},{112,96},{1... | collective-permute-start | bytes 393224 | tf_op jit(solution)/shard_map/ppermute | solution.py:837
  23.6 4.6 %collective-permute-start.7 = (f32[4,4,8,128]{3,2,1,0:T(8,128)S(1)}, f32[4,4,8,128]{3,2,1,0:T(8,128)S(1)}, u32[]{:S(2)}, u32[]{:S(2)}) collective-permute-start(f32[4,4,8,128]{3,2,1,0:T(8,128)S(1)} %get-tuple-element.39.rim), channel_id=1, source_target_pairs={{0,1},{1,0},{2,3},{3,2},{4,5},{5,4},{6,7},{7,6},{8,9},{9,8},{10,11... | collective-permute-start | bytes 196616 | tf_op jit(solution)/shard_map/ppermute | solution.py:849
  25.7 4.4 %collective-permute-start.6 = (f32[4,4,8,128]{3,2,1,0:T(8,128)S(1)}, f32[4,4,8,128]{3,2,1,0:T(8,128)S(1)}, u32[]{:S(2)}, u32[]{:S(2)}) collective-permute-start(f32[4,4,8,128]{3,2,1,0:T(8,128)S(1)} %get-tuple-element.39.rim), channel_id=1, source_target_pairs={{0,16},{16,0},{32,48},{48,32},{64,80},{80,64},{96,112},{112,96},{1... | collective-permute-start | bytes 196616 | tf_op jit(solution)/shard_map/ppermute | solution.py:848
  61.9 4.2 %collective-permute-start.8 = (f32[128,4,128]{2,1,0:T(4,128)S(1)}, f32[128,4,128]{2,1,0:T(4,128)S(1)}, u32[]{:S(2)}, u32[]{:S(2)}) collective-permute-start(f32[128,4,128]{2,1,0:T(4,128)S(1)} %all_to_all.5), channel_id=1, source_target_pairs={{0,1},{1,0},{2,3},{3,2},{4,5},{5,4},{6,7},{7,6},{8,9},{9,8},{10,11... | collective-permute-start | bytes 786440 | tf_op jit(solution)/shard_map/ppermute | solution.py:863

commit v8 on v6

--- a/solution.py
+++ b/solution.py
@@ -14,6 +14,15 @@
 
 def dot(a, b):
     return jnp.dot(a, b, precision=lax.Precision.HIGHEST, preferred_element_type=F32)
+
+
+def dot_exact(a, b):
+    high = a.astype(jnp.bfloat16)
+    low = (a - high.astype(F32)).astype(jnp.bfloat16)
+    b = b.astype(jnp.bfloat16)
+    return jnp.dot(
+        jnp.concatenate([high, low], axis=1), jnp.concatenate([b, b], axis=0), preferred_element_type=F32
+    )
 
 
 def iota(shape, dim):
@@ -158,15 +167,13 @@
     return result
 
 
-def face(total):
-    return jnp.where(total < 0.5, 1.0, jnp.where(total < 1.5, BETWEEN, 0.1))
-
-
 def fine_weights(own, six, omega):
-    faces = [face(own + other) for other in six]
-    diag = (faces[0] + faces[1]) + (faces[2] + faces[3]) + (faces[4] + faces[5])
+    base, slope = 1.0 + (BETWEEN - 1.0) * own, (BETWEEN - 1.0) + (1.1 - 2.0 * BETWEEN) * own
+    total = (six[0] + six[1]) + (six[2] + six[3]) + (six[4] + six[5])
+    diag = 6.0 * base + slope * total
     gain = omega * recip(diag)
-    return [gain * value for value in faces], 1.25 * diag
+    base, slope = gain * base, gain * slope
+    return [base + slope * other for other in six], 1.25 * diag
 
 
 def fine_sweep(w, f, own, six):
@@ -347,7 +354,7 @@
     value = None
     for half in range(2):
         pool = jnp.where(source // 2 + 64 * half == target, 0.125, 0.0)
-        part = dot(halves[:, 8 * half : 8 * half + 8].reshape(512, 128), pool)
+        part = dot_exact(halves[:, 8 * half : 8 * half + 8].reshape(512, 128), pool)
         value = part if value is None else value + part
     pooled[...] = value
     packed[...] = (pooled[pl.ds(0, 256, stride=2), :] + pooled[pl.ds(1, 256, stride=2), :]).reshape(4, 8, 8, 128)
@@ -422,7 +429,7 @@
     value = None
     for odd in range(2):
         pool = jnp.where(keep & (to + 64 * odd + 32 * (source // 64) == target), 0.125, 0.0)
-        part = dot(mixed[:, :, odd].reshape(256, 128), pool)
+        part = dot_exact(mixed[:, :, odd].reshape(256, 128), pool)
         value = part if value is None else value + part
     pooled[...] = value
     packed[...] = (pooled[pl.ds(0, 128, stride=2), :] + pooled[pl.ds(1, 128, stride=2), :]).reshape(4, 4, 8, 128)
@@ -430,13 +437,13 @@
 
 def base_kernel(two, rim, e_one, e_two, base, wide, spread):
     copy = jnp.where(iota((128, 128), 0) == iota((128, 128), 1) // 2, 1.0, 0.0)
-    value = dot(e_two[...].reshape(192, 128), copy)
+    value = dot_exact(e_two[...].reshape(192, 128), copy)
     for block in range(24):
         rows = value[8 * block : 8 * block + 4, :]
         wide[pl.ds(8 * block, 4, stride=2), :] = rows
         wide[pl.ds(8 * block + 1, 4, stride=2), :] = rows
     value = e_one[...].reshape(24, 2, 8, 128) + wide[...].reshape(24, 1, 8, 128)
-    value = dot(value.reshape(384, 128), copy)
+    value = dot_exact(value.reshape(384, 128), copy)
     flat = spread.reshape(768, 128)
     for block in range(48):
         rows = value[8 * block : 8 * block + 8, :]
@@ -460,11 +467,11 @@
 
 
 def resist(share):
-    return recip(1.0 - 0.9 * share)
+    return recip(2.0 - 1.8 * share)
 
 
 def level_weights(own, six, omega):
-    faces = [2.0 * recip(own + other) for other in six]
+    faces = [recip(own + other) for other in six]
     diag = (faces[0] + faces[1]) + (faces[2] + faces[3]) + (faces[4] + faces[5])
     gain = omega * recip(diag)
     return gain, [gain * w for w in faces], diag
@@ -484,7 +491,7 @@
             ref[f, 0] = jnp.zeros((32, 128), F32)
             ref[f, 17] = jnp.zeros((32, 128), F32)
     for z in (0, 17):
-        rest[z] = jnp.ones((32, 128), F32)
+        rest[z] = jnp.full((32, 128), 0.5, F32)
     lane = iota((8, 128), 1)
     even = lax.rem(gx, 2) == 0
     near_row, far_row = jnp.where(even, 16, 0), jnp.where(even, 0, 16)
@@ -511,7 +518,7 @@
                         else:
                             share[z, pl.ds(at, 8), :] = value
                             rest[z + 1, pl.ds(at, 8), :] = resist(value)
-                rest[z + 1, 24:32, :] = jnp.ones((8, 128), F32)
+                rest[z + 1, 24:32, :] = jnp.full((8, 128), 0.5, F32)
 
     loop(4, fill)
 
@@ -561,9 +568,9 @@
 
     source, target = iota((128, 128), 0), iota((128, 128), 1)
     pool = jnp.where(source // 2 + jnp.where(source >= 96, 64, 0) == target, 0.125, 0.0)
-    pooled[...] = dot(halves[...].reshape(4 * 8 * 24, 128), pool)
+    pooled[...] = dot_exact(halves[...].reshape(4 * 8 * 24, 128), pool)
     for z in (0, 9):
-        rest2[z] = jnp.ones((24, 128), F32)
+        rest2[z] = jnp.full((24, 128), 0.5, F32)
         for f in range(3):
             first2[f, z] = jnp.zeros((24, 128), F32)
             second2[f, z] = jnp.zeros((24, 128), F32)
@@ -688,11 +695,11 @@
 
     shares = {c: plane(3, *c) for c in cells}
     rests = {c: resist(shares[c]) for c in cells}
-    ones, zeros = jnp.ones((16, 128), F32), jnp.zeros((16, 128), F32)
+    outside, zeros = jnp.full((16, 128), 0.5, F32), jnp.zeros((16, 128), F32)
     for z, x, half in cells:
-        own, six = neighbours(lambda *c: rests[c], z, x, half, ones)
+        own, six = neighbours(lambda *c: rests[c], z, x, half, outside)
         masks = edge_masks(x, half)
-        six = [s if m is None else jnp.where(m, s, 1.0) for s, m in zip(six, masks)]
+        six = [s if m is None else jnp.where(m, s, 0.5) for s, m in zip(six, masks)]
         gain, w, diag = level_weights(own, six, 0.8)
         at = key(z, x, half)
         for i in range(6):
@@ -730,7 +737,7 @@
     source = iota((256, 128), 0)
     column = ((source % 128) // 16) * 16 + (source // 128) * 8 + (source % 16) // 2
     pool = jnp.where(column == iota((256, 128), 1), 0.125, 0.0)
-    level = dot(lefts[...].reshape(128, 256), pool)
+    level = dot_exact(lefts[...].reshape(128, 256), pool)
 
     def coarsest(ch, z):
         return level[(ch * 2 + z) * 16 : (ch * 2 + z) * 16 + 16, :]
@@ -741,7 +748,7 @@
     for z in range(2):
         own, other = resists[z], resists[1 - z]
         six = [roll(own, 1, 0), roll(own, -1, 0), roll(own, 1), roll(own, -1)]
-        six = [jnp.where(m, s, 1.0) for m, s in zip(masks, six)] + [other, ones]
+        six = [jnp.where(m, s, 0.5) for m, s in zip(masks, six)] + [other, outside]
         gain, w, diag = level_weights(own, six, 0.8)
         gains.append(gain)
         ds.append(diag)

time: 70.9 us -> 69.6 us (0.982)
  Pallas kernels: 25 us -> 23.9 us
where the time goes in v8:
time: 69.6 us; the launch traced here: 69.5 us
  blocking collectives  28.1 us (40%)
  Pallas kernels  23.9 us (34%)
  starting transfers between devices  15.5 us (22%)
  waiting for transfers between devices  1.88 us (3%)
    all_to_all x1, blocking collectives, local(): lax.all_to_all(sent, ('gx', 'gy'), split_axis=0, concat_axis=0, axis_inde...  28.1 us
    pallas_call x1, Pallas kernels, local(): call(own_kernel, [(3, 34, 32, 128)] * 2 + [(4, 16, 16, 128)] + [(4, 4, 16...  5 us
    pallas_call x1, Pallas kernels, local(): call(rows_edge_kernel, [(3, 34, 24, 128), (4, 8, 8, 128), (4, 16, 8, 128)...  4.96 us
    pallas_call x1, Pallas kernels, local(): call(top_kernel, [(3, 32, 16, 128)], [(4, 2, 128, 128), (3, 16, 16, 128),...  4.45 us
    pallas_call x1, Pallas kernels, local(): call(middle_kernel, [(CHIPS, 4, 128), (3, 16, 8, 128), (3, 8, 8, 128)], [...  3.26 us
    pallas_call x1, Pallas kernels, local(): call(rim_kernel, [(3, 16, 16, 128), (4, 4, 8, 128)], [(3, 18, 32, 128), (...  3.19 us
    ppermute x1, starting transfers between devices, local(): other = lax.ppermute(mine, 'gy', swap_near)  2.56 us
    ppermute x1, starting transfers between devices, local(): rim_near = lax.ppermute(rim_one, 'gx', swap_near)  2.56 us
  transfers between devices with their start and end apart: 9, of which 1 were waited for; matrix products, arithmetic and copies ran while one was open for 0% of the time, Pallas kernels for 21%

profile of v8, /device:TPU:1, one launch (start us, length us, event | category | flops | bytes accessed | tf_op | source)
XLA Modules:
  0.0 69.5 jit_solution(11686049125475375932)
XLA Ops:
  0.0 1.3 %shard_map.28 = (f32[12,32,128]{2,1,0:T(8,128)S(1)}, f32[12,32,128]{2,1,0:T(8,128)S(1)}, f32[4,32,16,128]{3,2,1,0:T(8,128)S(1)}) custom-call(f32[3,32,16,128]{3,2,1,0:T(8,128)} %guess.1, s32[32,16,128]{2,1,0:T(8,128)} %labels.1), custom_call_target="tpu_custom_call" | custom-call | flops 1000000 | bytes 4000000 | tf_op jit(solution)/shard_map/pallas_call | solution.py:812
  1.3 2.1 %collective-permute-start = (f32[12,32,128]{2,1,0:T(8,128)S(1)}, f32[12,32,128]{2,1,0:T(8,128)S(1)}, u32[]{:S(2)}, u32[]{:S(2)}) collective-permute-start(f32[12,32,128]{2,1,0:T(8,128)S(1)} %get-tuple-element.28), channel_id=1, source_target_pairs={{0,16},{16,0},{32,48},{48,32},{64,80},{80,64},{96,112},{112,96},{1... | collective-permute-start | bytes 589832 | tf_op jit(solution)/shard_map/ppermute | solution.py:818
  3.4 1.3 %collective-permute-start.1 = (f32[12,32,128]{2,1,0:T(8,128)S(1)}, f32[12,32,128]{2,1,0:T(8,128)S(1)}, u32[]{:S(2)}, u32[]{:S(2)}) collective-permute-start(f32[12,32,128]{2,1,0:T(8,128)S(1)} %get-tuple-element.29), channel_id=1, source_target_pairs={{0,1},{1,0},{2,3},{3,2},{4,5},{5,4},{6,7},{7,6},{8,9},{9,8},{10,11... | collective-permute-start | bytes 589832 | tf_op jit(solution)/shard_map/ppermute | solution.py:819
  4.7 5.0 %shard_map.29 = (f32[3,34,32,128]{3,2,1,0:T(8,128)S(1)}, f32[3,34,32,128]{3,2,1,0:T(8,128)S(1)}, f32[4,16,16,128]{3,2,1,0:T(8,128)S(1)}, f32[4,4,16,128]{3,2,1,0...) custom-call(f32[4,32,16,128]{3,2,1,0:T(8,128)S(1)} %get-tuple-element.25.own), custom_call_target="tpu_custom_call" | custom-call | flops 20000000 | bytes 4000000 | tf_op jit(solution)/shard_map/pallas_call | solution.py:820
  9.7 0.0 collective-permute-done.x_near
  9.7 0.0 collective-permute-done.1.x_far
  9.7 0.5 shard_map.30
  10.2 0.6 collective-permute-start.4
  10.8 1.2 %collective-permute-start.5 = (f32[4,4,24,128]{3,2,1,0:T(8,128)S(1)}, f32[4,4,24,128]{3,2,1,0:T(8,128)S(1)}, u32[]{:S(2)}, u32[]{:S(2)}) collective-permute-start(f32[4,4,24,128]{3,2,1,0:T(8,128)S(1)} %get-tuple-element.38), channel_id=1, source_target_pairs={{0,16},{1,2},{2,1},{3,4},{4,3},{5,6},{6,5},{7,8},{8,7},{9,10},{10,... | collective-permute-start | bytes 589832 | tf_op jit(solution)/shard_map/ppermute | solution.py:829
  12.0 5.0 %shard_map.31 = (f32[3,34,24,128]{3,2,1,0:T(8,128)S(1)}, f32[4,8,8,128]{3,2,1,0:T(8,128)S(1)}, f32[4,16,8,128]{3,2,1,0:T(8,128)S(1)}) custom-call(f32[4,32,16,128]{3,2,1,0:T(8,128)S(1)} %get-tuple-element.25.own, f32[4,32,8,128]{3,2,1,0:T(8,128)S(1)} %get-tuple-element.30.rim, f32[3,34,32,128]{3,2,1,0:T(8,128)S(1)} %get-tuple-element.31.own_one, ...), custom_call_target="tpu_custom_call" | custom-call | flops 10000000 | bytes 4000000 | tf_op jit(solution)/shard_map/pallas_call | solution.py:831
  16.9 1.1 %collective-permute-start.3 = (f32[4,8,8,128]{3,2,1,0:T(8,128)S(1)}, f32[4,8,8,128]{3,2,1,0:T(8,128)S(1)}, u32[]{:S(2)}, u32[]{:S(2)}) collective-permute-start(f32[4,8,8,128]{3,2,1,0:T(8,128)S(1)} %get-tuple-element.34.main), channel_id=1, source_target_pairs={{0,1},{1,0},{2,3},{3,2},{4,5},{5,4},{6,7},{7,6},{8,9},{9,8},{10,11... | collective-permute-start | bytes 393224 | tf_op jit(solution)/shard_map/ppermute | solution.py:839
  18.0 2.1 %collective-permute-start.2 = (f32[4,8,8,128]{3,2,1,0:T(8,128)S(1)}, f32[4,8,8,128]{3,2,1,0:T(8,128)S(1)}, u32[]{:S(2)}, u32[]{:S(2)}) collective-permute-start(f32[4,8,8,128]{3,2,1,0:T(8,128)S(1)} %get-tuple-element.34.main), channel_id=1, source_target_pairs={{0,16},{16,0},{32,48},{48,32},{64,80},{80,64},{96,112},{112,96},{1... | collective-permute-start | bytes 393224 | tf_op jit(solution)/shard_map/ppermute | solution.py:838
  20.1 0.0 collective-permute-done.4.near
  20.1 0.0 collective-permute-done.5.far
  20.1 3.2 %shard_map.32 = (f32[3,16,16,128]{3,2,1,0:T(8,128)S(1)}, f32[4,4,8,128]{3,2,1,0:T(8,128)S(1)}) custom-call(f32[4,16,16,128]{3,2,1,0:T(8,128)S(1)} %get-tuple-element.35.edges, f32[4,16,8,128]{3,2,1,0:T(8,128)S(1)} %get-tuple-element.36.edges_rim, f32[4,4,24,128]{3,2,1,0:T(8,128)S(1)} %collective-permute-done.4.near, ...), custom_call_target="tpu_custom_call" | custom-call | flops 10000000 | bytes 4000000 | tf_op jit(solution)/shard_map/pallas_call | solution.py:840
  23.3 2.1 %collective-permute-start.7 = (f32[4,4,8,128]{3,2,1,0:T(8,128)S(1)}, f32[4,4,8,128]{3,2,1,0:T(8,128)S(1)}, u32[]{:S(2)}, u32[]{:S(2)}) collective-permute-start(f32[4,4,8,128]{3,2,1,0:T(8,128)S(1)} %get-tuple-element.39.rim), channel_id=1, source_target_pairs={{0,1},{1,0},{2,3},{3,2},{4,5},{5,4},{6,7},{7,6},{8,9},{9,8},{10,11... | collective-permute-start | bytes 196616 | tf_op jit(solution)/shard_map/ppermute | solution.py:850
  25.3 2.6 %collective-permute-start.6 = (f32[4,4,8,128]{3,2,1,0:T(8,128)S(1)}, f32[4,4,8,128]{3,2,1,0:T(8,128)S(1)}, u32[]{:S(2)}, u32[]{:S(2)}) collective-permute-start(f32[4,4,8,128]{3,2,1,0:T(8,128)S(1)} %get-tuple-element.39.rim), channel_id=1, source_target_pairs={{0,16},{16,0},{32,48},{48,32},{64,80},{80,64},{96,112},{112,96},{1... | collective-permute-start | bytes 196616 | tf_op jit(solution)/shard_map/ppermute | solution.py:849
  27.9 0.0 collective-permute-done.3.main_far
  27.9 0.0 collective-permute-done.2.main_near
  27.9 0.0 collective-permute-done.7.rim_far
  27.9 1.9 %collective-permute-done.6.rim_near = f32[4,4,8,128]{3,2,1,0:T(8,128)S(1)} collective-permute-done((f32[4,4,8,128]{3,2,1,0:T(8,128)S(1)}, f32[4,4,8,128]{3,2,1,0:T(8,128)S(1)}, u32[]{:S(2)}, u32[]{:S(2)}) %collective-permute-start.6) | collective-permute-done | bytes 65568 | tf_op jit(solution)/shard_map/ppermute | solution.py:849
  29.8 3.3 %shard_map.33 = (f32[128,4,128]{2,1,0:T(4,128)S(1)}, f32[3,16,8,128]{3,2,1,0:T(8,128)S(1)}, f32[3,8,8,128]{3,2,1,0:T(8,128)S(1)}) custom-call(f32[4,8,8,128]{3,2,1,0:T(8,128)S(1)} %get-tuple-element.34.main, f32[4,8,8,128]{3,2,1,0:T(8,128)S(1)} %collective-permute-done.2.main_near, f32[4,8,8,128]{3,2,1,0:T(8,128)S(1)} %collective-permute-done.3.main_far, ...), custom_call_target="tpu_custom_call" | custom-call | flops 1000000 | bytes 4000000 | tf_op jit(solution)/shard_map/pallas_call | solution.py:851
  33.0 28.1 %all_to_all.5 = f32[128,4,128]{2,1,0:T(4,128)S(1)} all-to-all(f32[128,4,128]{2,1,0:T(4,128)S(1)} %get-tuple-element.40), channel_id=1, replica_groups={{0,2,4,6,8,10,12,14,16,18,20,22,24,26,28,30,32,34,36,38,40,42,44,46,48,..., dimensions={0} | all-to-all | bytes 524288 | tf_op jit(solution)/shard_map/all_to_all | solution.py:860
  61.1 2.6 %collective-permute-start.8 = (f32[128,4,128]{2,1,0:T(4,128)S(1)}, f32[128,4,128]{2,1,0:T(4,128)S(1)}, u32[]{:S(2)}, u32[]{:S(2)}) collective-permute-start(f32[128,4,128]{2,1,0:T(4,128)S(1)} %all_to_all.5), channel_id=1, source_target_pairs={{0,1},{1,0},{2,3},{3,2},{4,5},{5,4},{6,7},{7,6},{8,9},{9,8},{10,11... | collective-permute-start | bytes 786440 | tf_op jit(solution)/shard_map/ppermute | solution.py:864
  63.7 1.3 %shard_map.34.base = f32[3,32,16,128]{3,2,1,0:T(8,128)S(1)} custom-call(f32[3,34,24,128]{3,2,1,0:T(8,128)S(1)} %get-tuple-element.41.two, f32[3,16,16,128]{3,2,1,0:T(8,128)S(1)} %get-tuple-element.42.rim, f32[3,16,8,128]{3,2,1,0:T(8,128)S(1)} %get-tuple-element.43.e_one, f32[3,8,8,128]{3,2,1,0:T(8,128)S(1)} %get-tuple-element.44.e_two), custom_call_target="tpu_custom_call" | custom-call | flops 1000000 | bytes 4000000 | tf_op jit(solution)/shard_map/pallas_call | solution.py:863
  65.0 0.0 collective-permute-done.8
  65.0 4.5 %shard_map.35 = f32[3,32,16,128]{3,2,1,0:T(8,128)} custom-call(f32[512,128]{1,0:T(8,128)S(1)} %bitcast.2, f32[512,128]{1,0:T(8,128)S(1)} %bitcast.3, f32[3,32,16,128]{3,2,1,0:T(8,128)S(1)} %shard_map.34.base), custom_call_target="tpu_custom_call" | custom-call | flops 1000000 | bytes 4000000 | tf_op jit(solution)/shard_map/pallas_call | solution.py:865
Async XLA Ops:
  1.3 8.4 %collective-permute-start = (f32[12,32,128]{2,1,0:T(8,128)S(1)}, f32[12,32,128]{2,1,0:T(8,128)S(1)}, u32[]{:S(2)}, u32[]{:S(2)}) collective-permute-start(f32[12,32,128]{2,1,0:T(8,128)S(1)} %get-tuple-element.28), channel_id=1, source_target_pairs={{0,16},{16,0},{32,48},{48,32},{64,80},{80,64},{96,112},{112,96},{1... | collective-permute-start | bytes 589832 | tf_op jit(solution)/shard_map/ppermute | solution.py:818
  3.4 6.3 %collective-permute-start.1 = (f32[12,32,128]{2,1,0:T(8,128)S(1)}, f32[12,32,128]{2,1,0:T(8,128)S(1)}, u32[]{:S(2)}, u32[]{:S(2)}) collective-permute-start(f32[12,32,128]{2,1,0:T(8,128)S(1)} %get-tuple-element.29), channel_id=1, source_target_pairs={{0,1},{1,0},{2,3},{3,2},{4,5},{5,4},{6,7},{7,6},{8,9},{9,8},{10,11... | collective-permute-start | bytes 589832 | tf_op jit(solution)/shard_map/ppermute | solution.py:819
  10.2 9.9 %collective-permute-start.4 = (f32[4,4,24,128]{3,2,1,0:T(8,128)S(1)}, f32[4,4,24,128]{3,2,1,0:T(8,128)S(1)}, u32[]{:S(2)}, u32[]{:S(2)}) collective-permute-start(f32[4,4,24,128]{3,2,1,0:T(8,128)S(1)} %get-tuple-element.37), channel_id=1, source_target_pairs={{0,1},{1,0},{2,3},{3,2},{4,5},{5,4},{6,7},{7,6},{8,9},{9,8},{10,11... | collective-permute-start | bytes 589832 | tf_op jit(solution)/shard_map/ppermute | solution.py:830
  10.8 9.3 %collective-permute-start.5 = (f32[4,4,24,128]{3,2,1,0:T(8,128)S(1)}, f32[4,4,24,128]{3,2,1,0:T(8,128)S(1)}, u32[]{:S(2)}, u32[]{:S(2)}) collective-permute-start(f32[4,4,24,128]{3,2,1,0:T(8,128)S(1)} %get-tuple-element.38), channel_id=1, source_target_pairs={{0,16},{1,2},{2,1},{3,4},{4,3},{5,6},{6,5},{7,8},{8,7},{9,10},{10,... | collective-permute-start | bytes 589832 | tf_op jit(solution)/shard_map/ppermute | solution.py:829
  16.9 11.0 %collective-permute-start.3 = (f32[4,8,8,128]{3,2,1,0:T(8,128)S(1)}, f32[4,8,8,128]{3,2,1,0:T(8,128)S(1)}, u32[]{:S(2)}, u32[]{:S(2)}) collective-permute-start(f32[4,8,8,128]{3,2,1,0:T(8,128)S(1)} %get-tuple-element.34.main), channel_id=1, source_target_pairs={{0,1},{1,0},{2,3},{3,2},{4,5},{5,4},{6,7},{7,6},{8,9},{9,8},{10,11... | collective-permute-start | bytes 393224 | tf_op jit(solution)/shard_map/ppermute | solution.py:839
  18.0 9.9 %collective-permute-start.2 = (f32[4,8,8,128]{3,2,1,0:T(8,128)S(1)}, f32[4,8,8,128]{3,2,1,0:T(8,128)S(1)}, u32[]{:S(2)}, u32[]{:S(2)}) collective-permute-start(f32[4,8,8,128]{3,2,1,0:T(8,128)S(1)} %get-tuple-element.34.main), channel_id=1, source_target_pairs={{0,16},{16,0},{32,48},{48,32},{64,80},{80,64},{96,112},{112,96},{1... | collective-permute-start | bytes 393224 | tf_op jit(solution)/shard_map/ppermute | solution.py:838
  23.3 4.6 %collective-permute-start.7 = (f32[4,4,8,128]{3,2,1,0:T(8,128)S(1)}, f32[4,4,8,128]{3,2,1,0:T(8,128)S(1)}, u32[]{:S(2)}, u32[]{:S(2)}) collective-permute-start(f32[4,4,8,128]{3,2,1,0:T(8,128)S(1)} %get-tuple-element.39.rim), channel_id=1, source_target_pairs={{0,1},{1,0},{2,3},{3,2},{4,5},{5,4},{6,7},{7,6},{8,9},{9,8},{10,11... | collective-permute-start | bytes 196616 | tf_op jit(solution)/shard_map/ppermute | solution.py:850
  25.3 4.4 %collective-permute-start.6 = (f32[4,4,8,128]{3,2,1,0:T(8,128)S(1)}, f32[4,4,8,128]{3,2,1,0:T(8,128)S(1)}, u32[]{:S(2)}, u32[]{:S(2)}) collective-permute-start(f32[4,4,8,128]{3,2,1,0:T(8,128)S(1)} %get-tuple-element.39.rim), channel_id=1, source_target_pairs={{0,16},{16,0},{32,48},{48,32},{64,80},{80,64},{96,112},{112,96},{1... | collective-permute-start | bytes 196616 | tf_op jit(solution)/shard_map/ppermute | solution.py:849
  61.1 3.9 %collective-permute-start.8 = (f32[128,4,128]{2,1,0:T(4,128)S(1)}, f32[128,4,128]{2,1,0:T(4,128)S(1)}, u32[]{:S(2)}, u32[]{:S(2)}) collective-permute-start(f32[128,4,128]{2,1,0:T(4,128)S(1)} %all_to_all.5), channel_id=1, source_target_pairs={{0,1},{1,0},{2,3},{3,2},{4,5},{5,4},{6,7},{7,6},{8,9},{9,8},{10,11... | collective-permute-start | bytes 786440 | tf_op jit(solution)/shard_map/ppermute | solution.py:864

commit v9 on v8

--- a/solution.py
+++ b/solution.py
@@ -8,6 +8,7 @@
 
 F32 = jnp.float32
 NX, NY, CHIPS = 16, 16, 128
+STEP, WIDE = 8, 16
 BETWEEN = 2.0 * 0.1 / 1.1
 ANY = pl.BlockSpec(memory_space=pltpu.HBM)
 
@@ -113,7 +114,7 @@
                 near[ch, low, at, :] = jnp.where(first_core, right, left)
                 far[ch, low, at, :] = jnp.where(first_core, left, right)
 
-    loop(4, some)
+    loop(4, some, 4)
 
 
 def pack_planes(plane, low, shape):
@@ -188,49 +189,49 @@
     first, count = windows[0]
 
     def first_sweep(step):
-        z = 4 * step
+        z = STEP * step
         w = []
-        for k, (own, six) in enumerate(block_of(share, (), z + 1, 4, first, count)):
+        for k, (own, six) in enumerate(block_of(share, (), z + 1, STEP, first, count)):
             now, diag = fine_weights(own, six, omega)
             diags[z + k, pl.ds(first, count), :] = diag
             for i in range(6):
                 weights[i, z + k, pl.ds(first, count), :] = now[i]
             w.append(now)
         for f in range(3):
-            for k, (own, six) in enumerate(block_of(start, (f,), z + 1, 4, first, count)):
+            for k, (own, six) in enumerate(block_of(start, (f,), z + 1, STEP, first, count)):
                 one[f, z + k + 1, pl.ds(first, count), :] = fine_sweep(w[k], f, own, six)
 
-    loop(planes // 4, first_sweep)
+    loop(planes // STEP, first_sweep)
     wrap(one)
     second, count2 = windows[1]
 
     def second_sweep(step):
-        z = 4 * step
-        w = [[weights[i, z + k, pl.ds(second, count2), :] for i in range(6)] for k in range(4)]
-        for f in range(3):
-            for k, (own, six) in enumerate(block_of(one, (f,), z + 1, 4, second, count2)):
+        z = STEP * step
+        w = [[weights[i, z + k, pl.ds(second, count2), :] for i in range(6)] for k in range(STEP)]
+        for f in range(3):
+            for k, (own, six) in enumerate(block_of(one, (f,), z + 1, STEP, second, count2)):
                 two[f, z + k + 1, pl.ds(second, count2), :] = fine_sweep(w[k], f, own, six)
 
-    loop(planes // 4, second_sweep)
+    loop(planes // STEP, second_sweep)
     wrap(two)
 
     def residual(step):
-        z = 4 * step
-        w = [[weights[i, z + k, 8:24, :] for i in range(6)] for k in range(4)]
-        diag = [diags[z + k, 8:24, :] for k in range(4)]
+        z = STEP * step
+        w = [[weights[i, z + k, 8:24, :] for i in range(6)] for k in range(STEP)]
+        diag = [diags[z + k, 8:24, :] for k in range(STEP)]
         for f in range(3):
             values = []
-            for k, (own, six) in enumerate(block_of(two, (f,), z + 1, 4, 8, 16)):
+            for k, (own, six) in enumerate(block_of(two, (f,), z + 1, STEP, 8, 16)):
                 if keep is not None:
                     keep[f, z + k] = own
                 values.append(fine_left(w[k], f, own, six, diag[k]))
-            for pair in range(2):
-                halves[f, 2 * step + pair] = values[2 * pair] + values[2 * pair + 1]
-        for pair in range(2):
+            for pair in range(STEP // 2):
+                halves[f, STEP // 2 * step + pair] = values[2 * pair] + values[2 * pair + 1]
+        for pair in range(STEP // 2):
             at = z + 2 * pair + 1
-            halves[3, 2 * step + pair] = share[at, 8:24, :] + share[at + 1, 8:24, :]
-
-    loop(planes // 4, residual)
+            halves[3, STEP // 2 * step + pair] = share[at, 8:24, :] + share[at + 1, 8:24, :]
+
+    loop(planes // STEP, residual)
 
 
 def own_kernel(own, one, two, halves, to_right, to_left, edges, held, weights, diags):
@@ -246,7 +247,7 @@
         for ch in range(4):
             held[ch, z + 1, 8:24, :] = own[ch, z]
 
-    loop(32, plane, 4)
+    loop(32, plane, 8)
     fine_sweeps(
         32, [(8, 16)] * 2, held, held.at[3], one, two, weights, diags, halves, 0.8, lambda ref: None, None
     )
@@ -255,13 +256,13 @@
         for ch in range(4):
             to_right[ch, low], to_left[ch, low] = pack_planes(lambda z: own[ch, z], low, (16, 128))
 
-    loop(4, some)
+    loop(4, some, 2)
 
     def edge(z):
         for ch in range(4):
             edges[ch, z] = edge_columns(lambda at: own[ch, at], z, (16, 128))
 
-    loop(16, edge, 2)
+    loop(16, edge, 8)
 
 
 def rows_edge_kernel(own, rim, own_one, own_two, own_halves, two, packed, edges, start, one, weights, diags, halves, pooled):
@@ -284,7 +285,7 @@
                 ref[f, z + 1, 0:8, :] = source[f, z + 1, 16:24, :]
                 ref[f, z + 1, 16:24, :] = source[f, z + 1, 8:16, :]
 
-    loop(32, fill, 4)
+    loop(32, fill, 8)
     upper = iota((8, 128), 0) < 4
 
     def both(ref, lead, step, shift=0):
@@ -293,9 +294,9 @@
         return jnp.where(upper, high, low)
 
     def block_both(ref, f, z, step):
-        own = [both(ref, (f, z + k), step) for k in range(-1, 5)]
+        own = [both(ref, (f, z + k), step) for k in range(-1, WIDE + 1)]
         result = []
-        for k in range(4):
+        for k in range(WIDE):
             value = own[k + 1]
             low, high = both(ref, (f, z + k), step, -1), both(ref, (f, z + k), step, 1)
             result.append((value, (low, high, roll(value, 1), roll(value, -1), own[k], own[k + 2])))
@@ -311,45 +312,45 @@
     omega = 0.8 * inside.astype(F32)
 
     def weigh_all(step):
-        z = 4 * step
-        for k, (value, six) in enumerate(block_of(start, (3,), z + 1, 4, 5, 16)):
+        z = WIDE * step
+        for k, (value, six) in enumerate(block_of(start, (3,), z + 1, WIDE, 5, 16)):
             w, diag = fine_weights(value, six, omega)
             diags[z + k, 5:21, :] = diag
             for i in range(6):
                 weights[i, z + k, 5:21, :] = w[i]
 
-    loop(8, weigh_all)
+    loop(32 // WIDE, weigh_all)
 
     for step, source, target in ((1, start, one), (2, one, two)):
 
         def sweep(block):
-            z = 4 * block
-            w = [[both(weights, (i, z + k), step) for i in range(6)] for k in range(4)]
+            z = WIDE * block
+            w = [[both(weights, (i, z + k), step) for i in range(6)] for k in range(WIDE)]
             for f in range(3):
                 for k, (value, six) in enumerate(block_both(source, f, z + 1, step)):
                     put(target, f, z + k + 1, step, fine_sweep(w[k], f, value, six))
 
-        loop(8, sweep)
+        loop(32 // WIDE, sweep)
 
     sub = iota((8, 128), 0)
 
     def residual(block):
-        z = 4 * block
-        w = [[both(weights, (i, z + k), 3) for i in range(6)] for k in range(4)]
-        diag = [both(diags, (z + k,), 3) for k in range(4)]
+        z = WIDE * block
+        w = [[both(weights, (i, z + k), 3) for i in range(6)] for k in range(WIDE)]
+        diag = [both(diags, (z + k,), 3) for k in range(WIDE)]
         for f in range(3):
             values = []
             for k, (value, six) in enumerate(block_both(two, f, z + 1, 3)):
                 values.append(fine_left(w[k], f, value, six, diag[k]))
-            for k in range(2):
-                pair = 2 * block + k
+            for k in range(WIDE // 2):
+                pair = WIDE // 2 * block + k
                 value = values[2 * k] + values[2 * k + 1]
                 halves[f, pair, 0:8, :] = jnp.where(sub < 3, roll(value, 3, 0), own_halves[f, pair, 0:8, :])
                 halves[f, pair, 8:16, :] = jnp.where(sub >= 5, roll(value, 5, 0), own_halves[f, pair, 8:16, :])
-        for k in range(2):
-            halves[3, 2 * block + k] = own_halves[3, 2 * block + k]
-
-    loop(8, residual)
+        for k in range(WIDE // 2):
+            halves[3, WIDE // 2 * block + k] = own_halves[3, WIDE // 2 * block + k]
+
+    loop(32 // WIDE, residual)
     source, target = iota((128, 128), 0), iota((128, 128), 1)
     value = None
     for half in range(2):
@@ -363,7 +364,7 @@
         for ch in range(4):
             edges[ch, z] = edge_columns(lambda at: rim[ch, at], z, (8, 128))
 
-    loop(16, edge, 2)
+    loop(16, edge, 8)
 
 
 def rim_kernel(
@@ -393,7 +394,7 @@
                 target[z + 1, 0:8, :] = value[16:24]
                 target[z + 1, 24:32, :] = value[16:24]
 
-    loop(4, unpack)
+    loop(4, unpack, 2)
 
     half_of = iota((32, 128), 1)
 
@@ -463,7 +464,7 @@
                     own = jnp.where(lane < 3, low, jnp.where(lane >= 125, high, own))
                     base[f, at] = own + spread[f, k + 8 * half]
 
-    loop(8, pair, 1)
+    loop(8, pair, 4)
 
 
 def resist(share):
@@ -528,8 +529,8 @@
     omega = 0.8 * (in_x * in_y).astype(F32)
 
     def start(step):
-        z = 4 * step
-        for k, (own, six) in enumerate(block_of(rest, (), z + 1, 4, 1, 24)):
+        z = STEP * step
+        for k, (own, six) in enumerate(block_of(rest, (), z + 1, STEP, 1, 24)):
             gain, w, diag = level_weights(own, six, omega)
             for i in range(6):
                 weights[i, z + k, 1:25, :] = w[i]
@@ -537,34 +538,34 @@
             for f in range(3):
                 first[f, z + k + 1, 1:25, :] = (4.0 * gain) * rhs[f, z + k, 1:25, :]
 
-    loop(4, start)
+    loop(16 // STEP, start)
 
     def sweep(step):
-        z = 4 * step
-        w = [[weights[i, z + k, 3:27, :] for i in range(6)] for k in range(4)]
-        for f in range(3):
-            for k, (own, six) in enumerate(block_of(first, (f,), z + 1, 4, 3, 24)):
+        z = STEP * step
+        w = [[weights[i, z + k, 3:27, :] for i in range(6)] for k in range(STEP)]
+        for f in range(3):
+            for k, (own, six) in enumerate(block_of(first, (f,), z + 1, STEP, 3, 24)):
                 second[f, z + k + 1, 3:27, :] = 1.2 * own + weigh(w[k], six)
 
-    loop(4, sweep)
+    loop(16 // STEP, sweep)
 
     def left(step):
-        z = 4 * step
-        w = [[weights[i, z + k, 4:20, :] for i in range(6)] for k in range(4)]
-        diag = [diags[z + k, 4:20, :] for k in range(4)]
+        z = STEP * step
+        w = [[weights[i, z + k, 4:20, :] for i in range(6)] for k in range(STEP)]
+        diag = [diags[z + k, 4:20, :] for k in range(STEP)]
         for f in range(3):
             values = []
-            for k, (own, six) in enumerate(block_of(second, (f,), z + 1, 4, 4, 16)):
+            for k, (own, six) in enumerate(block_of(second, (f,), z + 1, STEP, 4, 16)):
                 change = (first[f, z + k + 1, 4:20, :] - 0.8 * own) + weigh(w[k], six)
                 values.append(change * diag[k])
                 e_one[f, z + k] = second[f, z + k + 1, 8:16, :]
-            for k in range(2):
-                halves[f, 2 * step + k, 0:16, :] = values[2 * k] + values[2 * k + 1]
-                halves[f, 2 * step + k, 16:24, :] = jnp.zeros((8, 128), F32)
-        for k in range(2):
-            halves[3, 2 * step + k] = share[z + 2 * k] + share[z + 2 * k + 1]
-
-    loop(4, left)
+            for k in range(STEP // 2):
+                halves[f, STEP // 2 * step + k, 0:16, :] = values[2 * k] + values[2 * k + 1]
+                halves[f, STEP // 2 * step + k, 16:24, :] = jnp.zeros((8, 128), F32)
+        for k in range(STEP // 2):
+            halves[3, STEP // 2 * step + k] = share[z + 2 * k] + share[z + 2 * k + 1]
+
+    loop(16 // STEP, left)
 
     source, target = iota((128, 128), 0), iota((128, 128), 1)
     pool = jnp.where(source // 2 + jnp.where(source >= 96, 64, 0) == target, 0.125, 0.0)

time: 69.6 us -> 65.7 us (0.944)
  Pallas kernels: 23.9 us -> 19 us
  starting transfers between devices: 15.5 us -> 17.6 us
  blocking collectives: 28.1 us -> 26.8 us
    pallas_call x1, Pallas kernels: 4.96 us -> 2.89 us  [local(): call(rows_edge_kernel, [(3, 34, 24, 128), (4, 8, 8, 128), (4, 16, 8, 128)...]
    ppermute x1, starting transfers between devices: 0.62 us -> 1.96 us  [local(): from_near = lax.ppermute(to_near, 'gy', swap_near)]
    pallas_call x1, Pallas kernels: 5 us -> 3.66 us  [local(): call(own_kernel, [(3, 34, 32, 128)] * 2 + [(4, 16, 16, 128)] + [(4, 4, 16...]
    all_to_all x1, blocking collectives: 28.1 us -> 26.8 us  [local(): lax.all_to_all(sent, ('gx', 'gy'), split_axis=0, concat_axis=0, axis_inde...]
    ppermute x1, starting transfers between devices: 2.56 us -> 3.3 us  [local(): other = lax.ppermute(mine, 'gy', swap_near)]
  transfers between devices with their start and end apart: 9 -> 9, of which waited for: 1 -> 2; matrix products, arithmetic and copies ran while one was open for 0% -> 0% of each run, Pallas kernels for 21% -> 15%
where the time goes in v9:
time: 65.7 us; the launch traced here: 65.6 us
  blocking collectives  26.8 us (41%)
  Pallas kernels  19 us (29%)
  starting transfers between devices  17.6 us (27%)
  waiting for transfers between devices  2.13 us (3%)
    all_to_all x1, blocking collectives, local(): lax.all_to_all(sent, ('gx', 'gy'), split_axis=0, concat_axis=0, axis_inde...  26.8 us
    pallas_call x1, Pallas kernels, local(): call(top_kernel, [(3, 32, 16, 128)], [(4, 2, 128, 128), (3, 16, 16, 128),...  4.44 us
    pallas_call x1, Pallas kernels, local(): call(own_kernel, [(3, 34, 32, 128)] * 2 + [(4, 16, 16, 128)] + [(4, 4, 16...  3.66 us
    ppermute x1, starting transfers between devices, local(): other = lax.ppermute(mine, 'gy', swap_near)  3.3 us
    pallas_call x1, Pallas kernels, local(): call(rows_edge_kernel, [(3, 34, 24, 128), (4, 8, 8, 128), (4, 16, 8, 128)...  2.89 us
    pallas_call x1, Pallas kernels, local(): call(middle_kernel, [(CHIPS, 4, 128), (3, 16, 8, 128), (3, 8, 8, 128)], [...  2.89 us
    pallas_call x1, Pallas kernels, local(): call(rim_kernel, [(3, 16, 16, 128), (4, 4, 8, 128)], [(3, 18, 32, 128), (...  2.68 us
    ppermute x1, starting transfers between devices, local(): rim_near = lax.ppermute(rim_one, 'gx', swap_near)  2.55 us
  transfers between devices with their start and end apart: 9, of which 2 were waited for; matrix products, arithmetic and copies ran while one was open for 0% of the time, Pallas kernels for 15%

profile of v9, /device:TPU:1, one launch (start us, length us, event | category | flops | bytes accessed | tf_op | source)
XLA Modules:
  0.0 65.6 jit_solution(10529357745661474346)
XLA Ops:
  0.0 1.3 %shard_map.28 = (f32[12,32,128]{2,1,0:T(8,128)S(1)}, f32[12,32,128]{2,1,0:T(8,128)S(1)}, f32[4,32,16,128]{3,2,1,0:T(8,128)S(1)}) custom-call(f32[3,32,16,128]{3,2,1,0:T(8,128)} %guess.1, s32[32,16,128]{2,1,0:T(8,128)} %labels.1), custom_call_target="tpu_custom_call" | custom-call | flops 1000000 | bytes 4000000 | tf_op jit(solution)/shard_map/pallas_call | solution.py:813
  1.3 2.1 %collective-permute-start = (f32[12,32,128]{2,1,0:T(8,128)S(1)}, f32[12,32,128]{2,1,0:T(8,128)S(1)}, u32[]{:S(2)}, u32[]{:S(2)}) collective-permute-start(f32[12,32,128]{2,1,0:T(8,128)S(1)} %get-tuple-element.28), channel_id=1, source_target_pairs={{0,16},{16,0},{32,48},{48,32},{64,80},{80,64},{96,112},{112,96},{1... | collective-permute-start | bytes 589832 | tf_op jit(solution)/shard_map/ppermute | solution.py:819
  3.4 1.3 %collective-permute-start.1 = (f32[12,32,128]{2,1,0:T(8,128)S(1)}, f32[12,32,128]{2,1,0:T(8,128)S(1)}, u32[]{:S(2)}, u32[]{:S(2)}) collective-permute-start(f32[12,32,128]{2,1,0:T(8,128)S(1)} %get-tuple-element.29), channel_id=1, source_target_pairs={{0,1},{1,0},{2,3},{3,2},{4,5},{5,4},{6,7},{7,6},{8,9},{9,8},{10,11... | collective-permute-start | bytes 589832 | tf_op jit(solution)/shard_map/ppermute | solution.py:820
  4.7 3.7 %shard_map.29 = (f32[3,34,32,128]{3,2,1,0:T(8,128)S(1)}, f32[3,34,32,128]{3,2,1,0:T(8,128)S(1)}, f32[4,16,16,128]{3,2,1,0:T(8,128)S(1)}, f32[4,4,16,128]{3,2,1,0...) custom-call(f32[4,32,16,128]{3,2,1,0:T(8,128)S(1)} %get-tuple-element.25.own), custom_call_target="tpu_custom_call" | custom-call | flops 20000000 | bytes 4000000 | tf_op jit(solution)/shard_map/pallas_call | solution.py:821
  8.4 0.0 collective-permute-done.x_near
  8.4 0.0 collective-permute-done.1.x_far
  8.4 0.3 shard_map.30
  8.7 2.0 %collective-permute-start.4 = (f32[4,4,24,128]{3,2,1,0:T(8,128)S(1)}, f32[4,4,24,128]{3,2,1,0:T(8,128)S(1)}, u32[]{:S(2)}, u32[]{:S(2)}) collective-permute-start(f32[4,4,24,128]{3,2,1,0:T(8,128)S(1)} %get-tuple-element.37), channel_id=1, source_target_pairs={{0,1},{1,0},{2,3},{3,2},{4,5},{5,4},{6,7},{7,6},{8,9},{9,8},{10,11... | collective-permute-start | bytes 589832 | tf_op jit(solution)/shard_map/ppermute | solution.py:831
  10.7 0.9 %collective-permute-start.5 = (f32[4,4,24,128]{3,2,1,0:T(8,128)S(1)}, f32[4,4,24,128]{3,2,1,0:T(8,128)S(1)}, u32[]{:S(2)}, u32[]{:S(2)}) collective-permute-start(f32[4,4,24,128]{3,2,1,0:T(8,128)S(1)} %get-tuple-element.38), channel_id=1, source_target_pairs={{0,16},{1,2},{2,1},{3,4},{4,3},{5,6},{6,5},{7,8},{8,7},{9,10},{10,... | collective-permute-start | bytes 589832 | tf_op jit(solution)/shard_map/ppermute | solution.py:830
  11.5 2.9 %shard_map.31 = (f32[3,34,24,128]{3,2,1,0:T(8,128)S(1)}, f32[4,8,8,128]{3,2,1,0:T(8,128)S(1)}, f32[4,16,8,128]{3,2,1,0:T(8,128)S(1)}) custom-call(f32[4,32,16,128]{3,2,1,0:T(8,128)S(1)} %get-tuple-element.25.own, f32[4,32,8,128]{3,2,1,0:T(8,128)S(1)} %get-tuple-element.30.rim, f32[3,34,32,128]{3,2,1,0:T(8,128)S(1)} %get-tuple-element.31.own_one, ...), custom_call_target="tpu_custom_call" | custom-call | flops 10000000 | bytes 4000000 | tf_op jit(solution)/shard_map/pallas_call | solution.py:832
  14.4 1.4 %collective-permute-start.3 = (f32[4,8,8,128]{3,2,1,0:T(8,128)S(1)}, f32[4,8,8,128]{3,2,1,0:T(8,128)S(1)}, u32[]{:S(2)}, u32[]{:S(2)}) collective-permute-start(f32[4,8,8,128]{3,2,1,0:T(8,128)S(1)} %get-tuple-element.34.main), channel_id=1, source_target_pairs={{0,1},{1,0},{2,3},{3,2},{4,5},{5,4},{6,7},{7,6},{8,9},{9,8},{10,11... | collective-permute-start | bytes 393224 | tf_op jit(solution)/shard_map/ppermute | solution.py:840
  15.8 2.1 %collective-permute-start.2 = (f32[4,8,8,128]{3,2,1,0:T(8,128)S(1)}, f32[4,8,8,128]{3,2,1,0:T(8,128)S(1)}, u32[]{:S(2)}, u32[]{:S(2)}) collective-permute-start(f32[4,8,8,128]{3,2,1,0:T(8,128)S(1)} %get-tuple-element.34.main), channel_id=1, source_target_pairs={{0,16},{16,0},{32,48},{48,32},{64,80},{80,64},{96,112},{112,96},{1... | collective-permute-start | bytes 393224 | tf_op jit(solution)/shard_map/ppermute | solution.py:839
  17.8 0.0 collective-permute-done.4.near
  17.8 0.0 collective-permute-done.5.far
  17.8 2.7 %shard_map.32 = (f32[3,16,16,128]{3,2,1,0:T(8,128)S(1)}, f32[4,4,8,128]{3,2,1,0:T(8,128)S(1)}) custom-call(f32[4,16,16,128]{3,2,1,0:T(8,128)S(1)} %get-tuple-element.35.edges, f32[4,16,8,128]{3,2,1,0:T(8,128)S(1)} %get-tuple-element.36.edges_rim, f32[4,4,24,128]{3,2,1,0:T(8,128)S(1)} %collective-permute-done.4.near, ...), custom_call_target="tpu_custom_call" | custom-call | flops 10000000 | bytes 4000000 | tf_op jit(solution)/shard_map/pallas_call | solution.py:841
  20.5 2.1 %collective-permute-start.7 = (f32[4,4,8,128]{3,2,1,0:T(8,128)S(1)}, f32[4,4,8,128]{3,2,1,0:T(8,128)S(1)}, u32[]{:S(2)}, u32[]{:S(2)}) collective-permute-start(f32[4,4,8,128]{3,2,1,0:T(8,128)S(1)} %get-tuple-element.39.rim), channel_id=1, source_target_pairs={{0,1},{1,0},{2,3},{3,2},{4,5},{5,4},{6,7},{7,6},{8,9},{9,8},{10,11... | collective-permute-start | bytes 196616 | tf_op jit(solution)/shard_map/ppermute | solution.py:851
  22.6 2.6 %collective-permute-start.6 = (f32[4,4,8,128]{3,2,1,0:T(8,128)S(1)}, f32[4,4,8,128]{3,2,1,0:T(8,128)S(1)}, u32[]{:S(2)}, u32[]{:S(2)}) collective-permute-start(f32[4,4,8,128]{3,2,1,0:T(8,128)S(1)} %get-tuple-element.39.rim), channel_id=1, source_target_pairs={{0,16},{16,0},{32,48},{48,32},{64,80},{80,64},{96,112},{112,96},{1... | collective-permute-start | bytes 196616 | tf_op jit(solution)/shard_map/ppermute | solution.py:850
  25.2 0.0 collective-permute-done.3.main_far
  25.2 0.0 collective-permute-done.2.main_near
  25.2 0.0 collective-permute-done.7.rim_far
  25.2 1.9 %collective-permute-done.6.rim_near = f32[4,4,8,128]{3,2,1,0:T(8,128)S(1)} collective-permute-done((f32[4,4,8,128]{3,2,1,0:T(8,128)S(1)}, f32[4,4,8,128]{3,2,1,0:T(8,128)S(1)}, u32[]{:S(2)}, u32[]{:S(2)}) %collective-permute-start.6) | collective-permute-done | bytes 65568 | tf_op jit(solution)/shard_map/ppermute | solution.py:850
  27.0 2.9 %shard_map.33 = (f32[128,4,128]{2,1,0:T(4,128)S(1)}, f32[3,16,8,128]{3,2,1,0:T(8,128)S(1)}, f32[3,8,8,128]{3,2,1,0:T(8,128)S(1)}) custom-call(f32[4,8,8,128]{3,2,1,0:T(8,128)S(1)} %get-tuple-element.34.main, f32[4,8,8,128]{3,2,1,0:T(8,128)S(1)} %collective-permute-done.2.main_near, f32[4,8,8,128]{3,2,1,0:T(8,128)S(1)} %collective-permute-done.3.main_far, ...), custom_call_target="tpu_custom_call" | custom-call | flops 1000000 | bytes 4000000 | tf_op jit(solution)/shard_map/pallas_call | solution.py:852
  29.9 26.8 %all_to_all.5 = f32[128,4,128]{2,1,0:T(4,128)S(1)} all-to-all(f32[128,4,128]{2,1,0:T(4,128)S(1)} %get-tuple-element.40), channel_id=1, replica_groups={{0,2,4,6,8,10,12,14,16,18,20,22,24,26,28,30,32,34,36,38,40,42,44,46,48,..., dimensions={0} | all-to-all | bytes 524288 | tf_op jit(solution)/shard_map/all_to_all | solution.py:861
  56.7 3.3 %collective-permute-start.8 = (f32[128,4,128]{2,1,0:T(4,128)S(1)}, f32[128,4,128]{2,1,0:T(4,128)S(1)}, u32[]{:S(2)}, u32[]{:S(2)}) collective-permute-start(f32[128,4,128]{2,1,0:T(4,128)S(1)} %all_to_all.5), channel_id=1, source_target_pairs={{0,1},{1,0},{2,3},{3,2},{4,5},{5,4},{6,7},{7,6},{8,9},{9,8},{10,11... | collective-permute-start | bytes 786440 | tf_op jit(solution)/shard_map/ppermute | solution.py:865
  60.0 0.9 %shard_map.34.base = f32[3,32,16,128]{3,2,1,0:T(8,128)S(1)} custom-call(f32[3,34,24,128]{3,2,1,0:T(8,128)S(1)} %get-tuple-element.41.two, f32[3,16,16,128]{3,2,1,0:T(8,128)S(1)} %get-tuple-element.42.rim, f32[3,16,8,128]{3,2,1,0:T(8,128)S(1)} %get-tuple-element.43.e_one, f32[3,8,8,128]{3,2,1,0:T(8,128)S(1)} %get-tuple-element.44.e_two), custom_call_target="tpu_custom_call" | custom-call | flops 1000000 | bytes 4000000 | tf_op jit(solution)/shard_map/pallas_call | solution.py:864
  60.9 0.3 collective-permute-done.8
  61.2 4.4 %shard_map.35 = f32[3,32,16,128]{3,2,1,0:T(8,128)} custom-call(f32[512,128]{1,0:T(8,128)S(1)} %bitcast.2, f32[512,128]{1,0:T(8,128)S(1)} %bitcast.3, f32[3,32,16,128]{3,2,1,0:T(8,128)S(1)} %shard_map.34.base), custom_call_target="tpu_custom_call" | custom-call | flops 1000000 | bytes 4000000 | tf_op jit(solution)/shard_map/pallas_call | solution.py:866
Async XLA Ops:
  1.3 7.1 %collective-permute-start = (f32[12,32,128]{2,1,0:T(8,128)S(1)}, f32[12,32,128]{2,1,0:T(8,128)S(1)}, u32[]{:S(2)}, u32[]{:S(2)}) collective-permute-start(f32[12,32,128]{2,1,0:T(8,128)S(1)} %get-tuple-element.28), channel_id=1, source_target_pairs={{0,16},{16,0},{32,48},{48,32},{64,80},{80,64},{96,112},{112,96},{1... | collective-permute-start | bytes 589832 | tf_op jit(solution)/shard_map/ppermute | solution.py:819
  3.4 5.0 %collective-permute-start.1 = (f32[12,32,128]{2,1,0:T(8,128)S(1)}, f32[12,32,128]{2,1,0:T(8,128)S(1)}, u32[]{:S(2)}, u32[]{:S(2)}) collective-permute-start(f32[12,32,128]{2,1,0:T(8,128)S(1)} %get-tuple-element.29), channel_id=1, source_target_pairs={{0,1},{1,0},{2,3},{3,2},{4,5},{5,4},{6,7},{7,6},{8,9},{9,8},{10,11... | collective-permute-start | bytes 589832 | tf_op jit(solution)/shard_map/ppermute | solution.py:820
  8.7 9.1 %collective-permute-start.4 = (f32[4,4,24,128]{3,2,1,0:T(8,128)S(1)}, f32[4,4,24,128]{3,2,1,0:T(8,128)S(1)}, u32[]{:S(2)}, u32[]{:S(2)}) collective-permute-start(f32[4,4,24,128]{3,2,1,0:T(8,128)S(1)} %get-tuple-element.37), channel_id=1, source_target_pairs={{0,1},{1,0},{2,3},{3,2},{4,5},{5,4},{6,7},{7,6},{8,9},{9,8},{10,11... | collective-permute-start | bytes 589832 | tf_op jit(solution)/shard_map/ppermute | solution.py:831
  10.7 7.2 %collective-permute-start.5 = (f32[4,4,24,128]{3,2,1,0:T(8,128)S(1)}, f32[4,4,24,128]{3,2,1,0:T(8,128)S(1)}, u32[]{:S(2)}, u32[]{:S(2)}) collective-permute-start(f32[4,4,24,128]{3,2,1,0:T(8,128)S(1)} %get-tuple-element.38), channel_id=1, source_target_pairs={{0,16},{1,2},{2,1},{3,4},{4,3},{5,6},{6,5},{7,8},{8,7},{9,10},{10,... | collective-permute-start | bytes 589832 | tf_op jit(solution)/shard_map/ppermute | solution.py:830
  14.4 10.7 %collective-permute-start.3 = (f32[4,8,8,128]{3,2,1,0:T(8,128)S(1)}, f32[4,8,8,128]{3,2,1,0:T(8,128)S(1)}, u32[]{:S(2)}, u32[]{:S(2)}) collective-permute-start(f32[4,8,8,128]{3,2,1,0:T(8,128)S(1)} %get-tuple-element.34.main), channel_id=1, source_target_pairs={{0,1},{1,0},{2,3},{3,2},{4,5},{5,4},{6,7},{7,6},{8,9},{9,8},{10,11... | collective-permute-start | bytes 393224 | tf_op jit(solution)/shard_map/ppermute | solution.py:840
  15.8 9.4 %collective-permute-start.2 = (f32[4,8,8,128]{3,2,1,0:T(8,128)S(1)}, f32[4,8,8,128]{3,2,1,0:T(8,128)S(1)}, u32[]{:S(2)}, u32[]{:S(2)}) collective-permute-start(f32[4,8,8,128]{3,2,1,0:T(8,128)S(1)} %get-tuple-element.34.main), channel_id=1, source_target_pairs={{0,16},{16,0},{32,48},{48,32},{64,80},{80,64},{96,112},{112,96},{1... | collective-permute-start | bytes 393224 | tf_op jit(solution)/shard_map/ppermute | solution.py:839
  20.5 4.6 %collective-permute-start.7 = (f32[4,4,8,128]{3,2,1,0:T(8,128)S(1)}, f32[4,4,8,128]{3,2,1,0:T(8,128)S(1)}, u32[]{:S(2)}, u32[]{:S(2)}) collective-permute-start(f32[4,4,8,128]{3,2,1,0:T(8,128)S(1)} %get-tuple-element.39.rim), channel_id=1, source_target_pairs={{0,1},{1,0},{2,3},{3,2},{4,5},{5,4},{6,7},{7,6},{8,9},{9,8},{10,11... | collective-permute-start | bytes 196616 | tf_op jit(solution)/shard_map/ppermute | solution.py:851
  22.6 4.4 %collective-permute-start.6 = (f32[4,4,8,128]{3,2,1,0:T(8,128)S(1)}, f32[4,4,8,128]{3,2,1,0:T(8,128)S(1)}, u32[]{:S(2)}, u32[]{:S(2)}) collective-permute-start(f32[4,4,8,128]{3,2,1,0:T(8,128)S(1)} %get-tuple-element.39.rim), channel_id=1, source_target_pairs={{0,16},{16,0},{32,48},{48,32},{64,80},{80,64},{96,112},{112,96},{1... | collective-permute-start | bytes 196616 | tf_op jit(solution)/shard_map/ppermute | solution.py:850
  56.7 4.5 %collective-permute-start.8 = (f32[128,4,128]{2,1,0:T(4,128)S(1)}, f32[128,4,128]{2,1,0:T(4,128)S(1)}, u32[]{:S(2)}, u32[]{:S(2)}) collective-permute-start(f32[128,4,128]{2,1,0:T(4,128)S(1)} %all_to_all.5), channel_id=1, source_target_pairs={{0,1},{1,0},{2,3},{3,2},{4,5},{5,4},{6,7},{7,6},{8,9},{9,8},{10,11... | collective-permute-start | bytes 786440 | tf_op jit(solution)/shard_map/ppermute | solution.py:865

commit v10 on v9

--- a/solution.py
+++ b/solution.py
@@ -8,7 +8,7 @@
 
 F32 = jnp.float32
 NX, NY, CHIPS = 16, 16, 128
-STEP, WIDE = 8, 16
+STEP, WIDE = 16, 32
 BETWEEN = 2.0 * 0.1 / 1.1
 ANY = pl.BlockSpec(memory_space=pltpu.HBM)
 
@@ -185,53 +185,53 @@
     return (((w[2 * f + 1] - w[2 * f]) - 0.8 * own) + weigh(w, six)) * diag
 
 
-def fine_sweeps(planes, windows, start, share, one, two, weights, diags, halves, omega, wrap, keep):
+def fine_sweeps(planes, windows, start, share, one, two, weights, diags, halves, omega, wrap, keep, size):
     first, count = windows[0]
 
     def first_sweep(step):
-        z = STEP * step
+        z = size * step
         w = []
-        for k, (own, six) in enumerate(block_of(share, (), z + 1, STEP, first, count)):
+        for k, (own, six) in enumerate(block_of(share, (), z + 1, size, first, count)):
             now, diag = fine_weights(own, six, omega)
             diags[z + k, pl.ds(first, count), :] = diag
             for i in range(6):
                 weights[i, z + k, pl.ds(first, count), :] = now[i]
             w.append(now)
         for f in range(3):
-            for k, (own, six) in enumerate(block_of(start, (f,), z + 1, STEP, first, count)):
+            for k, (own, six) in enumerate(block_of(start, (f,), z + 1, size, first, count)):
                 one[f, z + k + 1, pl.ds(first, count), :] = fine_sweep(w[k], f, own, six)
 
-    loop(planes // STEP, first_sweep)
+    loop(planes // size, first_sweep)
     wrap(one)
     second, count2 = windows[1]
 
     def second_sweep(step):
-        z = STEP * step
-        w = [[weights[i, z + k, pl.ds(second, count2), :] for i in range(6)] for k in range(STEP)]
-        for f in range(3):
-            for k, (own, six) in enumerate(block_of(one, (f,), z + 1, STEP, second, count2)):
+        z = size * step
+        w = [[weights[i, z + k, pl.ds(second, count2), :] for i in range(6)] for k in range(size)]
+        for f in range(3):
+            for k, (own, six) in enumerate(block_of(one, (f,), z + 1, size, second, count2)):
                 two[f, z + k + 1, pl.ds(second, count2), :] = fine_sweep(w[k], f, own, six)
 
-    loop(planes // STEP, second_sweep)
+    loop(planes // size, second_sweep)
     wrap(two)
 
     def residual(step):
-        z = STEP * step
-        w = [[weights[i, z + k, 8:24, :] for i in range(6)] for k in range(STEP)]
-        diag = [diags[z + k, 8:24, :] for k in range(STEP)]
+        z = size * step
+        w = [[weights[i, z + k, 8:24, :] for i in range(6)] for k in range(size)]
+        diag = [diags[z + k, 8:24, :] for k in range(size)]
         for f in range(3):
             values = []
-            for k, (own, six) in enumerate(block_of(two, (f,), z + 1, STEP, 8, 16)):
+            for k, (own, six) in enumerate(block_of(two, (f,), z + 1, size, 8, 16)):
                 if keep is not None:
                     keep[f, z + k] = own
                 values.append(fine_left(w[k], f, own, six, diag[k]))
-            for pair in range(STEP // 2):
-                halves[f, STEP // 2 * step + pair] = values[2 * pair] + values[2 * pair + 1]
-        for pair in range(STEP // 2):
+            for pair in range(size // 2):
+                halves[f, size // 2 * step + pair] = values[2 * pair] + values[2 * pair + 1]
+        for pair in range(size // 2):
             at = z + 2 * pair + 1
-            halves[3, STEP // 2 * step + pair] = share[at, 8:24, :] + share[at + 1, 8:24, :]
-
-    loop(planes // STEP, residual)
+            halves[3, size // 2 * step + pair] = share[at, 8:24, :] + share[at + 1, 8:24, :]
+
+    loop(planes // size, residual)
 
 
 def own_kernel(own, one, two, halves, to_right, to_left, edges, held, weights, diags):
@@ -249,7 +249,7 @@
 
     loop(32, plane, 8)
     fine_sweeps(
-        32, [(8, 16)] * 2, held, held.at[3], one, two, weights, diags, halves, 0.8, lambda ref: None, None
+        32, [(8, 16)] * 2, held, held.at[3], one, two, weights, diags, halves, 0.8, lambda ref: None, None, 8
     )
 
     def some(low):
@@ -265,7 +265,7 @@
     loop(16, edge, 8)
 
 
-def rows_edge_kernel(own, rim, own_one, own_two, own_halves, two, packed, edges, start, one, weights, diags, halves, pooled):
+def rows_edge_kernel(own, rim, own_one, own_two, own_halves, two, coarse, edges, start, one, weights, diags, halves, pooled):
     gx = lax.axis_index("gx")
     zero = jnp.zeros((24, 128), F32)
     for z in (0, 33):
@@ -351,14 +351,9 @@
             halves[3, WIDE // 2 * block + k] = own_halves[3, WIDE // 2 * block + k]
 
     loop(32 // WIDE, residual)
-    source, target = iota((128, 128), 0), iota((128, 128), 1)
-    value = None
-    for half in range(2):
-        pool = jnp.where(source // 2 + 64 * half == target, 0.125, 0.0)
-        part = dot_exact(halves[:, 8 * half : 8 * half + 8].reshape(512, 128), pool)
-        value = part if value is None else value + part
-    pooled[...] = value
-    packed[...] = (pooled[pl.ds(0, 256, stride=2), :] + pooled[pl.ds(1, 256, stride=2), :]).reshape(4, 8, 8, 128)
+    pool = jnp.where(iota((128, 128), 0) // 2 == iota((128, 128), 1), 0.125, 0.0)
+    pooled[...] = dot_exact(halves[...].reshape(1024, 128), pool)
+    coarse[...] = (pooled[pl.ds(0, 512, stride=2), :] + pooled[pl.ds(1, 512, stride=2), :]).reshape(4, 16, 8, 128)
 
     def edge(z):
         for ch in range(4):
@@ -368,7 +363,7 @@
 
 
 def rim_kernel(
-    edges, edges_rim, near, far, field, packed,
+    edges, edges_rim, owned, near, far, field, coarse, packed,
     start, share, one, two, weights, diags, halves, pooled,
 ):
     gx, gy = lax.axis_index("gx"), lax.axis_index("gy")
@@ -418,22 +413,37 @@
     )
     omega = 0.8 * (inside_x * inside_y).astype(F32)
     fine_sweeps(
-        16, [(6, 24), (7, 24)], start, share, one, two, weights, diags, halves, omega, wrap, field
+        16, [(6, 24), (7, 24)], start, share, one, two, weights, diags, halves, omega, wrap, field, STEP
     )
 
     source, target = iota((128, 128), 0), iota((128, 128), 1)
     spot = source % 64
-    column = jnp.where(spot < 32, 121 + spot, 71 + spot) // 2
-    to = jnp.where(spot < 32, column - 62, column - 48)
-    keep = ((spot < 32) & (to >= 0) & (to < 9)) | ((spot >= 32) & (to >= 9) & (to < 18))
-    mixed = halves[...].reshape(4, 4, 2, 16, 128)
-    value = None
-    for odd in range(2):
-        pool = jnp.where(keep & (to + 64 * odd + 32 * (source // 64) == target), 0.125, 0.0)
-        part = dot_exact(mixed[:, :, odd].reshape(256, 128), pool)
-        value = part if value is None else value + part
-    pooled[...] = value
-    packed[...] = (pooled[pl.ds(0, 128, stride=2), :] + pooled[pl.ds(1, 128, stride=2), :]).reshape(4, 4, 8, 128)
+    column = jnp.where(spot < 32, 121 + spot, 128 + spot - 57)
+    to = jnp.where(spot < 32, column // 2, (column // 2 + 64) % 128)
+    from_rim = (iota((64, 128), 1) < 2) | (iota((64, 128), 1) >= 62)
+    mixed = halves[...].reshape(512, 128)
+    for half in range(2):
+        pool = jnp.where((to == target) & (source // 64 == half), 0.125, 0.0)
+        pooled[...] = dot_exact(mixed, pool)
+        for ch in range(4):
+            even = pooled[pl.ds(128 * ch, 64, stride=2), :]
+            odd = pooled[pl.ds(128 * ch + 1, 64, stride=2), :]
+            at = pl.ds(8 * half, 8)
+            rest = owned[ch, at].reshape(64, 128)
+            coarse[ch, at] = jnp.where(from_rim, even + odd, rest).reshape(8, 8, 128)
+
+    lane = iota((8, 128), 1)
+    for ch in range(4):
+        for group in range(2):
+            tiles = [None] * 5
+            for k in range(8):
+                moved = roll(coarse[ch, 8 * group + k], 8 + 80 * k)
+                tile, off = divmod(80 * k, 128)
+                tiles[tile] = moved if off == 0 else jnp.where(lane >= off, moved, tiles[tile])
+                if off + 80 > 128:
+                    tiles[tile + 1] = moved
+            for tile in range(5):
+                packed[ch, group, tile] = tiles[tile]
 
 
 def base_kernel(two, rim, e_one, e_two, base, wide, spread):
@@ -479,7 +489,7 @@
 
 
 def middle_kernel(
-    main, main_near, main_far, rim, rim_near, rim_far, sent, e_one, e_two,
+    mine, near, far, sent, e_one, e_two,
     share, rest, rhs, first, second, weights, diags, halves, pooled,
     rest2, first2, second2, rhs2, share2, weights2,
 ):
@@ -498,30 +508,30 @@
     near_row, far_row = jnp.where(even, 16, 0), jnp.where(even, 0, 16)
     starts = (pl.multiple_of(near_row, 8), pl.multiple_of(far_row, 8), 8)
 
-    sources = zip(starts, ((main_near, rim_near), (main_far, rim_far), (main, rim)))
-    sources = list(sources)
     has_far = inner(gx)
 
-    def fill(q):
-        for odd in range(2):
-            for half in range(2):
-                z = 2 * q + odd + 8 * half
-                base = 64 * odd + 32 * half
-                for at, (middle, outer) in sources:
-                    for ch in range(4):
-                        edge, body = outer[ch, q], middle[ch, 2 * q + odd]
-                        if outer is rim_far:
-                            edge, body = jnp.where(has_far, edge, 0.0), jnp.where(has_far, body, 0.0)
-                        value = jnp.where(lane < 62, roll(body, 64 * half), roll(edge, 62 - base))
-                        value = jnp.where((lane >= 96) | (lane < 2), roll(edge, 112 - base), value)
-                        if ch < 3:
-                            rhs[ch, z, pl.ds(at, 8), :] = value
-                        else:
-                            share[z, pl.ds(at, 8), :] = value
-                            rest[z + 1, pl.ds(at, 8), :] = resist(value)
-                rest[z + 1, 24:32, :] = jnp.full((8, 128), 0.5, F32)
-
-    loop(4, fill)
+    def fill(group):
+        for k in range(8):
+            z = 8 * group + k
+            tile, off = divmod(80 * k, 128)
+            for ch in range(4):
+                parts = []
+                for ref in (near, far):
+                    value = ref[ch, group, tile]
+                    if off + 80 > 128:
+                        value = jnp.where(lane >= off, value, ref[ch, group, tile + 1])
+                    value = value if ref is near else jnp.where(has_far, value, 0.0)
+                    parts.append(roll(value, -8 - 80 * k))
+                parts.append(mine[ch, z])
+                for at, value in zip(starts, parts):
+                    if ch < 3:
+                        rhs[ch, z, pl.ds(at, 8), :] = value
+                    else:
+                        share[z, pl.ds(at, 8), :] = value
+                        rest[z + 1, pl.ds(at, 8), :] = resist(value)
+            rest[z + 1, 24:32, :] = jnp.full((8, 128), 0.5, F32)
+
+    loop(2, fill, 2)
 
     row, lane = iota((24, 128), 0) + 1, iota((24, 128), 1)
     in_x = jnp.where(row < 8, low_x, jnp.where(row >= 16, high_x, 1))
@@ -663,7 +673,7 @@
                 jnp.where(first_core, pair[1], pair[0])
             )
 
-    loop(16, lay, 4)
+    loop(16, lay, 16)
     flat = natural.reshape(1024, 128)
 
     def plane(ch, z, x, half):
@@ -829,26 +839,24 @@
     )
     from_far = lax.ppermute(to_far, both, far_y)
     from_near = lax.ppermute(to_near, "gy", swap_near)
-    two, main, edges_rim = call(
+    two, part, edges_rim = call(
         rows_edge_kernel,
-        [(3, 34, 24, 128), (4, 8, 8, 128), (4, 16, 8, 128)],
+        [(3, 34, 24, 128), (4, 16, 8, 128), (4, 16, 8, 128)],
         [(4, 34, 24, 128), (3, 34, 24, 128), (6, 32, 24, 128), (32, 24, 128)]
-        + [(4, 16, 16, 128), (512, 128)],
+        + [(4, 16, 16, 128), (1024, 128)],
         flops=10_000_000,
     )(own, rim_rows, own_one, own_two, halves)
-    main_near = lax.ppermute(main, "gx", swap_near)
-    main_far = lax.ppermute(main, both, far_x)
-    rim, rim_one = call(
+    rim, coarse, packed = call(
         rim_kernel,
-        [(3, 16, 16, 128), (4, 4, 8, 128)],
+        [(3, 16, 16, 128), (4, 16, 8, 128), (4, 2, 5, 8, 128)],
         [(3, 18, 32, 128), (18, 32, 128)]
         + [(3, 18, 32, 128)] * 2
         + [(6, 16, 32, 128), (16, 32, 128)]
-        + [(4, 8, 16, 128), (256, 128)],
+        + [(4, 8, 16, 128), (512, 128)],
         flops=10_000_000,
-    )(edges, edges_rim, from_near, from_far)
-    rim_near = lax.ppermute(rim_one, "gx", swap_near)
-    rim_far = lax.ppermute(rim_one, both, far_x)
+    )(edges, edges_rim, part, from_near, from_far)
+    from_near = lax.ppermute(packed, "gx", swap_near)
+    from_far = lax.ppermute(packed, both, far_x)
     sent, e_one, e_two = call(
         middle_kernel,
         [(CHIPS, 4, 128), (3, 16, 8, 128), (3, 8, 8, 128)],
@@ -856,7 +864,7 @@
         + [(6, 16, 32, 128), (16, 32, 128), (4, 8, 24, 128), (768, 128)]
         + [(10, 24, 128), (3, 10, 24, 128), (3, 10, 24, 128), (3, 8, 8, 128), (8, 8, 128)]
         + [(7, 8, 16, 128)],
-    )(main, main_near, main_far, rim_one, rim_near, rim_far)
+    )(coarse, from_near, from_far)
     groups = [[i for i in range(NX * NY) if i % 2 == core] for core in range(2)]
     mine = lax.all_to_all(
         sent, ("gx", "gy"), split_axis=0, concat_axis=0, axis_index_groups=groups, tiled=True

time: 65.7 us -> 77.9 us (1.19)
  Pallas kernels: 19 us -> 28.6 us
  starting transfers between devices: 17.6 us -> 12.1 us
  blocking collectives: 26.8 us -> 31.6 us
  waiting for transfers between devices: 2.13 us -> 5.24 us
    pallas_call x1, Pallas kernels: 4.44 us -> 15.7 us  [local(): call(top_kernel, [(3, 32, 16, 128)], [(4, 2, 128, 128), (3, 16, 16, 128),...]
    ppermute x4 -> x2, starting transfers between devices: 8.04 us -> 2.67 us  [the longest x1 2.19 us: local(): from_near = lax.ppermute(packed, 'gx', swap_near)]
    all_to_all x1, blocking collectives: 26.8 us -> 31.6 us  [local(): lax.all_to_all(sent, ('gx', 'gy'), split_axis=0, concat_axis=0, axis_inde...]
    ppermute x1, waiting for transfers between devices: 0.01 us -> 2.27 us  [local(): from_far = lax.ppermute(to_far, both, far_y)]
    pallas_call x1, Pallas kernels: 2.89 us -> 1.93 us  [local(): call(middle_kernel, [(CHIPS, 4, 128), (3, 16, 8, 128), (3, 8, 8, 128)], [...]
    ppermute x4 -> x2, waiting for transfers between devices: 1.86 us -> 2.71 us  [the longest x1 2.7 us: local(): from_near = lax.ppermute(packed, 'gx', swap_near)]
  transfers between devices with their start and end apart: 9 -> 7, of which waited for: 2 -> 3; matrix products, arithmetic and copies ran while one was open for 0% -> 0% of each run, Pallas kernels for 15% -> 9%
where the time goes in v10:
time: 77.9 us; the launch traced here: 77.8 us
  blocking collectives  31.6 us (41%)
  Pallas kernels  28.6 us (37%)
  starting transfers between devices  12.1 us (16%)
  waiting for transfers between devices  5.24 us (7%)
    all_to_all x1, blocking collectives, local(): lax.all_to_all(sent, ('gx', 'gy'), split_axis=0, concat_axis=0, axis_inde...  31.6 us
    pallas_call x1, Pallas kernels, local(): call(top_kernel, [(3, 32, 16, 128)], [(4, 2, 128, 128), (3, 16, 16, 128),...  15.7 us
    pallas_call x1, Pallas kernels, local(): call(own_kernel, [(3, 34, 32, 128)] * 2 + [(4, 16, 16, 128)] + [(4, 4, 16...  3.66 us
    ppermute x1, starting transfers between devices, local(): other = lax.ppermute(mine, 'gy', swap_near)  3.19 us
    ppermute x1, waiting for transfers between devices, local(): from_near = lax.ppermute(packed, 'gx', swap_near)  2.7 us
    pallas_call x1, Pallas kernels, local(): call(rim_kernel, [(3, 16, 16, 128), (4, 16, 8, 128), (4, 2, 5, 8, 128)],...  2.63 us
    ppermute x1, waiting for transfers between devices, local(): from_far = lax.ppermute(to_far, both, far_y)  2.27 us
    pallas_call x1, Pallas kernels, local(): call(rows_edge_kernel, [(3, 34, 24, 128), (4, 16, 8, 128), (4, 16, 8, 128...  2.23 us
  transfers between devices with their start and end apart: 7, of which 3 were waited for; matrix products, arithmetic and copies ran while one was open for 0% of the time, Pallas kernels for 9%

profile of v10, /device:TPU:1, one launch (start us, length us, event | category | flops | bytes accessed | tf_op | source)
XLA Modules:
  0.0 77.8 jit_solution(16880090409875861672)
XLA Ops:
  0.0 1.3 %shard_map.28 = (f32[12,32,128]{2,1,0:T(8,128)S(1)}, f32[12,32,128]{2,1,0:T(8,128)S(1)}, f32[4,32,16,128]{3,2,1,0:T(8,128)S(1)}) custom-call(f32[3,32,16,128]{3,2,1,0:T(8,128)} %guess.1, s32[32,16,128]{2,1,0:T(8,128)} %labels.1), custom_call_target="tpu_custom_call" | custom-call | flops 1000000 | bytes 4000000 | tf_op jit(solution)/shard_map/pallas_call | solution.py:823
  1.3 2.1 %collective-permute-start = (f32[12,32,128]{2,1,0:T(8,128)S(1)}, f32[12,32,128]{2,1,0:T(8,128)S(1)}, u32[]{:S(2)}, u32[]{:S(2)}) collective-permute-start(f32[12,32,128]{2,1,0:T(8,128)S(1)} %get-tuple-element.30), channel_id=1, source_target_pairs={{0,16},{16,0},{32,48},{48,32},{64,80},{80,64},{96,112},{112,96},{1... | collective-permute-start | bytes 589832 | tf_op jit(solution)/shard_map/ppermute | solution.py:829
  3.4 1.3 %collective-permute-start.1 = (f32[12,32,128]{2,1,0:T(8,128)S(1)}, f32[12,32,128]{2,1,0:T(8,128)S(1)}, u32[]{:S(2)}, u32[]{:S(2)}) collective-permute-start(f32[12,32,128]{2,1,0:T(8,128)S(1)} %get-tuple-element.31), channel_id=1, source_target_pairs={{0,1},{1,0},{2,3},{3,2},{4,5},{5,4},{6,7},{7,6},{8,9},{9,8},{10,11... | collective-permute-start | bytes 589832 | tf_op jit(solution)/shard_map/ppermute | solution.py:830
  4.7 3.7 %shard_map.29 = (f32[3,34,32,128]{3,2,1,0:T(8,128)S(1)}, f32[3,34,32,128]{3,2,1,0:T(8,128)S(1)}, f32[4,16,16,128]{3,2,1,0:T(8,128)S(1)}, f32[4,4,16,128]{3,2,1,0...) custom-call(f32[4,32,16,128]{3,2,1,0:T(8,128)S(1)} %get-tuple-element.26.own), custom_call_target="tpu_custom_call" | custom-call | flops 20000000 | bytes 4000000 | tf_op jit(solution)/shard_map/pallas_call | solution.py:831
  8.4 0.0 collective-permute-done.x_near
  8.4 0.0 collective-permute-done.1.x_far
  8.4 0.3 shard_map.30
  8.7 2.0 %collective-permute-start.2 = (f32[4,4,24,128]{3,2,1,0:T(8,128)S(1)}, f32[4,4,24,128]{3,2,1,0:T(8,128)S(1)}, u32[]{:S(2)}, u32[]{:S(2)}) collective-permute-start(f32[4,4,24,128]{3,2,1,0:T(8,128)S(1)} %get-tuple-element.38), channel_id=1, source_target_pairs={{0,1},{1,0},{2,3},{3,2},{4,5},{5,4},{6,7},{7,6},{8,9},{9,8},{10,11... | collective-permute-start | bytes 589832 | tf_op jit(solution)/shard_map/ppermute | solution.py:841
  10.7 0.9 %collective-permute-start.3 = (f32[4,4,24,128]{3,2,1,0:T(8,128)S(1)}, f32[4,4,24,128]{3,2,1,0:T(8,128)S(1)}, u32[]{:S(2)}, u32[]{:S(2)}) collective-permute-start(f32[4,4,24,128]{3,2,1,0:T(8,128)S(1)} %get-tuple-element.39), channel_id=1, source_target_pairs={{0,16},{1,2},{2,1},{3,4},{4,3},{5,6},{6,5},{7,8},{8,7},{9,10},{10,... | collective-permute-start | bytes 589832 | tf_op jit(solution)/shard_map/ppermute | solution.py:840
  11.5 2.2 %shard_map.31 = (f32[3,34,24,128]{3,2,1,0:T(8,128)S(1)}, f32[4,16,8,128]{3,2,1,0:T(8,128)S(1)}, f32[4,16,8,128]{3,2,1,0:T(8,128)S(1)}) custom-call(f32[4,32,16,128]{3,2,1,0:T(8,128)S(1)} %get-tuple-element.26.own, f32[4,32,8,128]{3,2,1,0:T(8,128)S(1)} %get-tuple-element.32.rim, f32[3,34,32,128]{3,2,1,0:T(8,128)S(1)} %get-tuple-element.33.own_one, ...), custom_call_target="tpu_custom_call" | custom-call | flops 10000000 | bytes 4000000 | tf_op jit(solution)/shard_map/pallas_call | solution.py:842
  13.8 0.0 collective-permute-done.2.near
  13.8 2.3 %collective-permute-done.3.far = f32[4,4,24,128]{3,2,1,0:T(8,128)S(1)} collective-permute-done((f32[4,4,24,128]{3,2,1,0:T(8,128)S(1)}, f32[4,4,24,128]{3,2,1,0:T(8,128)S(1)}, u32[]{:S(2)}, u32[]{:S(2)}) %collective-permute-start.3) | collective-permute-done | bytes 196640 | tf_op jit(solution)/shard_map/ppermute | solution.py:840
  16.0 2.6 %shard_map.32 = (f32[3,16,16,128]{3,2,1,0:T(8,128)S(1)}, f32[4,16,8,128]{3,2,1,0:T(8,128)S(1)}, f32[4,2,5,8,128]{4,3,2,1,0:T(8,128)S(1)}) custom-call(f32[4,16,16,128]{3,2,1,0:T(8,128)S(1)} %get-tuple-element.27.edges, f32[4,16,8,128]{3,2,1,0:T(8,128)S(1)} %get-tuple-element.36.edges_rim, f32[4,16,8,128]{3,2,1,0:T(8,128)S(1)} %get-tuple-element.37.owned, ...), custom_call_target="tpu_custom_call" | custom-call | flops 10000000 | bytes 4000000 | tf_op jit(solution)/shard_map/pallas_call | solution.py:849
  18.7 0.5 collective-permute-start.5
  19.2 2.2 %collective-permute-start.4 = (f32[4,2,5,8,128]{4,3,2,1,0:T(8,128)S(1)}, f32[4,2,5,8,128]{4,3,2,1,0:T(8,128)S(1)}, u32[]{:S(2)}, u32[]{:S(2)}) collective-permute-start(f32[4,2,5,8,128]{4,3,2,1,0:T(8,128)S(1)} %get-tuple-element.41), channel_id=1, source_target_pairs={{0,16},{16,0},{32,48},{48,32},{64,80},{80,64},{96,112},{112,96},{1... | collective-permute-start | bytes 491528 | tf_op jit(solution)/shard_map/ppermute | solution.py:858
  21.3 0.0 collective-permute-done.5.far
  21.3 2.7 %collective-permute-done.4.near = f32[4,2,5,8,128]{4,3,2,1,0:T(8,128)S(1)} collective-permute-done((f32[4,2,5,8,128]{4,3,2,1,0:T(8,128)S(1)}, f32[4,2,5,8,128]{4,3,2,1,0:T(8,128)S(1)}, u32[]{:S(2)}, u32[]{:S(2)}) %collective-permute-start.4) | collective-permute-done | bytes 163872 | tf_op jit(solution)/shard_map/ppermute | solution.py:858
  24.1 1.9 %shard_map.33 = (f32[128,4,128]{2,1,0:T(4,128)S(1)}, f32[3,16,8,128]{3,2,1,0:T(8,128)S(1)}, f32[3,8,8,128]{3,2,1,0:T(8,128)S(1)}) custom-call(f32[4,16,8,128]{3,2,1,0:T(8,128)S(1)} %get-tuple-element.40.mine, f32[4,2,5,8,128]{4,3,2,1,0:T(8,128)S(1)} %collective-permute-done.4.near, f32[4,2,5,8,128]{4,3,2,1,0:T(8,128)S(1)} %collective-permute-done.5.far), custom_call_target="tpu_custom_call" | custom-call | flops 1000000 | bytes 4000000 | tf_op jit(solution)/shard_map/pallas_call | solution.py:860
  26.0 31.6 %all_to_all.5 = f32[128,4,128]{2,1,0:T(4,128)S(1)} all-to-all(f32[128,4,128]{2,1,0:T(4,128)S(1)} %get-tuple-element.42), channel_id=1, replica_groups={{0,2,4,6,8,10,12,14,16,18,20,22,24,26,28,30,32,34,36,38,40,42,44,46,48,..., dimensions={0} | all-to-all | bytes 524288 | tf_op jit(solution)/shard_map/all_to_all | solution.py:869
  57.6 3.2 %collective-permute-start.6 = (f32[128,4,128]{2,1,0:T(4,128)S(1)}, f32[128,4,128]{2,1,0:T(4,128)S(1)}, u32[]{:S(2)}, u32[]{:S(2)}) collective-permute-start(f32[128,4,128]{2,1,0:T(4,128)S(1)} %all_to_all.5), channel_id=1, source_target_pairs={{0,1},{1,0},{2,3},{3,2},{4,5},{5,4},{6,7},{7,6},{8,9},{9,8},{10,11... | collective-permute-start | bytes 786440 | tf_op jit(solution)/shard_map/ppermute | solution.py:873
  60.8 0.9 %shard_map.34.base = f32[3,32,16,128]{3,2,1,0:T(8,128)S(1)} custom-call(f32[3,34,24,128]{3,2,1,0:T(8,128)S(1)} %get-tuple-element.43.two, f32[3,16,16,128]{3,2,1,0:T(8,128)S(1)} %get-tuple-element.44.rim, f32[3,16,8,128]{3,2,1,0:T(8,128)S(1)} %get-tuple-element.45.e_one, f32[3,8,8,128]{3,2,1,0:T(8,128)S(1)} %get-tuple-element.46.e_two), custom_call_target="tpu_custom_call" | custom-call | flops 1000000 | bytes 4000000 | tf_op jit(solution)/shard_map/pallas_call | solution.py:872
  61.7 0.3 collective-permute-done.6
  62.0 15.7 %shard_map.35 = f32[3,32,16,128]{3,2,1,0:T(8,128)} custom-call(f32[512,128]{1,0:T(8,128)S(1)} %bitcast.2, f32[512,128]{1,0:T(8,128)S(1)} %bitcast.3, f32[3,32,16,128]{3,2,1,0:T(8,128)S(1)} %shard_map.34.base), custom_call_target="tpu_custom_call" | custom-call | flops 1000000 | bytes 4000000 | tf_op jit(solution)/shard_map/pallas_call | solution.py:874
Async XLA Ops:
  1.3 7.1 %collective-permute-start = (f32[12,32,128]{2,1,0:T(8,128)S(1)}, f32[12,32,128]{2,1,0:T(8,128)S(1)}, u32[]{:S(2)}, u32[]{:S(2)}) collective-permute-start(f32[12,32,128]{2,1,0:T(8,128)S(1)} %get-tuple-element.30), channel_id=1, source_target_pairs={{0,16},{16,0},{32,48},{48,32},{64,80},{80,64},{96,112},{112,96},{1... | collective-permute-start | bytes 589832 | tf_op jit(solution)/shard_map/ppermute | solution.py:829
  3.4 5.0 %collective-permute-start.1 = (f32[12,32,128]{2,1,0:T(8,128)S(1)}, f32[12,32,128]{2,1,0:T(8,128)S(1)}, u32[]{:S(2)}, u32[]{:S(2)}) collective-permute-start(f32[12,32,128]{2,1,0:T(8,128)S(1)} %get-tuple-element.31), channel_id=1, source_target_pairs={{0,1},{1,0},{2,3},{3,2},{4,5},{5,4},{6,7},{7,6},{8,9},{9,8},{10,11... | collective-permute-start | bytes 589832 | tf_op jit(solution)/shard_map/ppermute | solution.py:830
  8.7 5.1 %collective-permute-start.2 = (f32[4,4,24,128]{3,2,1,0:T(8,128)S(1)}, f32[4,4,24,128]{3,2,1,0:T(8,128)S(1)}, u32[]{:S(2)}, u32[]{:S(2)}) collective-permute-start(f32[4,4,24,128]{3,2,1,0:T(8,128)S(1)} %get-tuple-element.38), channel_id=1, source_target_pairs={{0,1},{1,0},{2,3},{3,2},{4,5},{5,4},{6,7},{7,6},{8,9},{9,8},{10,11... | collective-permute-start | bytes 589832 | tf_op jit(solution)/shard_map/ppermute | solution.py:841
  10.7 5.4 %collective-permute-start.3 = (f32[4,4,24,128]{3,2,1,0:T(8,128)S(1)}, f32[4,4,24,128]{3,2,1,0:T(8,128)S(1)}, u32[]{:S(2)}, u32[]{:S(2)}) collective-permute-start(f32[4,4,24,128]{3,2,1,0:T(8,128)S(1)} %get-tuple-element.39), channel_id=1, source_target_pairs={{0,16},{1,2},{2,1},{3,4},{4,3},{5,6},{6,5},{7,8},{8,7},{9,10},{10,... | collective-permute-start | bytes 589832 | tf_op jit(solution)/shard_map/ppermute | solution.py:840
  18.7 2.7 %collective-permute-start.5 = (f32[4,2,5,8,128]{4,3,2,1,0:T(8,128)S(1)}, f32[4,2,5,8,128]{4,3,2,1,0:T(8,128)S(1)}, u32[]{:S(2)}, u32[]{:S(2)}) collective-permute-start(f32[4,2,5,8,128]{4,3,2,1,0:T(8,128)S(1)} %get-tuple-element.41), channel_id=1, source_target_pairs={{0,1},{1,0},{2,3},{3,2},{4,5},{5,4},{6,7},{7,6},{8,9},{9,8},{10,11... | collective-permute-start | bytes 491528 | tf_op jit(solution)/shard_map/ppermute | solution.py:859
  19.2 4.9 %collective-permute-start.4 = (f32[4,2,5,8,128]{4,3,2,1,0:T(8,128)S(1)}, f32[4,2,5,8,128]{4,3,2,1,0:T(8,128)S(1)}, u32[]{:S(2)}, u32[]{:S(2)}) collective-permute-start(f32[4,2,5,8,128]{4,3,2,1,0:T(8,128)S(1)} %get-tuple-element.41), channel_id=1, source_target_pairs={{0,16},{16,0},{32,48},{48,32},{64,80},{80,64},{96,112},{112,96},{1... | collective-permute-start | bytes 491528 | tf_op jit(solution)/shard_map/ppermute | solution.py:858
  57.6 4.4 %collective-permute-start.6 = (f32[128,4,128]{2,1,0:T(4,128)S(1)}, f32[128,4,128]{2,1,0:T(4,128)S(1)}, u32[]{:S(2)}, u32[]{:S(2)}) collective-permute-start(f32[128,4,128]{2,1,0:T(4,128)S(1)} %all_to_all.5), channel_id=1, source_target_pairs={{0,1},{1,0},{2,3},{3,2},{4,5},{5,4},{6,7},{7,6},{8,9},{9,8},{10,11... | collective-permute-start | bytes 786440 | tf_op jit(solution)/shard_map/ppermute | solution.py:873

commit v11 on v9

--- a/solution.py
+++ b/solution.py
@@ -8,7 +8,7 @@
 
 F32 = jnp.float32
 NX, NY, CHIPS = 16, 16, 128
-STEP, WIDE = 8, 16
+STEP, WIDE = 16, 32
 BETWEEN = 2.0 * 0.1 / 1.1
 ANY = pl.BlockSpec(memory_space=pltpu.HBM)
 
@@ -185,53 +185,53 @@
     return (((w[2 * f + 1] - w[2 * f]) - 0.8 * own) + weigh(w, six)) * diag
 
 
-def fine_sweeps(planes, windows, start, share, one, two, weights, diags, halves, omega, wrap, keep):
+def fine_sweeps(planes, windows, start, share, one, two, weights, diags, halves, omega, wrap, keep, size):
     first, count = windows[0]
 
     def first_sweep(step):
-        z = STEP * step
+        z = size * step
         w = []
-        for k, (own, six) in enumerate(block_of(share, (), z + 1, STEP, first, count)):
+        for k, (own, six) in enumerate(block_of(share, (), z + 1, size, first, count)):
             now, diag = fine_weights(own, six, omega)
             diags[z + k, pl.ds(first, count), :] = diag
             for i in range(6):
                 weights[i, z + k, pl.ds(first, count), :] = now[i]
             w.append(now)
         for f in range(3):
-            for k, (own, six) in enumerate(block_of(start, (f,), z + 1, STEP, first, count)):
+            for k, (own, six) in enumerate(block_of(start, (f,), z + 1, size, first, count)):
                 one[f, z + k + 1, pl.ds(first, count), :] = fine_sweep(w[k], f, own, six)
 
-    loop(planes // STEP, first_sweep)
+    loop(planes // size, first_sweep)
     wrap(one)
     second, count2 = windows[1]
 
     def second_sweep(step):
-        z = STEP * step
-        w = [[weights[i, z + k, pl.ds(second, count2), :] for i in range(6)] for k in range(STEP)]
-        for f in range(3):
-            for k, (own, six) in enumerate(block_of(one, (f,), z + 1, STEP, second, count2)):
+        z = size * step
+        w = [[weights[i, z + k, pl.ds(second, count2), :] for i in range(6)] for k in range(size)]
+        for f in range(3):
+            for k, (own, six) in enumerate(block_of(one, (f,), z + 1, size, second, count2)):
                 two[f, z + k + 1, pl.ds(second, count2), :] = fine_sweep(w[k], f, own, six)
 
-    loop(planes // STEP, second_sweep)
+    loop(planes // size, second_sweep)
     wrap(two)
 
     def residual(step):
-        z = STEP * step
-        w = [[weights[i, z + k, 8:24, :] for i in range(6)] for k in range(STEP)]
-        diag = [diags[z + k, 8:24, :] for k in range(STEP)]
+        z = size * step
+        w = [[weights[i, z + k, 8:24, :] for i in range(6)] for k in range(size)]
+        diag = [diags[z + k, 8:24, :] for k in range(size)]
         for f in range(3):
             values = []
-            for k, (own, six) in enumerate(block_of(two, (f,), z + 1, STEP, 8, 16)):
+            for k, (own, six) in enumerate(block_of(two, (f,), z + 1, size, 8, 16)):
                 if keep is not None:
                     keep[f, z + k] = own
                 values.append(fine_left(w[k], f, own, six, diag[k]))
-            for pair in range(STEP // 2):
-                halves[f, STEP // 2 * step + pair] = values[2 * pair] + values[2 * pair + 1]
-        for pair in range(STEP // 2):
+            for pair in range(size // 2):
+                halves[f, size // 2 * step + pair] = values[2 * pair] + values[2 * pair + 1]
+        for pair in range(size // 2):
             at = z + 2 * pair + 1
-            halves[3, STEP // 2 * step + pair] = share[at, 8:24, :] + share[at + 1, 8:24, :]
-
-    loop(planes // STEP, residual)
+            halves[3, size // 2 * step + pair] = share[at, 8:24, :] + share[at + 1, 8:24, :]
+
+    loop(planes // size, residual)
 
 
 def own_kernel(own, one, two, halves, to_right, to_left, edges, held, weights, diags):
@@ -249,7 +249,7 @@
 
     loop(32, plane, 8)
     fine_sweeps(
-        32, [(8, 16)] * 2, held, held.at[3], one, two, weights, diags, halves, 0.8, lambda ref: None, None
+        32, [(8, 16)] * 2, held, held.at[3], one, two, weights, diags, halves, 0.8, lambda ref: None, None, 8
     )
 
     def some(low):
@@ -418,7 +418,7 @@
     )
     omega = 0.8 * (inside_x * inside_y).astype(F32)
     fine_sweeps(
-        16, [(6, 24), (7, 24)], start, share, one, two, weights, diags, halves, omega, wrap, field
+        16, [(6, 24), (7, 24)], start, share, one, two, weights, diags, halves, omega, wrap, field, STEP
     )
 
     source, target = iota((128, 128), 0), iota((128, 128), 1)
@@ -521,7 +521,7 @@
                             rest[z + 1, pl.ds(at, 8), :] = resist(value)
                 rest[z + 1, 24:32, :] = jnp.full((8, 128), 0.5, F32)
 
-    loop(4, fill)
+    loop(4, fill, 2)
 
     row, lane = iota((24, 128), 0) + 1, iota((24, 128), 1)
     in_x = jnp.where(row < 8, low_x, jnp.where(row >= 16, high_x, 1))

time: 65.7 us -> 65.3 us (level)
  Pallas kernels: 19 us -> 17.7 us
  blocking collectives: 26.8 us -> 27.5 us
    all_to_all x1, blocking collectives: 26.8 us -> 27.5 us  [local(): lax.all_to_all(sent, ('gx', 'gy'), split_axis=0, concat_axis=0, axis_inde...]
  transfers between devices with their start and end apart: 9 -> 9, of which waited for: 2 -> 2; matrix products, arithmetic and copies ran while one was open for 0% -> 0% of each run, Pallas kernels for 15% -> 14%
where the time goes in v11:
time: 65.3 us; the launch traced here: 65.2 us
  blocking collectives  27.5 us (42%)
  Pallas kernels  17.7 us (27%)
  starting transfers between devices  17.6 us (27%)
  waiting for transfers between devices  2.14 us (3%)
    all_to_all x1, blocking collectives, local(): lax.all_to_all(sent, ('gx', 'gy'), split_axis=0, concat_axis=0, axis_inde...  27.5 us
    pallas_call x1, Pallas kernels, local(): call(top_kernel, [(3, 32, 16, 128)], [(4, 2, 128, 128), (3, 16, 16, 128),...  4.44 us
    pallas_call x1, Pallas kernels, local(): call(own_kernel, [(3, 34, 32, 128)] * 2 + [(4, 16, 16, 128)] + [(4, 4, 16...  3.66 us
    ppermute x1, starting transfers between devices, local(): other = lax.ppermute(mine, 'gy', swap_near)  3.3 us
    ppermute x1, starting transfers between devices, local(): rim_near = lax.ppermute(rim_one, 'gx', swap_near)  2.56 us
    pallas_call x1, Pallas kernels, local(): call(middle_kernel, [(CHIPS, 4, 128), (3, 16, 8, 128), (3, 8, 8, 128)], [...  2.45 us
    pallas_call x1, Pallas kernels, local(): call(rim_kernel, [(3, 16, 16, 128), (4, 4, 8, 128)], [(3, 18, 32, 128), (...  2.39 us
    pallas_call x1, Pallas kernels, local(): call(rows_edge_kernel, [(3, 34, 24, 128), (4, 8, 8, 128), (4, 16, 8, 128)...  2.3 us
  transfers between devices with their start and end apart: 9, of which 2 were waited for; matrix products, arithmetic and copies ran while one was open for 0% of the time, Pallas kernels for 14%

profile of v11, /device:TPU:1, one launch (start us, length us, event | category | flops | bytes accessed | tf_op | source)
XLA Modules:
  0.0 65.2 jit_solution(14659386874474370363)
XLA Ops:
  0.0 1.3 %shard_map.28 = (f32[12,32,128]{2,1,0:T(8,128)S(1)}, f32[12,32,128]{2,1,0:T(8,128)S(1)}, f32[4,32,16,128]{3,2,1,0:T(8,128)S(1)}) custom-call(f32[3,32,16,128]{3,2,1,0:T(8,128)} %guess.1, s32[32,16,128]{2,1,0:T(8,128)} %labels.1), custom_call_target="tpu_custom_call" | custom-call | flops 1000000 | bytes 4000000 | tf_op jit(solution)/shard_map/pallas_call | solution.py:813
  1.3 2.1 %collective-permute-start = (f32[12,32,128]{2,1,0:T(8,128)S(1)}, f32[12,32,128]{2,1,0:T(8,128)S(1)}, u32[]{:S(2)}, u32[]{:S(2)}) collective-permute-start(f32[12,32,128]{2,1,0:T(8,128)S(1)} %get-tuple-element.28), channel_id=1, source_target_pairs={{0,16},{16,0},{32,48},{48,32},{64,80},{80,64},{96,112},{112,96},{1... | collective-permute-start | bytes 589832 | tf_op jit(solution)/shard_map/ppermute | solution.py:819
  3.4 1.3 %collective-permute-start.1 = (f32[12,32,128]{2,1,0:T(8,128)S(1)}, f32[12,32,128]{2,1,0:T(8,128)S(1)}, u32[]{:S(2)}, u32[]{:S(2)}) collective-permute-start(f32[12,32,128]{2,1,0:T(8,128)S(1)} %get-tuple-element.29), channel_id=1, source_target_pairs={{0,1},{1,0},{2,3},{3,2},{4,5},{5,4},{6,7},{7,6},{8,9},{9,8},{10,11... | collective-permute-start | bytes 589832 | tf_op jit(solution)/shard_map/ppermute | solution.py:820
  4.7 3.7 %shard_map.29 = (f32[3,34,32,128]{3,2,1,0:T(8,128)S(1)}, f32[3,34,32,128]{3,2,1,0:T(8,128)S(1)}, f32[4,16,16,128]{3,2,1,0:T(8,128)S(1)}, f32[4,4,16,128]{3,2,1,0...) custom-call(f32[4,32,16,128]{3,2,1,0:T(8,128)S(1)} %get-tuple-element.25.own), custom_call_target="tpu_custom_call" | custom-call | flops 20000000 | bytes 4000000 | tf_op jit(solution)/shard_map/pallas_call | solution.py:821
  8.4 0.0 collective-permute-done.x_near
  8.4 0.0 collective-permute-done.1.x_far
  8.4 0.3 shard_map.30
  8.7 2.0 %collective-permute-start.4 = (f32[4,4,24,128]{3,2,1,0:T(8,128)S(1)}, f32[4,4,24,128]{3,2,1,0:T(8,128)S(1)}, u32[]{:S(2)}, u32[]{:S(2)}) collective-permute-start(f32[4,4,24,128]{3,2,1,0:T(8,128)S(1)} %get-tuple-element.37), channel_id=1, source_target_pairs={{0,1},{1,0},{2,3},{3,2},{4,5},{5,4},{6,7},{7,6},{8,9},{9,8},{10,11... | collective-permute-start | bytes 589832 | tf_op jit(solution)/shard_map/ppermute | solution.py:831
  10.7 0.9 %collective-permute-start.5 = (f32[4,4,24,128]{3,2,1,0:T(8,128)S(1)}, f32[4,4,24,128]{3,2,1,0:T(8,128)S(1)}, u32[]{:S(2)}, u32[]{:S(2)}) collective-permute-start(f32[4,4,24,128]{3,2,1,0:T(8,128)S(1)} %get-tuple-element.38), channel_id=1, source_target_pairs={{0,16},{1,2},{2,1},{3,4},{4,3},{5,6},{6,5},{7,8},{8,7},{9,10},{10,... | collective-permute-start | bytes 589832 | tf_op jit(solution)/shard_map/ppermute | solution.py:830
  11.5 2.3 %shard_map.31 = (f32[3,34,24,128]{3,2,1,0:T(8,128)S(1)}, f32[4,8,8,128]{3,2,1,0:T(8,128)S(1)}, f32[4,16,8,128]{3,2,1,0:T(8,128)S(1)}) custom-call(f32[4,32,16,128]{3,2,1,0:T(8,128)S(1)} %get-tuple-element.25.own, f32[4,32,8,128]{3,2,1,0:T(8,128)S(1)} %get-tuple-element.30.rim, f32[3,34,32,128]{3,2,1,0:T(8,128)S(1)} %get-tuple-element.31.own_one, ...), custom_call_target="tpu_custom_call" | custom-call | flops 10000000 | bytes 4000000 | tf_op jit(solution)/shard_map/pallas_call | solution.py:832
  13.8 1.4 %collective-permute-start.3 = (f32[4,8,8,128]{3,2,1,0:T(8,128)S(1)}, f32[4,8,8,128]{3,2,1,0:T(8,128)S(1)}, u32[]{:S(2)}, u32[]{:S(2)}) collective-permute-start(f32[4,8,8,128]{3,2,1,0:T(8,128)S(1)} %get-tuple-element.34.main), channel_id=1, source_target_pairs={{0,1},{1,0},{2,3},{3,2},{4,5},{5,4},{6,7},{7,6},{8,9},{9,8},{10,11... | collective-permute-start | bytes 393224 | tf_op jit(solution)/shard_map/ppermute | solution.py:840
  15.2 2.1 %collective-permute-start.2 = (f32[4,8,8,128]{3,2,1,0:T(8,128)S(1)}, f32[4,8,8,128]{3,2,1,0:T(8,128)S(1)}, u32[]{:S(2)}, u32[]{:S(2)}) collective-permute-start(f32[4,8,8,128]{3,2,1,0:T(8,128)S(1)} %get-tuple-element.34.main), channel_id=1, source_target_pairs={{0,16},{16,0},{32,48},{48,32},{64,80},{80,64},{96,112},{112,96},{1... | collective-permute-start | bytes 393224 | tf_op jit(solution)/shard_map/ppermute | solution.py:839
  17.3 0.0 collective-permute-done.4.near
  17.3 0.0 collective-permute-done.5.far
  17.3 2.4 %shard_map.32 = (f32[3,16,16,128]{3,2,1,0:T(8,128)S(1)}, f32[4,4,8,128]{3,2,1,0:T(8,128)S(1)}) custom-call(f32[4,16,16,128]{3,2,1,0:T(8,128)S(1)} %get-tuple-element.35.edges, f32[4,16,8,128]{3,2,1,0:T(8,128)S(1)} %get-tuple-element.36.edges_rim, f32[4,4,24,128]{3,2,1,0:T(8,128)S(1)} %collective-permute-done.4.near, ...), custom_call_target="tpu_custom_call" | custom-call | flops 10000000 | bytes 4000000 | tf_op jit(solution)/shard_map/pallas_call | solution.py:841
  19.6 2.1 %collective-permute-start.7 = (f32[4,4,8,128]{3,2,1,0:T(8,128)S(1)}, f32[4,4,8,128]{3,2,1,0:T(8,128)S(1)}, u32[]{:S(2)}, u32[]{:S(2)}) collective-permute-start(f32[4,4,8,128]{3,2,1,0:T(8,128)S(1)} %get-tuple-element.39.rim), channel_id=1, source_target_pairs={{0,1},{1,0},{2,3},{3,2},{4,5},{5,4},{6,7},{7,6},{8,9},{9,8},{10,11... | collective-permute-start | bytes 196616 | tf_op jit(solution)/shard_map/ppermute | solution.py:851
  21.7 2.6 %collective-permute-start.6 = (f32[4,4,8,128]{3,2,1,0:T(8,128)S(1)}, f32[4,4,8,128]{3,2,1,0:T(8,128)S(1)}, u32[]{:S(2)}, u32[]{:S(2)}) collective-permute-start(f32[4,4,8,128]{3,2,1,0:T(8,128)S(1)} %get-tuple-element.39.rim), channel_id=1, source_target_pairs={{0,16},{16,0},{32,48},{48,32},{64,80},{80,64},{96,112},{112,96},{1... | collective-permute-start | bytes 196616 | tf_op jit(solution)/shard_map/ppermute | solution.py:850
  24.3 0.0 collective-permute-done.3.main_far
  24.3 0.0 collective-permute-done.2.main_near
  24.3 0.0 collective-permute-done.7.rim_far
  24.3 1.9 %collective-permute-done.6.rim_near = f32[4,4,8,128]{3,2,1,0:T(8,128)S(1)} collective-permute-done((f32[4,4,8,128]{3,2,1,0:T(8,128)S(1)}, f32[4,4,8,128]{3,2,1,0:T(8,128)S(1)}, u32[]{:S(2)}, u32[]{:S(2)}) %collective-permute-start.6) | collective-permute-done | bytes 65568 | tf_op jit(solution)/shard_map/ppermute | solution.py:850
  26.1 2.4 %shard_map.33 = (f32[128,4,128]{2,1,0:T(4,128)S(1)}, f32[3,16,8,128]{3,2,1,0:T(8,128)S(1)}, f32[3,8,8,128]{3,2,1,0:T(8,128)S(1)}) custom-call(f32[4,8,8,128]{3,2,1,0:T(8,128)S(1)} %get-tuple-element.34.main, f32[4,8,8,128]{3,2,1,0:T(8,128)S(1)} %collective-permute-done.2.main_near, f32[4,8,8,128]{3,2,1,0:T(8,128)S(1)} %collective-permute-done.3.main_far, ...), custom_call_target="tpu_custom_call" | custom-call | flops 1000000 | bytes 4000000 | tf_op jit(solution)/shard_map/pallas_call | solution.py:852
  28.6 27.5 %all_to_all.5 = f32[128,4,128]{2,1,0:T(4,128)S(1)} all-to-all(f32[128,4,128]{2,1,0:T(4,128)S(1)} %get-tuple-element.40), channel_id=1, replica_groups={{0,2,4,6,8,10,12,14,16,18,20,22,24,26,28,30,32,34,36,38,40,42,44,46,48,..., dimensions={0} | all-to-all | bytes 524288 | tf_op jit(solution)/shard_map/all_to_all | solution.py:861
  56.1 3.3 %collective-permute-start.8 = (f32[128,4,128]{2,1,0:T(4,128)S(1)}, f32[128,4,128]{2,1,0:T(4,128)S(1)}, u32[]{:S(2)}, u32[]{:S(2)}) collective-permute-start(f32[128,4,128]{2,1,0:T(4,128)S(1)} %all_to_all.5), channel_id=1, source_target_pairs={{0,1},{1,0},{2,3},{3,2},{4,5},{5,4},{6,7},{7,6},{8,9},{9,8},{10,11... | collective-permute-start | bytes 786440 | tf_op jit(solution)/shard_map/ppermute | solution.py:865
  59.4 0.9 %shard_map.34.base = f32[3,32,16,128]{3,2,1,0:T(8,128)S(1)} custom-call(f32[3,34,24,128]{3,2,1,0:T(8,128)S(1)} %get-tuple-element.41.two, f32[3,16,16,128]{3,2,1,0:T(8,128)S(1)} %get-tuple-element.42.rim, f32[3,16,8,128]{3,2,1,0:T(8,128)S(1)} %get-tuple-element.43.e_one, f32[3,8,8,128]{3,2,1,0:T(8,128)S(1)} %get-tuple-element.44.e_two), custom_call_target="tpu_custom_call" | custom-call | flops 1000000 | bytes 4000000 | tf_op jit(solution)/shard_map/pallas_call | solution.py:864
  60.3 0.3 collective-permute-done.8
  60.6 4.4 %shard_map.35 = f32[3,32,16,128]{3,2,1,0:T(8,128)} custom-call(f32[512,128]{1,0:T(8,128)S(1)} %bitcast.2, f32[512,128]{1,0:T(8,128)S(1)} %bitcast.3, f32[3,32,16,128]{3,2,1,0:T(8,128)S(1)} %shard_map.34.base), custom_call_target="tpu_custom_call" | custom-call | flops 1000000 | bytes 4000000 | tf_op jit(solution)/shard_map/pallas_call | solution.py:866
Async XLA Ops:
  1.3 7.1 %collective-permute-start = (f32[12,32,128]{2,1,0:T(8,128)S(1)}, f32[12,32,128]{2,1,0:T(8,128)S(1)}, u32[]{:S(2)}, u32[]{:S(2)}) collective-permute-start(f32[12,32,128]{2,1,0:T(8,128)S(1)} %get-tuple-element.28), channel_id=1, source_target_pairs={{0,16},{16,0},{32,48},{48,32},{64,80},{80,64},{96,112},{112,96},{1... | collective-permute-start | bytes 589832 | tf_op jit(solution)/shard_map/ppermute | solution.py:819
  3.4 5.0 %collective-permute-start.1 = (f32[12,32,128]{2,1,0:T(8,128)S(1)}, f32[12,32,128]{2,1,0:T(8,128)S(1)}, u32[]{:S(2)}, u32[]{:S(2)}) collective-permute-start(f32[12,32,128]{2,1,0:T(8,128)S(1)} %get-tuple-element.29), channel_id=1, source_target_pairs={{0,1},{1,0},{2,3},{3,2},{4,5},{5,4},{6,7},{7,6},{8,9},{9,8},{10,11... | collective-permute-start | bytes 589832 | tf_op jit(solution)/shard_map/ppermute | solution.py:820
  8.7 8.6 %collective-permute-start.4 = (f32[4,4,24,128]{3,2,1,0:T(8,128)S(1)}, f32[4,4,24,128]{3,2,1,0:T(8,128)S(1)}, u32[]{:S(2)}, u32[]{:S(2)}) collective-permute-start(f32[4,4,24,128]{3,2,1,0:T(8,128)S(1)} %get-tuple-element.37), channel_id=1, source_target_pairs={{0,1},{1,0},{2,3},{3,2},{4,5},{5,4},{6,7},{7,6},{8,9},{9,8},{10,11... | collective-permute-start | bytes 589832 | tf_op jit(solution)/shard_map/ppermute | solution.py:831
  10.7 6.6 %collective-permute-start.5 = (f32[4,4,24,128]{3,2,1,0:T(8,128)S(1)}, f32[4,4,24,128]{3,2,1,0:T(8,128)S(1)}, u32[]{:S(2)}, u32[]{:S(2)}) collective-permute-start(f32[4,4,24,128]{3,2,1,0:T(8,128)S(1)} %get-tuple-element.38), channel_id=1, source_target_pairs={{0,16},{1,2},{2,1},{3,4},{4,3},{5,6},{6,5},{7,8},{8,7},{9,10},{10,... | collective-permute-start | bytes 589832 | tf_op jit(solution)/shard_map/ppermute | solution.py:830
  13.8 10.4 %collective-permute-start.3 = (f32[4,8,8,128]{3,2,1,0:T(8,128)S(1)}, f32[4,8,8,128]{3,2,1,0:T(8,128)S(1)}, u32[]{:S(2)}, u32[]{:S(2)}) collective-permute-start(f32[4,8,8,128]{3,2,1,0:T(8,128)S(1)} %get-tuple-element.34.main), channel_id=1, source_target_pairs={{0,1},{1,0},{2,3},{3,2},{4,5},{5,4},{6,7},{7,6},{8,9},{9,8},{10,11... | collective-permute-start | bytes 393224 | tf_op jit(solution)/shard_map/ppermute | solution.py:840
  15.2 9.1 %collective-permute-start.2 = (f32[4,8,8,128]{3,2,1,0:T(8,128)S(1)}, f32[4,8,8,128]{3,2,1,0:T(8,128)S(1)}, u32[]{:S(2)}, u32[]{:S(2)}) collective-permute-start(f32[4,8,8,128]{3,2,1,0:T(8,128)S(1)} %get-tuple-element.34.main), channel_id=1, source_target_pairs={{0,16},{16,0},{32,48},{48,32},{64,80},{80,64},{96,112},{112,96},{1... | collective-permute-start | bytes 393224 | tf_op jit(solution)/shard_map/ppermute | solution.py:839
  19.6 4.6 %collective-permute-start.7 = (f32[4,4,8,128]{3,2,1,0:T(8,128)S(1)}, f32[4,4,8,128]{3,2,1,0:T(8,128)S(1)}, u32[]{:S(2)}, u32[]{:S(2)}) collective-permute-start(f32[4,4,8,128]{3,2,1,0:T(8,128)S(1)} %get-tuple-element.39.rim), channel_id=1, source_target_pairs={{0,1},{1,0},{2,3},{3,2},{4,5},{5,4},{6,7},{7,6},{8,9},{9,8},{10,11... | collective-permute-start | bytes 196616 | tf_op jit(solution)/shard_map/ppermute | solution.py:851
  21.7 4.4 %collective-permute-start.6 = (f32[4,4,8,128]{3,2,1,0:T(8,128)S(1)}, f32[4,4,8,128]{3,2,1,0:T(8,128)S(1)}, u32[]{:S(2)}, u32[]{:S(2)}) collective-permute-start(f32[4,4,8,128]{3,2,1,0:T(8,128)S(1)} %get-tuple-element.39.rim), channel_id=1, source_target_pairs={{0,16},{16,0},{32,48},{48,32},{64,80},{80,64},{96,112},{112,96},{1... | collective-permute-start | bytes 196616 | tf_op jit(solution)/shard_map/ppermute | solution.py:850
  56.1 4.5 %collective-permute-start.8 = (f32[128,4,128]{2,1,0:T(4,128)S(1)}, f32[128,4,128]{2,1,0:T(4,128)S(1)}, u32[]{:S(2)}, u32[]{:S(2)}) collective-permute-start(f32[128,4,128]{2,1,0:T(4,128)S(1)} %all_to_all.5), channel_id=1, source_target_pairs={{0,1},{1,0},{2,3},{3,2},{4,5},{5,4},{6,7},{7,6},{8,9},{9,8},{10,11... | collective-permute-start | bytes 786440 | tf_op jit(solution)/shard_map/ppermute | solution.py:865

commit v12 on v11

--- a/solution.py
+++ b/solution.py
@@ -481,7 +481,7 @@
 def middle_kernel(
     main, main_near, main_far, rim, rim_near, rim_far, sent, e_one, e_two,
     share, rest, rhs, first, second, weights, diags, halves, pooled,
-    rest2, first2, second2, rhs2, share2, weights2,
+    rest2, first2, second2, rhs2, share2, weights2, placed,
 ):
     gx, gy = lax.axis_index("gx"), lax.axis_index("gy")
     low_x, high_x = jnp.where(gx > 0, 1, 0), jnp.where(gx < NX - 1, 1, 0)
@@ -498,22 +498,27 @@
     near_row, far_row = jnp.where(even, 16, 0), jnp.where(even, 0, 16)
     starts = (pl.multiple_of(near_row, 8), pl.multiple_of(far_row, 8), 8)
 
-    sources = zip(starts, ((main_near, rim_near), (main_far, rim_far), (main, rim)))
-    sources = list(sources)
     has_far = inner(gx)
+    source, target = iota((128, 128), 0), iota((128, 128), 1)
+    rims = [rim_near[...].reshape(128, 128), jnp.where(has_far, rim_far[...].reshape(128, 128), 0.0)]
+    rims = jnp.concatenate(rims + [rim[...].reshape(128, 128)], axis=0)
+    for odd in range(2):
+        for half in range(2):
+            spot = source - (64 * odd + 32 * half)
+            to = jnp.where(spot < 9, 62 + spot, (112 + spot) % 128)
+            put = jnp.where((spot >= 0) & (spot < 18) & (to == target), 1.0, 0.0)
+            placed[odd, half] = dot_exact(rims, put).reshape(3, 4, 4, 8, 128)
 
     def fill(q):
         for odd in range(2):
             for half in range(2):
                 z = 2 * q + odd + 8 * half
-                base = 64 * odd + 32 * half
-                for at, (middle, outer) in sources:
+                for i, (at, middle) in enumerate(zip(starts, (main_near, main_far, main))):
                     for ch in range(4):
-                        edge, body = outer[ch, q], middle[ch, 2 * q + odd]
-                        if outer is rim_far:
-                            edge, body = jnp.where(has_far, edge, 0.0), jnp.where(has_far, body, 0.0)
-                        value = jnp.where(lane < 62, roll(body, 64 * half), roll(edge, 62 - base))
-                        value = jnp.where((lane >= 96) | (lane < 2), roll(edge, 112 - base), value)
+                        body = roll(middle[ch, 2 * q + odd], 64 * half)
+                        if i == 1:
+                            body = jnp.where(has_far, body, 0.0)
+                        value = jnp.where((lane >= 2) & (lane < 62), body, placed[odd, half, i, ch, q])
                         if ch < 3:
                             rhs[ch, z, pl.ds(at, 8), :] = value
                         else:
@@ -766,28 +771,30 @@
         values = [
             [(0.2 * values[f][z] + begin[f][z]) + around(values[f], z) for z in range(2)] for f in range(3)
         ]
+    shifts = []
     for f in range(3):
         change = [(begin[f][z] - 0.8 * values[f][z]) + around(values[f], z) for z in range(2)]
-        total = jnp.sum(1.25 * (change[0] * ds[0] + change[1] * ds[1]), keepdims=True)
+        shifts.append(jnp.sum(1.25 * (change[0] * ds[0] + change[1] * ds[1]), keepdims=True) / whole)
         for z in range(2):
-            four[2 * f + z] = values[f][z] + total / whole
-
-    copy = jnp.where(iota((128, 128), 0) == iota((128, 128), 1) // 2, 1.0, 0.0)
+            four[2 * f + z] = values[f][z]
+
     rows = four.reshape(96, 128)[pl.ds(gx, 6, stride=16), :]
-    rows = jnp.concatenate([jnp.broadcast_to(rows[i : i + 1], (4, 128)) for i in range(6)], axis=0)
-    three = dot(turn(rows, -8 * gy), copy)
+    upper = jnp.concatenate([jnp.broadcast_to(rows[i : i + 1], (4, 128)) for i in range(6)], axis=0)
     flat = second.reshape(768, 128)
     halves = [flat[pl.ds(gx + 384 * half, 24, stride=16), :] for half in range(2)]
-    three = three + turn(jnp.where(first_core, halves[0], halves[1]), -16 * lax.div(gy, 2))
-
-    copy = jnp.where(iota((128, 128), 0) == iota((128, 128), 1) // 8, 1.0, 0.0)
-    three = dot(three, copy)
+    three = turn(jnp.where(first_core, halves[0], halves[1]), -16 * lax.div(gy, 2))
+    both = jnp.concatenate([turn(upper, -8 * gy), three], axis=1)
+    both = jnp.concatenate([both, jnp.zeros((8, 256), F32)], axis=0)
+    source, target = iota((256, 128), 0), iota((256, 128), 1)
+    copy = jnp.where(source == jnp.where(source < 128, target // 16, 128 + target // 8), 1.0, 0.0)
+    three = dot_exact(both, copy)
+
     copies = []
     for f in range(3):
         for z in range(4):
             for x in range(2):
                 at = f * 8 + z * 2 + x
-                value = jnp.broadcast_to(three[at : at + 1], (8, 128))
+                value = jnp.broadcast_to(three[at : at + 1] + shifts[f], (8, 128))
                 for k in range(8 * z, 8 * z + 8):
                     final[f, k, 8 * x : 8 * x + 8, :] = base[f, k, 8 * x : 8 * x + 8, :] + value
             if z % 2 == 1:
@@ -855,7 +862,7 @@
         [(16, 24, 128), (18, 32, 128), (3, 16, 32, 128), (3, 18, 32, 128), (3, 18, 32, 128)]
         + [(6, 16, 32, 128), (16, 32, 128), (4, 8, 24, 128), (768, 128)]
         + [(10, 24, 128), (3, 10, 24, 128), (3, 10, 24, 128), (3, 8, 8, 128), (8, 8, 128)]
-        + [(7, 8, 16, 128)],
+        + [(7, 8, 16, 128), (2, 2, 3, 4, 4, 8, 128)],
     )(main, main_near, main_far, rim_one, rim_near, rim_far)
     groups = [[i for i in range(NX * NY) if i % 2 == core] for core in range(2)]
     mine = lax.all_to_all(

time: 65.3 us -> 65 us (level)
  no operation moved by 1% of the time
where the time goes in v12:
time: 65 us; the launch traced here: 64.9 us
  blocking collectives  27.6 us (42%)
  starting transfers between devices  17.6 us (27%)
  Pallas kernels  17.4 us (27%)
  waiting for transfers between devices  2.14 us (3%)
    all_to_all x1, blocking collectives, local(): lax.all_to_all(sent, ('gx', 'gy'), split_axis=0, concat_axis=0, axis_inde...  27.6 us
    pallas_call x1, Pallas kernels, local(): call(top_kernel, [(3, 32, 16, 128)], [(4, 2, 128, 128), (3, 16, 16, 128),...  4 us
    pallas_call x1, Pallas kernels, local(): call(own_kernel, [(3, 34, 32, 128)] * 2 + [(4, 16, 16, 128)] + [(4, 4, 16...  3.66 us
    ppermute x1, starting transfers between devices, local(): other = lax.ppermute(mine, 'gy', swap_near)  3.3 us
    pallas_call x1, Pallas kernels, local(): call(middle_kernel, [(CHIPS, 4, 128), (3, 16, 8, 128), (3, 8, 8, 128)], [...  2.59 us
    ppermute x1, starting transfers between devices, local(): rim_near = lax.ppermute(rim_one, 'gx', swap_near)  2.56 us
    pallas_call x1, Pallas kernels, local(): call(rim_kernel, [(3, 16, 16, 128), (4, 4, 8, 128)], [(3, 18, 32, 128), (...  2.39 us
    pallas_call x1, Pallas kernels, local(): call(rows_edge_kernel, [(3, 34, 24, 128), (4, 8, 8, 128), (4, 16, 8, 128)...  2.3 us
  transfers between devices with their start and end apart: 9, of which 2 were waited for; matrix products, arithmetic and copies ran while one was open for 0% of the time, Pallas kernels for 14%

profile of v12, /device:TPU:1, one launch (start us, length us, event | category | flops | bytes accessed | tf_op | source)
XLA Modules:
  0.0 64.9 jit_solution(10338795664272417593)
XLA Ops:
  0.0 1.3 %shard_map.28 = (f32[12,32,128]{2,1,0:T(8,128)S(1)}, f32[12,32,128]{2,1,0:T(8,128)S(1)}, f32[4,32,16,128]{3,2,1,0:T(8,128)S(1)}) custom-call(f32[3,32,16,128]{3,2,1,0:T(8,128)} %guess.1, s32[32,16,128]{2,1,0:T(8,128)} %labels.1), custom_call_target="tpu_custom_call" | custom-call | flops 1000000 | bytes 4000000 | tf_op jit(solution)/shard_map/pallas_call | solution.py:820
  1.3 2.1 %collective-permute-start = (f32[12,32,128]{2,1,0:T(8,128)S(1)}, f32[12,32,128]{2,1,0:T(8,128)S(1)}, u32[]{:S(2)}, u32[]{:S(2)}) collective-permute-start(f32[12,32,128]{2,1,0:T(8,128)S(1)} %get-tuple-element.28), channel_id=1, source_target_pairs={{0,16},{16,0},{32,48},{48,32},{64,80},{80,64},{96,112},{112,96},{1... | collective-permute-start | bytes 589832 | tf_op jit(solution)/shard_map/ppermute | solution.py:826
  3.4 1.3 %collective-permute-start.1 = (f32[12,32,128]{2,1,0:T(8,128)S(1)}, f32[12,32,128]{2,1,0:T(8,128)S(1)}, u32[]{:S(2)}, u32[]{:S(2)}) collective-permute-start(f32[12,32,128]{2,1,0:T(8,128)S(1)} %get-tuple-element.29), channel_id=1, source_target_pairs={{0,1},{1,0},{2,3},{3,2},{4,5},{5,4},{6,7},{7,6},{8,9},{9,8},{10,11... | collective-permute-start | bytes 589832 | tf_op jit(solution)/shard_map/ppermute | solution.py:827
  4.7 3.7 %shard_map.29 = (f32[3,34,32,128]{3,2,1,0:T(8,128)S(1)}, f32[3,34,32,128]{3,2,1,0:T(8,128)S(1)}, f32[4,16,16,128]{3,2,1,0:T(8,128)S(1)}, f32[4,4,16,128]{3,2,1,0...) custom-call(f32[4,32,16,128]{3,2,1,0:T(8,128)S(1)} %get-tuple-element.25.own), custom_call_target="tpu_custom_call" | custom-call | flops 20000000 | bytes 4000000 | tf_op jit(solution)/shard_map/pallas_call | solution.py:828
  8.4 0.0 collective-permute-done.x_near
  8.4 0.0 collective-permute-done.1.x_far
  8.4 0.3 shard_map.30
  8.7 2.0 %collective-permute-start.4 = (f32[4,4,24,128]{3,2,1,0:T(8,128)S(1)}, f32[4,4,24,128]{3,2,1,0:T(8,128)S(1)}, u32[]{:S(2)}, u32[]{:S(2)}) collective-permute-start(f32[4,4,24,128]{3,2,1,0:T(8,128)S(1)} %get-tuple-element.37), channel_id=1, source_target_pairs={{0,1},{1,0},{2,3},{3,2},{4,5},{5,4},{6,7},{7,6},{8,9},{9,8},{10,11... | collective-permute-start | bytes 589832 | tf_op jit(solution)/shard_map/ppermute | solution.py:838
  10.7 0.9 %collective-permute-start.5 = (f32[4,4,24,128]{3,2,1,0:T(8,128)S(1)}, f32[4,4,24,128]{3,2,1,0:T(8,128)S(1)}, u32[]{:S(2)}, u32[]{:S(2)}) collective-permute-start(f32[4,4,24,128]{3,2,1,0:T(8,128)S(1)} %get-tuple-element.38), channel_id=1, source_target_pairs={{0,16},{1,2},{2,1},{3,4},{4,3},{5,6},{6,5},{7,8},{8,7},{9,10},{10,... | collective-permute-start | bytes 589832 | tf_op jit(solution)/shard_map/ppermute | solution.py:837
  11.5 2.3 %shard_map.31 = (f32[3,34,24,128]{3,2,1,0:T(8,128)S(1)}, f32[4,8,8,128]{3,2,1,0:T(8,128)S(1)}, f32[4,16,8,128]{3,2,1,0:T(8,128)S(1)}) custom-call(f32[4,32,16,128]{3,2,1,0:T(8,128)S(1)} %get-tuple-element.25.own, f32[4,32,8,128]{3,2,1,0:T(8,128)S(1)} %get-tuple-element.30.rim, f32[3,34,32,128]{3,2,1,0:T(8,128)S(1)} %get-tuple-element.31.own_one, ...), custom_call_target="tpu_custom_call" | custom-call | flops 10000000 | bytes 4000000 | tf_op jit(solution)/shard_map/pallas_call | solution.py:839
  13.8 1.4 %collective-permute-start.3 = (f32[4,8,8,128]{3,2,1,0:T(8,128)S(1)}, f32[4,8,8,128]{3,2,1,0:T(8,128)S(1)}, u32[]{:S(2)}, u32[]{:S(2)}) collective-permute-start(f32[4,8,8,128]{3,2,1,0:T(8,128)S(1)} %get-tuple-element.34.main), channel_id=1, source_target_pairs={{0,1},{1,0},{2,3},{3,2},{4,5},{5,4},{6,7},{7,6},{8,9},{9,8},{10,11... | collective-permute-start | bytes 393224 | tf_op jit(solution)/shard_map/ppermute | solution.py:847
  15.2 2.1 %collective-permute-start.2 = (f32[4,8,8,128]{3,2,1,0:T(8,128)S(1)}, f32[4,8,8,128]{3,2,1,0:T(8,128)S(1)}, u32[]{:S(2)}, u32[]{:S(2)}) collective-permute-start(f32[4,8,8,128]{3,2,1,0:T(8,128)S(1)} %get-tuple-element.34.main), channel_id=1, source_target_pairs={{0,16},{16,0},{32,48},{48,32},{64,80},{80,64},{96,112},{112,96},{1... | collective-permute-start | bytes 393224 | tf_op jit(solution)/shard_map/ppermute | solution.py:846
  17.3 0.0 collective-permute-done.4.near
  17.3 0.0 collective-permute-done.5.far
  17.3 2.4 %shard_map.32 = (f32[3,16,16,128]{3,2,1,0:T(8,128)S(1)}, f32[4,4,8,128]{3,2,1,0:T(8,128)S(1)}) custom-call(f32[4,16,16,128]{3,2,1,0:T(8,128)S(1)} %get-tuple-element.35.edges, f32[4,16,8,128]{3,2,1,0:T(8,128)S(1)} %get-tuple-element.36.edges_rim, f32[4,4,24,128]{3,2,1,0:T(8,128)S(1)} %collective-permute-done.4.near, ...), custom_call_target="tpu_custom_call" | custom-call | flops 10000000 | bytes 4000000 | tf_op jit(solution)/shard_map/pallas_call | solution.py:848
  19.6 2.1 %collective-permute-start.7 = (f32[4,4,8,128]{3,2,1,0:T(8,128)S(1)}, f32[4,4,8,128]{3,2,1,0:T(8,128)S(1)}, u32[]{:S(2)}, u32[]{:S(2)}) collective-permute-start(f32[4,4,8,128]{3,2,1,0:T(8,128)S(1)} %get-tuple-element.39.rim), channel_id=1, source_target_pairs={{0,1},{1,0},{2,3},{3,2},{4,5},{5,4},{6,7},{7,6},{8,9},{9,8},{10,11... | collective-permute-start | bytes 196616 | tf_op jit(solution)/shard_map/ppermute | solution.py:858
  21.7 2.6 %collective-permute-start.6 = (f32[4,4,8,128]{3,2,1,0:T(8,128)S(1)}, f32[4,4,8,128]{3,2,1,0:T(8,128)S(1)}, u32[]{:S(2)}, u32[]{:S(2)}) collective-permute-start(f32[4,4,8,128]{3,2,1,0:T(8,128)S(1)} %get-tuple-element.39.rim), channel_id=1, source_target_pairs={{0,16},{16,0},{32,48},{48,32},{64,80},{80,64},{96,112},{112,96},{1... | collective-permute-start | bytes 196616 | tf_op jit(solution)/shard_map/ppermute | solution.py:857
  24.3 0.0 collective-permute-done.3.main_far
  24.3 0.0 collective-permute-done.2.main_near
  24.3 0.0 collective-permute-done.7.rim_far
  24.3 1.9 %collective-permute-done.6.rim_near = f32[4,4,8,128]{3,2,1,0:T(8,128)S(1)} collective-permute-done((f32[4,4,8,128]{3,2,1,0:T(8,128)S(1)}, f32[4,4,8,128]{3,2,1,0:T(8,128)S(1)}, u32[]{:S(2)}, u32[]{:S(2)}) %collective-permute-start.6) | collective-permute-done | bytes 65568 | tf_op jit(solution)/shard_map/ppermute | solution.py:857
  26.1 2.6 %shard_map.33 = (f32[128,4,128]{2,1,0:T(4,128)S(1)}, f32[3,16,8,128]{3,2,1,0:T(8,128)S(1)}, f32[3,8,8,128]{3,2,1,0:T(8,128)S(1)}) custom-call(f32[4,8,8,128]{3,2,1,0:T(8,128)S(1)} %get-tuple-element.34.main, f32[4,8,8,128]{3,2,1,0:T(8,128)S(1)} %collective-permute-done.2.main_near, f32[4,8,8,128]{3,2,1,0:T(8,128)S(1)} %collective-permute-done.3.main_far, ...), custom_call_target="tpu_custom_call" | custom-call | flops 1000000 | bytes 4000000 | tf_op jit(solution)/shard_map/pallas_call | solution.py:859
  28.7 27.6 %all_to_all.5 = f32[128,4,128]{2,1,0:T(4,128)S(1)} all-to-all(f32[128,4,128]{2,1,0:T(4,128)S(1)} %get-tuple-element.40), channel_id=1, replica_groups={{0,2,4,6,8,10,12,14,16,18,20,22,24,26,28,30,32,34,36,38,40,42,44,46,48,..., dimensions={0} | all-to-all | bytes 524288 | tf_op jit(solution)/shard_map/all_to_all | solution.py:868
  56.3 3.3 %collective-permute-start.8 = (f32[128,4,128]{2,1,0:T(4,128)S(1)}, f32[128,4,128]{2,1,0:T(4,128)S(1)}, u32[]{:S(2)}, u32[]{:S(2)}) collective-permute-start(f32[128,4,128]{2,1,0:T(4,128)S(1)} %all_to_all.5), channel_id=1, source_target_pairs={{0,1},{1,0},{2,3},{3,2},{4,5},{5,4},{6,7},{7,6},{8,9},{9,8},{10,11... | collective-permute-start | bytes 786440 | tf_op jit(solution)/shard_map/ppermute | solution.py:872
  59.6 0.9 %shard_map.34.base = f32[3,32,16,128]{3,2,1,0:T(8,128)S(1)} custom-call(f32[3,34,24,128]{3,2,1,0:T(8,128)S(1)} %get-tuple-element.41.two, f32[3,16,16,128]{3,2,1,0:T(8,128)S(1)} %get-tuple-element.42.rim, f32[3,16,8,128]{3,2,1,0:T(8,128)S(1)} %get-tuple-element.43.e_one, f32[3,8,8,128]{3,2,1,0:T(8,128)S(1)} %get-tuple-element.44.e_two), custom_call_target="tpu_custom_call" | custom-call | flops 1000000 | bytes 4000000 | tf_op jit(solution)/shard_map/pallas_call | solution.py:871
  60.5 0.3 collective-permute-done.8
  60.7 4.0 %shard_map.35 = f32[3,32,16,128]{3,2,1,0:T(8,128)} custom-call(f32[512,128]{1,0:T(8,128)S(1)} %bitcast.2, f32[512,128]{1,0:T(8,128)S(1)} %bitcast.3, f32[3,32,16,128]{3,2,1,0:T(8,128)S(1)} %shard_map.34.base), custom_call_target="tpu_custom_call" | custom-call | flops 1000000 | bytes 4000000 | tf_op jit(solution)/shard_map/pallas_call | solution.py:873
Async XLA Ops:
  1.3 7.1 %collective-permute-start = (f32[12,32,128]{2,1,0:T(8,128)S(1)}, f32[12,32,128]{2,1,0:T(8,128)S(1)}, u32[]{:S(2)}, u32[]{:S(2)}) collective-permute-start(f32[12,32,128]{2,1,0:T(8,128)S(1)} %get-tuple-element.28), channel_id=1, source_target_pairs={{0,16},{16,0},{32,48},{48,32},{64,80},{80,64},{96,112},{112,96},{1... | collective-permute-start | bytes 589832 | tf_op jit(solution)/shard_map/ppermute | solution.py:826
  3.4 5.0 %collective-permute-start.1 = (f32[12,32,128]{2,1,0:T(8,128)S(1)}, f32[12,32,128]{2,1,0:T(8,128)S(1)}, u32[]{:S(2)}, u32[]{:S(2)}) collective-permute-start(f32[12,32,128]{2,1,0:T(8,128)S(1)} %get-tuple-element.29), channel_id=1, source_target_pairs={{0,1},{1,0},{2,3},{3,2},{4,5},{5,4},{6,7},{7,6},{8,9},{9,8},{10,11... | collective-permute-start | bytes 589832 | tf_op jit(solution)/shard_map/ppermute | solution.py:827
  8.7 8.6 %collective-permute-start.4 = (f32[4,4,24,128]{3,2,1,0:T(8,128)S(1)}, f32[4,4,24,128]{3,2,1,0:T(8,128)S(1)}, u32[]{:S(2)}, u32[]{:S(2)}) collective-permute-start(f32[4,4,24,128]{3,2,1,0:T(8,128)S(1)} %get-tuple-element.37), channel_id=1, source_target_pairs={{0,1},{1,0},{2,3},{3,2},{4,5},{5,4},{6,7},{7,6},{8,9},{9,8},{10,11... | collective-permute-start | bytes 589832 | tf_op jit(solution)/shard_map/ppermute | solution.py:838
  10.7 6.6 %collective-permute-start.5 = (f32[4,4,24,128]{3,2,1,0:T(8,128)S(1)}, f32[4,4,24,128]{3,2,1,0:T(8,128)S(1)}, u32[]{:S(2)}, u32[]{:S(2)}) collective-permute-start(f32[4,4,24,128]{3,2,1,0:T(8,128)S(1)} %get-tuple-element.38), channel_id=1, source_target_pairs={{0,16},{1,2},{2,1},{3,4},{4,3},{5,6},{6,5},{7,8},{8,7},{9,10},{10,... | collective-permute-start | bytes 589832 | tf_op jit(solution)/shard_map/ppermute | solution.py:837
  13.8 10.4 %collective-permute-start.3 = (f32[4,8,8,128]{3,2,1,0:T(8,128)S(1)}, f32[4,8,8,128]{3,2,1,0:T(8,128)S(1)}, u32[]{:S(2)}, u32[]{:S(2)}) collective-permute-start(f32[4,8,8,128]{3,2,1,0:T(8,128)S(1)} %get-tuple-element.34.main), channel_id=1, source_target_pairs={{0,1},{1,0},{2,3},{3,2},{4,5},{5,4},{6,7},{7,6},{8,9},{9,8},{10,11... | collective-permute-start | bytes 393224 | tf_op jit(solution)/shard_map/ppermute | solution.py:847
  15.2 9.1 %collective-permute-start.2 = (f32[4,8,8,128]{3,2,1,0:T(8,128)S(1)}, f32[4,8,8,128]{3,2,1,0:T(8,128)S(1)}, u32[]{:S(2)}, u32[]{:S(2)}) collective-permute-start(f32[4,8,8,128]{3,2,1,0:T(8,128)S(1)} %get-tuple-element.34.main), channel_id=1, source_target_pairs={{0,16},{16,0},{32,48},{48,32},{64,80},{80,64},{96,112},{112,96},{1... | collective-permute-start | bytes 393224 | tf_op jit(solution)/shard_map/ppermute | solution.py:846
  19.6 4.6 %collective-permute-start.7 = (f32[4,4,8,128]{3,2,1,0:T(8,128)S(1)}, f32[4,4,8,128]{3,2,1,0:T(8,128)S(1)}, u32[]{:S(2)}, u32[]{:S(2)}) collective-permute-start(f32[4,4,8,128]{3,2,1,0:T(8,128)S(1)} %get-tuple-element.39.rim), channel_id=1, source_target_pairs={{0,1},{1,0},{2,3},{3,2},{4,5},{5,4},{6,7},{7,6},{8,9},{9,8},{10,11... | collective-permute-start | bytes 196616 | tf_op jit(solution)/shard_map/ppermute | solution.py:858
  21.7 4.4 %collective-permute-start.6 = (f32[4,4,8,128]{3,2,1,0:T(8,128)S(1)}, f32[4,4,8,128]{3,2,1,0:T(8,128)S(1)}, u32[]{:S(2)}, u32[]{:S(2)}) collective-permute-start(f32[4,4,8,128]{3,2,1,0:T(8,128)S(1)} %get-tuple-element.39.rim), channel_id=1, source_target_pairs={{0,16},{16,0},{32,48},{48,32},{64,80},{80,64},{96,112},{112,96},{1... | collective-permute-start | bytes 196616 | tf_op jit(solution)/shard_map/ppermute | solution.py:857
  56.3 4.5 %collective-permute-start.8 = (f32[128,4,128]{2,1,0:T(4,128)S(1)}, f32[128,4,128]{2,1,0:T(4,128)S(1)}, u32[]{:S(2)}, u32[]{:S(2)}) collective-permute-start(f32[128,4,128]{2,1,0:T(4,128)S(1)} %all_to_all.5), channel_id=1, source_target_pairs={{0,1},{1,0},{2,3},{3,2},{4,5},{5,4},{6,7},{7,6},{8,9},{9,8},{10,11... | collective-permute-start | bytes 786440 | tf_op jit(solution)/shard_map/ppermute | solution.py:872

commit v13 on v11

--- a/solution.py
+++ b/solution.py
@@ -11,10 +11,6 @@
 STEP, WIDE = 16, 32
 BETWEEN = 2.0 * 0.1 / 1.1
 ANY = pl.BlockSpec(memory_space=pltpu.HBM)
-
-
-def dot(a, b):
-    return jnp.dot(a, b, precision=lax.Precision.HIGHEST, preferred_element_type=F32)
 
 
 def dot_exact(a, b):
@@ -619,7 +615,7 @@
 
     pool = jnp.where((source < 32) & (source // 2 == target % 16), 0.125, 0.0)
     rows = jnp.concatenate([parts[pair][ch] for ch in range(4) for pair in range(4)], axis=0)
-    spread = dot(rows, pool)
+    spread = dot_exact(rows, pool)
     at, to = iota((32, 128), 0), iota((32, 128), 1)
     keep = (at // 8 == to // 32) & ((at % 8) // 2 == (to // 16) % 2)
     result = jnp.concatenate(
@@ -643,6 +639,15 @@
     return x
 
 
+def lay_kernel(mine, laid):
+    def lay(g):
+        for ch in range(4):
+            tile = swap_blocks(mine[pl.ds(32 * g + ch, 8, stride=4), :])
+            laid[ch, pl.ds(pl.multiple_of(8 * g, 8), 8), :] = tile
+
+    loop(16, lay, 4)
+
+
 def top_kernel(
     mine, other, base, out,
     natural, first, second, four, weights, diags, lefts, final, sems,
@@ -652,16 +657,13 @@
     lane, sub = iota((16, 128), 1), iota((16, 128), 0)
     cells = [(z, x, half) for z in range(4) for x in range(2) for half in range(2)]
 
+    parity = lax.rem(gy, 2)
+
     def lay(g):
         for ch in range(4):
-            rows = pl.ds(32 * g + ch, 8, stride=4)
-            pair = mine[rows, :], other[rows, :]
-            natural[ch, 0, pl.ds(pl.multiple_of(8 * g, 8), 8), :] = swap_blocks(
-                jnp.where(first_core, pair[0], pair[1])
-            )
-            natural[ch, 1, pl.ds(pl.multiple_of(8 * g, 8), 8), :] = swap_blocks(
-                jnp.where(first_core, pair[1], pair[0])
-            )
+            at = pl.ds(pl.multiple_of(8 * g, 8), 8)
+            natural[ch, parity, at, :] = mine[ch, at, :]
+            natural[ch, 1 - parity, at, :] = swap_blocks(other[pl.ds(32 * g + ch, 8, stride=4), :])
 
     loop(16, lay, 4)
     flat = natural.reshape(1024, 128)
@@ -766,28 +768,30 @@
         values = [
             [(0.2 * values[f][z] + begin[f][z]) + around(values[f], z) for z in range(2)] for f in range(3)
         ]
+    shifts = []
     for f in range(3):
         change = [(begin[f][z] - 0.8 * values[f][z]) + around(values[f], z) for z in range(2)]
-        total = jnp.sum(1.25 * (change[0] * ds[0] + change[1] * ds[1]), keepdims=True)
+        shifts.append(jnp.sum(1.25 * (change[0] * ds[0] + change[1] * ds[1]), keepdims=True) / whole)
         for z in range(2):
-            four[2 * f + z] = values[f][z] + total / whole
-
-    copy = jnp.where(iota((128, 128), 0) == iota((128, 128), 1) // 2, 1.0, 0.0)
+            four[2 * f + z] = values[f][z]
+
     rows = four.reshape(96, 128)[pl.ds(gx, 6, stride=16), :]
-    rows = jnp.concatenate([jnp.broadcast_to(rows[i : i + 1], (4, 128)) for i in range(6)], axis=0)
-    three = dot(turn(rows, -8 * gy), copy)
+    upper = jnp.concatenate([jnp.broadcast_to(rows[i : i + 1], (4, 128)) for i in range(6)], axis=0)
     flat = second.reshape(768, 128)
     halves = [flat[pl.ds(gx + 384 * half, 24, stride=16), :] for half in range(2)]
-    three = three + turn(jnp.where(first_core, halves[0], halves[1]), -16 * lax.div(gy, 2))
-
-    copy = jnp.where(iota((128, 128), 0) == iota((128, 128), 1) // 8, 1.0, 0.0)
-    three = dot(three, copy)
+    three = turn(jnp.where(first_core, halves[0], halves[1]), -16 * lax.div(gy, 2))
+    both = jnp.concatenate([turn(upper, -8 * gy), three], axis=1)
+    both = jnp.concatenate([both, jnp.zeros((8, 256), F32)], axis=0)
+    source, target = iota((256, 128), 0), iota((256, 128), 1)
+    copy = jnp.where(source == jnp.where(source < 128, target // 16, 128 + target // 8), 1.0, 0.0)
+    three = dot_exact(both, copy)
+
     copies = []
     for f in range(3):
         for z in range(4):
             for x in range(2):
                 at = f * 8 + z * 2 + x
-                value = jnp.broadcast_to(three[at : at + 1], (8, 128))
+                value = jnp.broadcast_to(three[at : at + 1] + shifts[f], (8, 128))
                 for k in range(8 * z, 8 * z + 8):
                     final[f, k, 8 * x : 8 * x + 8, :] = base[f, k, 8 * x : 8 * x + 8, :] + value
             if z % 2 == 1:
@@ -863,13 +867,14 @@
     )
     (base,) = call(base_kernel, [(3, 32, 16, 128)], [(192, 128), (3, 16, 16, 128)])(two, rim, e_one, e_two)
     other = lax.ppermute(mine, "gy", swap_near)
+    (laid,) = call(lay_kernel, [(4, 128, 128)], [])(mine.reshape(512, 128))
     (out,) = call(
         top_kernel,
         [(3, 32, 16, 128)],
         [(4, 2, 128, 128), (3, 16, 16, 128), (2, 3, 8, 16, 128), (6, 16, 128), (6, 16, 16, 128)]
         + [(16, 16, 128), (4, 2, 16, 256), (3, 32, 16, 128), pltpu.SemaphoreType.DMA((6,))],
         out_specs=[ANY],
-    )(mine.reshape(512, 128), other.reshape(512, 128), base)
+    )(laid, other.reshape(512, 128), base)
     return out
 
 

time: 65.3 us -> 65.4 us (level)
    pallas_call x0 -> x1, Pallas kernels: none -> 0.96 us  [local(): laid, = call(lay_kernel, [(4, 128, 128)], [])(mine.reshape(512, 128))]
  transfers between devices with their start and end apart: 9 -> 9, of which waited for: 2 -> 1; matrix products, arithmetic and copies ran while one was open for 0% -> 0% of each run, Pallas kernels for 14% -> 16%
where the time goes in v13:
time: 65.4 us; the launch traced here: 65.3 us
  blocking collectives  27.5 us (42%)
  Pallas kernels  18 us (28%)
  starting transfers between devices  17.6 us (27%)
  waiting for transfers between devices  1.88 us (3%)
    all_to_all x1, blocking collectives, local(): lax.all_to_all(sent, ('gx', 'gy'), split_axis=0, concat_axis=0, axis_inde...  27.5 us
    pallas_call x1, Pallas kernels, local(): call(top_kernel, [(3, 32, 16, 128)], [(4, 2, 128, 128), (3, 16, 16, 128),...  3.88 us
    pallas_call x1, Pallas kernels, local(): call(own_kernel, [(3, 34, 32, 128)] * 2 + [(4, 16, 16, 128)] + [(4, 4, 16...  3.66 us
    ppermute x1, starting transfers between devices, local(): other = lax.ppermute(mine, 'gy', swap_near)  3.3 us
    ppermute x1, starting transfers between devices, local(): rim_near = lax.ppermute(rim_one, 'gx', swap_near)  2.56 us
    pallas_call x1, Pallas kernels, local(): call(rim_kernel, [(3, 16, 16, 128), (4, 4, 8, 128)], [(3, 18, 32, 128), (...  2.39 us
    pallas_call x1, Pallas kernels, local(): call(middle_kernel, [(CHIPS, 4, 128), (3, 16, 8, 128), (3, 8, 8, 128)], [...  2.38 us
    pallas_call x1, Pallas kernels, local(): call(rows_edge_kernel, [(3, 34, 24, 128), (4, 8, 8, 128), (4, 16, 8, 128)...  2.3 us
  transfers between devices with their start and end apart: 9, of which 1 were waited for; matrix products, arithmetic and copies ran while one was open for 0% of the time, Pallas kernels for 16%

profile of v13, /device:TPU:1, one launch (start us, length us, event | category | flops | bytes accessed | tf_op | source)
XLA Modules:
  0.0 65.3 jit_solution(9537602208111996487)
XLA Ops:
  0.0 1.3 %shard_map.28 = (f32[12,32,128]{2,1,0:T(8,128)S(1)}, f32[12,32,128]{2,1,0:T(8,128)S(1)}, f32[4,32,16,128]{3,2,1,0:T(8,128)S(1)}) custom-call(f32[3,32,16,128]{3,2,1,0:T(8,128)} %guess.1, s32[32,16,128]{2,1,0:T(8,128)} %labels.1), custom_call_target="tpu_custom_call" | custom-call | flops 1000000 | bytes 4000000 | tf_op jit(solution)/shard_map/pallas_call | solution.py:817
  1.3 2.1 %collective-permute-start = (f32[12,32,128]{2,1,0:T(8,128)S(1)}, f32[12,32,128]{2,1,0:T(8,128)S(1)}, u32[]{:S(2)}, u32[]{:S(2)}) collective-permute-start(f32[12,32,128]{2,1,0:T(8,128)S(1)} %get-tuple-element.28), channel_id=1, source_target_pairs={{0,16},{16,0},{32,48},{48,32},{64,80},{80,64},{96,112},{112,96},{1... | collective-permute-start | bytes 589832 | tf_op jit(solution)/shard_map/ppermute | solution.py:823
  3.4 1.3 %collective-permute-start.1 = (f32[12,32,128]{2,1,0:T(8,128)S(1)}, f32[12,32,128]{2,1,0:T(8,128)S(1)}, u32[]{:S(2)}, u32[]{:S(2)}) collective-permute-start(f32[12,32,128]{2,1,0:T(8,128)S(1)} %get-tuple-element.29), channel_id=1, source_target_pairs={{0,1},{1,0},{2,3},{3,2},{4,5},{5,4},{6,7},{7,6},{8,9},{9,8},{10,11... | collective-permute-start | bytes 589832 | tf_op jit(solution)/shard_map/ppermute | solution.py:824
  4.7 3.7 %shard_map.29 = (f32[3,34,32,128]{3,2,1,0:T(8,128)S(1)}, f32[3,34,32,128]{3,2,1,0:T(8,128)S(1)}, f32[4,16,16,128]{3,2,1,0:T(8,128)S(1)}, f32[4,4,16,128]{3,2,1,0...) custom-call(f32[4,32,16,128]{3,2,1,0:T(8,128)S(1)} %get-tuple-element.25.own), custom_call_target="tpu_custom_call" | custom-call | flops 20000000 | bytes 4000000 | tf_op jit(solution)/shard_map/pallas_call | solution.py:825
  8.4 0.0 collective-permute-done.x_near
  8.4 0.0 collective-permute-done.1.x_far
  8.4 0.3 shard_map.30
  8.7 2.0 %collective-permute-start.4 = (f32[4,4,24,128]{3,2,1,0:T(8,128)S(1)}, f32[4,4,24,128]{3,2,1,0:T(8,128)S(1)}, u32[]{:S(2)}, u32[]{:S(2)}) collective-permute-start(f32[4,4,24,128]{3,2,1,0:T(8,128)S(1)} %get-tuple-element.37), channel_id=1, source_target_pairs={{0,1},{1,0},{2,3},{3,2},{4,5},{5,4},{6,7},{7,6},{8,9},{9,8},{10,11... | collective-permute-start | bytes 589832 | tf_op jit(solution)/shard_map/ppermute | solution.py:835
  10.7 0.9 %collective-permute-start.5 = (f32[4,4,24,128]{3,2,1,0:T(8,128)S(1)}, f32[4,4,24,128]{3,2,1,0:T(8,128)S(1)}, u32[]{:S(2)}, u32[]{:S(2)}) collective-permute-start(f32[4,4,24,128]{3,2,1,0:T(8,128)S(1)} %get-tuple-element.38), channel_id=1, source_target_pairs={{0,16},{1,2},{2,1},{3,4},{4,3},{5,6},{6,5},{7,8},{8,7},{9,10},{10,... | collective-permute-start | bytes 589832 | tf_op jit(solution)/shard_map/ppermute | solution.py:834
  11.5 2.3 %shard_map.31 = (f32[3,34,24,128]{3,2,1,0:T(8,128)S(1)}, f32[4,8,8,128]{3,2,1,0:T(8,128)S(1)}, f32[4,16,8,128]{3,2,1,0:T(8,128)S(1)}) custom-call(f32[4,32,16,128]{3,2,1,0:T(8,128)S(1)} %get-tuple-element.25.own, f32[4,32,8,128]{3,2,1,0:T(8,128)S(1)} %get-tuple-element.30.rim, f32[3,34,32,128]{3,2,1,0:T(8,128)S(1)} %get-tuple-element.31.own_one, ...), custom_call_target="tpu_custom_call" | custom-call | flops 10000000 | bytes 4000000 | tf_op jit(solution)/shard_map/pallas_call | solution.py:836
  13.8 1.4 %collective-permute-start.3 = (f32[4,8,8,128]{3,2,1,0:T(8,128)S(1)}, f32[4,8,8,128]{3,2,1,0:T(8,128)S(1)}, u32[]{:S(2)}, u32[]{:S(2)}) collective-permute-start(f32[4,8,8,128]{3,2,1,0:T(8,128)S(1)} %get-tuple-element.34.main), channel_id=1, source_target_pairs={{0,1},{1,0},{2,3},{3,2},{4,5},{5,4},{6,7},{7,6},{8,9},{9,8},{10,11... | collective-permute-start | bytes 393224 | tf_op jit(solution)/shard_map/ppermute | solution.py:844
  15.2 2.1 %collective-permute-start.2 = (f32[4,8,8,128]{3,2,1,0:T(8,128)S(1)}, f32[4,8,8,128]{3,2,1,0:T(8,128)S(1)}, u32[]{:S(2)}, u32[]{:S(2)}) collective-permute-start(f32[4,8,8,128]{3,2,1,0:T(8,128)S(1)} %get-tuple-element.34.main), channel_id=1, source_target_pairs={{0,16},{16,0},{32,48},{48,32},{64,80},{80,64},{96,112},{112,96},{1... | collective-permute-start | bytes 393224 | tf_op jit(solution)/shard_map/ppermute | solution.py:843
  17.3 0.0 collective-permute-done.4.near
  17.3 0.0 collective-permute-done.5.far
  17.3 2.4 %shard_map.32 = (f32[3,16,16,128]{3,2,1,0:T(8,128)S(1)}, f32[4,4,8,128]{3,2,1,0:T(8,128)S(1)}) custom-call(f32[4,16,16,128]{3,2,1,0:T(8,128)S(1)} %get-tuple-element.35.edges, f32[4,16,8,128]{3,2,1,0:T(8,128)S(1)} %get-tuple-element.36.edges_rim, f32[4,4,24,128]{3,2,1,0:T(8,128)S(1)} %collective-permute-done.4.near, ...), custom_call_target="tpu_custom_call" | custom-call | flops 10000000 | bytes 4000000 | tf_op jit(solution)/shard_map/pallas_call | solution.py:845
  19.6 2.1 %collective-permute-start.7 = (f32[4,4,8,128]{3,2,1,0:T(8,128)S(1)}, f32[4,4,8,128]{3,2,1,0:T(8,128)S(1)}, u32[]{:S(2)}, u32[]{:S(2)}) collective-permute-start(f32[4,4,8,128]{3,2,1,0:T(8,128)S(1)} %get-tuple-element.39.rim), channel_id=1, source_target_pairs={{0,1},{1,0},{2,3},{3,2},{4,5},{5,4},{6,7},{7,6},{8,9},{9,8},{10,11... | collective-permute-start | bytes 196616 | tf_op jit(solution)/shard_map/ppermute | solution.py:855
  21.7 2.6 %collective-permute-start.6 = (f32[4,4,8,128]{3,2,1,0:T(8,128)S(1)}, f32[4,4,8,128]{3,2,1,0:T(8,128)S(1)}, u32[]{:S(2)}, u32[]{:S(2)}) collective-permute-start(f32[4,4,8,128]{3,2,1,0:T(8,128)S(1)} %get-tuple-element.39.rim), channel_id=1, source_target_pairs={{0,16},{16,0},{32,48},{48,32},{64,80},{80,64},{96,112},{112,96},{1... | collective-permute-start | bytes 196616 | tf_op jit(solution)/shard_map/ppermute | solution.py:854
  24.3 0.0 collective-permute-done.3.main_far
  24.3 0.0 collective-permute-done.2.main_near
  24.3 0.0 collective-permute-done.7.rim_far
  24.3 1.9 %collective-permute-done.6.rim_near = f32[4,4,8,128]{3,2,1,0:T(8,128)S(1)} collective-permute-done((f32[4,4,8,128]{3,2,1,0:T(8,128)S(1)}, f32[4,4,8,128]{3,2,1,0:T(8,128)S(1)}, u32[]{:S(2)}, u32[]{:S(2)}) %collective-permute-start.6) | collective-permute-done | bytes 65568 | tf_op jit(solution)/shard_map/ppermute | solution.py:854
  26.1 2.4 %shard_map.33 = (f32[128,4,128]{2,1,0:T(4,128)S(1)}, f32[3,16,8,128]{3,2,1,0:T(8,128)S(1)}, f32[3,8,8,128]{3,2,1,0:T(8,128)S(1)}) custom-call(f32[4,8,8,128]{3,2,1,0:T(8,128)S(1)} %get-tuple-element.34.main, f32[4,8,8,128]{3,2,1,0:T(8,128)S(1)} %collective-permute-done.2.main_near, f32[4,8,8,128]{3,2,1,0:T(8,128)S(1)} %collective-permute-done.3.main_far, ...), custom_call_target="tpu_custom_call" | custom-call | flops 1000000 | bytes 4000000 | tf_op jit(solution)/shard_map/pallas_call | solution.py:856
  28.5 27.5 %all_to_all.5 = f32[128,4,128]{2,1,0:T(4,128)S(1)} all-to-all(f32[128,4,128]{2,1,0:T(4,128)S(1)} %get-tuple-element.40), channel_id=1, replica_groups={{0,2,4,6,8,10,12,14,16,18,20,22,24,26,28,30,32,34,36,38,40,42,44,46,48,..., dimensions={0} | all-to-all | bytes 524288 | tf_op jit(solution)/shard_map/all_to_all | solution.py:865
  56.1 3.3 %collective-permute-start.8 = (f32[128,4,128]{2,1,0:T(4,128)S(1)}, f32[128,4,128]{2,1,0:T(4,128)S(1)}, u32[]{:S(2)}, u32[]{:S(2)}) collective-permute-start(f32[128,4,128]{2,1,0:T(4,128)S(1)} %all_to_all.5), channel_id=1, source_target_pairs={{0,1},{1,0},{2,3},{3,2},{4,5},{5,4},{6,7},{7,6},{8,9},{9,8},{10,11... | collective-permute-start | bytes 786440 | tf_op jit(solution)/shard_map/ppermute | solution.py:869
  59.4 0.9 %shard_map.35.base = f32[3,32,16,128]{3,2,1,0:T(8,128)S(1)} custom-call(f32[3,34,24,128]{3,2,1,0:T(8,128)S(1)} %get-tuple-element.41.two, f32[3,16,16,128]{3,2,1,0:T(8,128)S(1)} %get-tuple-element.42.rim, f32[3,16,8,128]{3,2,1,0:T(8,128)S(1)} %get-tuple-element.43.e_one, f32[3,8,8,128]{3,2,1,0:T(8,128)S(1)} %get-tuple-element.44.e_two), custom_call_target="tpu_custom_call" | custom-call | flops 1000000 | bytes 4000000 | tf_op jit(solution)/shard_map/pallas_call | solution.py:868
  60.3 1.0 %shard_map.34.mine = f32[4,128,128]{2,1,0:T(8,128)S(1)} custom-call(f32[512,128]{1,0:T(8,128)S(1)} %bitcast.2), custom_call_target="tpu_custom_call" | custom-call | flops 1000000 | bytes 4000000 | tf_op jit(solution)/shard_map/pallas_call | solution.py:870
  61.2 0.0 collective-permute-done.8
  61.3 3.9 %shard_map.36 = f32[3,32,16,128]{3,2,1,0:T(8,128)} custom-call(f32[4,128,128]{2,1,0:T(8,128)S(1)} %shard_map.34.mine, f32[512,128]{1,0:T(8,128)S(1)} %bitcast.3, f32[3,32,16,128]{3,2,1,0:T(8,128)S(1)} %shard_map.35.base), custom_call_target="tpu_custom_call" | custom-call | flops 1000000 | bytes 4000000 | tf_op jit(solution)/shard_map/pallas_call | solution.py:871
Async XLA Ops:
  1.3 7.1 %collective-permute-start = (f32[12,32,128]{2,1,0:T(8,128)S(1)}, f32[12,32,128]{2,1,0:T(8,128)S(1)}, u32[]{:S(2)}, u32[]{:S(2)}) collective-permute-start(f32[12,32,128]{2,1,0:T(8,128)S(1)} %get-tuple-element.28), channel_id=1, source_target_pairs={{0,16},{16,0},{32,48},{48,32},{64,80},{80,64},{96,112},{112,96},{1... | collective-permute-start | bytes 589832 | tf_op jit(solution)/shard_map/ppermute | solution.py:823
  3.4 5.0 %collective-permute-start.1 = (f32[12,32,128]{2,1,0:T(8,128)S(1)}, f32[12,32,128]{2,1,0:T(8,128)S(1)}, u32[]{:S(2)}, u32[]{:S(2)}) collective-permute-start(f32[12,32,128]{2,1,0:T(8,128)S(1)} %get-tuple-element.29), channel_id=1, source_target_pairs={{0,1},{1,0},{2,3},{3,2},{4,5},{5,4},{6,7},{7,6},{8,9},{9,8},{10,11... | collective-permute-start | bytes 589832 | tf_op jit(solution)/shard_map/ppermute | solution.py:824
  8.7 8.6 %collective-permute-start.4 = (f32[4,4,24,128]{3,2,1,0:T(8,128)S(1)}, f32[4,4,24,128]{3,2,1,0:T(8,128)S(1)}, u32[]{:S(2)}, u32[]{:S(2)}) collective-permute-start(f32[4,4,24,128]{3,2,1,0:T(8,128)S(1)} %get-tuple-element.37), channel_id=1, source_target_pairs={{0,1},{1,0},{2,3},{3,2},{4,5},{5,4},{6,7},{7,6},{8,9},{9,8},{10,11... | collective-permute-start | bytes 589832 | tf_op jit(solution)/shard_map/ppermute | solution.py:835
  10.7 6.6 %collective-permute-start.5 = (f32[4,4,24,128]{3,2,1,0:T(8,128)S(1)}, f32[4,4,24,128]{3,2,1,0:T(8,128)S(1)}, u32[]{:S(2)}, u32[]{:S(2)}) collective-permute-start(f32[4,4,24,128]{3,2,1,0:T(8,128)S(1)} %get-tuple-element.38), channel_id=1, source_target_pairs={{0,16},{1,2},{2,1},{3,4},{4,3},{5,6},{6,5},{7,8},{8,7},{9,10},{10,... | collective-permute-start | bytes 589832 | tf_op jit(solution)/shard_map/ppermute | solution.py:834
  13.8 10.4 %collective-permute-start.3 = (f32[4,8,8,128]{3,2,1,0:T(8,128)S(1)}, f32[4,8,8,128]{3,2,1,0:T(8,128)S(1)}, u32[]{:S(2)}, u32[]{:S(2)}) collective-permute-start(f32[4,8,8,128]{3,2,1,0:T(8,128)S(1)} %get-tuple-element.34.main), channel_id=1, source_target_pairs={{0,1},{1,0},{2,3},{3,2},{4,5},{5,4},{6,7},{7,6},{8,9},{9,8},{10,11... | collective-permute-start | bytes 393224 | tf_op jit(solution)/shard_map/ppermute | solution.py:844
  15.2 9.1 %collective-permute-start.2 = (f32[4,8,8,128]{3,2,1,0:T(8,128)S(1)}, f32[4,8,8,128]{3,2,1,0:T(8,128)S(1)}, u32[]{:S(2)}, u32[]{:S(2)}) collective-permute-start(f32[4,8,8,128]{3,2,1,0:T(8,128)S(1)} %get-tuple-element.34.main), channel_id=1, source_target_pairs={{0,16},{16,0},{32,48},{48,32},{64,80},{80,64},{96,112},{112,96},{1... | collective-permute-start | bytes 393224 | tf_op jit(solution)/shard_map/ppermute | solution.py:843
  19.6 4.6 %collective-permute-start.7 = (f32[4,4,8,128]{3,2,1,0:T(8,128)S(1)}, f32[4,4,8,128]{3,2,1,0:T(8,128)S(1)}, u32[]{:S(2)}, u32[]{:S(2)}) collective-permute-start(f32[4,4,8,128]{3,2,1,0:T(8,128)S(1)} %get-tuple-element.39.rim), channel_id=1, source_target_pairs={{0,1},{1,0},{2,3},{3,2},{4,5},{5,4},{6,7},{7,6},{8,9},{9,8},{10,11... | collective-permute-start | bytes 196616 | tf_op jit(solution)/shard_map/ppermute | solution.py:855
  21.7 4.4 %collective-permute-start.6 = (f32[4,4,8,128]{3,2,1,0:T(8,128)S(1)}, f32[4,4,8,128]{3,2,1,0:T(8,128)S(1)}, u32[]{:S(2)}, u32[]{:S(2)}) collective-permute-start(f32[4,4,8,128]{3,2,1,0:T(8,128)S(1)} %get-tuple-element.39.rim), channel_id=1, source_target_pairs={{0,16},{16,0},{32,48},{48,32},{64,80},{80,64},{96,112},{112,96},{1... | collective-permute-start | bytes 196616 | tf_op jit(solution)/shard_map/ppermute | solution.py:854
  56.1 5.2 %collective-permute-start.8 = (f32[128,4,128]{2,1,0:T(4,128)S(1)}, f32[128,4,128]{2,1,0:T(4,128)S(1)}, u32[]{:S(2)}, u32[]{:S(2)}) collective-permute-start(f32[128,4,128]{2,1,0:T(4,128)S(1)} %all_to_all.5), channel_id=1, source_target_pairs={{0,1},{1,0},{2,3},{3,2},{4,5},{5,4},{6,7},{7,6},{8,9},{9,8},{10,11... | collective-permute-start | bytes 786440 | tf_op jit(solution)/shard_map/ppermute | solution.py:869

commit v14 on v13

--- a/solution.py
+++ b/solution.py
@@ -73,17 +73,19 @@
 def rows_kernel(guess, labels, near, far, own, phase, sems):
     even = lax.rem(lax.axis_index("gx"), 2) == 0
     near_row, far_row = jnp.where(even, 13, 0), jnp.where(even, 0, 13)
-    copies = [pltpu.make_async_copy(labels, phase, sems.at[3])]
-    for f in range(3):
-        copies.append(pltpu.make_async_copy(guess.at[f], own.at[f], sems.at[f]))
-    for copy in copies:
-        copy.start()
-    copies[0].wait()
-    own[3] = jnp.where(phase[...] == 1, 0.0, 1.0).astype(F32)
+    copies = {}
+    for ch in (3, 0, 1, 2):
+        source, target = (labels, phase) if ch == 3 else (guess.at[ch], own.at[ch])
+        for part in range(4):
+            at = pl.ds(8 * part, 8)
+            copies[ch, part] = pltpu.make_async_copy(source.at[at], target.at[at], sems.at[4 * ch + part])
+            copies[ch, part].start()
     flat = own.reshape(4 * 32 * 16, 128)
     for ch in (3, 0, 1, 2):
-        if ch < 3:
-            copies[ch + 1].wait()
+        for part in range(4):
+            copies[ch, part].wait()
+        if ch == 3:
+            own[3] = jnp.where(phase[...] == 1, 0.0, 1.0).astype(F32)
         for row in range(3):
             near[3 * ch + row] = flat[pl.ds(512 * ch + near_row + row, 32, stride=16), :]
             far[3 * ch + row] = flat[pl.ds(512 * ch + far_row + row, 32, stride=16), :]
@@ -639,15 +641,6 @@
     return x
 
 
-def lay_kernel(mine, laid):
-    def lay(g):
-        for ch in range(4):
-            tile = swap_blocks(mine[pl.ds(32 * g + ch, 8, stride=4), :])
-            laid[ch, pl.ds(pl.multiple_of(8 * g, 8), 8), :] = tile
-
-    loop(16, lay, 4)
-
-
 def top_kernel(
     mine, other, base, out,
     natural, first, second, four, weights, diags, lefts, final, sems,
@@ -657,15 +650,22 @@
     lane, sub = iota((16, 128), 1), iota((16, 128), 0)
     cells = [(z, x, half) for z in range(4) for x in range(2) for half in range(2)]
 
-    parity = lax.rem(gy, 2)
-
     def lay(g):
         for ch in range(4):
-            at = pl.ds(pl.multiple_of(8 * g, 8), 8)
-            natural[ch, parity, at, :] = mine[ch, at, :]
-            natural[ch, 1 - parity, at, :] = swap_blocks(other[pl.ds(32 * g + ch, 8, stride=4), :])
-
-    loop(16, lay, 4)
+            rows = pl.ds(32 * g + ch, 8, stride=4)
+            pair = mine[rows, :], other[rows, :]
+            natural[ch, 0, pl.ds(pl.multiple_of(8 * g, 8), 8), :] = swap_blocks(
+                jnp.where(first_core, pair[0], pair[1])
+            )
+            natural[ch, 1, pl.ds(pl.multiple_of(8 * g, 8), 8), :] = swap_blocks(
+                jnp.where(first_core, pair[1], pair[0])
+            )
+
+    def lay_some(step):
+        for k in range(8):
+            lay(8 * step + k)
+
+    loop(2, lay_some)
     flat = natural.reshape(1024, 128)
 
     def plane(ch, z, x, half):
@@ -794,11 +794,10 @@
                 value = jnp.broadcast_to(three[at : at + 1] + shifts[f], (8, 128))
                 for k in range(8 * z, 8 * z + 8):
                     final[f, k, 8 * x : 8 * x + 8, :] = base[f, k, 8 * x : 8 * x + 8, :] + value
-            if z % 2 == 1:
-                part = (f, pl.ds(8 * z - 8, 16))
-                copy = pltpu.make_async_copy(final.at[part], out.at[part], sems.at[len(copies)])
-                copy.start()
-                copies.append(copy)
+            part = (f, pl.ds(8 * z, 8))
+            copy = pltpu.make_async_copy(final.at[part], out.at[part], sems.at[len(copies)])
+            copy.start()
+            copies.append(copy)
     for copy in copies:
         copy.wait()
 
@@ -817,7 +816,7 @@
     to_near, to_far, own = call(
         rows_kernel,
         [(12, 32, 128)] * 2 + [(4, 32, 16, 128)],
-        [pltpu.VMEM((32, 16, 128), jnp.int32), pltpu.SemaphoreType.DMA((4,))],
+        [pltpu.VMEM((32, 16, 128), jnp.int32), pltpu.SemaphoreType.DMA((16,))],
         in_specs=[ANY, ANY],
     )(pltpu.with_memory_space_constraint(guess, pltpu.HBM), pltpu.with_memory_space_constraint(labels, pltpu.HBM))
     from_near = lax.ppermute(to_near, "gx", swap_near)
@@ -867,14 +866,13 @@
     )
     (base,) = call(base_kernel, [(3, 32, 16, 128)], [(192, 128), (3, 16, 16, 128)])(two, rim, e_one, e_two)
     other = lax.ppermute(mine, "gy", swap_near)
-    (laid,) = call(lay_kernel, [(4, 128, 128)], [])(mine.reshape(512, 128))
     (out,) = call(
         top_kernel,
         [(3, 32, 16, 128)],
         [(4, 2, 128, 128), (3, 16, 16, 128), (2, 3, 8, 16, 128), (6, 16, 128), (6, 16, 16, 128)]
-        + [(16, 16, 128), (4, 2, 16, 256), (3, 32, 16, 128), pltpu.SemaphoreType.DMA((6,))],
+        + [(16, 16, 128), (4, 2, 16, 256), (3, 32, 16, 128), pltpu.SemaphoreType.DMA((12,))],
         out_specs=[ANY],
-    )(laid, other.reshape(512, 128), base)
+    )(mine.reshape(512, 128), other.reshape(512, 128), base)
     return out
 
 

time: 65.4 us -> 70.2 us (1.073)
  Pallas kernels: 18 us -> 22.5 us
    pallas_call x1, Pallas kernels: 3.88 us -> 9.17 us  [local(): call(top_kernel, [(3, 32, 16, 128)], [(4, 2, 128, 128), (3, 16, 16, 128),...]
    pallas_call x1 -> x0, Pallas kernels: 0.96 us -> none  [local(): laid, = call(lay_kernel, [(4, 128, 128)], [])(mine.reshape(512, 128))]
  transfers between devices with their start and end apart: 9 -> 9, of which waited for: 1 -> 2; matrix products, arithmetic and copies ran while one was open for 0% -> 0% of each run, Pallas kernels for 16% -> 13%
where the time goes in v14:
time: 70.2 us; the launch traced here: 70 us
  blocking collectives  27.5 us (39%)
  Pallas kernels  22.5 us (32%)
  starting transfers between devices  17.6 us (25%)
  waiting for transfers between devices  2.14 us (3%)
    all_to_all x1, blocking collectives, local(): lax.all_to_all(sent, ('gx', 'gy'), split_axis=0, concat_axis=0, axis_inde...  27.5 us
    pallas_call x1, Pallas kernels, local(): call(top_kernel, [(3, 32, 16, 128)], [(4, 2, 128, 128), (3, 16, 16, 128),...  9.17 us
    pallas_call x1, Pallas kernels, local(): call(own_kernel, [(3, 34, 32, 128)] * 2 + [(4, 16, 16, 128)] + [(4, 4, 16...  3.66 us
    ppermute x1, starting transfers between devices, local(): other = lax.ppermute(mine, 'gy', swap_near)  3.3 us
    ppermute x1, starting transfers between devices, local(): rim_near = lax.ppermute(rim_one, 'gx', swap_near)  2.56 us
    pallas_call x1, Pallas kernels, local(): call(rim_kernel, [(3, 16, 16, 128), (4, 4, 8, 128)], [(3, 18, 32, 128), (...  2.39 us
    pallas_call x1, Pallas kernels, local(): call(middle_kernel, [(CHIPS, 4, 128), (3, 16, 8, 128), (3, 8, 8, 128)], [...  2.38 us
    pallas_call x1, Pallas kernels, local(): call(rows_edge_kernel, [(3, 34, 24, 128), (4, 8, 8, 128), (4, 16, 8, 128)...  2.3 us
  transfers between devices with their start and end apart: 9, of which 2 were waited for; matrix products, arithmetic and copies ran while one was open for 0% of the time, Pallas kernels for 13%

profile of v14, /device:TPU:1, one launch (start us, length us, event | category | flops | bytes accessed | tf_op | source)
XLA Modules:
  0.0 70.0 jit_solution(11868557845328418490)
XLA Ops:
  0.0 1.4 %shard_map.28 = (f32[12,32,128]{2,1,0:T(8,128)S(1)}, f32[12,32,128]{2,1,0:T(8,128)S(1)}, f32[4,32,16,128]{3,2,1,0:T(8,128)S(1)}) custom-call(f32[3,32,16,128]{3,2,1,0:T(8,128)} %guess.1, s32[32,16,128]{2,1,0:T(8,128)} %labels.1), custom_call_target="tpu_custom_call" | custom-call | flops 1000000 | bytes 4000000 | tf_op jit(solution)/shard_map/pallas_call | solution.py:816
  1.4 2.1 %collective-permute-start = (f32[12,32,128]{2,1,0:T(8,128)S(1)}, f32[12,32,128]{2,1,0:T(8,128)S(1)}, u32[]{:S(2)}, u32[]{:S(2)}) collective-permute-start(f32[12,32,128]{2,1,0:T(8,128)S(1)} %get-tuple-element.28), channel_id=1, source_target_pairs={{0,16},{16,0},{32,48},{48,32},{64,80},{80,64},{96,112},{112,96},{1... | collective-permute-start | bytes 589832 | tf_op jit(solution)/shard_map/ppermute | solution.py:822
  3.5 1.3 %collective-permute-start.1 = (f32[12,32,128]{2,1,0:T(8,128)S(1)}, f32[12,32,128]{2,1,0:T(8,128)S(1)}, u32[]{:S(2)}, u32[]{:S(2)}) collective-permute-start(f32[12,32,128]{2,1,0:T(8,128)S(1)} %get-tuple-element.29), channel_id=1, source_target_pairs={{0,1},{1,0},{2,3},{3,2},{4,5},{5,4},{6,7},{7,6},{8,9},{9,8},{10,11... | collective-permute-start | bytes 589832 | tf_op jit(solution)/shard_map/ppermute | solution.py:823
  4.8 3.7 %shard_map.29 = (f32[3,34,32,128]{3,2,1,0:T(8,128)S(1)}, f32[3,34,32,128]{3,2,1,0:T(8,128)S(1)}, f32[4,16,16,128]{3,2,1,0:T(8,128)S(1)}, f32[4,4,16,128]{3,2,1,0...) custom-call(f32[4,32,16,128]{3,2,1,0:T(8,128)S(1)} %get-tuple-element.25.own), custom_call_target="tpu_custom_call" | custom-call | flops 20000000 | bytes 4000000 | tf_op jit(solution)/shard_map/pallas_call | solution.py:824
  8.5 0.0 collective-permute-done.x_near
  8.5 0.0 collective-permute-done.1.x_far
  8.5 0.3 shard_map.30
  8.8 2.0 %collective-permute-start.4 = (f32[4,4,24,128]{3,2,1,0:T(8,128)S(1)}, f32[4,4,24,128]{3,2,1,0:T(8,128)S(1)}, u32[]{:S(2)}, u32[]{:S(2)}) collective-permute-start(f32[4,4,24,128]{3,2,1,0:T(8,128)S(1)} %get-tuple-element.37), channel_id=1, source_target_pairs={{0,1},{1,0},{2,3},{3,2},{4,5},{5,4},{6,7},{7,6},{8,9},{9,8},{10,11... | collective-permute-start | bytes 589832 | tf_op jit(solution)/shard_map/ppermute | solution.py:834
  10.8 0.9 %collective-permute-start.5 = (f32[4,4,24,128]{3,2,1,0:T(8,128)S(1)}, f32[4,4,24,128]{3,2,1,0:T(8,128)S(1)}, u32[]{:S(2)}, u32[]{:S(2)}) collective-permute-start(f32[4,4,24,128]{3,2,1,0:T(8,128)S(1)} %get-tuple-element.38), channel_id=1, source_target_pairs={{0,16},{1,2},{2,1},{3,4},{4,3},{5,6},{6,5},{7,8},{8,7},{9,10},{10,... | collective-permute-start | bytes 589832 | tf_op jit(solution)/shard_map/ppermute | solution.py:833
  11.7 2.3 %shard_map.31 = (f32[3,34,24,128]{3,2,1,0:T(8,128)S(1)}, f32[4,8,8,128]{3,2,1,0:T(8,128)S(1)}, f32[4,16,8,128]{3,2,1,0:T(8,128)S(1)}) custom-call(f32[4,32,16,128]{3,2,1,0:T(8,128)S(1)} %get-tuple-element.25.own, f32[4,32,8,128]{3,2,1,0:T(8,128)S(1)} %get-tuple-element.30.rim, f32[3,34,32,128]{3,2,1,0:T(8,128)S(1)} %get-tuple-element.31.own_one, ...), custom_call_target="tpu_custom_call" | custom-call | flops 10000000 | bytes 4000000 | tf_op jit(solution)/shard_map/pallas_call | solution.py:835
  14.0 1.4 %collective-permute-start.3 = (f32[4,8,8,128]{3,2,1,0:T(8,128)S(1)}, f32[4,8,8,128]{3,2,1,0:T(8,128)S(1)}, u32[]{:S(2)}, u32[]{:S(2)}) collective-permute-start(f32[4,8,8,128]{3,2,1,0:T(8,128)S(1)} %get-tuple-element.34.main), channel_id=1, source_target_pairs={{0,1},{1,0},{2,3},{3,2},{4,5},{5,4},{6,7},{7,6},{8,9},{9,8},{10,11... | collective-permute-start | bytes 393224 | tf_op jit(solution)/shard_map/ppermute | solution.py:843
  15.3 2.1 %collective-permute-start.2 = (f32[4,8,8,128]{3,2,1,0:T(8,128)S(1)}, f32[4,8,8,128]{3,2,1,0:T(8,128)S(1)}, u32[]{:S(2)}, u32[]{:S(2)}) collective-permute-start(f32[4,8,8,128]{3,2,1,0:T(8,128)S(1)} %get-tuple-element.34.main), channel_id=1, source_target_pairs={{0,16},{16,0},{32,48},{48,32},{64,80},{80,64},{96,112},{112,96},{1... | collective-permute-start | bytes 393224 | tf_op jit(solution)/shard_map/ppermute | solution.py:842
  17.4 0.0 collective-permute-done.4.near
  17.4 0.0 collective-permute-done.5.far
  17.4 2.4 %shard_map.32 = (f32[3,16,16,128]{3,2,1,0:T(8,128)S(1)}, f32[4,4,8,128]{3,2,1,0:T(8,128)S(1)}) custom-call(f32[4,16,16,128]{3,2,1,0:T(8,128)S(1)} %get-tuple-element.35.edges, f32[4,16,8,128]{3,2,1,0:T(8,128)S(1)} %get-tuple-element.36.edges_rim, f32[4,4,24,128]{3,2,1,0:T(8,128)S(1)} %collective-permute-done.4.near, ...), custom_call_target="tpu_custom_call" | custom-call | flops 10000000 | bytes 4000000 | tf_op jit(solution)/shard_map/pallas_call | solution.py:844
  19.8 2.1 %collective-permute-start.7 = (f32[4,4,8,128]{3,2,1,0:T(8,128)S(1)}, f32[4,4,8,128]{3,2,1,0:T(8,128)S(1)}, u32[]{:S(2)}, u32[]{:S(2)}) collective-permute-start(f32[4,4,8,128]{3,2,1,0:T(8,128)S(1)} %get-tuple-element.39.rim), channel_id=1, source_target_pairs={{0,1},{1,0},{2,3},{3,2},{4,5},{5,4},{6,7},{7,6},{8,9},{9,8},{10,11... | collective-permute-start | bytes 196616 | tf_op jit(solution)/shard_map/ppermute | solution.py:854
  21.9 2.6 %collective-permute-start.6 = (f32[4,4,8,128]{3,2,1,0:T(8,128)S(1)}, f32[4,4,8,128]{3,2,1,0:T(8,128)S(1)}, u32[]{:S(2)}, u32[]{:S(2)}) collective-permute-start(f32[4,4,8,128]{3,2,1,0:T(8,128)S(1)} %get-tuple-element.39.rim), channel_id=1, source_target_pairs={{0,16},{16,0},{32,48},{48,32},{64,80},{80,64},{96,112},{112,96},{1... | collective-permute-start | bytes 196616 | tf_op jit(solution)/shard_map/ppermute | solution.py:853
  24.4 0.0 collective-permute-done.3.main_far
  24.4 0.0 collective-permute-done.2.main_near
  24.4 0.0 collective-permute-done.7.rim_far
  24.4 1.9 %collective-permute-done.6.rim_near = f32[4,4,8,128]{3,2,1,0:T(8,128)S(1)} collective-permute-done((f32[4,4,8,128]{3,2,1,0:T(8,128)S(1)}, f32[4,4,8,128]{3,2,1,0:T(8,128)S(1)}, u32[]{:S(2)}, u32[]{:S(2)}) %collective-permute-start.6) | collective-permute-done | bytes 65568 | tf_op jit(solution)/shard_map/ppermute | solution.py:853
  26.3 2.4 %shard_map.33 = (f32[128,4,128]{2,1,0:T(4,128)S(1)}, f32[3,16,8,128]{3,2,1,0:T(8,128)S(1)}, f32[3,8,8,128]{3,2,1,0:T(8,128)S(1)}) custom-call(f32[4,8,8,128]{3,2,1,0:T(8,128)S(1)} %get-tuple-element.34.main, f32[4,8,8,128]{3,2,1,0:T(8,128)S(1)} %collective-permute-done.2.main_near, f32[4,8,8,128]{3,2,1,0:T(8,128)S(1)} %collective-permute-done.3.main_far, ...), custom_call_target="tpu_custom_call" | custom-call | flops 1000000 | bytes 4000000 | tf_op jit(solution)/shard_map/pallas_call | solution.py:855
  28.7 27.5 %all_to_all.5 = f32[128,4,128]{2,1,0:T(4,128)S(1)} all-to-all(f32[128,4,128]{2,1,0:T(4,128)S(1)} %get-tuple-element.40), channel_id=1, replica_groups={{0,2,4,6,8,10,12,14,16,18,20,22,24,26,28,30,32,34,36,38,40,42,44,46,48,..., dimensions={0} | all-to-all | bytes 524288 | tf_op jit(solution)/shard_map/all_to_all | solution.py:864
  56.2 3.3 %collective-permute-start.8 = (f32[128,4,128]{2,1,0:T(4,128)S(1)}, f32[128,4,128]{2,1,0:T(4,128)S(1)}, u32[]{:S(2)}, u32[]{:S(2)}) collective-permute-start(f32[128,4,128]{2,1,0:T(4,128)S(1)} %all_to_all.5), channel_id=1, source_target_pairs={{0,1},{1,0},{2,3},{3,2},{4,5},{5,4},{6,7},{7,6},{8,9},{9,8},{10,11... | collective-permute-start | bytes 786440 | tf_op jit(solution)/shard_map/ppermute | solution.py:868
  59.5 0.9 %shard_map.34.base = f32[3,32,16,128]{3,2,1,0:T(8,128)S(1)} custom-call(f32[3,34,24,128]{3,2,1,0:T(8,128)S(1)} %get-tuple-element.41.two, f32[3,16,16,128]{3,2,1,0:T(8,128)S(1)} %get-tuple-element.42.rim, f32[3,16,8,128]{3,2,1,0:T(8,128)S(1)} %get-tuple-element.43.e_one, f32[3,8,8,128]{3,2,1,0:T(8,128)S(1)} %get-tuple-element.44.e_two), custom_call_target="tpu_custom_call" | custom-call | flops 1000000 | bytes 4000000 | tf_op jit(solution)/shard_map/pallas_call | solution.py:867
  60.4 0.3 collective-permute-done.8
  60.7 9.2 %shard_map.35 = f32[3,32,16,128]{3,2,1,0:T(8,128)} custom-call(f32[512,128]{1,0:T(8,128)S(1)} %bitcast.2, f32[512,128]{1,0:T(8,128)S(1)} %bitcast.3, f32[3,32,16,128]{3,2,1,0:T(8,128)S(1)} %shard_map.34.base), custom_call_target="tpu_custom_call" | custom-call | flops 1000000 | bytes 4000000 | tf_op jit(solution)/shard_map/pallas_call | solution.py:869
Async XLA Ops:
  1.4 7.1 %collective-permute-start = (f32[12,32,128]{2,1,0:T(8,128)S(1)}, f32[12,32,128]{2,1,0:T(8,128)S(1)}, u32[]{:S(2)}, u32[]{:S(2)}) collective-permute-start(f32[12,32,128]{2,1,0:T(8,128)S(1)} %get-tuple-element.28), channel_id=1, source_target_pairs={{0,16},{16,0},{32,48},{48,32},{64,80},{80,64},{96,112},{112,96},{1... | collective-permute-start | bytes 589832 | tf_op jit(solution)/shard_map/ppermute | solution.py:822
  3.5 5.0 %collective-permute-start.1 = (f32[12,32,128]{2,1,0:T(8,128)S(1)}, f32[12,32,128]{2,1,0:T(8,128)S(1)}, u32[]{:S(2)}, u32[]{:S(2)}) collective-permute-start(f32[12,32,128]{2,1,0:T(8,128)S(1)} %get-tuple-element.29), channel_id=1, source_target_pairs={{0,1},{1,0},{2,3},{3,2},{4,5},{5,4},{6,7},{7,6},{8,9},{9,8},{10,11... | collective-permute-start | bytes 589832 | tf_op jit(solution)/shard_map/ppermute | solution.py:823
  8.8 8.6 %collective-permute-start.4 = (f32[4,4,24,128]{3,2,1,0:T(8,128)S(1)}, f32[4,4,24,128]{3,2,1,0:T(8,128)S(1)}, u32[]{:S(2)}, u32[]{:S(2)}) collective-permute-start(f32[4,4,24,128]{3,2,1,0:T(8,128)S(1)} %get-tuple-element.37), channel_id=1, source_target_pairs={{0,1},{1,0},{2,3},{3,2},{4,5},{5,4},{6,7},{7,6},{8,9},{9,8},{10,11... | collective-permute-start | bytes 589832 | tf_op jit(solution)/shard_map/ppermute | solution.py:834
  10.8 6.6 %collective-permute-start.5 = (f32[4,4,24,128]{3,2,1,0:T(8,128)S(1)}, f32[4,4,24,128]{3,2,1,0:T(8,128)S(1)}, u32[]{:S(2)}, u32[]{:S(2)}) collective-permute-start(f32[4,4,24,128]{3,2,1,0:T(8,128)S(1)} %get-tuple-element.38), channel_id=1, source_target_pairs={{0,16},{1,2},{2,1},{3,4},{4,3},{5,6},{6,5},{7,8},{8,7},{9,10},{10,... | collective-permute-start | bytes 589832 | tf_op jit(solution)/shard_map/ppermute | solution.py:833
  14.0 10.4 %collective-permute-start.3 = (f32[4,8,8,128]{3,2,1,0:T(8,128)S(1)}, f32[4,8,8,128]{3,2,1,0:T(8,128)S(1)}, u32[]{:S(2)}, u32[]{:S(2)}) collective-permute-start(f32[4,8,8,128]{3,2,1,0:T(8,128)S(1)} %get-tuple-element.34.main), channel_id=1, source_target_pairs={{0,1},{1,0},{2,3},{3,2},{4,5},{5,4},{6,7},{7,6},{8,9},{9,8},{10,11... | collective-permute-start | bytes 393224 | tf_op jit(solution)/shard_map/ppermute | solution.py:843
  15.3 9.1 %collective-permute-start.2 = (f32[4,8,8,128]{3,2,1,0:T(8,128)S(1)}, f32[4,8,8,128]{3,2,1,0:T(8,128)S(1)}, u32[]{:S(2)}, u32[]{:S(2)}) collective-permute-start(f32[4,8,8,128]{3,2,1,0:T(8,128)S(1)} %get-tuple-element.34.main), channel_id=1, source_target_pairs={{0,16},{16,0},{32,48},{48,32},{64,80},{80,64},{96,112},{112,96},{1... | collective-permute-start | bytes 393224 | tf_op jit(solution)/shard_map/ppermute | solution.py:842
  19.8 4.6 %collective-permute-start.7 = (f32[4,4,8,128]{3,2,1,0:T(8,128)S(1)}, f32[4,4,8,128]{3,2,1,0:T(8,128)S(1)}, u32[]{:S(2)}, u32[]{:S(2)}) collective-permute-start(f32[4,4,8,128]{3,2,1,0:T(8,128)S(1)} %get-tuple-element.39.rim), channel_id=1, source_target_pairs={{0,1},{1,0},{2,3},{3,2},{4,5},{5,4},{6,7},{7,6},{8,9},{9,8},{10,11... | collective-permute-start | bytes 196616 | tf_op jit(solution)/shard_map/ppermute | solution.py:854
  21.9 4.4 %collective-permute-start.6 = (f32[4,4,8,128]{3,2,1,0:T(8,128)S(1)}, f32[4,4,8,128]{3,2,1,0:T(8,128)S(1)}, u32[]{:S(2)}, u32[]{:S(2)}) collective-permute-start(f32[4,4,8,128]{3,2,1,0:T(8,128)S(1)} %get-tuple-element.39.rim), channel_id=1, source_target_pairs={{0,16},{16,0},{32,48},{48,32},{64,80},{80,64},{96,112},{112,96},{1... | collective-permute-start | bytes 196616 | tf_op jit(solution)/shard_map/ppermute | solution.py:853
  56.2 4.5 %collective-permute-start.8 = (f32[128,4,128]{2,1,0:T(4,128)S(1)}, f32[128,4,128]{2,1,0:T(4,128)S(1)}, u32[]{:S(2)}, u32[]{:S(2)}) collective-permute-start(f32[128,4,128]{2,1,0:T(4,128)S(1)} %all_to_all.5), channel_id=1, source_target_pairs={{0,1},{1,0},{2,3},{3,2},{4,5},{5,4},{6,7},{7,6},{8,9},{9,8},{10,11... | collective-permute-start | bytes 786440 | tf_op jit(solution)/shard_map/ppermute | solution.py:868

commit v15 on v13

--- a/solution.py
+++ b/solution.py
@@ -639,15 +639,6 @@
     return x
 
 
-def lay_kernel(mine, laid):
-    def lay(g):
-        for ch in range(4):
-            tile = swap_blocks(mine[pl.ds(32 * g + ch, 8, stride=4), :])
-            laid[ch, pl.ds(pl.multiple_of(8 * g, 8), 8), :] = tile
-
-    loop(16, lay, 4)
-
-
 def top_kernel(
     mine, other, base, out,
     natural, first, second, four, weights, diags, lefts, final, sems,
@@ -657,13 +648,16 @@
     lane, sub = iota((16, 128), 1), iota((16, 128), 0)
     cells = [(z, x, half) for z in range(4) for x in range(2) for half in range(2)]
 
-    parity = lax.rem(gy, 2)
-
     def lay(g):
         for ch in range(4):
-            at = pl.ds(pl.multiple_of(8 * g, 8), 8)
-            natural[ch, parity, at, :] = mine[ch, at, :]
-            natural[ch, 1 - parity, at, :] = swap_blocks(other[pl.ds(32 * g + ch, 8, stride=4), :])
+            rows = pl.ds(32 * g + ch, 8, stride=4)
+            pair = mine[rows, :], other[rows, :]
+            natural[ch, 0, pl.ds(pl.multiple_of(8 * g, 8), 8), :] = swap_blocks(
+                jnp.where(first_core, pair[0], pair[1])
+            )
+            natural[ch, 1, pl.ds(pl.multiple_of(8 * g, 8), 8), :] = swap_blocks(
+                jnp.where(first_core, pair[1], pair[0])
+            )
 
     loop(16, lay, 4)
     flat = natural.reshape(1024, 128)
@@ -711,31 +705,37 @@
         for f in range(3):
             first[f, at] = (64.0 * gain) * plane(f, z, x, half)
 
-    for z, x, half in cells:
-        at = key(z, x, half)
-        w = [weights[i, at] for i in range(6)]
-        for f in range(3):
+    def sweep(f):
+        for z, x, half in cells:
+            at = key(z, x, half)
+            w = [weights[i, at] for i in range(6)]
             own, six = neighbours(lambda *c: first[f, key(*c)], z, x, half, zeros)
             second[half, f, z * 2 + x] = 1.2 * own + weigh(w, six)
 
+    loop(3, sweep)
+
+    def left(f):
+        for z4 in range(2):
+            for half in range(2):
+                total = None
+                for z in (2 * z4, 2 * z4 + 1):
+                    for x in range(2):
+                        at = key(z, x, half)
+                        w = [weights[i, at] for i in range(6)]
+                        own, six = neighbours(lambda c, d, e: second[e, f, c * 2 + d], z, x, half, zeros)
+                        value = ((first[f, at] - 0.8 * own) + weigh(w, six)) * diags[at]
+                        total = value if total is None else total + value
+                lefts[f, z4, :, 128 * half : 128 * half + 128] = total
+
+    loop(3, left)
     for z4 in range(2):
         for half in range(2):
-            sums = [None] * 4
+            total = None
             for z in (2 * z4, 2 * z4 + 1):
                 for x in range(2):
-                    at = key(z, x, half)
-                    w = [weights[i, at] for i in range(6)]
-                    diag = diags[at]
-                    for f in range(3):
-                        own, six = neighbours(
-                            lambda c, d, e: second[e, f, c * 2 + d], z, x, half, zeros
-                        )
-                        value = ((first[f, at] - 0.8 * own) + weigh(w, six)) * diag
-                        sums[f] = value if sums[f] is None else sums[f] + value
                     share = shares[z, x, half]
-                    sums[3] = share if sums[3] is None else sums[3] + share
-            for ch in range(4):
-                lefts[ch, z4, :, 128 * half : 128 * half + 128] = sums[ch]
+                    total = share if total is None else total + share
+            lefts[3, z4, :, 128 * half : 128 * half + 128] = total
 
     source = iota((256, 128), 0)
     column = ((source % 128) // 16) * 16 + (source // 128) * 8 + (source % 16) // 2
@@ -867,14 +867,13 @@
     )
     (base,) = call(base_kernel, [(3, 32, 16, 128)], [(192, 128), (3, 16, 16, 128)])(two, rim, e_one, e_two)
     other = lax.ppermute(mine, "gy", swap_near)
-    (laid,) = call(lay_kernel, [(4, 128, 128)], [])(mine.reshape(512, 128))
     (out,) = call(
         top_kernel,
         [(3, 32, 16, 128)],
         [(4, 2, 128, 128), (3, 16, 16, 128), (2, 3, 8, 16, 128), (6, 16, 128), (6, 16, 16, 128)]
         + [(16, 16, 128), (4, 2, 16, 256), (3, 32, 16, 128), pltpu.SemaphoreType.DMA((6,))],
         out_specs=[ANY],
-    )(laid, other.reshape(512, 128), base)
+    )(mine.reshape(512, 128), other.reshape(512, 128), base)
     return out
 
 

time: 65.4 us -> 65.4 us (level)
    pallas_call x1 -> x0, Pallas kernels: 0.96 us -> none  [local(): laid, = call(lay_kernel, [(4, 128, 128)], [])(mine.reshape(512, 128))]
    pallas_call x1, Pallas kernels: 3.88 us -> 4.59 us  [local(): call(top_kernel, [(3, 32, 16, 128)], [(4, 2, 128, 128), (3, 16, 16, 128),...]
  transfers between devices with their start and end apart: 9 -> 9, of which waited for: 1 -> 2; matrix products, arithmetic and copies ran while one was open for 0% -> 0% of each run, Pallas kernels for 16% -> 14%
where the time goes in v15:
time: 65.4 us; the launch traced here: 65.3 us
  blocking collectives  27.5 us (42%)
  Pallas kernels  17.8 us (27%)
  starting transfers between devices  17.6 us (27%)
  waiting for transfers between devices  2.14 us (3%)
    all_to_all x1, blocking collectives, local(): lax.all_to_all(sent, ('gx', 'gy'), split_axis=0, concat_axis=0, axis_inde...  27.5 us
    pallas_call x1, Pallas kernels, local(): call(top_kernel, [(3, 32, 16, 128)], [(4, 2, 128, 128), (3, 16, 16, 128),...  4.59 us
    pallas_call x1, Pallas kernels, local(): call(own_kernel, [(3, 34, 32, 128)] * 2 + [(4, 16, 16, 128)] + [(4, 4, 16...  3.66 us
    ppermute x1, starting transfers between devices, local(): other = lax.ppermute(mine, 'gy', swap_near)  3.3 us
    ppermute x1, starting transfers between devices, local(): rim_near = lax.ppermute(rim_one, 'gx', swap_near)  2.56 us
    pallas_call x1, Pallas kernels, local(): call(rim_kernel, [(3, 16, 16, 128), (4, 4, 8, 128)], [(3, 18, 32, 128), (...  2.39 us
    pallas_call x1, Pallas kernels, local(): call(middle_kernel, [(CHIPS, 4, 128), (3, 16, 8, 128), (3, 8, 8, 128)], [...  2.38 us
    pallas_call x1, Pallas kernels, local(): call(rows_edge_kernel, [(3, 34, 24, 128), (4, 8, 8, 128), (4, 16, 8, 128)...  2.3 us
  transfers between devices with their start and end apart: 9, of which 2 were waited for; matrix products, arithmetic and copies ran while one was open for 0% of the time, Pallas kernels for 14%

profile of v15, /device:TPU:1, one launch (start us, length us, event | category | flops | bytes accessed | tf_op | source)
XLA Modules:
  0.0 65.3 jit_solution(3281375436415389680)
XLA Ops:
  0.0 1.3 %shard_map.28 = (f32[12,32,128]{2,1,0:T(8,128)S(1)}, f32[12,32,128]{2,1,0:T(8,128)S(1)}, f32[4,32,16,128]{3,2,1,0:T(8,128)S(1)}) custom-call(f32[3,32,16,128]{3,2,1,0:T(8,128)} %guess.1, s32[32,16,128]{2,1,0:T(8,128)} %labels.1), custom_call_target="tpu_custom_call" | custom-call | flops 1000000 | bytes 4000000 | tf_op jit(solution)/shard_map/pallas_call | solution.py:817
  1.3 2.1 %collective-permute-start = (f32[12,32,128]{2,1,0:T(8,128)S(1)}, f32[12,32,128]{2,1,0:T(8,128)S(1)}, u32[]{:S(2)}, u32[]{:S(2)}) collective-permute-start(f32[12,32,128]{2,1,0:T(8,128)S(1)} %get-tuple-element.28), channel_id=1, source_target_pairs={{0,16},{16,0},{32,48},{48,32},{64,80},{80,64},{96,112},{112,96},{1... | collective-permute-start | bytes 589832 | tf_op jit(solution)/shard_map/ppermute | solution.py:823
  3.4 1.3 %collective-permute-start.1 = (f32[12,32,128]{2,1,0:T(8,128)S(1)}, f32[12,32,128]{2,1,0:T(8,128)S(1)}, u32[]{:S(2)}, u32[]{:S(2)}) collective-permute-start(f32[12,32,128]{2,1,0:T(8,128)S(1)} %get-tuple-element.29), channel_id=1, source_target_pairs={{0,1},{1,0},{2,3},{3,2},{4,5},{5,4},{6,7},{7,6},{8,9},{9,8},{10,11... | collective-permute-start | bytes 589832 | tf_op jit(solution)/shard_map/ppermute | solution.py:824
  4.7 3.7 %shard_map.29 = (f32[3,34,32,128]{3,2,1,0:T(8,128)S(1)}, f32[3,34,32,128]{3,2,1,0:T(8,128)S(1)}, f32[4,16,16,128]{3,2,1,0:T(8,128)S(1)}, f32[4,4,16,128]{3,2,1,0...) custom-call(f32[4,32,16,128]{3,2,1,0:T(8,128)S(1)} %get-tuple-element.25.own), custom_call_target="tpu_custom_call" | custom-call | flops 20000000 | bytes 4000000 | tf_op jit(solution)/shard_map/pallas_call | solution.py:825
  8.4 0.0 collective-permute-done.x_near
  8.4 0.0 collective-permute-done.1.x_far
  8.4 0.3 shard_map.30
  8.7 2.0 %collective-permute-start.4 = (f32[4,4,24,128]{3,2,1,0:T(8,128)S(1)}, f32[4,4,24,128]{3,2,1,0:T(8,128)S(1)}, u32[]{:S(2)}, u32[]{:S(2)}) collective-permute-start(f32[4,4,24,128]{3,2,1,0:T(8,128)S(1)} %get-tuple-element.37), channel_id=1, source_target_pairs={{0,1},{1,0},{2,3},{3,2},{4,5},{5,4},{6,7},{7,6},{8,9},{9,8},{10,11... | collective-permute-start | bytes 589832 | tf_op jit(solution)/shard_map/ppermute | solution.py:835
  10.7 0.9 %collective-permute-start.5 = (f32[4,4,24,128]{3,2,1,0:T(8,128)S(1)}, f32[4,4,24,128]{3,2,1,0:T(8,128)S(1)}, u32[]{:S(2)}, u32[]{:S(2)}) collective-permute-start(f32[4,4,24,128]{3,2,1,0:T(8,128)S(1)} %get-tuple-element.38), channel_id=1, source_target_pairs={{0,16},{1,2},{2,1},{3,4},{4,3},{5,6},{6,5},{7,8},{8,7},{9,10},{10,... | collective-permute-start | bytes 589832 | tf_op jit(solution)/shard_map/ppermute | solution.py:834
  11.5 2.3 %shard_map.31 = (f32[3,34,24,128]{3,2,1,0:T(8,128)S(1)}, f32[4,8,8,128]{3,2,1,0:T(8,128)S(1)}, f32[4,16,8,128]{3,2,1,0:T(8,128)S(1)}) custom-call(f32[4,32,16,128]{3,2,1,0:T(8,128)S(1)} %get-tuple-element.25.own, f32[4,32,8,128]{3,2,1,0:T(8,128)S(1)} %get-tuple-element.30.rim, f32[3,34,32,128]{3,2,1,0:T(8,128)S(1)} %get-tuple-element.31.own_one, ...), custom_call_target="tpu_custom_call" | custom-call | flops 10000000 | bytes 4000000 | tf_op jit(solution)/shard_map/pallas_call | solution.py:836
  13.8 1.4 %collective-permute-start.3 = (f32[4,8,8,128]{3,2,1,0:T(8,128)S(1)}, f32[4,8,8,128]{3,2,1,0:T(8,128)S(1)}, u32[]{:S(2)}, u32[]{:S(2)}) collective-permute-start(f32[4,8,8,128]{3,2,1,0:T(8,128)S(1)} %get-tuple-element.34.main), channel_id=1, source_target_pairs={{0,1},{1,0},{2,3},{3,2},{4,5},{5,4},{6,7},{7,6},{8,9},{9,8},{10,11... | collective-permute-start | bytes 393224 | tf_op jit(solution)/shard_map/ppermute | solution.py:844
  15.2 2.1 %collective-permute-start.2 = (f32[4,8,8,128]{3,2,1,0:T(8,128)S(1)}, f32[4,8,8,128]{3,2,1,0:T(8,128)S(1)}, u32[]{:S(2)}, u32[]{:S(2)}) collective-permute-start(f32[4,8,8,128]{3,2,1,0:T(8,128)S(1)} %get-tuple-element.34.main), channel_id=1, source_target_pairs={{0,16},{16,0},{32,48},{48,32},{64,80},{80,64},{96,112},{112,96},{1... | collective-permute-start | bytes 393224 | tf_op jit(solution)/shard_map/ppermute | solution.py:843
  17.3 0.0 collective-permute-done.4.near
  17.3 0.0 collective-permute-done.5.far
  17.3 2.4 %shard_map.32 = (f32[3,16,16,128]{3,2,1,0:T(8,128)S(1)}, f32[4,4,8,128]{3,2,1,0:T(8,128)S(1)}) custom-call(f32[4,16,16,128]{3,2,1,0:T(8,128)S(1)} %get-tuple-element.35.edges, f32[4,16,8,128]{3,2,1,0:T(8,128)S(1)} %get-tuple-element.36.edges_rim, f32[4,4,24,128]{3,2,1,0:T(8,128)S(1)} %collective-permute-done.4.near, ...), custom_call_target="tpu_custom_call" | custom-call | flops 10000000 | bytes 4000000 | tf_op jit(solution)/shard_map/pallas_call | solution.py:845
  19.6 2.1 %collective-permute-start.7 = (f32[4,4,8,128]{3,2,1,0:T(8,128)S(1)}, f32[4,4,8,128]{3,2,1,0:T(8,128)S(1)}, u32[]{:S(2)}, u32[]{:S(2)}) collective-permute-start(f32[4,4,8,128]{3,2,1,0:T(8,128)S(1)} %get-tuple-element.39.rim), channel_id=1, source_target_pairs={{0,1},{1,0},{2,3},{3,2},{4,5},{5,4},{6,7},{7,6},{8,9},{9,8},{10,11... | collective-permute-start | bytes 196616 | tf_op jit(solution)/shard_map/ppermute | solution.py:855
  21.7 2.6 %collective-permute-start.6 = (f32[4,4,8,128]{3,2,1,0:T(8,128)S(1)}, f32[4,4,8,128]{3,2,1,0:T(8,128)S(1)}, u32[]{:S(2)}, u32[]{:S(2)}) collective-permute-start(f32[4,4,8,128]{3,2,1,0:T(8,128)S(1)} %get-tuple-element.39.rim), channel_id=1, source_target_pairs={{0,16},{16,0},{32,48},{48,32},{64,80},{80,64},{96,112},{112,96},{1... | collective-permute-start | bytes 196616 | tf_op jit(solution)/shard_map/ppermute | solution.py:854
  24.3 0.0 collective-permute-done.3.main_far
  24.3 0.0 collective-permute-done.2.main_near
  24.3 0.0 collective-permute-done.7.rim_far
  24.3 1.9 %collective-permute-done.6.rim_near = f32[4,4,8,128]{3,2,1,0:T(8,128)S(1)} collective-permute-done((f32[4,4,8,128]{3,2,1,0:T(8,128)S(1)}, f32[4,4,8,128]{3,2,1,0:T(8,128)S(1)}, u32[]{:S(2)}, u32[]{:S(2)}) %collective-permute-start.6) | collective-permute-done | bytes 65568 | tf_op jit(solution)/shard_map/ppermute | solution.py:854
  26.1 2.4 %shard_map.33 = (f32[128,4,128]{2,1,0:T(4,128)S(1)}, f32[3,16,8,128]{3,2,1,0:T(8,128)S(1)}, f32[3,8,8,128]{3,2,1,0:T(8,128)S(1)}) custom-call(f32[4,8,8,128]{3,2,1,0:T(8,128)S(1)} %get-tuple-element.34.main, f32[4,8,8,128]{3,2,1,0:T(8,128)S(1)} %collective-permute-done.2.main_near, f32[4,8,8,128]{3,2,1,0:T(8,128)S(1)} %collective-permute-done.3.main_far, ...), custom_call_target="tpu_custom_call" | custom-call | flops 1000000 | bytes 4000000 | tf_op jit(solution)/shard_map/pallas_call | solution.py:856
  28.5 27.5 %all_to_all.5 = f32[128,4,128]{2,1,0:T(4,128)S(1)} all-to-all(f32[128,4,128]{2,1,0:T(4,128)S(1)} %get-tuple-element.40), channel_id=1, replica_groups={{0,2,4,6,8,10,12,14,16,18,20,22,24,26,28,30,32,34,36,38,40,42,44,46,48,..., dimensions={0} | all-to-all | bytes 524288 | tf_op jit(solution)/shard_map/all_to_all | solution.py:865
  56.1 3.3 %collective-permute-start.8 = (f32[128,4,128]{2,1,0:T(4,128)S(1)}, f32[128,4,128]{2,1,0:T(4,128)S(1)}, u32[]{:S(2)}, u32[]{:S(2)}) collective-permute-start(f32[128,4,128]{2,1,0:T(4,128)S(1)} %all_to_all.5), channel_id=1, source_target_pairs={{0,1},{1,0},{2,3},{3,2},{4,5},{5,4},{6,7},{7,6},{8,9},{9,8},{10,11... | collective-permute-start | bytes 786440 | tf_op jit(solution)/shard_map/ppermute | solution.py:869
  59.4 0.9 %shard_map.34.base = f32[3,32,16,128]{3,2,1,0:T(8,128)S(1)} custom-call(f32[3,34,24,128]{3,2,1,0:T(8,128)S(1)} %get-tuple-element.41.two, f32[3,16,16,128]{3,2,1,0:T(8,128)S(1)} %get-tuple-element.42.rim, f32[3,16,8,128]{3,2,1,0:T(8,128)S(1)} %get-tuple-element.43.e_one, f32[3,8,8,128]{3,2,1,0:T(8,128)S(1)} %get-tuple-element.44.e_two), custom_call_target="tpu_custom_call" | custom-call | flops 1000000 | bytes 4000000 | tf_op jit(solution)/shard_map/pallas_call | solution.py:868
  60.3 0.3 collective-permute-done.8
  60.5 4.6 %shard_map.35 = f32[3,32,16,128]{3,2,1,0:T(8,128)} custom-call(f32[512,128]{1,0:T(8,128)S(1)} %bitcast.2, f32[512,128]{1,0:T(8,128)S(1)} %bitcast.3, f32[3,32,16,128]{3,2,1,0:T(8,128)S(1)} %shard_map.34.base), custom_call_target="tpu_custom_call" | custom-call | flops 1000000 | bytes 4000000 | tf_op jit(solution)/shard_map/pallas_call | solution.py:870
Async XLA Ops:
  1.3 7.1 %collective-permute-start = (f32[12,32,128]{2,1,0:T(8,128)S(1)}, f32[12,32,128]{2,1,0:T(8,128)S(1)}, u32[]{:S(2)}, u32[]{:S(2)}) collective-permute-start(f32[12,32,128]{2,1,0:T(8,128)S(1)} %get-tuple-element.28), channel_id=1, source_target_pairs={{0,16},{16,0},{32,48},{48,32},{64,80},{80,64},{96,112},{112,96},{1... | collective-permute-start | bytes 589832 | tf_op jit(solution)/shard_map/ppermute | solution.py:823
  3.4 5.0 %collective-permute-start.1 = (f32[12,32,128]{2,1,0:T(8,128)S(1)}, f32[12,32,128]{2,1,0:T(8,128)S(1)}, u32[]{:S(2)}, u32[]{:S(2)}) collective-permute-start(f32[12,32,128]{2,1,0:T(8,128)S(1)} %get-tuple-element.29), channel_id=1, source_target_pairs={{0,1},{1,0},{2,3},{3,2},{4,5},{5,4},{6,7},{7,6},{8,9},{9,8},{10,11... | collective-permute-start | bytes 589832 | tf_op jit(solution)/shard_map/ppermute | solution.py:824
  8.7 8.6 %collective-permute-start.4 = (f32[4,4,24,128]{3,2,1,0:T(8,128)S(1)}, f32[4,4,24,128]{3,2,1,0:T(8,128)S(1)}, u32[]{:S(2)}, u32[]{:S(2)}) collective-permute-start(f32[4,4,24,128]{3,2,1,0:T(8,128)S(1)} %get-tuple-element.37), channel_id=1, source_target_pairs={{0,1},{1,0},{2,3},{3,2},{4,5},{5,4},{6,7},{7,6},{8,9},{9,8},{10,11... | collective-permute-start | bytes 589832 | tf_op jit(solution)/shard_map/ppermute | solution.py:835
  10.7 6.6 %collective-permute-start.5 = (f32[4,4,24,128]{3,2,1,0:T(8,128)S(1)}, f32[4,4,24,128]{3,2,1,0:T(8,128)S(1)}, u32[]{:S(2)}, u32[]{:S(2)}) collective-permute-start(f32[4,4,24,128]{3,2,1,0:T(8,128)S(1)} %get-tuple-element.38), channel_id=1, source_target_pairs={{0,16},{1,2},{2,1},{3,4},{4,3},{5,6},{6,5},{7,8},{8,7},{9,10},{10,... | collective-permute-start | bytes 589832 | tf_op jit(solution)/shard_map/ppermute | solution.py:834
  13.8 10.4 %collective-permute-start.3 = (f32[4,8,8,128]{3,2,1,0:T(8,128)S(1)}, f32[4,8,8,128]{3,2,1,0:T(8,128)S(1)}, u32[]{:S(2)}, u32[]{:S(2)}) collective-permute-start(f32[4,8,8,128]{3,2,1,0:T(8,128)S(1)} %get-tuple-element.34.main), channel_id=1, source_target_pairs={{0,1},{1,0},{2,3},{3,2},{4,5},{5,4},{6,7},{7,6},{8,9},{9,8},{10,11... | collective-permute-start | bytes 393224 | tf_op jit(solution)/shard_map/ppermute | solution.py:844
  15.2 9.1 %collective-permute-start.2 = (f32[4,8,8,128]{3,2,1,0:T(8,128)S(1)}, f32[4,8,8,128]{3,2,1,0:T(8,128)S(1)}, u32[]{:S(2)}, u32[]{:S(2)}) collective-permute-start(f32[4,8,8,128]{3,2,1,0:T(8,128)S(1)} %get-tuple-element.34.main), channel_id=1, source_target_pairs={{0,16},{16,0},{32,48},{48,32},{64,80},{80,64},{96,112},{112,96},{1... | collective-permute-start | bytes 393224 | tf_op jit(solution)/shard_map/ppermute | solution.py:843
  19.6 4.6 %collective-permute-start.7 = (f32[4,4,8,128]{3,2,1,0:T(8,128)S(1)}, f32[4,4,8,128]{3,2,1,0:T(8,128)S(1)}, u32[]{:S(2)}, u32[]{:S(2)}) collective-permute-start(f32[4,4,8,128]{3,2,1,0:T(8,128)S(1)} %get-tuple-element.39.rim), channel_id=1, source_target_pairs={{0,1},{1,0},{2,3},{3,2},{4,5},{5,4},{6,7},{7,6},{8,9},{9,8},{10,11... | collective-permute-start | bytes 196616 | tf_op jit(solution)/shard_map/ppermute | solution.py:855
  21.7 4.4 %collective-permute-start.6 = (f32[4,4,8,128]{3,2,1,0:T(8,128)S(1)}, f32[4,4,8,128]{3,2,1,0:T(8,128)S(1)}, u32[]{:S(2)}, u32[]{:S(2)}) collective-permute-start(f32[4,4,8,128]{3,2,1,0:T(8,128)S(1)} %get-tuple-element.39.rim), channel_id=1, source_target_pairs={{0,16},{16,0},{32,48},{48,32},{64,80},{80,64},{96,112},{112,96},{1... | collective-permute-start | bytes 196616 | tf_op jit(solution)/shard_map/ppermute | solution.py:854
  56.1 4.5 %collective-permute-start.8 = (f32[128,4,128]{2,1,0:T(4,128)S(1)}, f32[128,4,128]{2,1,0:T(4,128)S(1)}, u32[]{:S(2)}, u32[]{:S(2)}) collective-permute-start(f32[128,4,128]{2,1,0:T(4,128)S(1)} %all_to_all.5), channel_id=1, source_target_pairs={{0,1},{1,0},{2,3},{3,2},{4,5},{5,4},{6,7},{7,6},{8,9},{9,8},{10,11... | collective-permute-start | bytes 786440 | tf_op jit(solution)/shard_map/ppermute | solution.py:869

commit v16 on v13

--- a/solution.py
+++ b/solution.py
@@ -281,7 +281,7 @@
                 ref[f, z + 1, 0:8, :] = source[f, z + 1, 16:24, :]
                 ref[f, z + 1, 16:24, :] = source[f, z + 1, 8:16, :]
 
-    loop(32, fill, 8)
+    loop(32, fill, 16)
     upper = iota((8, 128), 0) < 4
 
     def both(ref, lead, step, shift=0):
@@ -360,7 +360,7 @@
         for ch in range(4):
             edges[ch, z] = edge_columns(lambda at: rim[ch, at], z, (8, 128))
 
-    loop(16, edge, 8)
+    loop(16, edge, 16)
 
 
 def rim_kernel(
@@ -390,7 +390,7 @@
                 target[z + 1, 0:8, :] = value[16:24]
                 target[z + 1, 24:32, :] = value[16:24]
 
-    loop(4, unpack, 2)
+    loop(4, unpack, 4)
 
     half_of = iota((32, 128), 1)
 
@@ -517,7 +517,7 @@
                             rest[z + 1, pl.ds(at, 8), :] = resist(value)
                 rest[z + 1, 24:32, :] = jnp.full((8, 128), 0.5, F32)
 
-    loop(4, fill, 2)
+    loop(4, fill, 4)
 
     row, lane = iota((24, 128), 0) + 1, iota((24, 128), 1)
     in_x = jnp.where(row < 8, low_x, jnp.where(row >= 16, high_x, 1))
@@ -639,15 +639,6 @@
     return x
 
 
-def lay_kernel(mine, laid):
-    def lay(g):
-        for ch in range(4):
-            tile = swap_blocks(mine[pl.ds(32 * g + ch, 8, stride=4), :])
-            laid[ch, pl.ds(pl.multiple_of(8 * g, 8), 8), :] = tile
-
-    loop(16, lay, 4)
-
-
 def top_kernel(
     mine, other, base, out,
     natural, first, second, four, weights, diags, lefts, final, sems,
@@ -657,13 +648,16 @@
     lane, sub = iota((16, 128), 1), iota((16, 128), 0)
     cells = [(z, x, half) for z in range(4) for x in range(2) for half in range(2)]
 
-    parity = lax.rem(gy, 2)
-
     def lay(g):
         for ch in range(4):
-            at = pl.ds(pl.multiple_of(8 * g, 8), 8)
-            natural[ch, parity, at, :] = mine[ch, at, :]
-            natural[ch, 1 - parity, at, :] = swap_blocks(other[pl.ds(32 * g + ch, 8, stride=4), :])
+            rows = pl.ds(32 * g + ch, 8, stride=4)
+            pair = mine[rows, :], other[rows, :]
+            natural[ch, 0, pl.ds(pl.multiple_of(8 * g, 8), 8), :] = swap_blocks(
+                jnp.where(first_core, pair[0], pair[1])
+            )
+            natural[ch, 1, pl.ds(pl.multiple_of(8 * g, 8), 8), :] = swap_blocks(
+                jnp.where(first_core, pair[1], pair[0])
+            )
 
     loop(16, lay, 4)
     flat = natural.reshape(1024, 128)
@@ -867,14 +861,13 @@
     )
     (base,) = call(base_kernel, [(3, 32, 16, 128)], [(192, 128), (3, 16, 16, 128)])(two, rim, e_one, e_two)
     other = lax.ppermute(mine, "gy", swap_near)
-    (laid,) = call(lay_kernel, [(4, 128, 128)], [])(mine.reshape(512, 128))
     (out,) = call(
         top_kernel,
         [(3, 32, 16, 128)],
         [(4, 2, 128, 128), (3, 16, 16, 128), (2, 3, 8, 16, 128), (6, 16, 128), (6, 16, 16, 128)]
         + [(16, 16, 128), (4, 2, 16, 256), (3, 32, 16, 128), pltpu.SemaphoreType.DMA((6,))],
         out_specs=[ANY],
-    )(laid, other.reshape(512, 128), base)
+    )(mine.reshape(512, 128), other.reshape(512, 128), base)
     return out
 
 

time: 65.4 us -> 64.5 us (0.986)
  Pallas kernels: 18 us -> 16.5 us
    pallas_call x1 -> x0, Pallas kernels: 0.96 us -> none  [local(): laid, = call(lay_kernel, [(4, 128, 128)], [])(mine.reshape(512, 128))]
  transfers between devices with their start and end apart: 9 -> 9, of which waited for: 1 -> 2; matrix products, arithmetic and copies ran while one was open for 0% -> 0% of each run, Pallas kernels for 16% -> 14%
where the time goes in v16:
time: 64.5 us; the launch traced here: 64.4 us
  blocking collectives  27.9 us (43%)
  starting transfers between devices  17.6 us (27%)
  Pallas kernels  16.5 us (26%)
  waiting for transfers between devices  2.14 us (3%)
    all_to_all x1, blocking collectives, local(): lax.all_to_all(sent, ('gx', 'gy'), split_axis=0, concat_axis=0, axis_inde...  27.9 us
    pallas_call x1, Pallas kernels, local(): call(top_kernel, [(3, 32, 16, 128)], [(4, 2, 128, 128), (3, 16, 16, 128),...  4 us
    pallas_call x1, Pallas kernels, local(): call(own_kernel, [(3, 34, 32, 128)] * 2 + [(4, 16, 16, 128)] + [(4, 4, 16...  3.66 us
    ppermute x1, starting transfers between devices, local(): other = lax.ppermute(mine, 'gy', swap_near)  3.3 us
    ppermute x1, starting transfers between devices, local(): rim_near = lax.ppermute(rim_one, 'gx', swap_near)  2.56 us
    pallas_call x1, Pallas kernels, local(): call(rim_kernel, [(3, 16, 16, 128), (4, 4, 8, 128)], [(3, 18, 32, 128), (...  2.24 us
    pallas_call x1, Pallas kernels, local(): call(middle_kernel, [(CHIPS, 4, 128), (3, 16, 8, 128), (3, 8, 8, 128)], [...  2.22 us
    ppermute x1, starting transfers between devices, local(): from_near = lax.ppermute(to_near, 'gx', swap_near)  2.13 us
  transfers between devices with their start and end apart: 9, of which 2 were waited for; matrix products, arithmetic and copies ran while one was open for 0% of the time, Pallas kernels for 14%

profile of v16, /device:TPU:1, one launch (start us, length us, event | category | flops | bytes accessed | tf_op | source)
XLA Modules:
  0.0 64.4 jit_solution(13195360247115833595)
XLA Ops:
  0.0 1.3 %shard_map.28 = (f32[12,32,128]{2,1,0:T(8,128)S(1)}, f32[12,32,128]{2,1,0:T(8,128)S(1)}, f32[4,32,16,128]{3,2,1,0:T(8,128)S(1)}) custom-call(f32[3,32,16,128]{3,2,1,0:T(8,128)} %guess.1, s32[32,16,128]{2,1,0:T(8,128)} %labels.1), custom_call_target="tpu_custom_call" | custom-call | flops 1000000 | bytes 4000000 | tf_op jit(solution)/shard_map/pallas_call | solution.py:811
  1.3 2.1 %collective-permute-start = (f32[12,32,128]{2,1,0:T(8,128)S(1)}, f32[12,32,128]{2,1,0:T(8,128)S(1)}, u32[]{:S(2)}, u32[]{:S(2)}) collective-permute-start(f32[12,32,128]{2,1,0:T(8,128)S(1)} %get-tuple-element.28), channel_id=1, source_target_pairs={{0,16},{16,0},{32,48},{48,32},{64,80},{80,64},{96,112},{112,96},{1... | collective-permute-start | bytes 589832 | tf_op jit(solution)/shard_map/ppermute | solution.py:817
  3.4 1.3 %collective-permute-start.1 = (f32[12,32,128]{2,1,0:T(8,128)S(1)}, f32[12,32,128]{2,1,0:T(8,128)S(1)}, u32[]{:S(2)}, u32[]{:S(2)}) collective-permute-start(f32[12,32,128]{2,1,0:T(8,128)S(1)} %get-tuple-element.29), channel_id=1, source_target_pairs={{0,1},{1,0},{2,3},{3,2},{4,5},{5,4},{6,7},{7,6},{8,9},{9,8},{10,11... | collective-permute-start | bytes 589832 | tf_op jit(solution)/shard_map/ppermute | solution.py:818
  4.7 3.7 %shard_map.29 = (f32[3,34,32,128]{3,2,1,0:T(8,128)S(1)}, f32[3,34,32,128]{3,2,1,0:T(8,128)S(1)}, f32[4,16,16,128]{3,2,1,0:T(8,128)S(1)}, f32[4,4,16,128]{3,2,1,0...) custom-call(f32[4,32,16,128]{3,2,1,0:T(8,128)S(1)} %get-tuple-element.25.own), custom_call_target="tpu_custom_call" | custom-call | flops 20000000 | bytes 4000000 | tf_op jit(solution)/shard_map/pallas_call | solution.py:819
  8.4 0.0 collective-permute-done.x_near
  8.4 0.0 collective-permute-done.1.x_far
  8.4 0.3 shard_map.30
  8.7 2.0 %collective-permute-start.4 = (f32[4,4,24,128]{3,2,1,0:T(8,128)S(1)}, f32[4,4,24,128]{3,2,1,0:T(8,128)S(1)}, u32[]{:S(2)}, u32[]{:S(2)}) collective-permute-start(f32[4,4,24,128]{3,2,1,0:T(8,128)S(1)} %get-tuple-element.37), channel_id=1, source_target_pairs={{0,1},{1,0},{2,3},{3,2},{4,5},{5,4},{6,7},{7,6},{8,9},{9,8},{10,11... | collective-permute-start | bytes 589832 | tf_op jit(solution)/shard_map/ppermute | solution.py:829
  10.7 0.9 %collective-permute-start.5 = (f32[4,4,24,128]{3,2,1,0:T(8,128)S(1)}, f32[4,4,24,128]{3,2,1,0:T(8,128)S(1)}, u32[]{:S(2)}, u32[]{:S(2)}) collective-permute-start(f32[4,4,24,128]{3,2,1,0:T(8,128)S(1)} %get-tuple-element.38), channel_id=1, source_target_pairs={{0,16},{1,2},{2,1},{3,4},{4,3},{5,6},{6,5},{7,8},{8,7},{9,10},{10,... | collective-permute-start | bytes 589832 | tf_op jit(solution)/shard_map/ppermute | solution.py:828
  11.5 2.0 %shard_map.31 = (f32[3,34,24,128]{3,2,1,0:T(8,128)S(1)}, f32[4,8,8,128]{3,2,1,0:T(8,128)S(1)}, f32[4,16,8,128]{3,2,1,0:T(8,128)S(1)}) custom-call(f32[4,32,16,128]{3,2,1,0:T(8,128)S(1)} %get-tuple-element.25.own, f32[4,32,8,128]{3,2,1,0:T(8,128)S(1)} %get-tuple-element.30.rim, f32[3,34,32,128]{3,2,1,0:T(8,128)S(1)} %get-tuple-element.31.own_one, ...), custom_call_target="tpu_custom_call" | custom-call | flops 10000000 | bytes 4000000 | tf_op jit(solution)/shard_map/pallas_call | solution.py:830
  13.5 1.4 %collective-permute-start.3 = (f32[4,8,8,128]{3,2,1,0:T(8,128)S(1)}, f32[4,8,8,128]{3,2,1,0:T(8,128)S(1)}, u32[]{:S(2)}, u32[]{:S(2)}) collective-permute-start(f32[4,8,8,128]{3,2,1,0:T(8,128)S(1)} %get-tuple-element.34.main), channel_id=1, source_target_pairs={{0,1},{1,0},{2,3},{3,2},{4,5},{5,4},{6,7},{7,6},{8,9},{9,8},{10,11... | collective-permute-start | bytes 393224 | tf_op jit(solution)/shard_map/ppermute | solution.py:838
  14.8 2.1 %collective-permute-start.2 = (f32[4,8,8,128]{3,2,1,0:T(8,128)S(1)}, f32[4,8,8,128]{3,2,1,0:T(8,128)S(1)}, u32[]{:S(2)}, u32[]{:S(2)}) collective-permute-start(f32[4,8,8,128]{3,2,1,0:T(8,128)S(1)} %get-tuple-element.34.main), channel_id=1, source_target_pairs={{0,16},{16,0},{32,48},{48,32},{64,80},{80,64},{96,112},{112,96},{1... | collective-permute-start | bytes 393224 | tf_op jit(solution)/shard_map/ppermute | solution.py:837
  16.9 0.0 collective-permute-done.4.near
  16.9 0.0 collective-permute-done.5.far
  16.9 2.2 %shard_map.32 = (f32[3,16,16,128]{3,2,1,0:T(8,128)S(1)}, f32[4,4,8,128]{3,2,1,0:T(8,128)S(1)}) custom-call(f32[4,16,16,128]{3,2,1,0:T(8,128)S(1)} %get-tuple-element.35.edges, f32[4,16,8,128]{3,2,1,0:T(8,128)S(1)} %get-tuple-element.36.edges_rim, f32[4,4,24,128]{3,2,1,0:T(8,128)S(1)} %collective-permute-done.4.near, ...), custom_call_target="tpu_custom_call" | custom-call | flops 10000000 | bytes 4000000 | tf_op jit(solution)/shard_map/pallas_call | solution.py:839
  19.2 2.1 %collective-permute-start.7 = (f32[4,4,8,128]{3,2,1,0:T(8,128)S(1)}, f32[4,4,8,128]{3,2,1,0:T(8,128)S(1)}, u32[]{:S(2)}, u32[]{:S(2)}) collective-permute-start(f32[4,4,8,128]{3,2,1,0:T(8,128)S(1)} %get-tuple-element.39.rim), channel_id=1, source_target_pairs={{0,1},{1,0},{2,3},{3,2},{4,5},{5,4},{6,7},{7,6},{8,9},{9,8},{10,11... | collective-permute-start | bytes 196616 | tf_op jit(solution)/shard_map/ppermute | solution.py:849
  21.2 2.6 %collective-permute-start.6 = (f32[4,4,8,128]{3,2,1,0:T(8,128)S(1)}, f32[4,4,8,128]{3,2,1,0:T(8,128)S(1)}, u32[]{:S(2)}, u32[]{:S(2)}) collective-permute-start(f32[4,4,8,128]{3,2,1,0:T(8,128)S(1)} %get-tuple-element.39.rim), channel_id=1, source_target_pairs={{0,16},{16,0},{32,48},{48,32},{64,80},{80,64},{96,112},{112,96},{1... | collective-permute-start | bytes 196616 | tf_op jit(solution)/shard_map/ppermute | solution.py:848
  23.8 0.0 collective-permute-done.3.main_far
  23.8 0.0 collective-permute-done.2.main_near
  23.8 0.0 collective-permute-done.7.rim_far
  23.8 1.9 %collective-permute-done.6.rim_near = f32[4,4,8,128]{3,2,1,0:T(8,128)S(1)} collective-permute-done((f32[4,4,8,128]{3,2,1,0:T(8,128)S(1)}, f32[4,4,8,128]{3,2,1,0:T(8,128)S(1)}, u32[]{:S(2)}, u32[]{:S(2)}) %collective-permute-start.6) | collective-permute-done | bytes 65568 | tf_op jit(solution)/shard_map/ppermute | solution.py:848
  25.7 2.2 %shard_map.33 = (f32[128,4,128]{2,1,0:T(4,128)S(1)}, f32[3,16,8,128]{3,2,1,0:T(8,128)S(1)}, f32[3,8,8,128]{3,2,1,0:T(8,128)S(1)}) custom-call(f32[4,8,8,128]{3,2,1,0:T(8,128)S(1)} %get-tuple-element.34.main, f32[4,8,8,128]{3,2,1,0:T(8,128)S(1)} %collective-permute-done.2.main_near, f32[4,8,8,128]{3,2,1,0:T(8,128)S(1)} %collective-permute-done.3.main_far, ...), custom_call_target="tpu_custom_call" | custom-call | flops 1000000 | bytes 4000000 | tf_op jit(solution)/shard_map/pallas_call | solution.py:850
  27.9 27.9 %all_to_all.5 = f32[128,4,128]{2,1,0:T(4,128)S(1)} all-to-all(f32[128,4,128]{2,1,0:T(4,128)S(1)} %get-tuple-element.40), channel_id=1, replica_groups={{0,2,4,6,8,10,12,14,16,18,20,22,24,26,28,30,32,34,36,38,40,42,44,46,48,..., dimensions={0} | all-to-all | bytes 524288 | tf_op jit(solution)/shard_map/all_to_all | solution.py:859
  55.8 3.3 %collective-permute-start.8 = (f32[128,4,128]{2,1,0:T(4,128)S(1)}, f32[128,4,128]{2,1,0:T(4,128)S(1)}, u32[]{:S(2)}, u32[]{:S(2)}) collective-permute-start(f32[128,4,128]{2,1,0:T(4,128)S(1)} %all_to_all.5), channel_id=1, source_target_pairs={{0,1},{1,0},{2,3},{3,2},{4,5},{5,4},{6,7},{7,6},{8,9},{9,8},{10,11... | collective-permute-start | bytes 786440 | tf_op jit(solution)/shard_map/ppermute | solution.py:863
  59.1 0.9 %shard_map.34.base = f32[3,32,16,128]{3,2,1,0:T(8,128)S(1)} custom-call(f32[3,34,24,128]{3,2,1,0:T(8,128)S(1)} %get-tuple-element.41.two, f32[3,16,16,128]{3,2,1,0:T(8,128)S(1)} %get-tuple-element.42.rim, f32[3,16,8,128]{3,2,1,0:T(8,128)S(1)} %get-tuple-element.43.e_one, f32[3,8,8,128]{3,2,1,0:T(8,128)S(1)} %get-tuple-element.44.e_two), custom_call_target="tpu_custom_call" | custom-call | flops 1000000 | bytes 4000000 | tf_op jit(solution)/shard_map/pallas_call | solution.py:862
  60.0 0.3 collective-permute-done.8
  60.2 4.0 %shard_map.35 = f32[3,32,16,128]{3,2,1,0:T(8,128)} custom-call(f32[512,128]{1,0:T(8,128)S(1)} %bitcast.2, f32[512,128]{1,0:T(8,128)S(1)} %bitcast.3, f32[3,32,16,128]{3,2,1,0:T(8,128)S(1)} %shard_map.34.base), custom_call_target="tpu_custom_call" | custom-call | flops 1000000 | bytes 4000000 | tf_op jit(solution)/shard_map/pallas_call | solution.py:864
Async XLA Ops:
  1.3 7.1 %collective-permute-start = (f32[12,32,128]{2,1,0:T(8,128)S(1)}, f32[12,32,128]{2,1,0:T(8,128)S(1)}, u32[]{:S(2)}, u32[]{:S(2)}) collective-permute-start(f32[12,32,128]{2,1,0:T(8,128)S(1)} %get-tuple-element.28), channel_id=1, source_target_pairs={{0,16},{16,0},{32,48},{48,32},{64,80},{80,64},{96,112},{112,96},{1... | collective-permute-start | bytes 589832 | tf_op jit(solution)/shard_map/ppermute | solution.py:817
  3.4 5.0 %collective-permute-start.1 = (f32[12,32,128]{2,1,0:T(8,128)S(1)}, f32[12,32,128]{2,1,0:T(8,128)S(1)}, u32[]{:S(2)}, u32[]{:S(2)}) collective-permute-start(f32[12,32,128]{2,1,0:T(8,128)S(1)} %get-tuple-element.29), channel_id=1, source_target_pairs={{0,1},{1,0},{2,3},{3,2},{4,5},{5,4},{6,7},{7,6},{8,9},{9,8},{10,11... | collective-permute-start | bytes 589832 | tf_op jit(solution)/shard_map/ppermute | solution.py:818
  8.7 8.2 %collective-permute-start.4 = (f32[4,4,24,128]{3,2,1,0:T(8,128)S(1)}, f32[4,4,24,128]{3,2,1,0:T(8,128)S(1)}, u32[]{:S(2)}, u32[]{:S(2)}) collective-permute-start(f32[4,4,24,128]{3,2,1,0:T(8,128)S(1)} %get-tuple-element.37), channel_id=1, source_target_pairs={{0,1},{1,0},{2,3},{3,2},{4,5},{5,4},{6,7},{7,6},{8,9},{9,8},{10,11... | collective-permute-start | bytes 589832 | tf_op jit(solution)/shard_map/ppermute | solution.py:829
  10.7 6.3 %collective-permute-start.5 = (f32[4,4,24,128]{3,2,1,0:T(8,128)S(1)}, f32[4,4,24,128]{3,2,1,0:T(8,128)S(1)}, u32[]{:S(2)}, u32[]{:S(2)}) collective-permute-start(f32[4,4,24,128]{3,2,1,0:T(8,128)S(1)} %get-tuple-element.38), channel_id=1, source_target_pairs={{0,16},{1,2},{2,1},{3,4},{4,3},{5,6},{6,5},{7,8},{8,7},{9,10},{10,... | collective-permute-start | bytes 589832 | tf_op jit(solution)/shard_map/ppermute | solution.py:828
  13.5 10.3 %collective-permute-start.3 = (f32[4,8,8,128]{3,2,1,0:T(8,128)S(1)}, f32[4,8,8,128]{3,2,1,0:T(8,128)S(1)}, u32[]{:S(2)}, u32[]{:S(2)}) collective-permute-start(f32[4,8,8,128]{3,2,1,0:T(8,128)S(1)} %get-tuple-element.34.main), channel_id=1, source_target_pairs={{0,1},{1,0},{2,3},{3,2},{4,5},{5,4},{6,7},{7,6},{8,9},{9,8},{10,11... | collective-permute-start | bytes 393224 | tf_op jit(solution)/shard_map/ppermute | solution.py:838
  14.8 8.9 %collective-permute-start.2 = (f32[4,8,8,128]{3,2,1,0:T(8,128)S(1)}, f32[4,8,8,128]{3,2,1,0:T(8,128)S(1)}, u32[]{:S(2)}, u32[]{:S(2)}) collective-permute-start(f32[4,8,8,128]{3,2,1,0:T(8,128)S(1)} %get-tuple-element.34.main), channel_id=1, source_target_pairs={{0,16},{16,0},{32,48},{48,32},{64,80},{80,64},{96,112},{112,96},{1... | collective-permute-start | bytes 393224 | tf_op jit(solution)/shard_map/ppermute | solution.py:837
  19.2 4.6 %collective-permute-start.7 = (f32[4,4,8,128]{3,2,1,0:T(8,128)S(1)}, f32[4,4,8,128]{3,2,1,0:T(8,128)S(1)}, u32[]{:S(2)}, u32[]{:S(2)}) collective-permute-start(f32[4,4,8,128]{3,2,1,0:T(8,128)S(1)} %get-tuple-element.39.rim), channel_id=1, source_target_pairs={{0,1},{1,0},{2,3},{3,2},{4,5},{5,4},{6,7},{7,6},{8,9},{9,8},{10,11... | collective-permute-start | bytes 196616 | tf_op jit(solution)/shard_map/ppermute | solution.py:849
  21.2 4.4 %collective-permute-start.6 = (f32[4,4,8,128]{3,2,1,0:T(8,128)S(1)}, f32[4,4,8,128]{3,2,1,0:T(8,128)S(1)}, u32[]{:S(2)}, u32[]{:S(2)}) collective-permute-start(f32[4,4,8,128]{3,2,1,0:T(8,128)S(1)} %get-tuple-element.39.rim), channel_id=1, source_target_pairs={{0,16},{16,0},{32,48},{48,32},{64,80},{80,64},{96,112},{112,96},{1... | collective-permute-start | bytes 196616 | tf_op jit(solution)/shard_map/ppermute | solution.py:848
  55.8 4.5 %collective-permute-start.8 = (f32[128,4,128]{2,1,0:T(4,128)S(1)}, f32[128,4,128]{2,1,0:T(4,128)S(1)}, u32[]{:S(2)}, u32[]{:S(2)}) collective-permute-start(f32[128,4,128]{2,1,0:T(4,128)S(1)} %all_to_all.5), channel_id=1, source_target_pairs={{0,1},{1,0},{2,3},{3,2},{4,5},{5,4},{6,7},{7,6},{8,9},{9,8},{10,11... | collective-permute-start | bytes 786440 | tf_op jit(solution)/shard_map/ppermute | solution.py:863

commit v17 on v16

--- a/solution.py
+++ b/solution.py
@@ -630,13 +630,14 @@
 
 
 def swap_blocks(x):
-    sub, group = iota((8, 128), 0), iota((8, 128), 1) // 16
-    for bit in (4, 2, 1):
-        up = roll(roll(x, -bit, 0), 16 * bit)
-        down = up if bit == 4 else roll(roll(x, bit, 0), -16 * bit)
-        sub_set, group_set = (sub & bit) != 0, (group & bit) != 0
-        x = jnp.where(sub_set == group_set, x, jnp.where(sub_set, down, up))
-    return x
+    apart = (iota((8, 128), 0) - iota((8, 128), 1) // 16) % 8
+    moved = [roll(roll(x, d, 0), -16 * d) for d in range(8)]
+    while len(moved) > 1:
+        bit = 8 // len(moved)
+        moved = [
+            jnp.where((apart & bit) == 0, even, odd) for even, odd in zip(moved[0::2], moved[1::2])
+        ]
+    return moved[0]
 
 
 def top_kernel(

time: 64.5 us -> 64.7 us (level)
  no operation moved by 1% of the time
where the time goes in v17:
time: 64.7 us; the launch traced here: 64.5 us
  blocking collectives  27.9 us (43%)
  starting transfers between devices  17.6 us (27%)
  Pallas kernels  16.7 us (26%)
  waiting for transfers between devices  2.14 us (3%)
    all_to_all x1, blocking collectives, local(): lax.all_to_all(sent, ('gx', 'gy'), split_axis=0, concat_axis=0, axis_inde...  27.9 us
    pallas_call x1, Pallas kernels, local(): call(top_kernel, [(3, 32, 16, 128)], [(4, 2, 128, 128), (3, 16, 16, 128),...  4.13 us
    pallas_call x1, Pallas kernels, local(): call(own_kernel, [(3, 34, 32, 128)] * 2 + [(4, 16, 16, 128)] + [(4, 4, 16...  3.66 us
    ppermute x1, starting transfers between devices, local(): other = lax.ppermute(mine, 'gy', swap_near)  3.3 us
    ppermute x1, starting transfers between devices, local(): rim_near = lax.ppermute(rim_one, 'gx', swap_near)  2.56 us
    pallas_call x1, Pallas kernels, local(): call(rim_kernel, [(3, 16, 16, 128), (4, 4, 8, 128)], [(3, 18, 32, 128), (...  2.24 us
    pallas_call x1, Pallas kernels, local(): call(middle_kernel, [(CHIPS, 4, 128), (3, 16, 8, 128), (3, 8, 8, 128)], [...  2.22 us
    ppermute x1, starting transfers between devices, local(): from_near = lax.ppermute(to_near, 'gx', swap_near)  2.13 us
  transfers between devices with their start and end apart: 9, of which 2 were waited for; matrix products, arithmetic and copies ran while one was open for 0% of the time, Pallas kernels for 14%

profile of v17, /device:TPU:1, one launch (start us, length us, event | category | flops | bytes accessed | tf_op | source)
XLA Modules:
  0.0 64.5 jit_solution(8209008623334308758)
XLA Ops:
  0.0 1.3 %shard_map.28 = (f32[12,32,128]{2,1,0:T(8,128)S(1)}, f32[12,32,128]{2,1,0:T(8,128)S(1)}, f32[4,32,16,128]{3,2,1,0:T(8,128)S(1)}) custom-call(f32[3,32,16,128]{3,2,1,0:T(8,128)} %guess.1, s32[32,16,128]{2,1,0:T(8,128)} %labels.1), custom_call_target="tpu_custom_call" | custom-call | flops 1000000 | bytes 4000000 | tf_op jit(solution)/shard_map/pallas_call | solution.py:812
  1.3 2.1 %collective-permute-start = (f32[12,32,128]{2,1,0:T(8,128)S(1)}, f32[12,32,128]{2,1,0:T(8,128)S(1)}, u32[]{:S(2)}, u32[]{:S(2)}) collective-permute-start(f32[12,32,128]{2,1,0:T(8,128)S(1)} %get-tuple-element.28), channel_id=1, source_target_pairs={{0,16},{16,0},{32,48},{48,32},{64,80},{80,64},{96,112},{112,96},{1... | collective-permute-start | bytes 589832 | tf_op jit(solution)/shard_map/ppermute | solution.py:818
  3.4 1.3 %collective-permute-start.1 = (f32[12,32,128]{2,1,0:T(8,128)S(1)}, f32[12,32,128]{2,1,0:T(8,128)S(1)}, u32[]{:S(2)}, u32[]{:S(2)}) collective-permute-start(f32[12,32,128]{2,1,0:T(8,128)S(1)} %get-tuple-element.29), channel_id=1, source_target_pairs={{0,1},{1,0},{2,3},{3,2},{4,5},{5,4},{6,7},{7,6},{8,9},{9,8},{10,11... | collective-permute-start | bytes 589832 | tf_op jit(solution)/shard_map/ppermute | solution.py:819
  4.7 3.7 %shard_map.29 = (f32[3,34,32,128]{3,2,1,0:T(8,128)S(1)}, f32[3,34,32,128]{3,2,1,0:T(8,128)S(1)}, f32[4,16,16,128]{3,2,1,0:T(8,128)S(1)}, f32[4,4,16,128]{3,2,1,0...) custom-call(f32[4,32,16,128]{3,2,1,0:T(8,128)S(1)} %get-tuple-element.25.own), custom_call_target="tpu_custom_call" | custom-call | flops 20000000 | bytes 4000000 | tf_op jit(solution)/shard_map/pallas_call | solution.py:820
  8.4 0.0 collective-permute-done.x_near
  8.4 0.0 collective-permute-done.1.x_far
  8.4 0.3 shard_map.30
  8.7 2.0 %collective-permute-start.4 = (f32[4,4,24,128]{3,2,1,0:T(8,128)S(1)}, f32[4,4,24,128]{3,2,1,0:T(8,128)S(1)}, u32[]{:S(2)}, u32[]{:S(2)}) collective-permute-start(f32[4,4,24,128]{3,2,1,0:T(8,128)S(1)} %get-tuple-element.37), channel_id=1, source_target_pairs={{0,1},{1,0},{2,3},{3,2},{4,5},{5,4},{6,7},{7,6},{8,9},{9,8},{10,11... | collective-permute-start | bytes 589832 | tf_op jit(solution)/shard_map/ppermute | solution.py:830
  10.7 0.9 %collective-permute-start.5 = (f32[4,4,24,128]{3,2,1,0:T(8,128)S(1)}, f32[4,4,24,128]{3,2,1,0:T(8,128)S(1)}, u32[]{:S(2)}, u32[]{:S(2)}) collective-permute-start(f32[4,4,24,128]{3,2,1,0:T(8,128)S(1)} %get-tuple-element.38), channel_id=1, source_target_pairs={{0,16},{1,2},{2,1},{3,4},{4,3},{5,6},{6,5},{7,8},{8,7},{9,10},{10,... | collective-permute-start | bytes 589832 | tf_op jit(solution)/shard_map/ppermute | solution.py:829
  11.5 2.0 %shard_map.31 = (f32[3,34,24,128]{3,2,1,0:T(8,128)S(1)}, f32[4,8,8,128]{3,2,1,0:T(8,128)S(1)}, f32[4,16,8,128]{3,2,1,0:T(8,128)S(1)}) custom-call(f32[4,32,16,128]{3,2,1,0:T(8,128)S(1)} %get-tuple-element.25.own, f32[4,32,8,128]{3,2,1,0:T(8,128)S(1)} %get-tuple-element.30.rim, f32[3,34,32,128]{3,2,1,0:T(8,128)S(1)} %get-tuple-element.31.own_one, ...), custom_call_target="tpu_custom_call" | custom-call | flops 10000000 | bytes 4000000 | tf_op jit(solution)/shard_map/pallas_call | solution.py:831
  13.5 1.4 %collective-permute-start.3 = (f32[4,8,8,128]{3,2,1,0:T(8,128)S(1)}, f32[4,8,8,128]{3,2,1,0:T(8,128)S(1)}, u32[]{:S(2)}, u32[]{:S(2)}) collective-permute-start(f32[4,8,8,128]{3,2,1,0:T(8,128)S(1)} %get-tuple-element.34.main), channel_id=1, source_target_pairs={{0,1},{1,0},{2,3},{3,2},{4,5},{5,4},{6,7},{7,6},{8,9},{9,8},{10,11... | collective-permute-start | bytes 393224 | tf_op jit(solution)/shard_map/ppermute | solution.py:839
  14.8 2.1 %collective-permute-start.2 = (f32[4,8,8,128]{3,2,1,0:T(8,128)S(1)}, f32[4,8,8,128]{3,2,1,0:T(8,128)S(1)}, u32[]{:S(2)}, u32[]{:S(2)}) collective-permute-start(f32[4,8,8,128]{3,2,1,0:T(8,128)S(1)} %get-tuple-element.34.main), channel_id=1, source_target_pairs={{0,16},{16,0},{32,48},{48,32},{64,80},{80,64},{96,112},{112,96},{1... | collective-permute-start | bytes 393224 | tf_op jit(solution)/shard_map/ppermute | solution.py:838
  16.9 0.0 collective-permute-done.4.near
  16.9 0.0 collective-permute-done.5.far
  16.9 2.2 %shard_map.32 = (f32[3,16,16,128]{3,2,1,0:T(8,128)S(1)}, f32[4,4,8,128]{3,2,1,0:T(8,128)S(1)}) custom-call(f32[4,16,16,128]{3,2,1,0:T(8,128)S(1)} %get-tuple-element.35.edges, f32[4,16,8,128]{3,2,1,0:T(8,128)S(1)} %get-tuple-element.36.edges_rim, f32[4,4,24,128]{3,2,1,0:T(8,128)S(1)} %collective-permute-done.4.near, ...), custom_call_target="tpu_custom_call" | custom-call | flops 10000000 | bytes 4000000 | tf_op jit(solution)/shard_map/pallas_call | solution.py:840
  19.2 2.1 %collective-permute-start.7 = (f32[4,4,8,128]{3,2,1,0:T(8,128)S(1)}, f32[4,4,8,128]{3,2,1,0:T(8,128)S(1)}, u32[]{:S(2)}, u32[]{:S(2)}) collective-permute-start(f32[4,4,8,128]{3,2,1,0:T(8,128)S(1)} %get-tuple-element.39.rim), channel_id=1, source_target_pairs={{0,1},{1,0},{2,3},{3,2},{4,5},{5,4},{6,7},{7,6},{8,9},{9,8},{10,11... | collective-permute-start | bytes 196616 | tf_op jit(solution)/shard_map/ppermute | solution.py:850
  21.2 2.6 %collective-permute-start.6 = (f32[4,4,8,128]{3,2,1,0:T(8,128)S(1)}, f32[4,4,8,128]{3,2,1,0:T(8,128)S(1)}, u32[]{:S(2)}, u32[]{:S(2)}) collective-permute-start(f32[4,4,8,128]{3,2,1,0:T(8,128)S(1)} %get-tuple-element.39.rim), channel_id=1, source_target_pairs={{0,16},{16,0},{32,48},{48,32},{64,80},{80,64},{96,112},{112,96},{1... | collective-permute-start | bytes 196616 | tf_op jit(solution)/shard_map/ppermute | solution.py:849
  23.8 0.0 collective-permute-done.3.main_far
  23.8 0.0 collective-permute-done.2.main_near
  23.8 0.0 collective-permute-done.7.rim_far
  23.8 1.9 %collective-permute-done.6.rim_near = f32[4,4,8,128]{3,2,1,0:T(8,128)S(1)} collective-permute-done((f32[4,4,8,128]{3,2,1,0:T(8,128)S(1)}, f32[4,4,8,128]{3,2,1,0:T(8,128)S(1)}, u32[]{:S(2)}, u32[]{:S(2)}) %collective-permute-start.6) | collective-permute-done | bytes 65568 | tf_op jit(solution)/shard_map/ppermute | solution.py:849
  25.7 2.2 %shard_map.33 = (f32[128,4,128]{2,1,0:T(4,128)S(1)}, f32[3,16,8,128]{3,2,1,0:T(8,128)S(1)}, f32[3,8,8,128]{3,2,1,0:T(8,128)S(1)}) custom-call(f32[4,8,8,128]{3,2,1,0:T(8,128)S(1)} %get-tuple-element.34.main, f32[4,8,8,128]{3,2,1,0:T(8,128)S(1)} %collective-permute-done.2.main_near, f32[4,8,8,128]{3,2,1,0:T(8,128)S(1)} %collective-permute-done.3.main_far, ...), custom_call_target="tpu_custom_call" | custom-call | flops 1000000 | bytes 4000000 | tf_op jit(solution)/shard_map/pallas_call | solution.py:851
  27.9 27.9 %all_to_all.5 = f32[128,4,128]{2,1,0:T(4,128)S(1)} all-to-all(f32[128,4,128]{2,1,0:T(4,128)S(1)} %get-tuple-element.40), channel_id=1, replica_groups={{0,2,4,6,8,10,12,14,16,18,20,22,24,26,28,30,32,34,36,38,40,42,44,46,48,..., dimensions={0} | all-to-all | bytes 524288 | tf_op jit(solution)/shard_map/all_to_all | solution.py:860
  55.8 3.3 %collective-permute-start.8 = (f32[128,4,128]{2,1,0:T(4,128)S(1)}, f32[128,4,128]{2,1,0:T(4,128)S(1)}, u32[]{:S(2)}, u32[]{:S(2)}) collective-permute-start(f32[128,4,128]{2,1,0:T(4,128)S(1)} %all_to_all.5), channel_id=1, source_target_pairs={{0,1},{1,0},{2,3},{3,2},{4,5},{5,4},{6,7},{7,6},{8,9},{9,8},{10,11... | collective-permute-start | bytes 786440 | tf_op jit(solution)/shard_map/ppermute | solution.py:864
  59.1 0.9 %shard_map.34.base = f32[3,32,16,128]{3,2,1,0:T(8,128)S(1)} custom-call(f32[3,34,24,128]{3,2,1,0:T(8,128)S(1)} %get-tuple-element.41.two, f32[3,16,16,128]{3,2,1,0:T(8,128)S(1)} %get-tuple-element.42.rim, f32[3,16,8,128]{3,2,1,0:T(8,128)S(1)} %get-tuple-element.43.e_one, f32[3,8,8,128]{3,2,1,0:T(8,128)S(1)} %get-tuple-element.44.e_two), custom_call_target="tpu_custom_call" | custom-call | flops 1000000 | bytes 4000000 | tf_op jit(solution)/shard_map/pallas_call | solution.py:863
  60.0 0.3 collective-permute-done.8
  60.2 4.1 %shard_map.35 = f32[3,32,16,128]{3,2,1,0:T(8,128)} custom-call(f32[512,128]{1,0:T(8,128)S(1)} %bitcast.2, f32[512,128]{1,0:T(8,128)S(1)} %bitcast.3, f32[3,32,16,128]{3,2,1,0:T(8,128)S(1)} %shard_map.34.base), custom_call_target="tpu_custom_call" | custom-call | flops 1000000 | bytes 4000000 | tf_op jit(solution)/shard_map/pallas_call | solution.py:865
Async XLA Ops:
  1.3 7.1 %collective-permute-start = (f32[12,32,128]{2,1,0:T(8,128)S(1)}, f32[12,32,128]{2,1,0:T(8,128)S(1)}, u32[]{:S(2)}, u32[]{:S(2)}) collective-permute-start(f32[12,32,128]{2,1,0:T(8,128)S(1)} %get-tuple-element.28), channel_id=1, source_target_pairs={{0,16},{16,0},{32,48},{48,32},{64,80},{80,64},{96,112},{112,96},{1... | collective-permute-start | bytes 589832 | tf_op jit(solution)/shard_map/ppermute | solution.py:818
  3.4 5.0 %collective-permute-start.1 = (f32[12,32,128]{2,1,0:T(8,128)S(1)}, f32[12,32,128]{2,1,0:T(8,128)S(1)}, u32[]{:S(2)}, u32[]{:S(2)}) collective-permute-start(f32[12,32,128]{2,1,0:T(8,128)S(1)} %get-tuple-element.29), channel_id=1, source_target_pairs={{0,1},{1,0},{2,3},{3,2},{4,5},{5,4},{6,7},{7,6},{8,9},{9,8},{10,11... | collective-permute-start | bytes 589832 | tf_op jit(solution)/shard_map/ppermute | solution.py:819
  8.7 8.2 %collective-permute-start.4 = (f32[4,4,24,128]{3,2,1,0:T(8,128)S(1)}, f32[4,4,24,128]{3,2,1,0:T(8,128)S(1)}, u32[]{:S(2)}, u32[]{:S(2)}) collective-permute-start(f32[4,4,24,128]{3,2,1,0:T(8,128)S(1)} %get-tuple-element.37), channel_id=1, source_target_pairs={{0,1},{1,0},{2,3},{3,2},{4,5},{5,4},{6,7},{7,6},{8,9},{9,8},{10,11... | collective-permute-start | bytes 589832 | tf_op jit(solution)/shard_map/ppermute | solution.py:830
  10.7 6.3 %collective-permute-start.5 = (f32[4,4,24,128]{3,2,1,0:T(8,128)S(1)}, f32[4,4,24,128]{3,2,1,0:T(8,128)S(1)}, u32[]{:S(2)}, u32[]{:S(2)}) collective-permute-start(f32[4,4,24,128]{3,2,1,0:T(8,128)S(1)} %get-tuple-element.38), channel_id=1, source_target_pairs={{0,16},{1,2},{2,1},{3,4},{4,3},{5,6},{6,5},{7,8},{8,7},{9,10},{10,... | collective-permute-start | bytes 589832 | tf_op jit(solution)/shard_map/ppermute | solution.py:829
  13.5 10.3 %collective-permute-start.3 = (f32[4,8,8,128]{3,2,1,0:T(8,128)S(1)}, f32[4,8,8,128]{3,2,1,0:T(8,128)S(1)}, u32[]{:S(2)}, u32[]{:S(2)}) collective-permute-start(f32[4,8,8,128]{3,2,1,0:T(8,128)S(1)} %get-tuple-element.34.main), channel_id=1, source_target_pairs={{0,1},{1,0},{2,3},{3,2},{4,5},{5,4},{6,7},{7,6},{8,9},{9,8},{10,11... | collective-permute-start | bytes 393224 | tf_op jit(solution)/shard_map/ppermute | solution.py:839
  14.8 8.9 %collective-permute-start.2 = (f32[4,8,8,128]{3,2,1,0:T(8,128)S(1)}, f32[4,8,8,128]{3,2,1,0:T(8,128)S(1)}, u32[]{:S(2)}, u32[]{:S(2)}) collective-permute-start(f32[4,8,8,128]{3,2,1,0:T(8,128)S(1)} %get-tuple-element.34.main), channel_id=1, source_target_pairs={{0,16},{16,0},{32,48},{48,32},{64,80},{80,64},{96,112},{112,96},{1... | collective-permute-start | bytes 393224 | tf_op jit(solution)/shard_map/ppermute | solution.py:838
  19.2 4.6 %collective-permute-start.7 = (f32[4,4,8,128]{3,2,1,0:T(8,128)S(1)}, f32[4,4,8,128]{3,2,1,0:T(8,128)S(1)}, u32[]{:S(2)}, u32[]{:S(2)}) collective-permute-start(f32[4,4,8,128]{3,2,1,0:T(8,128)S(1)} %get-tuple-element.39.rim), channel_id=1, source_target_pairs={{0,1},{1,0},{2,3},{3,2},{4,5},{5,4},{6,7},{7,6},{8,9},{9,8},{10,11... | collective-permute-start | bytes 196616 | tf_op jit(solution)/shard_map/ppermute | solution.py:850
  21.2 4.4 %collective-permute-start.6 = (f32[4,4,8,128]{3,2,1,0:T(8,128)S(1)}, f32[4,4,8,128]{3,2,1,0:T(8,128)S(1)}, u32[]{:S(2)}, u32[]{:S(2)}) collective-permute-start(f32[4,4,8,128]{3,2,1,0:T(8,128)S(1)} %get-tuple-element.39.rim), channel_id=1, source_target_pairs={{0,16},{16,0},{32,48},{48,32},{64,80},{80,64},{96,112},{112,96},{1... | collective-permute-start | bytes 196616 | tf_op jit(solution)/shard_map/ppermute | solution.py:849
  55.8 4.5 %collective-permute-start.8 = (f32[128,4,128]{2,1,0:T(4,128)S(1)}, f32[128,4,128]{2,1,0:T(4,128)S(1)}, u32[]{:S(2)}, u32[]{:S(2)}) collective-permute-start(f32[128,4,128]{2,1,0:T(4,128)S(1)} %all_to_all.5), channel_id=1, source_target_pairs={{0,1},{1,0},{2,3},{3,2},{4,5},{5,4},{6,7},{7,6},{8,9},{9,8},{10,11... | collective-permute-start | bytes 786440 | tf_op jit(solution)/shard_map/ppermute | solution.py:864

commit v18 on v16

--- a/solution.py
+++ b/solution.py
@@ -281,7 +281,7 @@
                 ref[f, z + 1, 0:8, :] = source[f, z + 1, 16:24, :]
                 ref[f, z + 1, 16:24, :] = source[f, z + 1, 8:16, :]
 
-    loop(32, fill, 16)
+    loop(32, fill, 32)
     upper = iota((8, 128), 0) < 4
 
     def both(ref, lead, step, shift=0):
@@ -460,7 +460,7 @@
                     own = jnp.where(lane < 3, low, jnp.where(lane >= 125, high, own))
                     base[f, at] = own + spread[f, k + 8 * half]
 
-    loop(8, pair, 4)
+    loop(8, pair, 8)
 
 
 def resist(share):

time: 64.5 us -> 64.5 us (level)
  transfers between devices with their start and end apart: 9 -> 9, of which waited for: 2 -> 2; matrix products, arithmetic and copies ran while one was open for 0% -> 0% of each run, Pallas kernels for 14% -> 13%
where the time goes in v18:
time: 64.5 us; the launch traced here: 64.4 us
  blocking collectives  27.9 us (43%)
  starting transfers between devices  17.6 us (27%)
  Pallas kernels  16.1 us (25%)
  waiting for transfers between devices  2.52 us (4%)
    all_to_all x1, blocking collectives, local(): lax.all_to_all(sent, ('gx', 'gy'), split_axis=0, concat_axis=0, axis_inde...  27.9 us
    pallas_call x1, Pallas kernels, local(): call(top_kernel, [(3, 32, 16, 128)], [(4, 2, 128, 128), (3, 16, 16, 128),...  4 us
    pallas_call x1, Pallas kernels, local(): call(own_kernel, [(3, 34, 32, 128)] * 2 + [(4, 16, 16, 128)] + [(4, 4, 16...  3.66 us
    ppermute x1, starting transfers between devices, local(): other = lax.ppermute(mine, 'gy', swap_near)  3.3 us
    ppermute x1, starting transfers between devices, local(): rim_near = lax.ppermute(rim_one, 'gx', swap_near)  2.56 us
    pallas_call x1, Pallas kernels, local(): call(rim_kernel, [(3, 16, 16, 128), (4, 4, 8, 128)], [(3, 18, 32, 128), (...  2.24 us
    pallas_call x1, Pallas kernels, local(): call(middle_kernel, [(CHIPS, 4, 128), (3, 16, 8, 128), (3, 8, 8, 128)], [...  2.22 us
    ppermute x1, starting transfers between devices, local(): from_near = lax.ppermute(to_near, 'gx', swap_near)  2.13 us
  transfers between devices with their start and end apart: 9, of which 2 were waited for; matrix products, arithmetic and copies ran while one was open for 0% of the time, Pallas kernels for 13%

profile of v18, /device:TPU:1, one launch (start us, length us, event | category | flops | bytes accessed | tf_op | source)
XLA Modules:
  0.0 64.4 jit_solution(16058477855902197202)
XLA Ops:
  0.0 1.3 %shard_map.28 = (f32[12,32,128]{2,1,0:T(8,128)S(1)}, f32[12,32,128]{2,1,0:T(8,128)S(1)}, f32[4,32,16,128]{3,2,1,0:T(8,128)S(1)}) custom-call(f32[3,32,16,128]{3,2,1,0:T(8,128)} %guess.1, s32[32,16,128]{2,1,0:T(8,128)} %labels.1), custom_call_target="tpu_custom_call" | custom-call | flops 1000000 | bytes 4000000 | tf_op jit(solution)/shard_map/pallas_call | solution.py:811
  1.3 2.1 %collective-permute-start = (f32[12,32,128]{2,1,0:T(8,128)S(1)}, f32[12,32,128]{2,1,0:T(8,128)S(1)}, u32[]{:S(2)}, u32[]{:S(2)}) collective-permute-start(f32[12,32,128]{2,1,0:T(8,128)S(1)} %get-tuple-element.28), channel_id=1, source_target_pairs={{0,16},{16,0},{32,48},{48,32},{64,80},{80,64},{96,112},{112,96},{1... | collective-permute-start | bytes 589832 | tf_op jit(solution)/shard_map/ppermute | solution.py:817
  3.4 1.3 %collective-permute-start.1 = (f32[12,32,128]{2,1,0:T(8,128)S(1)}, f32[12,32,128]{2,1,0:T(8,128)S(1)}, u32[]{:S(2)}, u32[]{:S(2)}) collective-permute-start(f32[12,32,128]{2,1,0:T(8,128)S(1)} %get-tuple-element.29), channel_id=1, source_target_pairs={{0,1},{1,0},{2,3},{3,2},{4,5},{5,4},{6,7},{7,6},{8,9},{9,8},{10,11... | collective-permute-start | bytes 589832 | tf_op jit(solution)/shard_map/ppermute | solution.py:818
  4.7 3.7 %shard_map.29 = (f32[3,34,32,128]{3,2,1,0:T(8,128)S(1)}, f32[3,34,32,128]{3,2,1,0:T(8,128)S(1)}, f32[4,16,16,128]{3,2,1,0:T(8,128)S(1)}, f32[4,4,16,128]{3,2,1,0...) custom-call(f32[4,32,16,128]{3,2,1,0:T(8,128)S(1)} %get-tuple-element.25.own), custom_call_target="tpu_custom_call" | custom-call | flops 20000000 | bytes 4000000 | tf_op jit(solution)/shard_map/pallas_call | solution.py:819
  8.4 0.0 collective-permute-done.x_near
  8.4 0.0 collective-permute-done.1.x_far
  8.4 0.3 shard_map.30
  8.7 2.0 %collective-permute-start.4 = (f32[4,4,24,128]{3,2,1,0:T(8,128)S(1)}, f32[4,4,24,128]{3,2,1,0:T(8,128)S(1)}, u32[]{:S(2)}, u32[]{:S(2)}) collective-permute-start(f32[4,4,24,128]{3,2,1,0:T(8,128)S(1)} %get-tuple-element.37), channel_id=1, source_target_pairs={{0,1},{1,0},{2,3},{3,2},{4,5},{5,4},{6,7},{7,6},{8,9},{9,8},{10,11... | collective-permute-start | bytes 589832 | tf_op jit(solution)/shard_map/ppermute | solution.py:829
  10.7 0.9 %collective-permute-start.5 = (f32[4,4,24,128]{3,2,1,0:T(8,128)S(1)}, f32[4,4,24,128]{3,2,1,0:T(8,128)S(1)}, u32[]{:S(2)}, u32[]{:S(2)}) collective-permute-start(f32[4,4,24,128]{3,2,1,0:T(8,128)S(1)} %get-tuple-element.38), channel_id=1, source_target_pairs={{0,16},{1,2},{2,1},{3,4},{4,3},{5,6},{6,5},{7,8},{8,7},{9,10},{10,... | collective-permute-start | bytes 589832 | tf_op jit(solution)/shard_map/ppermute | solution.py:828
  11.5 1.9 %shard_map.31 = (f32[3,34,24,128]{3,2,1,0:T(8,128)S(1)}, f32[4,8,8,128]{3,2,1,0:T(8,128)S(1)}, f32[4,16,8,128]{3,2,1,0:T(8,128)S(1)}) custom-call(f32[4,32,16,128]{3,2,1,0:T(8,128)S(1)} %get-tuple-element.25.own, f32[4,32,8,128]{3,2,1,0:T(8,128)S(1)} %get-tuple-element.30.rim, f32[3,34,32,128]{3,2,1,0:T(8,128)S(1)} %get-tuple-element.31.own_one, ...), custom_call_target="tpu_custom_call" | custom-call | flops 10000000 | bytes 4000000 | tf_op jit(solution)/shard_map/pallas_call | solution.py:830
  13.5 1.4 %collective-permute-start.3 = (f32[4,8,8,128]{3,2,1,0:T(8,128)S(1)}, f32[4,8,8,128]{3,2,1,0:T(8,128)S(1)}, u32[]{:S(2)}, u32[]{:S(2)}) collective-permute-start(f32[4,8,8,128]{3,2,1,0:T(8,128)S(1)} %get-tuple-element.34.main), channel_id=1, source_target_pairs={{0,1},{1,0},{2,3},{3,2},{4,5},{5,4},{6,7},{7,6},{8,9},{9,8},{10,11... | collective-permute-start | bytes 393224 | tf_op jit(solution)/shard_map/ppermute | solution.py:838
  14.8 2.1 %collective-permute-start.2 = (f32[4,8,8,128]{3,2,1,0:T(8,128)S(1)}, f32[4,8,8,128]{3,2,1,0:T(8,128)S(1)}, u32[]{:S(2)}, u32[]{:S(2)}) collective-permute-start(f32[4,8,8,128]{3,2,1,0:T(8,128)S(1)} %get-tuple-element.34.main), channel_id=1, source_target_pairs={{0,16},{16,0},{32,48},{48,32},{64,80},{80,64},{96,112},{112,96},{1... | collective-permute-start | bytes 393224 | tf_op jit(solution)/shard_map/ppermute | solution.py:837
  16.9 0.0 collective-permute-done.4.near
  16.9 0.0 collective-permute-done.5.far
  16.9 2.2 %shard_map.32 = (f32[3,16,16,128]{3,2,1,0:T(8,128)S(1)}, f32[4,4,8,128]{3,2,1,0:T(8,128)S(1)}) custom-call(f32[4,16,16,128]{3,2,1,0:T(8,128)S(1)} %get-tuple-element.35.edges, f32[4,16,8,128]{3,2,1,0:T(8,128)S(1)} %get-tuple-element.36.edges_rim, f32[4,4,24,128]{3,2,1,0:T(8,128)S(1)} %collective-permute-done.4.near, ...), custom_call_target="tpu_custom_call" | custom-call | flops 10000000 | bytes 4000000 | tf_op jit(solution)/shard_map/pallas_call | solution.py:839
  19.1 2.1 %collective-permute-start.7 = (f32[4,4,8,128]{3,2,1,0:T(8,128)S(1)}, f32[4,4,8,128]{3,2,1,0:T(8,128)S(1)}, u32[]{:S(2)}, u32[]{:S(2)}) collective-permute-start(f32[4,4,8,128]{3,2,1,0:T(8,128)S(1)} %get-tuple-element.39.rim), channel_id=1, source_target_pairs={{0,1},{1,0},{2,3},{3,2},{4,5},{5,4},{6,7},{7,6},{8,9},{9,8},{10,11... | collective-permute-start | bytes 196616 | tf_op jit(solution)/shard_map/ppermute | solution.py:849
  21.2 2.6 %collective-permute-start.6 = (f32[4,4,8,128]{3,2,1,0:T(8,128)S(1)}, f32[4,4,8,128]{3,2,1,0:T(8,128)S(1)}, u32[]{:S(2)}, u32[]{:S(2)}) collective-permute-start(f32[4,4,8,128]{3,2,1,0:T(8,128)S(1)} %get-tuple-element.39.rim), channel_id=1, source_target_pairs={{0,16},{16,0},{32,48},{48,32},{64,80},{80,64},{96,112},{112,96},{1... | collective-permute-start | bytes 196616 | tf_op jit(solution)/shard_map/ppermute | solution.py:848
  23.8 0.0 collective-permute-done.3.main_far
  23.8 0.0 collective-permute-done.2.main_near
  23.8 0.0 collective-permute-done.7.rim_far
  23.8 1.9 %collective-permute-done.6.rim_near = f32[4,4,8,128]{3,2,1,0:T(8,128)S(1)} collective-permute-done((f32[4,4,8,128]{3,2,1,0:T(8,128)S(1)}, f32[4,4,8,128]{3,2,1,0:T(8,128)S(1)}, u32[]{:S(2)}, u32[]{:S(2)}) %collective-permute-start.6) | collective-permute-done | bytes 65568 | tf_op jit(solution)/shard_map/ppermute | solution.py:848
  25.6 2.2 %shard_map.33 = (f32[128,4,128]{2,1,0:T(4,128)S(1)}, f32[3,16,8,128]{3,2,1,0:T(8,128)S(1)}, f32[3,8,8,128]{3,2,1,0:T(8,128)S(1)}) custom-call(f32[4,8,8,128]{3,2,1,0:T(8,128)S(1)} %get-tuple-element.34.main, f32[4,8,8,128]{3,2,1,0:T(8,128)S(1)} %collective-permute-done.2.main_near, f32[4,8,8,128]{3,2,1,0:T(8,128)S(1)} %collective-permute-done.3.main_far, ...), custom_call_target="tpu_custom_call" | custom-call | flops 1000000 | bytes 4000000 | tf_op jit(solution)/shard_map/pallas_call | solution.py:850
  27.8 27.9 %all_to_all.5 = f32[128,4,128]{2,1,0:T(4,128)S(1)} all-to-all(f32[128,4,128]{2,1,0:T(4,128)S(1)} %get-tuple-element.40), channel_id=1, replica_groups={{0,2,4,6,8,10,12,14,16,18,20,22,24,26,28,30,32,34,36,38,40,42,44,46,48,..., dimensions={0} | all-to-all | bytes 524288 | tf_op jit(solution)/shard_map/all_to_all | solution.py:859
  55.8 3.3 %collective-permute-start.8 = (f32[128,4,128]{2,1,0:T(4,128)S(1)}, f32[128,4,128]{2,1,0:T(4,128)S(1)}, u32[]{:S(2)}, u32[]{:S(2)}) collective-permute-start(f32[128,4,128]{2,1,0:T(4,128)S(1)} %all_to_all.5), channel_id=1, source_target_pairs={{0,1},{1,0},{2,3},{3,2},{4,5},{5,4},{6,7},{7,6},{8,9},{9,8},{10,11... | collective-permute-start | bytes 786440 | tf_op jit(solution)/shard_map/ppermute | solution.py:863
  59.1 0.5 shard_map.34.base
  59.6 0.6 %collective-permute-done.8 = f32[128,4,128]{2,1,0:T(4,128)S(1)} collective-permute-done((f32[128,4,128]{2,1,0:T(4,128)S(1)}, f32[128,4,128]{2,1,0:T(4,128)S(1)}, u32[]{:S(2)}, u32[]{:S(2)}) %collective-permute-start.8) | collective-permute-done | bytes 262176 | tf_op jit(solution)/shard_map/ppermute | solution.py:863
  60.2 4.0 %shard_map.35 = f32[3,32,16,128]{3,2,1,0:T(8,128)} custom-call(f32[512,128]{1,0:T(8,128)S(1)} %bitcast.2, f32[512,128]{1,0:T(8,128)S(1)} %bitcast.3, f32[3,32,16,128]{3,2,1,0:T(8,128)S(1)} %shard_map.34.base), custom_call_target="tpu_custom_call" | custom-call | flops 1000000 | bytes 4000000 | tf_op jit(solution)/shard_map/pallas_call | solution.py:864
Async XLA Ops:
  1.3 7.1 %collective-permute-start = (f32[12,32,128]{2,1,0:T(8,128)S(1)}, f32[12,32,128]{2,1,0:T(8,128)S(1)}, u32[]{:S(2)}, u32[]{:S(2)}) collective-permute-start(f32[12,32,128]{2,1,0:T(8,128)S(1)} %get-tuple-element.28), channel_id=1, source_target_pairs={{0,16},{16,0},{32,48},{48,32},{64,80},{80,64},{96,112},{112,96},{1... | collective-permute-start | bytes 589832 | tf_op jit(solution)/shard_map/ppermute | solution.py:817
  3.4 5.0 %collective-permute-start.1 = (f32[12,32,128]{2,1,0:T(8,128)S(1)}, f32[12,32,128]{2,1,0:T(8,128)S(1)}, u32[]{:S(2)}, u32[]{:S(2)}) collective-permute-start(f32[12,32,128]{2,1,0:T(8,128)S(1)} %get-tuple-element.29), channel_id=1, source_target_pairs={{0,1},{1,0},{2,3},{3,2},{4,5},{5,4},{6,7},{7,6},{8,9},{9,8},{10,11... | collective-permute-start | bytes 589832 | tf_op jit(solution)/shard_map/ppermute | solution.py:818
  8.7 8.2 %collective-permute-start.4 = (f32[4,4,24,128]{3,2,1,0:T(8,128)S(1)}, f32[4,4,24,128]{3,2,1,0:T(8,128)S(1)}, u32[]{:S(2)}, u32[]{:S(2)}) collective-permute-start(f32[4,4,24,128]{3,2,1,0:T(8,128)S(1)} %get-tuple-element.37), channel_id=1, source_target_pairs={{0,1},{1,0},{2,3},{3,2},{4,5},{5,4},{6,7},{7,6},{8,9},{9,8},{10,11... | collective-permute-start | bytes 589832 | tf_op jit(solution)/shard_map/ppermute | solution.py:829
  10.7 6.2 %collective-permute-start.5 = (f32[4,4,24,128]{3,2,1,0:T(8,128)S(1)}, f32[4,4,24,128]{3,2,1,0:T(8,128)S(1)}, u32[]{:S(2)}, u32[]{:S(2)}) collective-permute-start(f32[4,4,24,128]{3,2,1,0:T(8,128)S(1)} %get-tuple-element.38), channel_id=1, source_target_pairs={{0,16},{1,2},{2,1},{3,4},{4,3},{5,6},{6,5},{7,8},{8,7},{9,10},{10,... | collective-permute-start | bytes 589832 | tf_op jit(solution)/shard_map/ppermute | solution.py:828
  13.5 10.3 %collective-permute-start.3 = (f32[4,8,8,128]{3,2,1,0:T(8,128)S(1)}, f32[4,8,8,128]{3,2,1,0:T(8,128)S(1)}, u32[]{:S(2)}, u32[]{:S(2)}) collective-permute-start(f32[4,8,8,128]{3,2,1,0:T(8,128)S(1)} %get-tuple-element.34.main), channel_id=1, source_target_pairs={{0,1},{1,0},{2,3},{3,2},{4,5},{5,4},{6,7},{7,6},{8,9},{9,8},{10,11... | collective-permute-start | bytes 393224 | tf_op jit(solution)/shard_map/ppermute | solution.py:838
  14.8 8.9 %collective-permute-start.2 = (f32[4,8,8,128]{3,2,1,0:T(8,128)S(1)}, f32[4,8,8,128]{3,2,1,0:T(8,128)S(1)}, u32[]{:S(2)}, u32[]{:S(2)}) collective-permute-start(f32[4,8,8,128]{3,2,1,0:T(8,128)S(1)} %get-tuple-element.34.main), channel_id=1, source_target_pairs={{0,16},{16,0},{32,48},{48,32},{64,80},{80,64},{96,112},{112,96},{1... | collective-permute-start | bytes 393224 | tf_op jit(solution)/shard_map/ppermute | solution.py:837
  19.1 4.6 %collective-permute-start.7 = (f32[4,4,8,128]{3,2,1,0:T(8,128)S(1)}, f32[4,4,8,128]{3,2,1,0:T(8,128)S(1)}, u32[]{:S(2)}, u32[]{:S(2)}) collective-permute-start(f32[4,4,8,128]{3,2,1,0:T(8,128)S(1)} %get-tuple-element.39.rim), channel_id=1, source_target_pairs={{0,1},{1,0},{2,3},{3,2},{4,5},{5,4},{6,7},{7,6},{8,9},{9,8},{10,11... | collective-permute-start | bytes 196616 | tf_op jit(solution)/shard_map/ppermute | solution.py:849
  21.2 4.4 %collective-permute-start.6 = (f32[4,4,8,128]{3,2,1,0:T(8,128)S(1)}, f32[4,4,8,128]{3,2,1,0:T(8,128)S(1)}, u32[]{:S(2)}, u32[]{:S(2)}) collective-permute-start(f32[4,4,8,128]{3,2,1,0:T(8,128)S(1)} %get-tuple-element.39.rim), channel_id=1, source_target_pairs={{0,16},{16,0},{32,48},{48,32},{64,80},{80,64},{96,112},{112,96},{1... | collective-permute-start | bytes 196616 | tf_op jit(solution)/shard_map/ppermute | solution.py:848
  55.8 4.5 %collective-permute-start.8 = (f32[128,4,128]{2,1,0:T(4,128)S(1)}, f32[128,4,128]{2,1,0:T(4,128)S(1)}, u32[]{:S(2)}, u32[]{:S(2)}) collective-permute-start(f32[128,4,128]{2,1,0:T(4,128)S(1)} %all_to_all.5), channel_id=1, source_target_pairs={{0,1},{1,0},{2,3},{3,2},{4,5},{5,4},{6,7},{7,6},{8,9},{9,8},{10,11... | collective-permute-start | bytes 786440 | tf_op jit(solution)/shard_map/ppermute | solution.py:863
